TPU v7x, 32 devices: a whole 2x2x4 slice. The times are simulated.
32 devices in a mesh: dp: 8 (over z, core), tensor: 4 (over y, x).
Axes of the slice: x: 2, y: 2, z: 4, core: 2. Of those that a mesh axis runs over, the one named last changes fastest.
Arguments:
- features: bfloat16 [4096, 6144], P('tensor', 'dp'), may hold values from -6 to 6
- cotangent: bfloat16 [4096, 6144], P('tensor', 'dp'), may hold values from -6 to 6
- up_blocks: bfloat16 [16, 256, 1024], P('tensor'), may hold values from -0.375 to 0.375
- down_blocks: bfloat16 [16, 1024, 256], P('tensor'), may hold values from -0.1875 to 0.1875
Outputs:
- outputs: bfloat16 [4096, 6144], P('tensor', 'dp')
- feature_grads: bfloat16 [4096, 6144], P('tensor', 'dp')
- up_grads: float32 [16, 256, 1024], P('tensor', 'dp')
- down_grads: float32 [16, 1024, 256], P('tensor', 'dp')
All inputs are finite; a program needn't handle non-finite values.
Results may differ from a plain program's by a relative error of at most 0.015.
Values may be sent and summed in bfloat16 or wider, within the bound.
No kernel may reach another device: no remote copies, remote signals or barrier semaphores. Data moves between devices by JAX's collectives and lax.ppermute only.
A program may use at most 64 MiB of HBM per device.

v0:
```python
import math

import jax
import jax.numpy as jnp
from jax import lax
from jax.sharding import PartitionSpec as P

BLOCKS = 16
SUB = 64


INV_ROOT2 = 0.7071067811865476
INV_ROOT2PI = 0.3989422804014327


def gelu_value(value):
    return 0.5 * value * (1.0 + lax.erf(value * INV_ROOT2))


def gelu_slope(value):
    return (
        0.5 * (1.0 + lax.erf(value * INV_ROOT2))
        + value * jnp.exp(-0.5 * value * value) * INV_ROOT2PI
    )


def on_device(features, cotangent, up_blocks, down_blocks):
    local_blocks = up_blocks.shape[0]
    block_feat = up_blocks.shape[1]
    block_hidden = up_blocks.shape[2]
    tokens_here = features.shape[1]
    factor = 1.0 / math.sqrt(tokens_here * lax.axis_size("dp"))
    x_local = features.reshape(local_blocks, block_feat, tokens_here)
    dy_local = cotangent.reshape(local_blocks, block_feat, tokens_here)
    down_four = down_blocks.reshape(local_blocks, BLOCKS, SUB, block_feat)
    preact = jnp.einsum(
        "bdn,bdf->bfn", x_local, up_blocks, preferred_element_type=jnp.float32
    ).astype(jnp.bfloat16)
    pre_wide = preact.astype(jnp.float32)
    hidden = (
        gelu_value(pre_wide).astype(jnp.bfloat16).reshape(local_blocks, BLOCKS, SUB, tokens_here)
    )
    mixed = lax.all_to_all(hidden, "tensor", split_axis=1, concat_axis=0, tiled=True)
    out_three = jnp.einsum(
        "ijsn,jise->jen", mixed, down_four, preferred_element_type=jnp.float32
    ).astype(jnp.bfloat16)
    outputs = out_three.reshape(local_blocks * block_feat, tokens_here)
    down_term = jnp.einsum("ijsn,jen->isje", mixed, dy_local, preferred_element_type=jnp.float32)
    down_term = down_term.reshape(block_hidden, local_blocks, block_feat)
    back = jnp.einsum(
        "jen,jise->ijsn", dy_local, down_four, preferred_element_type=jnp.float32
    ).astype(jnp.bfloat16)
    back_home = lax.all_to_all(back, "tensor", split_axis=0, concat_axis=1, tiled=True)
    back_home = back_home.reshape(local_blocks, block_hidden, tokens_here)
    slope = (back_home.astype(jnp.float32) * gelu_slope(pre_wide)).astype(jnp.bfloat16)
    up_term = jnp.einsum("bdn,bfn->dbf", x_local, slope, preferred_element_type=jnp.float32)
    up_share, down_share = (
        lax.psum_scatter(up_term, "dp", scatter_dimension=0, tiled=True),
        lax.psum_scatter(down_term, "dp", scatter_dimension=0, tiled=True),
    )
    dx_three = jnp.einsum(
        "bfn,bdf->bdn", slope, up_blocks, preferred_element_type=jnp.float32
    ).astype(jnp.bfloat16)
    feature_grads = dx_three.reshape(local_blocks * block_feat, tokens_here)
    up_grads = jnp.transpose(up_share, (1, 0, 2)) * factor
    down_grads = jnp.transpose(down_share, (1, 0, 2)) * factor
    return (outputs, feature_grads, up_grads, down_grads)


def solution(mesh):
    in_specs = (
        P("tensor", "dp"),
        P("tensor", "dp"),
        P("tensor", None, None),
        P("tensor", None, None),
    )
    out_specs = (
        P("tensor", "dp"),
        P("tensor", "dp"),
        P("tensor", "dp", None),
        P("tensor", "dp", None),
    )
    return jax.shard_map(
        on_device, mesh=mesh, in_specs=in_specs, out_specs=out_specs, check_vma=False
    )
```

profile of v0, /device:TPU:12, one launch (start us, length us, event | category | flops | bytes accessed | tf_op | source)
XLA Modules:
  0.0 281.4 jit_solution(14979877089805694914)
XLA Ops:
  7.2 0.0 copy-start
  7.2 4.0 %convert_bitcast_fusion = bf16[16,4,64,768]{3,2,0,1:T(8,128)(2,1)S(1)} fusion(bf16[4,16,64,256]{3,2,1,0:T(8,128)(2,1)} %bitcast.58, bf16[4,256,768,1]{2,1,3,0:T(8,128)(2,1)} %bitcast.56), kind=kOutput, calls=%fused_computation.14 | convolution fusion | flops 1613758464 | bytes 9961472 | tf_op jit(solution)/shard_map/jen,jise->ijsn/dot_general | solution.py:50
  11.2 0.7 copy.15
  11.9 73.2 %all_to_all.27 = bf16[16,4,64,768]{3,2,1,0:T(8,128)(2,1)S(1)} all-to-all(bf16[16,4,64,768]{3,2,1,0:T(8,128)(2,1)S(1)} %copy.15), channel_id=1, replica_groups=mesh['dp'=8,'tensor'=4] {'tensor'}, dimensions={0} | all-to-all | bytes 12582912 | tf_op jit(solution)/shard_map/all_to_all | solution.py:53
  85.1 0.0 copy-start.3
  85.1 6.3 %copy.16 = f32[4,4,4,64,768]{4,3,2,0,1:T(8,128)} copy(bf16[4,4,4,64,768]{4,3,2,1,0:T(8,128)(2,1)S(1)} %bitcast.53) | data formatting | bytes 18874368 | tf_op jit(solution)/shard_map/convert_element_type | solution.py:55
  91.4 0.0 copy-done
  91.4 0.0 copy-done.3
  91.4 12.4 %fusion.8 = (bf16[4,1024,768]{2,1,0:T(8,128)(2,1)}, bf16[4,1024,768]{2,1,0:T(8,128)(2,1)S(1)}) fusion(f32[4,4,4,64,768]{4,3,2,0,1:T(8,128)} %copy.16, bf16[4,256,1024]{2,1,0:T(8,128)(2,1)S(1)} %copy-done, bf16[4,256,768]{2,1,0:T(8,128)(2,1)S(1)} %bitcast.61), kind=kOutput, calls=%fused_computation.13 | convolution fusion | flops 1657798656 | bytes 28835840 | tf_op jit(solution)/shard_map/bdn,bdf->bfn/dot_general | solution.py:36
  103.8 3.0 %copy.13 = bf16[4,16,64,768]{3,2,0,1:T(8,128)(2,1)} copy(bf16[4,16,64,768]{3,2,1,0:T(8,128)(2,1)S(1)} %bitcast.55) | data formatting | bytes 12582912 | tf_op jit(solution)/shard_map/reshape | solution.py:41
  106.8 6.3 %all-to-all-start = ((bf16[4,16,64,768]{3,2,0,1:T(8,128)(2,1)}), bf16[4,16,64,768]{3,2,0,1:T(8,128)(2,1)}, u32[]{:S(2)}, u32[]{:S(2)}) async-start(bf16[4,16,64,768]{3,2,0,1:T(8,128)(2,1)} %copy.13), calls=%async_computation | async-start | bytes 12582912 | tf_op jit(solution)/shard_map/all_to_all | solution.py:43
  113.1 0.0 all-reduce.3.cloned.1.call-start
  113.1 7.1 %convolution_bitcast_fusion = f32[256,4,1024]{0,2,1:T(8,128)} fusion(bf16[4,1024,768]{2,1,0:T(8,128)(2,1)} %get-tuple-element.12, bf16[4,256,768]{2,1,0:T(8,128)(2,1)} %bitcast.60), kind=kOutput, calls=%fused_computation.17 | convolution fusion | flops 1610612736 | bytes 12058624 | tf_op jit(solution)/shard_map/bdn,bfn->dbf/dot_general | solution.py:56
  120.2 5.6 %copy.17 = f32[256,4,1024]{2,1,0:T(4,128)} copy(f32[256,4,1024]{0,2,1:T(8,128)} %convolution_bitcast_fusion) | data formatting | bytes 8388608 | tf_op jit(solution)/shard_map/bdn,bfn->dbf/transpose | solution.py:56
  125.8 0.0 all-reduce.3.cloned.1.call-update
  125.9 0.2 reduce-scatter.2.cloned.1.call-start
  126.1 55.1 %all-to-all-done = bf16[4,16,64,768]{3,2,0,1:T(8,128)(2,1)} async-done(((bf16[4,16,64,768]{3,2,0,1:T(8,128)(2,1)}), bf16[4,16,64,768]{3,2,0,1:T(8,128)(2,1)}, u32[]{:S(2)}, u32[]{:S(2)}) %all-to-all-start) | async-done | bytes 6291488 | tf_op jit(solution)/shard_map/all_to_all | solution.py:43
  181.2 3.6 %copy.14 = bf16[4,4,4,64,768]{4,3,0,1,2:T(8,128)(2,1)S(1)} copy(bf16[4,4,4,64,768]{4,3,0,2,1:T(8,128)(2,1)} %bitcast.2) | data formatting | bytes 12582912 | tf_op jit(solution)/shard_map/all_to_all | solution.py:43
  184.9 0.0 copy-start.1
  184.9 2.7 copy-done.1
  187.6 0.0 copy-done.2
  187.6 3.8 %fusion.10 = f32[4,16,64,256]{3,2,1,0:T(8,128)} fusion(bf16[16,4,64,768]{3,2,0,1:T(8,128)(2,1)S(1)} %bitcast.51, bf16[4,256,768,1]{2,1,3,0:T(8,128)(2,1)S(1)} %bitcast.57), kind=kOutput, calls=%fused_computation.22 | convolution fusion | flops 1610612736 | bytes 12058624 | tf_op jit(solution)/shard_map/ijsn,jen->isje/dot_general | solution.py:48
  191.4 0.0 reduce-scatter.2.cloned.1.call-update
  191.4 0.0 copy-done.4
  191.5 0.6 dynamic-slice
  192.7 5.8 %convolution_convert_fusion.1 = bf16[4,768,256]{1,2,0:T(8,128)(2,1)} fusion(bf16[4,256,1024]{2,1,0:T(8,128)(2,1)S(1)} %copy-done, bf16[4,1024,768]{2,1,0:T(8,128)(2,1)} %get-tuple-element.12), kind=kOutput, calls=%fused_computation.18 | convolution fusion | flops 1611399168 | bytes 9961472 | tf_op jit(solution)/shard_map/bfn,bdf->bdn/dot_general | solution.py:61
  198.5 25.1 %all-reduce.3.cloned.1.call-done = f32[256,4,1024]{2,1,0:T(4,128)} async-done(((f32[256,4,1024]{2,1,0:T(4,128)}), f32[256,4,1024]{2,1,0:T(4,128)}) %all-reduce.3.cloned.1.call-update) | async-done | bytes 4194320
  223.6 1.2 fusion.9
  224.8 1.1 copy.18
  225.9 6.4 %bitcast_convert_fusion = bf16[4,768,256]{1,2,0:T(8,128)(2,1)} fusion(bf16[16,4,64,768]{3,2,0,1:T(8,128)(2,1)} %bitcast.52, bf16[4,16,64,256]{3,2,1,0:T(8,128)(2,1)} %bitcast.59), kind=kOutput, calls=%fused_computation.16 | convolution fusion | flops 1611399168 | bytes 9961472 | tf_op jit(solution)/shard_map/ijsn,jise->jen/dot_general | solution.py:44
  232.3 40.3 %reduce-scatter.2.cloned.1.call-done = f32[128,4,256]{2,0,1:T(8,128)} async-done(((f32[1024,4,256]{2,0,1:T(8,128)}), f32[128,4,256]{2,0,1:T(8,128)}) %reduce-scatter.2.cloned.1.call-update) | async-done | bytes 524304 | tf_op jit(solution)/shard_map/reduce_scatter | solution.py:59
  272.6 1.9 multiply_bitcast_fusion
  (2 shorter events, 0.0 us)
Async XLA Ops:
  7.2 84.3 %copy-start = (bf16[4,256,1024]{2,1,0:T(8,128)(2,1)S(1)}, bf16[4,256,1024]{2,1,0:T(8,128)(2,1)}, u32[]{:S(2)}) copy-start(bf16[4,256,1024]{2,1,0:T(8,128)(2,1)} %param.6) | copy-start | bytes 6291460
  85.1 6.3 %copy-start.3 = (bf16[1024,768]{1,0:T(8,128)(2,1)S(1)}, bf16[1024,768]{1,0:T(8,128)(2,1)}, u32[]{:S(2)}) copy-start(bf16[1024,768]{1,0:T(8,128)(2,1)} %param.4) | copy-start | bytes 4718596
  106.8 74.4 %all-to-all-start = ((bf16[4,16,64,768]{3,2,0,1:T(8,128)(2,1)}), bf16[4,16,64,768]{3,2,0,1:T(8,128)(2,1)}, u32[]{:S(2)}, u32[]{:S(2)}) async-start(bf16[4,16,64,768]{3,2,0,1:T(8,128)(2,1)} %copy.13), calls=%async_computation | async-start | bytes 12582912 | tf_op jit(solution)/shard_map/all_to_all | solution.py:43
  113.1 110.5 %all-reduce.3.cloned.1.call-start = ((), (), s32[]{:S(2)}) async-start(), calls=%async_computation.4 | async-start | bytes 8388608
  125.9 146.8 %reduce-scatter.2.cloned.1.call-start = ((), (), s32[]{:S(2)}) async-start(), calls=%async_computation.3 | async-start | bytes 4718592 | tf_op jit(solution)/shard_map/reduce_scatter | solution.py:59
  181.2 6.3 %copy-start.2 = (bf16[1024,768]{1,0:T(8,128)(2,1)S(1)}, bf16[1024,768]{1,0:T(8,128)(2,1)}, u32[]{:S(2)}) copy-start(bf16[1024,768]{1,0:T(8,128)(2,1)} %param.5) | copy-start | bytes 4718596
  184.9 2.7 copy-start.1
  187.6 3.9 %copy-start.4 = (u32[32]{0:T(128)S(1)}, u32[32]{0:T(128)}, u32[]{:S(2)}) copy-start(u32[32]{0:T(128)} %constant.15) | copy-start | bytes 388
Sparse Core Ops, SparseCore 0:
  126.0 97.5 all-reduce.2
  225.9 46.6 reduce-scatter.1
where the time goes:
time: 287 us; the launch traced here: 281 us
  waiting for transfers between devices  121 us (42%)
  blocking collectives  73.2 us (26%)
  matrix products  39.5 us (14%)
  local copies, waits for them, and re-layouts  23.7 us (8%)
  between operations  14.7 us (5%)
  starting transfers between devices  6.53 us (2%)
  other arithmetic  3.07 us (1%)
    all_to_all x1, blocking collectives, on_device(): lax.all_to_all(back, 'tensor', split_axis=0, concat_axis=1, tiled=True)  73.2 us
    all_to_all x1, waiting for transfers between devices, on_device(): lax.all_to_all(hidden, 'tensor', split_axis=1, concat_axis=0, tiled=True)  55.1 us
    reduce_scatter x1, waiting for transfers between devices, on_device(): lax.psum_scatter(down_term, 'dp', scatter_dimension=0, tiled=True)  40.3 us
    unnamed x3, waiting for transfers between devices  25.2 us
    dot_general x1, matrix products, on_device(): jnp.einsum('bdn,bdf->bfn', x_local, up_blocks, preferred_element_type=jnp...  12.4 us
    dot_general x1, matrix products, on_device(): jnp.einsum('bdn,bfn->dbf', x_local, slope, preferred_element_type=jnp.flo...  7.11 us
    dot_general x1, matrix products, on_device(): jnp.einsum('ijsn,jise->jen', mixed, down_four, preferred_element_type=jnp...  6.39 us
    all_to_all x1, starting transfers between devices, on_device(): lax.all_to_all(hidden, 'tensor', split_axis=1, concat_axis=0, tiled=True)  6.31 us
  transfers between devices with their start and end apart: 3, of which 3 were waited for; matrix products, arithmetic and copies ran while one was open for 13% of the time, Pallas kernels for 0%

commit v1 on v0

v1 whole, which is shorter than its diff:
```python
import functools
import math

import jax
import jax.numpy as jnp
from jax import lax
from jax.experimental import pallas as pl
from jax.experimental.pallas import tpu as pltpu
from jax.sharding import PartitionSpec as P

BF16 = jnp.bfloat16
F32 = jnp.float32
INV_ROOT2 = 0.7071067811865476
INV_ROOT2PI = 0.3989422804014327
MIB = 1024 * 1024


def gelu_value(value):
    return 0.5 * value * (1.0 + lax.erf(value * INV_ROOT2))


def gelu_slope(value):
    return (
        0.5 * (1.0 + lax.erf(value * INV_ROOT2))
        + value * jnp.exp(-0.5 * value * value) * INV_ROOT2PI
    )


def generic_device(features, cotangent, up_blocks, down_blocks):
    local_blocks, block_feat, block_hidden = up_blocks.shape
    blocks = local_blocks * lax.axis_size("tensor")
    sub = block_hidden // blocks
    tokens_here = features.shape[1]
    factor = 1.0 / math.sqrt(tokens_here * lax.axis_size("dp"))
    x_local = features.reshape(local_blocks, block_feat, tokens_here)
    dy_local = cotangent.reshape(local_blocks, block_feat, tokens_here)
    down_four = down_blocks.reshape(local_blocks, blocks, sub, block_feat)
    preact = jnp.einsum("bdn,bdf->bfn", x_local, up_blocks, preferred_element_type=F32)
    pre_wide = preact.astype(BF16).astype(F32)
    hidden = gelu_value(pre_wide).astype(BF16).reshape(local_blocks, blocks, sub, tokens_here)
    mixed = lax.all_to_all(hidden, "tensor", split_axis=1, concat_axis=0, tiled=True)
    out_three = jnp.einsum("ijsn,jise->jen", mixed, down_four, preferred_element_type=F32)
    outputs = out_three.astype(BF16).reshape(local_blocks * block_feat, tokens_here)
    down_term = jnp.einsum("ijsn,jen->isje", mixed, dy_local, preferred_element_type=F32)
    down_term = down_term.reshape(block_hidden, local_blocks, block_feat)
    back = jnp.einsum("jen,jise->ijsn", dy_local, down_four, preferred_element_type=F32)
    back_home = lax.all_to_all(
        back.astype(BF16), "tensor", split_axis=0, concat_axis=1, tiled=True
    ).reshape(local_blocks, block_hidden, tokens_here)
    slope = (back_home.astype(F32) * gelu_slope(pre_wide)).astype(BF16)
    up_term = jnp.einsum("bdn,bfn->dbf", x_local, slope, preferred_element_type=F32)
    up_share = lax.psum_scatter(up_term, "dp", scatter_dimension=0, tiled=True)
    down_share = lax.psum_scatter(down_term, "dp", scatter_dimension=0, tiled=True)
    dx_three = jnp.einsum("bfn,bdf->bdn", slope, up_blocks, preferred_element_type=F32)
    feature_grads = dx_three.astype(BF16).reshape(local_blocks * block_feat, tokens_here)
    up_grads = jnp.transpose(up_share, (1, 0, 2)) * factor
    down_grads = jnp.transpose(down_share, (1, 0, 2)) * factor
    return (outputs, feature_grads, up_grads, down_grads)


def dot_tn(a, b):
    return lax.dot_general(a, b, (((0,), (0,)), ((), ())), preferred_element_type=F32)


def dot_nn(a, b):
    return lax.dot_general(a, b, (((1,), (0,)), ((), ())), preferred_element_type=F32)


def dot_nt(a, b):
    return lax.dot_general(a, b, (((1,), (1,)), ((), ())), preferred_element_type=F32)


def call(body, place, grid, ins, outs, mib, scratch=(), span=0.0):
    return pl.pallas_call(
        body,
        grid_spec=pltpu.PrefetchScalarGridSpec(
            num_scalar_prefetch=1,
            grid=grid,
            in_specs=[pl.BlockSpec(b, m) for _, b, m in ins],
            out_specs=[pl.BlockSpec(b, m) for _, _, b, m in outs],
            scratch_shapes=list(scratch),
        ),
        out_shape=[jax.ShapeDtypeStruct(s, d) for s, d, _, _ in outs],
        compiler_params=pltpu.CompilerParams(vmem_limit_bytes=mib * MIB),
        cost_estimate=pl.CostEstimate(
            flops=int(span * 1e9), bytes_accessed=0, transcendentals=0
        ),
    )(place, *[a for a, _, _ in ins])


def block_of(ref, block, where):
    at = []
    for size, extent, index in zip(block, ref.shape, where):
        if size == extent:
            at.append(slice(None))
        elif isinstance(index, int):
            at.append(slice(index * size, (index + 1) * size))
        else:
            at.append(pl.ds(pl.multiple_of(index * size, size), size))
    return ref.at[tuple(at)]


def call_once(body, place, steps, ins, outs, mib, scratch=(), span=0.0):
    def every_step(place, *refs):
        blocks = [(b, m) for _, b, m in ins] + [(b, m) for _, _, b, m in outs]
        held, rest = refs[: len(blocks)], refs[len(blocks) :]
        for step in range(steps):
            views = [block_of(ref, b, m(step, place)) for ref, (b, m) in zip(held, blocks)]
            body(step, steps, place, *views, *rest)

    return call(
        every_step,
        place,
        (1,),
        [whole(a) for a, _, _ in ins],
        [whole_out(s, d) for s, d, _, _ in outs],
        mib,
        scratch=scratch,
        span=span,
    )


def by_grid(body):
    return lambda place, *refs: body(pl.program_id(0), pl.num_programs(0), place, *refs)


def whole(array):
    rank = array.ndim
    return (array, array.shape, lambda *at: (0,) * rank)


def whole_out(shape, kind):
    rank = len(shape)
    return (shape, kind, shape, lambda *at: (0,) * rank)


def after(values, *earlier):
    return lax.optimization_barrier((tuple(values), earlier))[0]


def square(ref):
    block = ref[...]
    width = block.shape[-1]
    return block.reshape(block.size // width, width)


def hidden_body(place, x_ref, up_ref, hidden_ref, gate_ref):
    pre = dot_tn(square(up_ref), square(x_ref)).astype(BF16).astype(F32)
    half_cdf = 0.5 + 0.5 * lax.erf(pre * INV_ROOT2)
    gate = half_cdf + pre * jnp.exp(-0.5 * pre * pre) * INV_ROOT2PI
    hidden_ref[...] = (pre * half_cdf).astype(BF16).reshape(hidden_ref.shape)
    gate_ref[...] = gate.astype(BF16).reshape(gate_ref.shape)


def weights_body(place, *refs):
    low, core, out_ref = place[1] % 2, place[2], refs[-1]
    for at in range(2):
        out_ref[:, :, :, core * 2 + (low ^ at)] = refs[at][...]
        out_ref[:, :, :, (1 - core) * 2 + (low ^ at)] = refs[2 + at][...]


def halves(step, steps, work, lo, hi):
    if isinstance(step, int):
        work(*(lo if step < steps // 2 else hi))
        return
    pl.when(step < steps // 2)(functools.partial(work, *lo))
    pl.when(step >= steps // 2)(functools.partial(work, *hi))


def put_slope(cot, down_ref, gate_ref, slope_ref):
    back = dot_nn(square(down_ref), cot).astype(BF16).astype(F32)
    slope = (back * square(gate_ref).astype(F32)).astype(BF16)
    slope_ref[...] = slope.reshape(slope_ref.shape)


def slope_body(step, steps, place, cot_ref, down_ref, gate_ref, slope_ref):
    put_slope(square(cot_ref), down_ref, gate_ref, slope_ref)


def late_slopes_body(step, steps, place, own_ref, near_lo, near_hi, *refs):
    downs, gates, slopes = refs[:4], refs[4:8], refs[8:]
    put_slope(square(own_ref), downs[3], gates[3], slopes[3])

    def work(near_ref):
        for at in range(3):
            put_slope(square(near_ref), downs[at], gates[at], slopes[at])

    halves(step, steps, work, (near_lo,), (near_hi,))


def own_terms_body(step, steps, place, cot_ref, hid_ref, x_ref, slope_ref, give_ref, keep_ref, down_s, up_s):
    core = place[2]
    up_s[...] = dot_nt(square(x_ref), square(slope_ref)).astype(BF16).reshape(up_s.shape)
    count = up_s.shape[2]
    strip = slice(step * count, (step + 1) * count)
    give_ref[0, :, strip] = up_s[:, 1 - core]
    keep_ref[0, :, strip] = up_s[:, core]
    down_s[...] = dot_nt(square(hid_ref), square(cot_ref)).astype(BF16).reshape(down_s.shape)
    give_ref[1, step] = down_s[1 - core]
    keep_ref[1, step] = down_s[core]


def down_terms_body(step, steps, place, own_ref, near_lo, near_hi, sn, ns_lo, ns_hi, nn_lo, nn_hi, give_own, give_near, keep_ref, term_s):
    core = place[2]

    def put(pair, lo, hi, cot, give):
        term_s[0], term_s[1] = (dot_nt(v, cot).astype(BF16) for v in (lo, hi))
        give[...] = term_s[1 - core].reshape(give.shape)
        keep_ref[pair, 0] = term_s[core]

    def work(near_ref):
        own, near = square(own_ref), square(near_ref)
        mixed = square(sn)
        part = mixed.shape[0] // 2
        put(0, mixed[:part], mixed[part:], near, give_own)
        put(1, square(ns_lo), square(ns_hi), own, give_near.at[0])
        put(2, square(nn_lo), square(nn_hi), near, give_near.at[1])

    halves(step, steps, work, (near_lo,), (near_hi,))


def put_up_term(pair, core, x, slope_ref, give_ref, keep_ref, term_s):
    term_s[...] = dot_nt(x, square(slope_ref)).astype(BF16).reshape(term_s.shape)
    give_ref[pair] = term_s[:, 1 - core]
    keep_ref[pair] = term_s[:, core]


def up_terms_body(step, steps, place, x_ref, x_lo, x_hi, sn, lo_s, lo_n, hi_s, hi_n, give_lo, give_hi, keep_ref, term_s):
    def work(x_near, from_own, from_near, give_ref):
        near = square(x_near)
        for pair, (x, ref) in enumerate(((square(x_ref), sn), (near, from_own), (near, from_near))):
            put_up_term(pair, place[2], x, ref, give_ref, keep_ref, term_s)

    lo, hi = (x_lo, lo_s, lo_n, give_lo), (x_hi, hi_s, hi_n, give_hi)
    halves(step, steps, work, lo, hi)


def outputs_body(step, steps, place, d_own, d_lo, d_hi, hid_ref, lo_ref, hi_ref, *rest):
    total = dot_tn(square(d_own), square(hid_ref))
    total = total + dot_tn(square(d_lo), square(lo_ref))
    total = total + dot_tn(square(d_hi), square(hi_ref))
    for ref in rest[:-1]:
        total = total + ref[0].astype(F32)
    rest[-1][0] = total.astype(BF16)


def near_grads_body(step, steps, place, up_own, up_near, lo_s, lo_n, hi_s, hi_n, out_ref):
    def work(slope_own, slope_near):
        total = dot_nn(square(up_own), square(slope_own))
        total = total + dot_nn(square(up_near), square(slope_near))
        out_ref[0] = total.astype(BF16)

    halves(step, steps, work, (lo_s, lo_n), (hi_s, hi_n))


def grads_body(step, steps, place, up_own, up_near, slope_own, slope_near, add_ref, out_ref):
    total = dot_nn(square(up_own), square(slope_own)) + dot_nn(square(up_near), square(slope_near))
    out_ref[0] = (total + add_ref[0].astype(F32)).astype(BF16)


def down_meet_body(place, first, first_got, keep_ref, got_own, got_near, send_ref, mine_ref, total_s):
    stay = (place[0] ^ place[1]) & 1
    total_s[0, 0] = first[1].astype(F32) + first_got[1].astype(F32)
    total_s[0, 1] = keep_ref[0].astype(F32) + got_own[...].astype(F32)
    total_s[1] = keep_ref[1:].astype(F32) + got_near[...].astype(F32)
    mine_ref[...] = total_s[stay]
    send_ref[...] = total_s[1 - stay].astype(BF16)


def down_again_body(place, mine_ref, got_ref, send_ref, own_ref):
    stay = (place[0] // 2) ^ (place[1] // 2)
    own_ref[...] = mine_ref[stay] + got_ref[stay].astype(F32)
    send_ref[...] = (mine_ref[1 - stay] + got_ref[1 - stay].astype(F32)).astype(BF16)


def down_sum_body(factor, place, own_ref, got_ref, out_ref):
    out_ref[...] = ((own_ref[...] + got_ref[...].astype(F32)) * factor).astype(BF16)


def up_meet_body(parts, place, keep_ref, *refs):
    gots, sends, mine_ref = refs[:parts], refs[parts:-1], refs[-1]
    rows = gots[0].shape[2]
    for hop in range(4):
        there = place[1] ^ hop
        for at, got_ref in enumerate(gots):
            strip = slice(at * rows, (at + 1) * rows)
            total = keep_ref[:, there, strip].astype(F32) + got_ref[:, there].astype(F32)
            if hop % 2:
                sends[hop // 2][:, strip] = total.astype(BF16)
            else:
                mine_ref[hop // 2, :, strip] = total


def up_again_body(place, mine_ref, got_ref, got_far, send_ref, own_ref):
    send_ref[...] = (mine_ref[1] + got_far[...].astype(F32)).astype(BF16)
    own_ref[...] = mine_ref[0] + got_ref[...].astype(F32)


def up_sum_body(factor, place, first_ref, first_got, own_ref, got_ref, send_ref, mine_ref):
    mine_ref[0] = (first_ref[0] + first_got[0].astype(F32)) * factor
    total = (own_ref[...] + got_ref[...].astype(F32)) * factor
    mine_ref[1] = total[0]
    send_ref[...] = total[1:].astype(BF16)


def place_body(place, mine_ref, got_ref, down_in, up_ref, down_ref):
    down_ref[...] = down_in[...].astype(F32)
    width = mine_ref.shape[-1]
    for ref, side in ((mine_ref, 0), (got_ref, 1)):
        for at in range(2):
            where = place[0] ^ side ^ (2 * at)
            lanes = pl.ds(pl.multiple_of(where * width, width), width)
            up_ref[:, :, lanes] = ref[at].astype(F32).reshape(*up_ref.shape[:2], width)


def square_device(features, cotangent, up_blocks, down_blocks):
    local, feat, block_hidden = up_blocks.shape
    tokens = features.shape[1]
    n_dp, n_tensor = lax.axis_size("dp"), lax.axis_size("tensor")
    sub = block_hidden // (local * n_tensor)
    rows = local * sub
    half, part = local // 2, rows // 2
    factor = 1.0 / math.sqrt(tokens * n_dp)
    me = lax.axis_index("tensor").astype(jnp.int32)
    rank = lax.axis_index("dp").astype(jnp.int32)
    z, core = rank >> 1, rank & 1
    place = jnp.stack([me, z, core])
    x = features.reshape(local, feat, tokens)
    cot = cotangent.reshape(local, feat, tokens)
    one = (1, feat, tokens)
    blocks = (local, feat, tokens)
    every = lambda i, p: (i, 0, 0)
    least = lambda a, b: min(a, b) if isinstance(a, int) else jnp.minimum(a, b)
    most = lambda a, b: max(a, b) if isinstance(a, int) else jnp.maximum(a, b)
    low = lambda i, p: (least(i, half - 1), 0, 0)
    high = lambda i, p: (most(i - half, 0), 0, 0)

    def send(value, hop):
        return lax.ppermute(value, "tensor", [(t, t ^ hop) for t in range(n_tensor)])

    def send_z(value, hop):
        return lax.ppermute(value, "dp", [(d, d ^ (2 * hop)) for d in range(n_dp)])

    def send_core(value):
        return lax.ppermute(value, "dp", [(d, d ^ 1) for d in range(n_dp)])

    quarter = rows // 4
    at = (core * 2 + (z & 1)) * quarter
    to_x = jnp.stack(
        [
            lax.dynamic_slice(up_blocks, (0, at, (me ^ k) * rows), (local, quarter, rows))
            for k in (1, 3)
        ]
    )
    to_y = jnp.stack(
        [
            lax.dynamic_slice(down_blocks, (0, (me ^ k) * rows + at, 0), (local, quarter, feat))
            for k in (2, 3)
        ]
    )
    from_x, from_y = send(to_x, 1), send(to_y, 2)
    firsts = after((x[:half], x[half:], cot[:half], cot[half:]), to_x, to_y)
    x_lo, cot_lo = send(firsts[0], 1), send(firsts[2], 2)
    x_hi, cot_hi = send(firsts[1], 1), send(firsts[3], 2)

    def hidden_of(source, count, up, span):
        unit = (2, local, count, sub, tokens)
        block = (1, local, 1, sub, tokens)
        where = lambda j, i, p: (j, 0, i, 0, 0)
        return call(
            hidden_body,
            place,
            (2, count),
            [(source, one, lambda j, i, p: (i, 0, 0)), up],
            [(unit, BF16, block, where), (unit, BF16, block, where)],
            16,
        )

    hid, gate = hidden_of(
        x, local, (up_blocks, (1, feat, rows), lambda j, i, p: (i, 0, p[0] ^ (2 * j))), 0.0
    )
    from_x, from_y = after((from_x, from_y), hid)
    share = jnp.stack([from_x, from_y])
    share_z = send_z(share, 1)

    def unit_of(array, j):
        return (array, (1, 1) + array.shape[2:], lambda i, p: (j, i, 0, 0, 0))

    def down_of(j, which):
        if j == 0:
            if which == 0:
                return (down_blocks, (1, rows, feat), lambda i, p: (i, p[0], 0))
            return (
                down_blocks,
                (1, part, feat),
                lambda i, p: (i, 2 * (p[0] ^ 1) + which - 1, 0),
            )
        if which == 0:
            return (weights, (1, 1, 1, rows, feat), lambda i, p: (1, 0, i, 0, 0))
        return (weights, (1, 1, 1, part, feat), lambda i, p: (1, 1, i, which - 1, 0))

    def own_slope(which, array):
        return call_once(
            slope_body,
            place,
            local,
            [(cot, one, every), down_of(0, which), unit_of(array, 0)],
            [(array.shape[1:], BF16, (1,) + array.shape[2:], lambda i, p: (i, 0, 0, 0))],
            20,
        )[0]

    slope_ss = own_slope(0, gate)
    at_i = lambda i, p: (0, i, 0, 0)
    strip = (local, 1, sub, tokens)
    shard_u = (n_dp // 2, local * feat // n_dp, rows)

    def up_terms(body, ins, count, gives, span):
        block = (count, n_dp // 2, feat // n_dp, rows)
        wide = (count,) + shard_u
        part_u = (count, n_dp // 2, shard_u[1] // len(gives), rows)
        return call_once(
            body,
            place,
            local,
            ins,
            [
                (part_u, BF16, block, functools.partial(lambda m, i, p: (0, 0, m(i), 0), m))
                for m in gives
            ]
            + [(wide, BF16, block, lambda i, p: (0, 0, i, 0))],
            20,
            scratch=[pltpu.VMEM((n_dp // 2, 2, feat // n_dp, rows), BF16)],
            span=span,
        )

    def up_meet(count, keep, gots):
        piece = (count,) + shard_u[1:]
        return call(
            functools.partial(up_meet_body, len(gots)),
            place,
            (1,),
            [(v, (count,) + v.shape[1:], lambda i, p: (0, 0, 0, 0)) for v in (keep, *gots)],
            [whole_out(piece, BF16)] * 2 + [whole_out((2,) + piece, F32)],
            16,
        )

    def up_again(mine, got, far):
        piece = mine.shape[1:]
        return call(
            up_again_body,
            place,
            (1,),
            [whole(mine), whole(got), whole(far)],
            [whole_out(piece, BF16), whole_out(piece, F32)],
            16,
        )

    give_e, keep_e = call_once(
        own_terms_body,
        place,
        local,
        [
            (cot, one, every),
            unit_of(hid, 0),
            (x, one, every),
            (slope_ss, strip, at_i),
        ],
        [whole_out((2,) + shard_u, BF16)] * 2,
        20,
        scratch=[
            pltpu.VMEM((2, part, feat), BF16),
            pltpu.VMEM((n_dp // 2, 2, feat // n_dp, rows), BF16),
        ],
    )
    share, share_z, x_lo, cot_lo = after((share, share_z, x_lo, cot_lo), give_e)
    core_parts = after((share, share_z), x_lo, cot_lo)
    weights = call(
        weights_body,
        place,
        (1,),
        [whole(v) for v in (share, share_z, *map(send_core, core_parts))],
        [whole_out((2, 2, local, 4, quarter, feat), BF16)],
        16,
    )[0].reshape(2, 2, local, rows, feat)

    def near_hidden(source, which):
        up = (
            weights,
            (1, 1, 1, feat, rows),
            lambda j, i, p: (0, j, which * half + i, 0, 0),
        )
        return hidden_of(source, half, up, 0.0)

    give_e = after((give_e,), x_lo, cot_lo)[0]
    first_got = send_core(give_e)
    send_e, far_e, mine_e = up_meet(1, keep_e, [first_got])
    got_e, far_e = send_z(send_e, 1), send_z(far_e, 1)
    x_lo = after((x_lo,), weights, send_e)[0]
    hid_lo, gate_lo = near_hidden(x_lo, 0)
    slope_lo_s = own_slope(1, gate_lo)

    got_e, far_e = after((got_e, far_e), slope_lo_s)
    send_e, mine_e = up_again(mine_e, got_e, far_e)
    got_e = send_z(send_e, 2)

    x_hi, cot_hi = after((x_hi, cot_hi), got_e)
    hid_hi, gate_hi = near_hidden(x_hi, 1)

    def outputs_of(j, hid, adds):
        run = functools.partial(call, by_grid(outputs_body), place, (local,))
        if not adds:
            run = functools.partial(call_once, outputs_body, place, local)
        return run(
            [down_of(j, which) for which in range(3)]
            + [unit_of(array, j) for array in (hid, hid_lo, hid_hi)]
            + [(a, one, every) for a in adds],
            [(blocks, BF16, one, every)],
            16,
        )[0]

    shard = (2, 2, local, part, feat)
    strip_d = (1, part, feat)
    give_own, give_near, keep_d = call_once(
        down_terms_body,
        place,
        local,
        [(cot, one, every), (cot_lo, one, low), (cot_hi, one, high)]
        + [unit_of(hid, 1)]
        + [unit_of(array, j) for j in (0, 1) for array in (hid_lo, hid_hi)],
        [
            (shard[2:], BF16, strip_d, every),
            (shard[1:], BF16, (2,) + strip_d, lambda i, p: (0, i, 0, 0)),
            ((3,) + shard[2:], BF16, (3,) + strip_d, lambda i, p: (0, i, 0, 0)),
        ],
        16,
        scratch=[pltpu.VMEM((2, part, feat), BF16)],
    )
    core_own, core_near = send_core(give_own), send_core(give_near)
    hid_b = after((hid,), give_own)[0]
    near_out = outputs_of(1, hid_b, [])
    got_out = send(near_out, 2)
    core_own, core_near = after((core_own, core_near), near_out)
    parts_d = (keep_e, first_got, keep_d, core_own, core_near)
    send_d, mine_d = call(
        down_meet_body,
        place,
        (1,),
        [whole(v) for v in parts_d],
        [whole_out(shard[1:], BF16), whole_out(shard[1:], F32)],
        16,
        scratch=[pltpu.VMEM(shard, F32)],
    )
    got_d = send_z(send_d, 1)
    cot_b, *near_b = after((cot, cot_lo, cot_hi), send_d)
    late = [(1, 0, gate), (1, 1, gate_lo), (1, 2, gate_hi), (0, 2, gate_hi)]
    slope_sn, slope_lo_n, slope_hi_n, slope_hi_s = call_once(
        late_slopes_body,
        place,
        local,
        [(cot_b, one, every), (near_b[0], one, low), (near_b[1], one, high)]
        + [down_of(j, which) for j, which, _ in late]
        + [unit_of(array, j) for j, _, array in late],
        [
            (array.shape[1:], BF16, (1,) + array.shape[2:], lambda i, p: (i, 0, 0, 0))
            for _, _, array in late
        ],
        20,
    )

    at_lo = lambda i, p: (0, least(i, half - 1), 0, 0)
    at_hi = lambda i, p: (0, most(i - half, 0), 0, 0)
    near_up = lambda j: (weights, (1, 1, 1, feat, rows), lambda i, p: (0, j, i, 0, 0))
    near_grads = call_once(
        near_grads_body,
        place,
        local,
        [
            near_up(0),
            near_up(1),
            (slope_lo_s, strip, at_lo),
            (slope_lo_n, strip, at_lo),
            (slope_hi_s, strip, at_hi),
            (slope_hi_n, strip, at_hi),
        ],
        [(blocks, BF16, one, every)],
        16,
    )[0]
    got_grads = send(near_grads, 1)

    x_b = after((x,), near_grads)[0]
    give_lo, give_hi, keep_u = up_terms(
        up_terms_body,
        [(x_b, one, every), (x_lo, one, low), (x_hi, one, high), (slope_sn, strip, at_i)]
        + [(slope_lo_s, strip, at_lo), (slope_lo_n, strip, at_lo)]
        + [(slope_hi_s, strip, at_hi), (slope_hi_n, strip, at_hi)],
        3,
        [lambda i: least(i, half - 1), lambda i: most(i - half, 0)],
        16.0,
    )
    send_u, far_u, mine_u = up_meet(3, keep_u, [send_core(give_lo), send_core(give_hi)])
    got_u, far_u = send_z(send_u, 1), send_z(far_u, 1)

    got_d = after((got_d,), send_u)[0]
    send_d, mine_d = call(
        down_again_body,
        place,
        (1,),
        [whole(mine_d), whole(got_d)],
        [whole_out(shard[2:], BF16), whole_out(shard[2:], F32)],
        16,
    )
    got_d = send_z(send_d, 2)

    got_u, far_u = after((got_u, far_u), send_d)
    send_u, mine_u = up_again(mine_u, got_u, far_u)
    got_u = send_z(send_u, 2)

    got_d = after((got_d,), send_u)[0]
    sum_d = call(
        functools.partial(down_sum_body, factor),
        place,
        (1,),
        [whole(mine_d), whole(got_d)],
        [whole_out(shard[2:], BF16)],
        8,
    )[0]
    swaps = []
    for device in range(n_dp * n_tensor):
        dp, t = device // n_tensor, device % n_tensor
        z_high, y = dp // 4, t // 2
        swaps.append((device, (y * 4 + dp % 4) * n_tensor + z_high * 2 + t % 2))
    home_d = lax.ppermute(sum_d, ("dp", "tensor"), swaps)

    got_out = after((got_out,), sum_d)[0]
    outputs = outputs_of(0, hid, [got_out])

    got_u = after((got_u,), outputs)[0]
    send_u, mine_u = call(
        functools.partial(up_sum_body, factor),
        place,
        (1,),
        [whole(v) for v in (mine_e, got_e, mine_u, got_u)],
        [whole_out((2,) + shard_u[1:], BF16), whole_out((2,) + shard_u[1:], F32)],
        8,
    )
    got_u = send(send_u, 1)

    got_grads = after((got_grads,), send_u)[0]
    feature_grads = call(
        by_grid(grads_body),
        place,
        (local,),
        [
            (up_blocks, (1, feat, rows), lambda i, p: (i, 0, p[0])),
            (up_blocks, (1, feat, rows), lambda i, p: (i, 0, p[0] ^ 2)),
            (slope_ss, strip, at_i),
            (slope_sn, strip, at_i),
            (got_grads, one, every),
        ],
        [(blocks, BF16, one, every)],
        16,
    )[0]

    got_u, home_d = after((got_u, home_d), feature_grads)
    up_grads, down_grads = call(
        place_body,
        place,
        (1,),
        [whole(mine_u), whole(got_u), whole(home_d)],
        [
            whole_out((local, feat // n_dp, block_hidden), F32),
            whole_out((local, part, feat), F32),
        ],
        8,
    )
    wide = (local * feat, tokens)
    return (outputs.reshape(wide), feature_grads.reshape(wide), up_grads, down_grads)


def solution(mesh):
    in_specs = (
        P("tensor", "dp"),
        P("tensor", "dp"),
        P("tensor", None, None),
        P("tensor", None, None),
    )
    out_specs = (
        P("tensor", "dp"),
        P("tensor", "dp"),
        P("tensor", "dp", None),
        P("tensor", "dp", None),
    )
    small = mesh.shape["tensor"] == 4 and mesh.shape["dp"] == 8
    return jax.shard_map(
        square_device if small else generic_device,
        mesh=mesh,
        in_specs=in_specs,
        out_specs=out_specs,
        check_vma=False,
    )
```

time: 287 us -> 112 us (0.39)
  the two profiles are of different devices: /device:TPU:12 before, /device:TPU:0 now
where the time goes in v1:
time: 112 us
  Pallas kernels  41.5 us (37%)
  waiting for transfers between devices  40 us (36%)
  starting transfers between devices  27.1 us (24%)
  local copies, waits for them, and re-layouts  2.33 us (2%)
    pallas_call x23, Pallas kernels, call(): pl.pallas_call(body, grid_spec=pltpu.PrefetchScalarGridSpec(num_scalar_pr...  41.5 us
    ppermute x9, waiting for transfers between devices, send_z(): return lax.ppermute(value, 'dp', [(d, d ^ 2 * hop) for d in range(n_dp)])  25.1 us
    ppermute x9, starting transfers between devices, send_z(): return lax.ppermute(value, 'dp', [(d, d ^ 2 * hop) for d in range(n_dp)])  13.5 us
    ppermute x9, waiting for transfers between devices, send(): lax.ppermute(value, 'tensor', [(t, t ^ hop) for t in range(n_tensor)])  11.8 us
    ppermute x9, starting transfers between devices, send(): lax.ppermute(value, 'tensor', [(t, t ^ hop) for t in range(n_tensor)])  11.3 us
    ppermute x7, waiting for transfers between devices, send_core(): return lax.ppermute(value, 'dp', [(d, d ^ 1) for d in range(n_dp)])  3.18 us
  transfers between devices with their start and end apart: 26, of which 13 were waited for; matrix products, arithmetic and copies ran while one was open for 1% of the time, Pallas kernels for 29%

profile of v1, /device:TPU:0, one launch (start us, length us, event | category | flops | bytes accessed | tf_op | source)
XLA Modules:
  0.0 112.1 jit_solution(11686981277805455714)
XLA Ops:
  1.8 3.0 %collective-permute-start.1 = (bf16[2,4,64,256]{3,2,1,0:T(8,128)(2,1)S(1)}, bf16[2,4,64,256]{3,2,1,0:T(8,128)(2,1)S(1)}, u32[]{:S(2)}, u32[]{:S(2)}) collective-permute-start(bf16[2,4,64,256]{3,2,1,0:T(8,128)(2,1)S(1)} %pad_maximum_fusion.2), channel_id=1, source_target_pairs={{0,2},{1,3},{2,0},{3,1},{4,6},{5,7},{6,4},{7,5},{8,10},{9,11},{10,... | collective-permute-start | bytes 786440 | tf_op jit(solution)/shard_map/ppermute | solution.py:339
  5.9 1.6 %collective-permute-start = (bf16[2,4,64,256]{3,2,1,0:T(8,128)(2,1)S(1)}, bf16[2,4,64,256]{3,2,1,0:T(8,128)(2,1)S(1)}, u32[]{:S(2)}, u32[]{:S(2)}) collective-permute-start(bf16[2,4,64,256]{3,2,1,0:T(8,128)(2,1)S(1)} %pad_maximum_fusion.1), channel_id=1, source_target_pairs={{0,1},{1,0},{2,3},{3,2},{4,5},{5,4},{6,7},{7,6},{8,9},{9,8},{10,11... | collective-permute-start | bytes 786440 | tf_op jit(solution)/shard_map/ppermute | solution.py:339
  7.7 1.3 %collective-permute-start.3 = (bf16[2,256,768]{2,1,0:T(8,128)(2,1)S(1)}, bf16[2,256,768]{2,1,0:T(8,128)(2,1)S(1)}, u32[]{:S(2)}, u32[]{:S(2)}) collective-permute-start(bf16[2,256,768]{2,1,0:T(8,128)(2,1)S(1)} %bitcast.45), channel_id=1, source_target_pairs={{0,1},{1,0},{2,3},{3,2},{4,5},{5,4},{6,7},{7,6},{8,9},{9,8},{10,11... | collective-permute-start | bytes 2359304 | tf_op jit(solution)/shard_map/ppermute | solution.py:339
  9.5 5.8 %shard_map.75 = (bf16[2,4,4,64,768]{4,3,2,1,0:T(8,128)(2,1)S(1)}, bf16[2,4,4,64,768]{4,3,2,1,0:T(8,128)(2,1)S(1)}) custom-call(s32[3]{0:T(128)S(1)} %pad_add_fusion.place, bf16[4,256,768]{2,1,0:T(8,128)(2,1)S(1)} %bitcast.37, bf16[4,256,1024]{2,1,0:T(8,128)(2,1)S(1)} %copy-done.2), custom_call_target="tpu_custom_call" | custom-call | tf_op jit(solution)/shard_map/pallas_call | solution.py:74
  15.5 1.6 %collective-permute-start.2 = (bf16[2,2,4,64,256]{4,3,2,1,0:T(8,128)(2,1)S(1)}, bf16[2,2,4,64,256]{4,3,2,1,0:T(8,128)(2,1)S(1)}, u32[]{:S(2)}, u32[]{:S(2)}) collective-permute-start(bf16[2,2,4,64,256]{4,3,2,1,0:T(8,128)(2,1)S(1)} %pad_maximum_fusion.refs_0_), channel_id=1, source_target_pairs={{0,8},{4,12},{8,0},{12,4},{16,24},{20,28},{24,16},{28,20},{1,9},{5... | collective-permute-start | bytes 1572872 | tf_op jit(solution)/shard_map/ppermute | solution.py:342
  17.1 1.3 %collective-permute-start.8 = (bf16[2,256,768]{2,1,0:T(8,128)(2,1)S(1)}, bf16[2,256,768]{2,1,0:T(8,128)(2,1)S(1)}, u32[]{:S(2)}, u32[]{:S(2)}) collective-permute-start(bf16[2,256,768]{2,1,0:T(8,128)(2,1)S(1)} %bitcast.43), channel_id=1, source_target_pairs={{0,1},{1,0},{2,3},{3,2},{4,5},{5,4},{6,7},{7,6},{8,9},{9,8},{10,11... | collective-permute-start | bytes 2359304 | tf_op jit(solution)/shard_map/ppermute | solution.py:339
  20.6 1.6 %shard_map.77 = (bf16[2,4,128,256]{3,2,1,0:T(8,128)(2,1)S(1)}, bf16[2,4,128,256]{3,2,1,0:T(8,128)(2,1)S(1)}) custom-call(s32[3]{0:T(128)S(1)} %pad_add_fusion.place, bf16[4,256,768]{2,1,0:T(8,128)(2,1)S(1)} %bitcast.33, bf16[2,4,4,64,768]{4,3,2,1,0:T(8,128)(2,1)S(1)} %get-tuple-element.104.refs_1_.refs_3_, bf16[4,256,768]{2,1,0:T(8,128)(2,1)S(1)} %bitcast.38, ...), custom_call_target="tpu_custom_call" | custom-call | tf_op jit(solution)/shard_map/pallas_call | solution.py:74
  22.2 6.1 %collective-permute-done.2.refs_1_ = bf16[2,2,4,64,256]{4,3,2,1,0:T(8,128)(2,1)S(1)} collective-permute-done((bf16[2,2,4,64,256]{4,3,2,1,0:T(8,128)(2,1)S(1)}, bf16[2,2,4,64,256]{4,3,2,1,0:T(8,128)(2,1)S(1)}, u32[]{:S(2)}, u32[]{:S(2)}) %collective-permute-start.2) | collective-permute-done | bytes 524320 | tf_op jit(solution)/shard_map/ppermute | solution.py:342
  28.3 3.7 %collective-permute-done.3.x_ref.refs_1_ = bf16[2,256,768]{2,1,0:T(8,128)(2,1)S(1)} collective-permute-done((bf16[2,256,768]{2,1,0:T(8,128)(2,1)S(1)}, bf16[2,256,768]{2,1,0:T(8,128)(2,1)S(1)}, u32[]{:S(2)}, u32[]{:S(2)}) %collective-permute-start.3) | collective-permute-done | bytes 786464 | tf_op jit(solution)/shard_map/ppermute | solution.py:339
  32.6 1.4 %collective-permute-done.7.refs_0_.first_got = bf16[2,4,128,256]{3,2,1,0:T(8,128)(2,1)S(1)} collective-permute-done((bf16[2,4,128,256]{3,2,1,0:T(8,128)(2,1)S(1)}, bf16[2,4,128,256]{3,2,1,0:T(8,128)(2,1)S(1)}, u32[]{:S(2)}, u32[]{:S(2)}) %collective-permute-start.7) | collective-permute-done | bytes 524320 | tf_op jit(solution)/shard_map/ppermute | solution.py:345
  34.6 1.6 %collective-permute-start.11 = (bf16[1,128,256]{2,1,0:T(8,128)(2,1)S(1)}, bf16[1,128,256]{2,1,0:T(8,128)(2,1)S(1)}, u32[]{:S(2)}, u32[]{:S(2)}) collective-permute-start(bf16[1,128,256]{2,1,0:T(8,128)(2,1)S(1)} %get-tuple-element.95), channel_id=1, source_target_pairs={{0,8},{4,12},{8,0},{12,4},{16,24},{20,28},{24,16},{28,20},{1,9},{5... | collective-permute-start | bytes 196616 | tf_op jit(solution)/shard_map/ppermute | solution.py:342
  37.3 3.1 %shard_map.80 = (bf16[2,4,2,64,768]{4,3,2,1,0:T(8,128)(2,1)S(1)}, bf16[2,4,2,64,768]{4,3,2,1,0:T(8,128)(2,1)S(1)}) custom-call(s32[3]{0:T(128)S(1)} %pad_add_fusion.place, bf16[2,256,768]{2,1,0:T(8,128)(2,1)S(1)} %collective-permute-done.3.x_ref.refs_1_, bf16[2,2,4,256,256]{4,3,2,1,0:T(8,128)(2,1)S(1)} %bitcast.22), custom_call_target="tpu_custom_call" | custom-call | tf_op jit(solution)/shard_map/pallas_call | solution.py:74
  42.0 2.7 %collective-permute-start.12 = (bf16[1,128,256]{2,1,0:T(8,128)(2,1)S(1)}, bf16[1,128,256]{2,1,0:T(8,128)(2,1)S(1)}, u32[]{:S(2)}, u32[]{:S(2)}) collective-permute-start(bf16[1,128,256]{2,1,0:T(8,128)(2,1)S(1)} %get-tuple-element.99), channel_id=1, source_target_pairs={{0,16},{4,20},{8,24},{12,28},{16,0},{20,4},{24,8},{28,12},{1,17},{... | collective-permute-start | bytes 196616 | tf_op jit(solution)/shard_map/ppermute | solution.py:342
  44.6 2.8 %collective-permute-done.8.x_ref.refs_2_ = bf16[2,256,768]{2,1,0:T(8,128)(2,1)S(1)} collective-permute-done((bf16[2,256,768]{2,1,0:T(8,128)(2,1)S(1)}, bf16[2,256,768]{2,1,0:T(8,128)(2,1)S(1)}, u32[]{:S(2)}, u32[]{:S(2)}) %collective-permute-start.8) | collective-permute-done | bytes 786464 | tf_op jit(solution)/shard_map/ppermute | solution.py:339
  47.5 3.3 %shard_map.83 = (bf16[2,4,2,64,768]{4,3,2,1,0:T(8,128)(2,1)S(1)}, bf16[2,4,2,64,768]{4,3,2,1,0:T(8,128)(2,1)S(1)}) custom-call(s32[3]{0:T(128)S(1)} %pad_add_fusion.place, bf16[2,256,768]{2,1,0:T(8,128)(2,1)S(1)} %collective-permute-done.8.x_ref.refs_2_, bf16[2,2,4,256,256]{4,3,2,1,0:T(8,128)(2,1)S(1)} %bitcast.23), custom_call_target="tpu_custom_call" | custom-call | tf_op jit(solution)/shard_map/pallas_call | solution.py:74
  50.8 3.6 %shard_map.84 = (bf16[4,128,256]{2,1,0:T(8,128)(2,1)S(1)}, bf16[2,4,128,256]{3,2,1,0:T(8,128)(2,1)S(1)}, bf16[3,4,128,256]{3,2,1,0:T(8,128)(2,1)S(1)}) custom-call(s32[3]{0:T(128)S(1)} %pad_add_fusion.place, bf16[4,256,768]{2,1,0:T(8,128)(2,1)S(1)} %bitcast.35, bf16[2,256,768]{2,1,0:T(8,128)(2,1)S(1)} %collective-permute-done.4.refs_1_, ...), custom_call_target="tpu_custom_call" | custom-call | tf_op jit(solution)/shard_map/pallas_call | solution.py:74
  55.0 1.9 %shard_map.85 = bf16[4,256,768]{2,1,0:T(8,128)(2,1)S(1)} custom-call(s32[3]{0:T(128)S(1)} %pad_add_fusion.place, bf16[2,2,4,256,256]{4,3,2,1,0:T(8,128)(2,1)S(1)} %bitcast.24, bf16[2,2,4,256,256]{4,3,2,1,0:T(8,128)(2,1)S(1)} %bitcast.25, bf16[2,2,4,256,256]{4,3,2,1,0:T(8,128)(2,1)S(1)} %bitcast.26, ...), custom_call_target="tpu_custom_call" | custom-call | tf_op jit(solution)/shard_map/pallas_call | solution.py:74
  58.6 1.5 %collective-permute-start.16 = (bf16[2,4,128,256]{3,2,1,0:T(8,128)(2,1)S(1)}, bf16[2,4,128,256]{3,2,1,0:T(8,128)(2,1)S(1)}, u32[]{:S(2)}, u32[]{:S(2)}) collective-permute-start(bf16[2,4,128,256]{3,2,1,0:T(8,128)(2,1)S(1)} %get-tuple-element.110), channel_id=1, source_target_pairs={{0,8},{4,12},{8,0},{12,4},{16,24},{20,28},{24,16},{28,20},{1,9},{5... | collective-permute-start | bytes 1572872 | tf_op jit(solution)/shard_map/ppermute | solution.py:342
  60.2 1.7 %shard_map.87 = (bf16[4,4,64,768]{3,2,1,0:T(8,128)(2,1)S(1)}, bf16[4,2,64,768]{3,2,1,0:T(8,128)(2,1)S(1)}, bf16[4,2,64,768]{3,2,1,0:T(8,128)(2,1)S(1)}, bf16[4,2,64,768]{3,2,1,0:T(8,128)(2,1)S(1)}) custom-call(s32[3]{0:T(128)S(1)} %pad_add_fusion.place, bf16[4,256,768]{2,1,0:T(8,128)(2,1)S(1)} %bitcast.36, ...), custom_call_target="tpu_custom_call" | custom-call | tf_op jit(solution)/shard_map/pallas_call | solution.py:74
  61.9 1.5 %shard_map.88 = bf16[4,256,768]{2,1,0:T(8,128)(2,1)S(1)} custom-call(s32[3]{0:T(128)S(1)} %pad_add_fusion.place, bf16[2,2,4,256,256]{4,3,2,1,0:T(8,128)(2,1)S(1)} %bitcast.30, bf16[2,2,4,256,256]{4,3,2,1,0:T(8,128)(2,1)S(1)} %bitcast.31, bf16[4,2,64,768]{3,2,1,0:T(8,128)(2,1)S(1)} %shard_map.81.refs_2_.refs_4_, ...), custom_call_target="tpu_custom_call" | custom-call | tf_op jit(solution)/shard_map/pallas_call | solution.py:74
  63.4 1.6 %collective-permute-start.22 = (bf16[4,256,768]{2,1,0:T(8,128)(2,1)S(1)}, bf16[4,256,768]{2,1,0:T(8,128)(2,1)S(1)}, u32[]{:S(2)}, u32[]{:S(2)}) collective-permute-start(bf16[4,256,768]{2,1,0:T(8,128)(2,1)S(1)} %shard_map.88), channel_id=1, source_target_pairs={{0,1},{1,0},{2,3},{3,2},{4,5},{5,4},{6,7},{7,6},{8,9},{9,8},{10,11... | collective-permute-start | bytes 4718600 | tf_op jit(solution)/shard_map/ppermute | solution.py:339
  65.0 2.1 %shard_map.89 = (bf16[3,4,64,256]{3,2,1,0:T(8,128)(2,1)S(1)}, bf16[3,4,64,256]{3,2,1,0:T(8,128)(2,1)S(1)}, bf16[3,4,128,256]{3,2,1,0:T(8,128)(2,1)S(1)}) custom-call(s32[3]{0:T(128)S(1)} %pad_add_fusion.place, bf16[4,256,768]{2,1,0:T(8,128)(2,1)S(1)} %bitcast.39, bf16[2,256,768]{2,1,0:T(8,128)(2,1)S(1)} %collective-permute-done.3.x_ref.refs_1_, ...), custom_call_target="tpu_custom_call" | custom-call | flops 16000000000 | tf_op jit(solution)/shard_map/pallas_call | solution.py:74
  70.7 1.5 %collective-permute-start.20 = (bf16[3,128,256]{2,1,0:T(8,128)(2,1)S(1)}, bf16[3,128,256]{2,1,0:T(8,128)(2,1)S(1)}, u32[]{:S(2)}, u32[]{:S(2)}) collective-permute-start(bf16[3,128,256]{2,1,0:T(8,128)(2,1)S(1)} %get-tuple-element.123), channel_id=1, source_target_pairs={{0,8},{4,12},{8,0},{12,4},{16,24},{20,28},{24,16},{28,20},{1,9},{5... | collective-permute-start | bytes 589832 | tf_op jit(solution)/shard_map/ppermute | solution.py:342
  73.0 2.9 %collective-permute-start.19 = (bf16[4,128,256]{2,1,0:T(8,128)(2,1)S(1)}, bf16[4,128,256]{2,1,0:T(8,128)(2,1)S(1)}, u32[]{:S(2)}, u32[]{:S(2)}) collective-permute-start(bf16[4,128,256]{2,1,0:T(8,128)(2,1)S(1)} %get-tuple-element.126), channel_id=1, source_target_pairs={{0,16},{4,20},{8,24},{12,28},{16,0},{20,4},{24,8},{28,12},{1,17},{... | collective-permute-start | bytes 786440 | tf_op jit(solution)/shard_map/ppermute | solution.py:342
  75.9 7.7 %collective-permute-done.21.got_far = bf16[3,128,256]{2,1,0:T(8,128)(2,1)S(1)} collective-permute-done((bf16[3,128,256]{2,1,0:T(8,128)(2,1)S(1)}, bf16[3,128,256]{2,1,0:T(8,128)(2,1)S(1)}, u32[]{:S(2)}, u32[]{:S(2)}) %collective-permute-start.21) | collective-permute-done | bytes 196640 | tf_op jit(solution)/shard_map/ppermute | solution.py:342
  83.6 3.4 %collective-permute-done.20.got_ref = bf16[3,128,256]{2,1,0:T(8,128)(2,1)S(1)} collective-permute-done((bf16[3,128,256]{2,1,0:T(8,128)(2,1)S(1)}, bf16[3,128,256]{2,1,0:T(8,128)(2,1)S(1)}, u32[]{:S(2)}, u32[]{:S(2)}) %collective-permute-start.20) | collective-permute-done | bytes 196640 | tf_op jit(solution)/shard_map/ppermute | solution.py:342
  89.4 4.0 %collective-permute-done.13.refs_6_ = bf16[4,256,768]{2,1,0:T(8,128)(2,1)S(1)} collective-permute-done((bf16[4,256,768]{2,1,0:T(8,128)(2,1)S(1)}, bf16[4,256,768]{2,1,0:T(8,128)(2,1)S(1)}, u32[]{:S(2)}, u32[]{:S(2)}) %collective-permute-start.13) | collective-permute-done | bytes 1572896 | tf_op jit(solution)/shard_map/ppermute | solution.py:339
  93.4 3.6 %shard_map.94 = bf16[4,256,768]{2,1,0:T(8,128)(2,1)} custom-call(s32[3]{0:T(128)S(1)} %pad_add_fusion.place, bf16[4,1024,256]{2,1,0:T(8,128)(2,1)S(1)} %copy-done, bf16[4,1024,256]{2,1,0:T(8,128)(2,1)S(1)} %copy-done, bf16[4,1024,256]{2,1,0:T(8,128)(2,1)S(1)} %copy-done, bf16[2,4,4,64,768]{4,3,2,1,0:T(8,128)(2,1)S(1)} %get-tuple-element.104.refs_1_.refs_3_, ...), custom_call_target="tpu_custom_call" | custom-call | tf_op jit(solution)/shard_map/pallas_call | solution.py:74
  97.0 7.6 %collective-permute-done.23.got_ref = bf16[3,128,256]{2,1,0:T(8,128)(2,1)S(1)} collective-permute-done((bf16[3,128,256]{2,1,0:T(8,128)(2,1)S(1)}, bf16[3,128,256]{2,1,0:T(8,128)(2,1)S(1)}, u32[]{:S(2)}, u32[]{:S(2)}) %collective-permute-start.23) | collective-permute-done | bytes 196640 | tf_op jit(solution)/shard_map/ppermute | solution.py:342
  105.7 3.5 %shard_map.96 = bf16[4,256,768]{2,1,0:T(8,128)(2,1)} custom-call(s32[3]{0:T(128)S(1)} %pad_add_fusion.place, bf16[4,256,1024]{2,1,0:T(8,128)(2,1)S(1)} %copy-done.2, bf16[4,256,1024]{2,1,0:T(8,128)(2,1)S(1)} %copy-done.2, bf16[4,4,64,768]{3,2,1,0:T(8,128)(2,1)S(1)} %shard_map.76.refs_3_.refs_2_, bf16[4,4,64,768]{3,2,1,0:T(8,128)(2,1)S(1)} %get-tuple-element.119.refs_3_, ...), custom_call_target="tpu_custom_call" | custom-call | tf_op jit(solution)/shard_map/pallas_call | solution.py:74
  109.2 1.3 %collective-permute-done.24.got_ref = bf16[2,128,256]{2,1,0:T(8,128)(2,1)S(1)} collective-permute-done((bf16[2,128,256]{2,1,0:T(8,128)(2,1)S(1)}, bf16[2,128,256]{2,1,0:T(8,128)(2,1)S(1)}, u32[]{:S(2)}, u32[]{:S(2)}) %collective-permute-start.24) | collective-permute-done | bytes 131104 | tf_op jit(solution)/shard_map/ppermute | solution.py:339
  110.5 1.6 %shard_map.97 = (f32[4,32,1024]{2,1,0:T(8,128)}, f32[4,128,256]{2,1,0:T(8,128)}) custom-call(s32[3]{0:T(128)S(1)} %pad_add_fusion.place, f32[2,128,256]{2,1,0:T(8,128)S(1)} %get-tuple-element.139.mine_ref, bf16[2,128,256]{2,1,0:T(8,128)(2,1)S(1)} %collective-permute-done.24.got_ref, bf16[4,128,256]{2,1,0:T(8,128)(2,1)S(1)} %collective-permute-done.25.down_in), custom_call_target="tpu_custom_call" | custom-call | tf_op jit(solution)/shard_map/pallas_call | solution.py:74
  (59 shorter events, 19.2 us)
Async XLA Ops:
  0.6 6.8 %copy-start.3 = (bf16[1024,768]{1,0:T(8,128)(2,1)S(1)}, bf16[1024,768]{1,0:T(8,128)(2,1)}, u32[]{:S(2)}) copy-start(bf16[1024,768]{1,0:T(8,128)(2,1)} %param.4) | copy-start | bytes 4718596
  1.8 13.6 %collective-permute-start.1 = (bf16[2,4,64,256]{3,2,1,0:T(8,128)(2,1)S(1)}, bf16[2,4,64,256]{3,2,1,0:T(8,128)(2,1)S(1)}, u32[]{:S(2)}, u32[]{:S(2)}) collective-permute-start(bf16[2,4,64,256]{3,2,1,0:T(8,128)(2,1)S(1)} %pad_maximum_fusion.2), channel_id=1, source_target_pairs={{0,2},{1,3},{2,0},{3,1},{4,6},{5,7},{6,4},{7,5},{8,10},{9,11},{10,... | collective-permute-start | bytes 786440 | tf_op jit(solution)/shard_map/ppermute | solution.py:339
  5.9 1.7 %copy-start.1 = (bf16[1024,768]{1,0:T(8,128)(2,1)S(1)}, bf16[1024,768]{1,0:T(8,128)(2,1)}, u32[]{:S(2)}) copy-start(bf16[1024,768]{1,0:T(8,128)(2,1)} %param.5) | copy-start | bytes 4718596
  5.9 9.5 %collective-permute-start = (bf16[2,4,64,256]{3,2,1,0:T(8,128)(2,1)S(1)}, bf16[2,4,64,256]{3,2,1,0:T(8,128)(2,1)S(1)}, u32[]{:S(2)}, u32[]{:S(2)}) collective-permute-start(bf16[2,4,64,256]{3,2,1,0:T(8,128)(2,1)S(1)} %pad_maximum_fusion.1), channel_id=1, source_target_pairs={{0,1},{1,0},{2,3},{3,2},{4,5},{5,4},{6,7},{7,6},{8,9},{9,8},{10,11... | collective-permute-start | bytes 786440 | tf_op jit(solution)/shard_map/ppermute | solution.py:339
  7.6 2.0 %copy-start.2 = (bf16[4,256,1024]{2,1,0:T(8,128)(2,1)S(1)}, bf16[4,256,1024]{2,1,0:T(8,128)(2,1)}, u32[]{:S(2)}) copy-start(bf16[4,256,1024]{2,1,0:T(8,128)(2,1)} %refs_1_.7) | copy-start | bytes 6291460
  7.7 24.4 %collective-permute-start.3 = (bf16[2,256,768]{2,1,0:T(8,128)(2,1)S(1)}, bf16[2,256,768]{2,1,0:T(8,128)(2,1)S(1)}, u32[]{:S(2)}, u32[]{:S(2)}) collective-permute-start(bf16[2,256,768]{2,1,0:T(8,128)(2,1)S(1)} %bitcast.45), channel_id=1, source_target_pairs={{0,1},{1,0},{2,3},{3,2},{4,5},{5,4},{6,7},{7,6},{8,9},{9,8},{10,11... | collective-permute-start | bytes 2359304 | tf_op jit(solution)/shard_map/ppermute | solution.py:339
  8.9 23.1 %collective-permute-start.4 = (bf16[2,256,768]{2,1,0:T(8,128)(2,1)S(1)}, bf16[2,256,768]{2,1,0:T(8,128)(2,1)S(1)}, u32[]{:S(2)}, u32[]{:S(2)}) collective-permute-start(bf16[2,256,768]{2,1,0:T(8,128)(2,1)S(1)} %bitcast.44), channel_id=1, source_target_pairs={{0,2},{1,3},{2,0},{3,1},{4,6},{5,7},{6,4},{7,5},{8,10},{9,11},{10,... | collective-permute-start | bytes 2359304 | tf_op jit(solution)/shard_map/ppermute | solution.py:339
  9.5 9.9 %copy-start = (bf16[4,1024,256]{2,1,0:T(8,128)(2,1)S(1)}, bf16[4,1024,256]{2,1,0:T(8,128)(2,1)}, u32[]{:S(2)}) copy-start(bf16[4,1024,256]{2,1,0:T(8,128)(2,1)} %refs_2_.1) | copy-start | bytes 6291460
  15.5 12.9 %collective-permute-start.2 = (bf16[2,2,4,64,256]{4,3,2,1,0:T(8,128)(2,1)S(1)}, bf16[2,2,4,64,256]{4,3,2,1,0:T(8,128)(2,1)S(1)}, u32[]{:S(2)}, u32[]{:S(2)}) collective-permute-start(bf16[2,2,4,64,256]{4,3,2,1,0:T(8,128)(2,1)S(1)} %pad_maximum_fusion.refs_0_), channel_id=1, source_target_pairs={{0,8},{4,12},{8,0},{12,4},{16,24},{20,28},{24,16},{28,20},{1,9},{5... | collective-permute-start | bytes 1572872 | tf_op jit(solution)/shard_map/ppermute | solution.py:342
  17.1 30.3 %collective-permute-start.8 = (bf16[2,256,768]{2,1,0:T(8,128)(2,1)S(1)}, bf16[2,256,768]{2,1,0:T(8,128)(2,1)S(1)}, u32[]{:S(2)}, u32[]{:S(2)}) collective-permute-start(bf16[2,256,768]{2,1,0:T(8,128)(2,1)S(1)} %bitcast.43), channel_id=1, source_target_pairs={{0,1},{1,0},{2,3},{3,2},{4,5},{5,4},{6,7},{7,6},{8,9},{9,8},{10,11... | collective-permute-start | bytes 2359304 | tf_op jit(solution)/shard_map/ppermute | solution.py:339
  18.4 29.1 %collective-permute-start.9 = (bf16[2,256,768]{2,1,0:T(8,128)(2,1)S(1)}, bf16[2,256,768]{2,1,0:T(8,128)(2,1)S(1)}, u32[]{:S(2)}, u32[]{:S(2)}) collective-permute-start(bf16[2,256,768]{2,1,0:T(8,128)(2,1)S(1)} %bitcast.42), channel_id=1, source_target_pairs={{0,2},{1,3},{2,0},{3,1},{4,6},{5,7},{6,4},{7,5},{8,10},{9,11},{10,... | collective-permute-start | bytes 2359304 | tf_op jit(solution)/shard_map/ppermute | solution.py:339
  32.0 1.9 %collective-permute-start.7 = (bf16[2,4,128,256]{3,2,1,0:T(8,128)(2,1)S(1)}, bf16[2,4,128,256]{3,2,1,0:T(8,128)(2,1)S(1)}, u32[]{:S(2)}, u32[]{:S(2)}) collective-permute-start(bf16[2,4,128,256]{3,2,1,0:T(8,128)(2,1)S(1)} %get-tuple-element.88), channel_id=1, source_target_pairs={{0,4},{4,0},{8,12},{12,8},{16,20},{20,16},{24,28},{28,24},{1,5},{5... | collective-permute-start | bytes 1572872 | tf_op jit(solution)/shard_map/ppermute | solution.py:345
  32.0 4.2 %collective-permute-start.5 = (bf16[2,2,4,64,256]{4,3,2,1,0:T(8,128)(2,1)S(1)}, bf16[2,2,4,64,256]{4,3,2,1,0:T(8,128)(2,1)S(1)}, u32[]{:S(2)}, u32[]{:S(2)}) collective-permute-start(bf16[2,2,4,64,256]{4,3,2,1,0:T(8,128)(2,1)S(1)} %pad_maximum_fusion.refs_0_), channel_id=1, source_target_pairs={{0,4},{4,0},{8,12},{12,8},{16,20},{20,16},{24,28},{28,24},{1,5},{5... | collective-permute-start | bytes 1572872 | tf_op jit(solution)/shard_map/ppermute | solution.py:345
  32.5 4.1 %collective-permute-start.6 = (bf16[2,2,4,64,256]{4,3,2,1,0:T(8,128)(2,1)S(1)}, bf16[2,2,4,64,256]{4,3,2,1,0:T(8,128)(2,1)S(1)}, u32[]{:S(2)}, u32[]{:S(2)}) collective-permute-start(bf16[2,2,4,64,256]{4,3,2,1,0:T(8,128)(2,1)S(1)} %collective-permute-done.2.refs_1_), channel_id=1, source_target_pairs={{0,4},{4,0},{8,12},{12,8},{16,20},{20,16},{24,28},{28,24},{1,5},{5... | collective-permute-start | bytes 1572872 | tf_op jit(solution)/shard_map/ppermute | solution.py:345
  34.6 6.8 %collective-permute-start.11 = (bf16[1,128,256]{2,1,0:T(8,128)(2,1)S(1)}, bf16[1,128,256]{2,1,0:T(8,128)(2,1)S(1)}, u32[]{:S(2)}, u32[]{:S(2)}) collective-permute-start(bf16[1,128,256]{2,1,0:T(8,128)(2,1)S(1)} %get-tuple-element.95), channel_id=1, source_target_pairs={{0,8},{4,12},{8,0},{12,4},{16,24},{20,28},{24,16},{28,20},{1,9},{5... | collective-permute-start | bytes 196616 | tf_op jit(solution)/shard_map/ppermute | solution.py:342
  36.2 5.2 %collective-permute-start.10 = (bf16[1,128,256]{2,1,0:T(8,128)(2,1)S(1)}, bf16[1,128,256]{2,1,0:T(8,128)(2,1)S(1)}, u32[]{:S(2)}, u32[]{:S(2)}) collective-permute-start(bf16[1,128,256]{2,1,0:T(8,128)(2,1)S(1)} %get-tuple-element.89), channel_id=1, source_target_pairs={{0,8},{4,12},{8,0},{12,4},{16,24},{20,28},{24,16},{28,20},{1,9},{5... | collective-permute-start | bytes 196616 | tf_op jit(solution)/shard_map/ppermute | solution.py:342
  42.0 5.6 %collective-permute-start.12 = (bf16[1,128,256]{2,1,0:T(8,128)(2,1)S(1)}, bf16[1,128,256]{2,1,0:T(8,128)(2,1)S(1)}, u32[]{:S(2)}, u32[]{:S(2)}) collective-permute-start(bf16[1,128,256]{2,1,0:T(8,128)(2,1)S(1)} %get-tuple-element.99), channel_id=1, source_target_pairs={{0,16},{4,20},{8,24},{12,28},{16,0},{20,4},{24,8},{28,12},{1,17},{... | collective-permute-start | bytes 196616 | tf_op jit(solution)/shard_map/ppermute | solution.py:342
  54.4 3.1 %collective-permute-start.15 = (bf16[2,4,128,256]{3,2,1,0:T(8,128)(2,1)S(1)}, bf16[2,4,128,256]{3,2,1,0:T(8,128)(2,1)S(1)}, u32[]{:S(2)}, u32[]{:S(2)}) collective-permute-start(bf16[2,4,128,256]{3,2,1,0:T(8,128)(2,1)S(1)} %get-tuple-element.106), channel_id=1, source_target_pairs={{0,4},{4,0},{8,12},{12,8},{16,20},{20,16},{24,28},{28,24},{1,5},{5... | collective-permute-start | bytes 1572872 | tf_op jit(solution)/shard_map/ppermute | solution.py:345
  54.5 3.0 %collective-permute-start.14 = (bf16[4,128,256]{2,1,0:T(8,128)(2,1)S(1)}, bf16[4,128,256]{2,1,0:T(8,128)(2,1)S(1)}, u32[]{:S(2)}, u32[]{:S(2)}) collective-permute-start(bf16[4,128,256]{2,1,0:T(8,128)(2,1)S(1)} %get-tuple-element.103), channel_id=1, source_target_pairs={{0,4},{4,0},{8,12},{12,8},{16,20},{20,16},{24,28},{28,24},{1,5},{5... | collective-permute-start | bytes 786440 | tf_op jit(solution)/shard_map/ppermute | solution.py:345
  57.0 36.4 %collective-permute-start.13 = (bf16[4,256,768]{2,1,0:T(8,128)(2,1)S(1)}, bf16[4,256,768]{2,1,0:T(8,128)(2,1)S(1)}, u32[]{:S(2)}, u32[]{:S(2)}) collective-permute-start(bf16[4,256,768]{2,1,0:T(8,128)(2,1)S(1)} %shard_map.85), channel_id=1, source_target_pairs={{0,2},{1,3},{2,0},{3,1},{4,6},{5,7},{6,4},{7,5},{8,10},{9,11},{10,... | collective-permute-start | bytes 4718600 | tf_op jit(solution)/shard_map/ppermute | solution.py:339
  58.6 13.7 %collective-permute-start.16 = (bf16[2,4,128,256]{3,2,1,0:T(8,128)(2,1)S(1)}, bf16[2,4,128,256]{3,2,1,0:T(8,128)(2,1)S(1)}, u32[]{:S(2)}, u32[]{:S(2)}) collective-permute-start(bf16[2,4,128,256]{3,2,1,0:T(8,128)(2,1)S(1)} %get-tuple-element.110), channel_id=1, source_target_pairs={{0,8},{4,12},{8,0},{12,4},{16,24},{20,28},{24,16},{28,20},{1,9},{5... | collective-permute-start | bytes 1572872 | tf_op jit(solution)/shard_map/ppermute | solution.py:342
  63.4 42.3 %collective-permute-start.22 = (bf16[4,256,768]{2,1,0:T(8,128)(2,1)S(1)}, bf16[4,256,768]{2,1,0:T(8,128)(2,1)S(1)}, u32[]{:S(2)}, u32[]{:S(2)}) collective-permute-start(bf16[4,256,768]{2,1,0:T(8,128)(2,1)S(1)} %shard_map.88), channel_id=1, source_target_pairs={{0,1},{1,0},{2,3},{3,2},{4,5},{5,4},{6,7},{7,6},{8,9},{9,8},{10,11... | collective-permute-start | bytes 4718600 | tf_op jit(solution)/shard_map/ppermute | solution.py:339
  67.1 1.8 %collective-permute-start.17 = (bf16[3,4,64,256]{3,2,1,0:T(8,128)(2,1)S(1)}, bf16[3,4,64,256]{3,2,1,0:T(8,128)(2,1)S(1)}, u32[]{:S(2)}, u32[]{:S(2)}) collective-permute-start(bf16[3,4,64,256]{3,2,1,0:T(8,128)(2,1)S(1)} %get-tuple-element.121), channel_id=1, source_target_pairs={{0,4},{4,0},{8,12},{12,8},{16,20},{20,16},{24,28},{28,24},{1,5},{5... | collective-permute-start | bytes 1179656 | tf_op jit(solution)/shard_map/ppermute | solution.py:345
  67.1 2.3 %collective-permute-start.18 = (bf16[3,4,64,256]{3,2,1,0:T(8,128)(2,1)S(1)}, bf16[3,4,64,256]{3,2,1,0:T(8,128)(2,1)S(1)}, u32[]{:S(2)}, u32[]{:S(2)}) collective-permute-start(bf16[3,4,64,256]{3,2,1,0:T(8,128)(2,1)S(1)} %get-tuple-element.122), channel_id=1, source_target_pairs={{0,4},{4,0},{8,12},{12,8},{16,20},{20,16},{24,28},{28,24},{1,5},{5... | collective-permute-start | bytes 1179656 | tf_op jit(solution)/shard_map/ppermute | solution.py:345
  70.1 13.4 %collective-permute-start.21 = (bf16[3,128,256]{2,1,0:T(8,128)(2,1)S(1)}, bf16[3,128,256]{2,1,0:T(8,128)(2,1)S(1)}, u32[]{:S(2)}, u32[]{:S(2)}) collective-permute-start(bf16[3,128,256]{2,1,0:T(8,128)(2,1)S(1)} %get-tuple-element.128), channel_id=1, source_target_pairs={{0,8},{4,12},{8,0},{12,4},{16,24},{20,28},{24,16},{28,20},{1,9},{5... | collective-permute-start | bytes 589832 | tf_op jit(solution)/shard_map/ppermute | solution.py:342
  70.7 16.2 %collective-permute-start.20 = (bf16[3,128,256]{2,1,0:T(8,128)(2,1)S(1)}, bf16[3,128,256]{2,1,0:T(8,128)(2,1)S(1)}, u32[]{:S(2)}, u32[]{:S(2)}) collective-permute-start(bf16[3,128,256]{2,1,0:T(8,128)(2,1)S(1)} %get-tuple-element.123), channel_id=1, source_target_pairs={{0,8},{4,12},{8,0},{12,4},{16,24},{20,28},{24,16},{28,20},{1,9},{5... | collective-permute-start | bytes 589832 | tf_op jit(solution)/shard_map/ppermute | solution.py:342
  73.0 15.2 %collective-permute-start.19 = (bf16[4,128,256]{2,1,0:T(8,128)(2,1)S(1)}, bf16[4,128,256]{2,1,0:T(8,128)(2,1)S(1)}, u32[]{:S(2)}, u32[]{:S(2)}) collective-permute-start(bf16[4,128,256]{2,1,0:T(8,128)(2,1)S(1)} %get-tuple-element.126), channel_id=1, source_target_pairs={{0,16},{4,20},{8,24},{12,28},{16,0},{20,4},{24,8},{28,12},{1,17},{... | collective-permute-start | bytes 786440 | tf_op jit(solution)/shard_map/ppermute | solution.py:342
  87.6 17.1 %collective-permute-start.23 = (bf16[3,128,256]{2,1,0:T(8,128)(2,1)S(1)}, bf16[3,128,256]{2,1,0:T(8,128)(2,1)S(1)}, u32[]{:S(2)}, u32[]{:S(2)}) collective-permute-start(bf16[3,128,256]{2,1,0:T(8,128)(2,1)S(1)} %get-tuple-element.131), channel_id=1, source_target_pairs={{0,16},{4,20},{8,24},{12,28},{16,0},{20,4},{24,8},{28,12},{1,17},{... | collective-permute-start | bytes 589832 | tf_op jit(solution)/shard_map/ppermute | solution.py:342
  88.7 20.5 %collective-permute-start.25 = (bf16[4,128,256]{2,1,0:T(8,128)(2,1)S(1)}, bf16[4,128,256]{2,1,0:T(8,128)(2,1)S(1)}, u32[]{:S(2)}, u32[]{:S(2)}) collective-permute-start(bf16[4,128,256]{2,1,0:T(8,128)(2,1)S(1)} %shard_map.93), channel_id=1, source_target_pairs={{0,0},{1,1},{2,16},{3,17},{4,4},{5,5},{6,20},{7,21},{8,8},{9,9},{1... | collective-permute-start | bytes 786440 | tf_op jit(solution)/shard_map/ppermute | solution.py:632
  105.2 5.3 %collective-permute-start.24 = (bf16[2,128,256]{2,1,0:T(8,128)(2,1)S(1)}, bf16[2,128,256]{2,1,0:T(8,128)(2,1)S(1)}, u32[]{:S(2)}, u32[]{:S(2)}) collective-permute-start(bf16[2,128,256]{2,1,0:T(8,128)(2,1)S(1)} %get-tuple-element.137), channel_id=1, source_target_pairs={{0,1},{1,0},{2,3},{3,2},{4,5},{5,4},{6,7},{7,6},{8,9},{9,8},{10,11... | collective-permute-start | bytes 393224 | tf_op jit(solution)/shard_map/ppermute | solution.py:339

commit v2 on v1

--- a/solution.py
+++ b/solution.py
@@ -167,23 +167,30 @@
     pl.when(step >= steps // 2)(functools.partial(work, *hi))
 
 
-def put_slope(cot, down_ref, gate_ref, slope_ref):
-    back = dot_nn(square(down_ref), cot).astype(BF16).astype(F32)
-    slope = (back * square(gate_ref).astype(F32)).astype(BF16)
-    slope_ref[...] = slope.reshape(slope_ref.shape)
+def stacked(refs, axis=0):
+    return jnp.concatenate([square(ref) for ref in refs], axis)
+
+
+def put_slopes(cot, downs, gates, slopes):
+    back = dot_nn(stacked(downs), cot).astype(BF16)
+    base = 0
+    for gate_ref, slope_ref in zip(gates, slopes):
+        gate = square(gate_ref).astype(F32)
+        mine = back[base : base + gate.shape[0]].astype(F32)
+        slope_ref[...] = (mine * gate).astype(BF16).reshape(slope_ref.shape)
+        base += gate.shape[0]
 
 
 def slope_body(step, steps, place, cot_ref, down_ref, gate_ref, slope_ref):
-    put_slope(square(cot_ref), down_ref, gate_ref, slope_ref)
+    put_slopes(square(cot_ref), [down_ref], [gate_ref], [slope_ref])
 
 
 def late_slopes_body(step, steps, place, own_ref, near_lo, near_hi, *refs):
     downs, gates, slopes = refs[:4], refs[4:8], refs[8:]
-    put_slope(square(own_ref), downs[3], gates[3], slopes[3])
+    put_slopes(square(own_ref), downs[3:], gates[3:], slopes[3:])
 
     def work(near_ref):
-        for at in range(3):
-            put_slope(square(near_ref), downs[at], gates[at], slopes[at])
+        put_slopes(square(near_ref), downs[:3], gates[:3], slopes[:3])
 
     halves(step, steps, work, (near_lo,), (near_hi,))
 
@@ -203,18 +210,17 @@
 def down_terms_body(step, steps, place, own_ref, near_lo, near_hi, sn, ns_lo, ns_hi, nn_lo, nn_hi, give_own, give_near, keep_ref, term_s):
     core = place[2]
 
-    def put(pair, lo, hi, cot, give):
-        term_s[0], term_s[1] = (dot_nt(v, cot).astype(BF16) for v in (lo, hi))
-        give[...] = term_s[1 - core].reshape(give.shape)
-        keep_ref[pair, 0] = term_s[core]
+    def put(pair, terms, give):
+        term_s[pair] = terms.astype(BF16).reshape(term_s.shape[1:])
+        give[...] = term_s[pair, 1 - core].reshape(give.shape)
+        keep_ref[pair, 0] = term_s[pair, core]
 
     def work(near_ref):
-        own, near = square(own_ref), square(near_ref)
-        mixed = square(sn)
-        part = mixed.shape[0] // 2
-        put(0, mixed[:part], mixed[part:], near, give_own)
-        put(1, square(ns_lo), square(ns_hi), own, give_near.at[0])
-        put(2, square(nn_lo), square(nn_hi), near, give_near.at[1])
+        rows = 2 * term_s.shape[2]
+        mixed = dot_nt(stacked((sn, nn_lo, nn_hi)), square(near_ref))
+        put(0, mixed[:rows], give_own)
+        put(1, dot_nt(stacked((ns_lo, ns_hi)), square(own_ref)), give_near.at[0])
+        put(2, mixed[rows:], give_near.at[1])
 
     halves(step, steps, work, (near_lo,), (near_hi,))
 
@@ -235,27 +241,24 @@
     halves(step, steps, work, lo, hi)
 
 
-def outputs_body(step, steps, place, d_own, d_lo, d_hi, hid_ref, lo_ref, hi_ref, *rest):
-    total = dot_tn(square(d_own), square(hid_ref))
-    total = total + dot_tn(square(d_lo), square(lo_ref))
-    total = total + dot_tn(square(d_hi), square(hi_ref))
-    for ref in rest[:-1]:
-        total = total + ref[0].astype(F32)
-    rest[-1][0] = total.astype(BF16)
+def outputs_body(step, steps, place, d_own, d_lo, d_hi, hid_ref, lo_ref, hi_ref, out_ref):
+    total = dot_tn(stacked((d_own, d_lo, d_hi)), stacked((hid_ref, lo_ref, hi_ref)))
+    out_ref[0] = total.astype(out_ref.dtype)
 
 
 def near_grads_body(step, steps, place, up_own, up_near, lo_s, lo_n, hi_s, hi_n, out_ref):
-    def work(slope_own, slope_near):
-        total = dot_nn(square(up_own), square(slope_own))
-        total = total + dot_nn(square(up_near), square(slope_near))
-        out_ref[0] = total.astype(BF16)
+    def work(*slopes):
+        out_ref[0] = dot_nn(stacked((up_own, up_near), 1), stacked(slopes)).astype(BF16)
 
     halves(step, steps, work, (lo_s, lo_n), (hi_s, hi_n))
 
 
-def grads_body(step, steps, place, up_own, up_near, slope_own, slope_near, add_ref, out_ref):
-    total = dot_nn(square(up_own), square(slope_own)) + dot_nn(square(up_near), square(slope_near))
-    out_ref[0] = (total + add_ref[0].astype(F32)).astype(BF16)
+def grads_body(step, steps, place, up_own, up_near, slope_own, slope_near, out_ref):
+    out_ref[0] = dot_nn(stacked((up_own, up_near), 1), stacked((slope_own, slope_near)))
+
+
+def add_body(place, own_ref, got_ref, out_ref):
+    out_ref[...] = (own_ref[...] + got_ref[...].astype(F32)).astype(BF16)
 
 
 def down_meet_body(place, first, first_got, keep_ref, got_own, got_near, send_ref, mine_ref, total_s):
@@ -263,8 +266,8 @@
     total_s[0, 0] = first[1].astype(F32) + first_got[1].astype(F32)
     total_s[0, 1] = keep_ref[0].astype(F32) + got_own[...].astype(F32)
     total_s[1] = keep_ref[1:].astype(F32) + got_near[...].astype(F32)
-    mine_ref[...] = total_s[stay]
-    send_ref[...] = total_s[1 - stay].astype(BF16)
+    mine_ref[...] = total_s[:, stay]
+    send_ref[...] = total_s[:, 1 - stay].astype(BF16)
 
 
 def down_again_body(place, mine_ref, got_ref, send_ref, own_ref):
@@ -291,14 +294,17 @@
                 mine_ref[hop // 2, :, strip] = total
 
 
-def up_again_body(place, mine_ref, got_ref, got_far, send_ref, own_ref):
-    send_ref[...] = (mine_ref[1] + got_far[...].astype(F32)).astype(BF16)
-    own_ref[...] = mine_ref[0] + got_ref[...].astype(F32)
-
-
-def up_sum_body(factor, place, first_ref, first_got, own_ref, got_ref, send_ref, mine_ref):
-    mine_ref[0] = (first_ref[0] + first_got[0].astype(F32)) * factor
-    total = (own_ref[...] + got_ref[...].astype(F32)) * factor
+def up_again_body(place, mine_ref, far_ref, send_ref):
+    send_ref[...] = (mine_ref[1] + far_ref[...].astype(F32)).astype(BF16)
+
+
+def up_sum_body(factor, place, *refs):
+    ins, (send_ref, mine_ref) = refs[:6], refs[6:]
+    first, total = (
+        (own[0] + near[...].astype(F32) + far[...].astype(F32)) * factor
+        for own, near, far in (ins[:3], ins[3:])
+    )
+    mine_ref[0] = first[0]
     mine_ref[1] = total[0]
     send_ref[...] = total[1:].astype(BF16)
 
@@ -308,7 +314,7 @@
     width = mine_ref.shape[-1]
     for ref, side in ((mine_ref, 0), (got_ref, 1)):
         for at in range(2):
-            where = place[0] ^ side ^ (2 * at)
+            where = place[0] ^ (2 * side) ^ at
             lanes = pl.ds(pl.multiple_of(where * width, width), width)
             up_ref[:, :, lanes] = ref[at].astype(F32).reshape(*up_ref.shape[:2], width)
 
@@ -346,22 +352,22 @@
 
     quarter = rows // 4
     at = (core * 2 + (z & 1)) * quarter
-    to_x = jnp.stack(
+    to_i = jnp.stack(
         [
             lax.dynamic_slice(up_blocks, (0, at, (me ^ k) * rows), (local, quarter, rows))
+            for k in (2, 3)
+        ]
+    )
+    to_j = jnp.stack(
+        [
+            lax.dynamic_slice(down_blocks, (0, (me ^ k) * rows + at, 0), (local, quarter, feat))
             for k in (1, 3)
         ]
     )
-    to_y = jnp.stack(
-        [
-            lax.dynamic_slice(down_blocks, (0, (me ^ k) * rows + at, 0), (local, quarter, feat))
-            for k in (2, 3)
-        ]
-    )
-    from_x, from_y = send(to_x, 1), send(to_y, 2)
-    firsts = after((x[:half], x[half:], cot[:half], cot[half:]), to_x, to_y)
-    x_lo, cot_lo = send(firsts[0], 1), send(firsts[2], 2)
-    x_hi, cot_hi = send(firsts[1], 1), send(firsts[3], 2)
+    from_i, from_j = send(to_i, 2), send(to_j, 1)
+    firsts = after((x[:half], x[half:], cot[:half], cot[half:]), to_i, to_j)
+    x_lo, cot_lo = send(firsts[0], 2), send(firsts[2], 1)
+    x_hi, cot_hi = send(firsts[1], 2), send(firsts[3], 1)
 
     def hidden_of(source, count, up, span):
         unit = (2, local, count, sub, tokens)
@@ -377,10 +383,10 @@
         )
 
     hid, gate = hidden_of(
-        x, local, (up_blocks, (1, feat, rows), lambda j, i, p: (i, 0, p[0] ^ (2 * j))), 0.0
-    )
-    from_x, from_y = after((from_x, from_y), hid)
-    share = jnp.stack([from_x, from_y])
+        x, local, (up_blocks, (1, feat, rows), lambda j, i, p: (i, 0, p[0] ^ j)), 0.0
+    )
+    from_i, from_j = after((from_i, from_j), hid)
+    share = jnp.stack([from_i, from_j])
     share_z = send_z(share, 1)
 
     def unit_of(array, j):
@@ -393,7 +399,7 @@
             return (
                 down_blocks,
                 (1, part, feat),
-                lambda i, p: (i, 2 * (p[0] ^ 1) + which - 1, 0),
+                lambda i, p: (i, 2 * (p[0] ^ 2) + which - 1, 0),
             )
         if which == 0:
             return (weights, (1, 1, 1, rows, feat), lambda i, p: (1, 0, i, 0, 0))
@@ -444,16 +450,11 @@
             16,
         )
 
-    def up_again(mine, got, far):
+    def up_again(mine, far):
         piece = mine.shape[1:]
         return call(
-            up_again_body,
-            place,
-            (1,),
-            [whole(mine), whole(got), whole(far)],
-            [whole_out(piece, BF16), whole_out(piece, F32)],
-            16,
-        )
+            up_again_body, place, (1,), [whole(mine), whole(far)], [whole_out(piece, BF16)], 16
+        )[0]
 
     give_e, keep_e = call_once(
         own_terms_body,
@@ -500,22 +501,32 @@
     slope_lo_s = own_slope(1, gate_lo)
 
     got_e, far_e = after((got_e, far_e), slope_lo_s)
-    send_e, mine_e = up_again(mine_e, got_e, far_e)
-    got_e = send_z(send_e, 2)
-
-    x_hi, cot_hi = after((x_hi, cot_hi), got_e)
+    last_e = send_z(up_again(mine_e, far_e), 2)
+
+    x_hi, cot_hi = after((x_hi, cot_hi), last_e)
     hid_hi, gate_hi = near_hidden(x_hi, 1)
 
-    def outputs_of(j, hid, adds):
-        run = functools.partial(call, by_grid(outputs_body), place, (local,))
-        if not adds:
-            run = functools.partial(call_once, outputs_body, place, local)
-        return run(
+    def outputs_of(j, hid, kind):
+        return call_once(
+            outputs_body,
+            place,
+            local,
             [down_of(j, which) for which in range(3)]
-            + [unit_of(array, j) for array in (hid, hid_lo, hid_hi)]
-            + [(a, one, every) for a in adds],
-            [(blocks, BF16, one, every)],
+            + [unit_of(array, j) for array in (hid, hid_lo, hid_hi)],
+            [(blocks, kind, one, every)],
             16,
+        )[0]
+
+    def added(own, got):
+        pairs_at = lambda i, p: (i, 0, 0)
+        two = (2, feat, tokens)
+        return call(
+            add_body,
+            place,
+            (local // 2,),
+            [(own, two, pairs_at), (got, two, pairs_at)],
+            [(blocks, BF16, two, pairs_at)],
+            20,
         )[0]
 
     shard = (2, 2, local, part, feat)
@@ -533,12 +544,12 @@
             ((3,) + shard[2:], BF16, (3,) + strip_d, lambda i, p: (0, i, 0, 0)),
         ],
         16,
-        scratch=[pltpu.VMEM((2, part, feat), BF16)],
+        scratch=[pltpu.VMEM((3, 2, part, feat), BF16)],
     )
     core_own, core_near = send_core(give_own), send_core(give_near)
     hid_b = after((hid,), give_own)[0]
-    near_out = outputs_of(1, hid_b, [])
-    got_out = send(near_out, 2)
+    near_out = outputs_of(1, hid_b, BF16)
+    got_out = send(near_out, 1)
     core_own, core_near = after((core_own, core_near), near_out)
     parts_d = (keep_e, first_got, keep_d, core_own, core_near)
     send_d, mine_d = call(
@@ -585,7 +596,7 @@
         [(blocks, BF16, one, every)],
         16,
     )[0]
-    got_grads = send(near_grads, 1)
+    got_grads = send(near_grads, 2)
 
     x_b = after((x,), near_grads)[0]
     give_lo, give_hi, keep_u = up_terms(
@@ -611,9 +622,25 @@
     )
     got_d = send_z(send_d, 2)
 
-    got_u, far_u = after((got_u, far_u), send_d)
-    send_u, mine_u = up_again(mine_u, got_u, far_u)
-    got_u = send_z(send_u, 2)
+    up_b = after((up_blocks,), send_d)[0]
+    own_grads = call_once(
+        grads_body,
+        place,
+        local,
+        [
+            (up_b, (1, feat, rows), lambda i, p: (i, 0, p[0])),
+            (up_b, (1, feat, rows), lambda i, p: (i, 0, p[0] ^ 1)),
+            (slope_ss, strip, at_i),
+            (slope_sn, strip, at_i),
+        ],
+        [(blocks, F32, one, every)],
+        16,
+    )[0]
+
+    own_out = outputs_of(0, after((hid,), own_grads)[0], F32)
+    far_u = after((far_u,), own_out)[0]
+    send_u = up_again(mine_u, far_u)
+    last_u = send_z(send_u, 2)
 
     got_d = after((got_d,), send_u)[0]
     sum_d = call(
@@ -627,39 +654,27 @@
     swaps = []
     for device in range(n_dp * n_tensor):
         dp, t = device // n_tensor, device % n_tensor
-        z_high, y = dp // 4, t // 2
-        swaps.append((device, (y * 4 + dp % 4) * n_tensor + z_high * 2 + t % 2))
+        z_low, x_at = dp // 2 % 2, t % 2
+        home = (dp // 4 * 4 + x_at * 2 + dp % 2) * n_tensor + t // 2 * 2 + z_low
+        swaps.append((device, home))
     home_d = lax.ppermute(sum_d, ("dp", "tensor"), swaps)
 
     got_out = after((got_out,), sum_d)[0]
-    outputs = outputs_of(0, hid, [got_out])
-
-    got_u = after((got_u,), outputs)[0]
+    outputs = added(own_out, got_out)
+
+    got_u, last_u = after((got_u, last_u), outputs)
     send_u, mine_u = call(
         functools.partial(up_sum_body, factor),
         place,
         (1,),
-        [whole(v) for v in (mine_e, got_e, mine_u, got_u)],
+        [whole(v) for v in (mine_e, got_e, last_e, mine_u, got_u, last_u)],
         [whole_out((2,) + shard_u[1:], BF16), whole_out((2,) + shard_u[1:], F32)],
         8,
     )
-    got_u = send(send_u, 1)
+    got_u = send(send_u, 2)
 
     got_grads = after((got_grads,), send_u)[0]
-    feature_grads = call(
-        by_grid(grads_body),
-        place,
-        (local,),
-        [
-            (up_blocks, (1, feat, rows), lambda i, p: (i, 0, p[0])),
-            (up_blocks, (1, feat, rows), lambda i, p: (i, 0, p[0] ^ 2)),
-            (slope_ss, strip, at_i),
-            (slope_sn, strip, at_i),
-            (got_grads, one, every),
-        ],
-        [(blocks, BF16, one, every)],
-        16,
-    )[0]
+    feature_grads = added(own_grads, got_grads)
 
     got_u, home_d = after((got_u, home_d), feature_grads)
     up_grads, down_grads = call(

time: 112 us -> 103 us (0.920)
  the two profiles are of different devices: /device:TPU:0 before, /device:TPU:12 now
where the time goes in v2:
time: 103 us
  Pallas kernels  39.1 us (38%)
  waiting for transfers between devices  33.7 us (33%)
  starting transfers between devices  25.8 us (25%)
  local copies, waits for them, and re-layouts  3.04 us (3%)
    pallas_call x25, Pallas kernels, call(): pl.pallas_call(body, grid_spec=pltpu.PrefetchScalarGridSpec(num_scalar_pr...  39.1 us
    ppermute x9, waiting for transfers between devices, send_z(): return lax.ppermute(value, 'dp', [(d, d ^ 2 * hop) for d in range(n_dp)])  20.4 us
    ppermute x9, starting transfers between devices, send_z(): return lax.ppermute(value, 'dp', [(d, d ^ 2 * hop) for d in range(n_dp)])  11.5 us
    ppermute x9, waiting for transfers between devices, send(): lax.ppermute(value, 'tensor', [(t, t ^ hop) for t in range(n_tensor)])  10.1 us
    ppermute x9, starting transfers between devices, send(): lax.ppermute(value, 'tensor', [(t, t ^ hop) for t in range(n_tensor)])  7.07 us
    ppermute x1, starting transfers between devices, square_device(): home_d = lax.ppermute(sum_d, ('dp', 'tensor'), swaps)  5.55 us
    ppermute x7, waiting for transfers between devices, send_core(): return lax.ppermute(value, 'dp', [(d, d ^ 1) for d in range(n_dp)])  3.18 us
  transfers between devices with their start and end apart: 26, of which 10 were waited for; matrix products, arithmetic and copies ran while one was open for 1% of the time, Pallas kernels for 31%

profile of v2, /device:TPU:12, one launch (start us, length us, event | category | flops | bytes accessed | tf_op | source)
XLA Modules:
  0.0 102.8 jit_solution(17593598781052398368)
XLA Ops:
  0.7 1.1 %dynamic-slice_bitcast_fusion.1 = (bf16[1,4,64,256]{3,2,1,0:T(8,128)(2,1)S(1)}, bf16[1,4,64,256]{3,2,1,0:T(8,128)(2,1)S(1)}) fusion(bf16[4,1024,256]{2,1,0:T(8,128)(2,1)} %refs_2_.1, s32[]{:T(128)S(6)} %select_n.19, s32[]{:T(128)S(6)} %select_n.20), kind=kLoop, calls=%fused_computation.4 | loop fusion | bytes 524296 | tf_op jit(solution)/shard_map/stack | solution.py:361
  1.8 1.6 %collective-permute-start.1 = (bf16[2,4,64,256]{3,2,1,0:T(8,128)(2,1)S(1)}, bf16[2,4,64,256]{3,2,1,0:T(8,128)(2,1)S(1)}, u32[]{:S(2)}, u32[]{:S(2)}) collective-permute-start(bf16[2,4,64,256]{3,2,1,0:T(8,128)(2,1)S(1)} %pad_maximum_fusion.2), channel_id=1, source_target_pairs={{0,1},{1,0},{2,3},{3,2},{4,5},{5,4},{6,7},{7,6},{8,9},{9,8},{10,11... | collective-permute-start | bytes 786440 | tf_op jit(solution)/shard_map/ppermute | solution.py:345
  7.4 5.8 %shard_map.75 = (bf16[2,4,4,64,768]{4,3,2,1,0:T(8,128)(2,1)S(1)}, bf16[2,4,4,64,768]{4,3,2,1,0:T(8,128)(2,1)S(1)}) custom-call(s32[3]{0:T(128)S(1)} %pad_add_fusion.place, bf16[4,256,768]{2,1,0:T(8,128)(2,1)S(1)} %bitcast.37, bf16[4,256,1024]{2,1,0:T(8,128)(2,1)S(1)} %copy-done.2), custom_call_target="tpu_custom_call" | custom-call | tf_op jit(solution)/shard_map/pallas_call | solution.py:74
  15.1 1.5 %collective-permute-start.7 = (bf16[2,256,768]{2,1,0:T(8,128)(2,1)S(1)}, bf16[2,256,768]{2,1,0:T(8,128)(2,1)S(1)}, u32[]{:S(2)}, u32[]{:S(2)}) collective-permute-start(bf16[2,256,768]{2,1,0:T(8,128)(2,1)S(1)} %bitcast.42), channel_id=1, source_target_pairs={{0,1},{1,0},{2,3},{3,2},{4,5},{5,4},{6,7},{7,6},{8,9},{9,8},{10,11... | collective-permute-start | bytes 2359304 | tf_op jit(solution)/shard_map/ppermute | solution.py:345
  16.6 1.1 %shard_map.76.refs_3_.refs_2_ = bf16[4,4,64,768]{3,2,1,0:T(8,128)(2,1)S(1)} custom-call(s32[3]{0:T(128)S(1)} %pad_add_fusion.place, bf16[4,256,768]{2,1,0:T(8,128)(2,1)S(1)} %bitcast.32, bf16[4,1024,256]{2,1,0:T(8,128)(2,1)S(1)} %copy-done, bf16[2,4,4,64,768]{4,3,2,1,0:T(8,128)(2,1)S(1)} %get-tuple-element.73.refs_2_.refs_7_), custom_call_target="tpu_custom_call" | custom-call | tf_op jit(solution)/shard_map/pallas_call | solution.py:74
  17.7 1.6 %shard_map.77 = (bf16[2,4,128,256]{3,2,1,0:T(8,128)(2,1)S(1)}, bf16[2,4,128,256]{3,2,1,0:T(8,128)(2,1)S(1)}) custom-call(s32[3]{0:T(128)S(1)} %pad_add_fusion.place, bf16[4,256,768]{2,1,0:T(8,128)(2,1)S(1)} %bitcast.33, bf16[2,4,4,64,768]{4,3,2,1,0:T(8,128)(2,1)S(1)} %get-tuple-element.123.refs_1_.refs_3_, bf16[4,256,768]{2,1,0:T(8,128)(2,1)S(1)} %bitcast.38, ...), custom_call_target="tpu_custom_call" | custom-call | tf_op jit(solution)/shard_map/pallas_call | solution.py:74
  19.3 7.5 %collective-permute-done.2.refs_1_ = bf16[2,2,4,64,256]{4,3,2,1,0:T(8,128)(2,1)S(1)} collective-permute-done((bf16[2,2,4,64,256]{4,3,2,1,0:T(8,128)(2,1)S(1)}, bf16[2,2,4,64,256]{4,3,2,1,0:T(8,128)(2,1)S(1)}, u32[]{:S(2)}, u32[]{:S(2)}) %collective-permute-start.2) | collective-permute-done | bytes 524320 | tf_op jit(solution)/shard_map/ppermute | solution.py:348
  26.8 3.8 %collective-permute-done.3.x_ref.refs_1_ = bf16[2,256,768]{2,1,0:T(8,128)(2,1)S(1)} collective-permute-done((bf16[2,256,768]{2,1,0:T(8,128)(2,1)S(1)}, bf16[2,256,768]{2,1,0:T(8,128)(2,1)S(1)}, u32[]{:S(2)}, u32[]{:S(2)}) %collective-permute-start.3) | collective-permute-done | bytes 786464 | tf_op jit(solution)/shard_map/ppermute | solution.py:345
  31.1 1.4 %collective-permute-done.5.refs_0_.first_got = bf16[2,4,128,256]{3,2,1,0:T(8,128)(2,1)S(1)} collective-permute-done((bf16[2,4,128,256]{3,2,1,0:T(8,128)(2,1)S(1)}, bf16[2,4,128,256]{3,2,1,0:T(8,128)(2,1)S(1)}, u32[]{:S(2)}, u32[]{:S(2)}) %collective-permute-start.5) | collective-permute-done | bytes 524320 | tf_op jit(solution)/shard_map/ppermute | solution.py:351
  33.6 1.6 %collective-permute-start.8 = (bf16[1,128,256]{2,1,0:T(8,128)(2,1)S(1)}, bf16[1,128,256]{2,1,0:T(8,128)(2,1)S(1)}, u32[]{:S(2)}, u32[]{:S(2)}) collective-permute-start(bf16[1,128,256]{2,1,0:T(8,128)(2,1)S(1)} %get-tuple-element.86), channel_id=1, source_target_pairs={{0,8},{4,12},{8,0},{12,4},{16,24},{20,28},{24,16},{28,20},{1,9},{5... | collective-permute-start | bytes 196616 | tf_op jit(solution)/shard_map/ppermute | solution.py:348
  35.9 3.1 %shard_map.80 = (bf16[2,4,2,64,768]{4,3,2,1,0:T(8,128)(2,1)S(1)}, bf16[2,4,2,64,768]{4,3,2,1,0:T(8,128)(2,1)S(1)}) custom-call(s32[3]{0:T(128)S(1)} %pad_add_fusion.place, bf16[2,256,768]{2,1,0:T(8,128)(2,1)S(1)} %collective-permute-done.3.x_ref.refs_1_, bf16[2,2,4,256,256]{4,3,2,1,0:T(8,128)(2,1)S(1)} %bitcast.22), custom_call_target="tpu_custom_call" | custom-call | tf_op jit(solution)/shard_map/pallas_call | solution.py:74
  40.5 2.7 %collective-permute-start.12 = (bf16[1,128,256]{2,1,0:T(8,128)(2,1)S(1)}, bf16[1,128,256]{2,1,0:T(8,128)(2,1)S(1)}, u32[]{:S(2)}, u32[]{:S(2)}) collective-permute-start(bf16[1,128,256]{2,1,0:T(8,128)(2,1)S(1)} %shard_map.82), channel_id=1, source_target_pairs={{0,16},{4,20},{8,24},{12,28},{16,0},{20,4},{24,8},{28,12},{1,17},{... | collective-permute-start | bytes 196616 | tf_op jit(solution)/shard_map/ppermute | solution.py:348
  43.1 2.8 %collective-permute-done.6.x_ref.refs_2_ = bf16[2,256,768]{2,1,0:T(8,128)(2,1)S(1)} collective-permute-done((bf16[2,256,768]{2,1,0:T(8,128)(2,1)S(1)}, bf16[2,256,768]{2,1,0:T(8,128)(2,1)S(1)}, u32[]{:S(2)}, u32[]{:S(2)}) %collective-permute-start.6) | collective-permute-done | bytes 786464 | tf_op jit(solution)/shard_map/ppermute | solution.py:345
  46.0 3.3 %shard_map.83 = (bf16[2,4,2,64,768]{4,3,2,1,0:T(8,128)(2,1)S(1)}, bf16[2,4,2,64,768]{4,3,2,1,0:T(8,128)(2,1)S(1)}) custom-call(s32[3]{0:T(128)S(1)} %pad_add_fusion.place, bf16[2,256,768]{2,1,0:T(8,128)(2,1)S(1)} %collective-permute-done.6.x_ref.refs_2_, bf16[2,2,4,256,256]{4,3,2,1,0:T(8,128)(2,1)S(1)} %bitcast.23), custom_call_target="tpu_custom_call" | custom-call | tf_op jit(solution)/shard_map/pallas_call | solution.py:74
  49.2 2.0 %shard_map.84 = (bf16[4,128,256]{2,1,0:T(8,128)(2,1)S(1)}, bf16[2,4,128,256]{3,2,1,0:T(8,128)(2,1)S(1)}, bf16[3,4,128,256]{3,2,1,0:T(8,128)(2,1)S(1)}) custom-call(s32[3]{0:T(128)S(1)} %pad_add_fusion.place, bf16[4,256,768]{2,1,0:T(8,128)(2,1)S(1)} %bitcast.35, bf16[2,256,768]{2,1,0:T(8,128)(2,1)S(1)} %collective-permute-done.4.refs_1_, ...), custom_call_target="tpu_custom_call" | custom-call | tf_op jit(solution)/shard_map/pallas_call | solution.py:74
  51.9 1.5 %shard_map.85 = bf16[4,256,768]{2,1,0:T(8,128)(2,1)S(1)} custom-call(s32[3]{0:T(128)S(1)} %pad_add_fusion.place, bf16[2,2,4,256,256]{4,3,2,1,0:T(8,128)(2,1)S(1)} %bitcast.24, bf16[2,2,4,256,256]{4,3,2,1,0:T(8,128)(2,1)S(1)} %bitcast.25, bf16[2,2,4,256,256]{4,3,2,1,0:T(8,128)(2,1)S(1)} %bitcast.26, ...), custom_call_target="tpu_custom_call" | custom-call | tf_op jit(solution)/shard_map/pallas_call | solution.py:74
  55.7 1.7 %shard_map.87 = (bf16[4,4,64,768]{3,2,1,0:T(8,128)(2,1)S(1)}, bf16[4,2,64,768]{3,2,1,0:T(8,128)(2,1)S(1)}, bf16[4,2,64,768]{3,2,1,0:T(8,128)(2,1)S(1)}, bf16[4,2,64,768]{3,2,1,0:T(8,128)(2,1)S(1)}) custom-call(s32[3]{0:T(128)S(1)} %pad_add_fusion.place, bf16[4,256,768]{2,1,0:T(8,128)(2,1)S(1)} %bitcast.36, ...), custom_call_target="tpu_custom_call" | custom-call | tf_op jit(solution)/shard_map/pallas_call | solution.py:74
  57.4 1.5 %shard_map.88 = bf16[4,256,768]{2,1,0:T(8,128)(2,1)S(1)} custom-call(s32[3]{0:T(128)S(1)} %pad_add_fusion.place, bf16[2,2,4,256,256]{4,3,2,1,0:T(8,128)(2,1)S(1)} %bitcast.30, bf16[2,2,4,256,256]{4,3,2,1,0:T(8,128)(2,1)S(1)} %bitcast.31, bf16[4,2,64,768]{3,2,1,0:T(8,128)(2,1)S(1)} %shard_map.81.refs_2_.refs_4_, ...), custom_call_target="tpu_custom_call" | custom-call | tf_op jit(solution)/shard_map/pallas_call | solution.py:74
  59.5 2.1 %shard_map.89 = (bf16[3,4,64,256]{3,2,1,0:T(8,128)(2,1)S(1)}, bf16[3,4,64,256]{3,2,1,0:T(8,128)(2,1)S(1)}, bf16[3,4,128,256]{3,2,1,0:T(8,128)(2,1)S(1)}) custom-call(s32[3]{0:T(128)S(1)} %pad_add_fusion.place, bf16[4,256,768]{2,1,0:T(8,128)(2,1)S(1)} %bitcast.39, bf16[2,256,768]{2,1,0:T(8,128)(2,1)S(1)} %collective-permute-done.3.x_ref.refs_1_, ...), custom_call_target="tpu_custom_call" | custom-call | flops 16000000000 | tf_op jit(solution)/shard_map/pallas_call | solution.py:74
  62.1 1.2 %collective-permute-done.16.refs_0_ = bf16[3,4,64,256]{3,2,1,0:T(8,128)(2,1)S(1)} collective-permute-done((bf16[3,4,64,256]{3,2,1,0:T(8,128)(2,1)S(1)}, bf16[3,4,64,256]{3,2,1,0:T(8,128)(2,1)S(1)}, u32[]{:S(2)}, u32[]{:S(2)}) %collective-permute-start.16) | collective-permute-done | bytes 393248 | tf_op jit(solution)/shard_map/ppermute | solution.py:351
  64.6 1.5 %collective-permute-start.20 = (bf16[3,128,256]{2,1,0:T(8,128)(2,1)S(1)}, bf16[3,128,256]{2,1,0:T(8,128)(2,1)S(1)}, u32[]{:S(2)}, u32[]{:S(2)}) collective-permute-start(bf16[3,128,256]{2,1,0:T(8,128)(2,1)S(1)} %get-tuple-element.126), channel_id=1, source_target_pairs={{0,8},{4,12},{8,0},{12,4},{16,24},{20,28},{24,16},{28,20},{1,9},{5... | collective-permute-start | bytes 589832 | tf_op jit(solution)/shard_map/ppermute | solution.py:348
  66.2 3.7 %collective-permute-done.15.got_ref = bf16[2,4,128,256]{3,2,1,0:T(8,128)(2,1)S(1)} collective-permute-done((bf16[2,4,128,256]{3,2,1,0:T(8,128)(2,1)S(1)}, bf16[2,4,128,256]{3,2,1,0:T(8,128)(2,1)S(1)}, u32[]{:S(2)}, u32[]{:S(2)}) %collective-permute-start.15) | collective-permute-done | bytes 524320 | tf_op jit(solution)/shard_map/ppermute | solution.py:348
  70.6 3.0 %collective-permute-start.19 = (bf16[4,128,256]{2,1,0:T(8,128)(2,1)S(1)}, bf16[4,128,256]{2,1,0:T(8,128)(2,1)S(1)}, u32[]{:S(2)}, u32[]{:S(2)}) collective-permute-start(bf16[4,128,256]{2,1,0:T(8,128)(2,1)S(1)} %get-tuple-element.121), channel_id=1, source_target_pairs={{0,16},{4,20},{8,24},{12,28},{16,0},{20,4},{24,8},{28,12},{1,17},{... | collective-permute-start | bytes 786440 | tf_op jit(solution)/shard_map/ppermute | solution.py:348
  73.6 1.5 %shard_map.92.own_ref = f32[4,256,768]{2,1,0:T(8,128)S(1)} custom-call(s32[3]{0:T(128)S(1)} %pad_add_fusion.place, bf16[4,256,1024]{2,1,0:T(8,128)(2,1)S(1)} %copy-done.2, bf16[4,256,1024]{2,1,0:T(8,128)(2,1)S(1)} %copy-done.2, bf16[4,4,64,768]{3,2,1,0:T(8,128)(2,1)S(1)} %shard_map.76.refs_3_.refs_2_, bf16[4,4,64,768]{3,2,1,0:T(8,128)(2,1)S(1)} %get-tuple-element.115.refs_3_), custom_call_target="tpu_custom_call" | custom-call | tf_op jit(solution)/shard_map/pallas_call | solution.py:74
  75.1 1.5 %shard_map.93.own_ref = f32[4,256,768]{2,1,0:T(8,128)S(1)} custom-call(s32[3]{0:T(128)S(1)} %pad_add_fusion.place, bf16[4,1024,256]{2,1,0:T(8,128)(2,1)S(1)} %copy-done, bf16[4,1024,256]{2,1,0:T(8,128)(2,1)S(1)} %copy-done, bf16[4,1024,256]{2,1,0:T(8,128)(2,1)S(1)} %copy-done, bf16[2,4,4,64,768]{4,3,2,1,0:T(8,128)(2,1)S(1)} %get-tuple-element.123.refs_1_.refs_3_, ...), custom_call_target="tpu_custom_call" | custom-call | tf_op jit(solution)/shard_map/pallas_call | solution.py:74
  77.3 1.1 %collective-permute-start.23 = (bf16[3,128,256]{2,1,0:T(8,128)(2,1)S(1)}, bf16[3,128,256]{2,1,0:T(8,128)(2,1)S(1)}, u32[]{:S(2)}, u32[]{:S(2)}) collective-permute-start(bf16[3,128,256]{2,1,0:T(8,128)(2,1)S(1)} %shard_map.94), channel_id=1, source_target_pairs={{0,16},{4,20},{8,24},{12,28},{16,0},{20,4},{24,8},{28,12},{1,17},{... | collective-permute-start | bytes 589832 | tf_op jit(solution)/shard_map/ppermute | solution.py:348
  78.4 9.2 %collective-permute-done.19.got_ref = bf16[4,128,256]{2,1,0:T(8,128)(2,1)S(1)} collective-permute-done((bf16[4,128,256]{2,1,0:T(8,128)(2,1)S(1)}, bf16[4,128,256]{2,1,0:T(8,128)(2,1)S(1)}, u32[]{:S(2)}, u32[]{:S(2)}) %collective-permute-start.19) | collective-permute-done | bytes 262176 | tf_op jit(solution)/shard_map/ppermute | solution.py:348
  88.2 5.5 %collective-permute-start.25 = (bf16[4,128,256]{2,1,0:T(8,128)(2,1)S(1)}, bf16[4,128,256]{2,1,0:T(8,128)(2,1)S(1)}, u32[]{:S(2)}, u32[]{:S(2)}) collective-permute-start(bf16[4,128,256]{2,1,0:T(8,128)(2,1)S(1)} %shard_map.95), channel_id=1, source_target_pairs={{0,0},{1,8},{2,2},{3,10},{4,4},{5,12},{6,6},{7,14},{8,1},{9,9},{10... | collective-permute-start | bytes 786440 | tf_op jit(solution)/shard_map/ppermute | solution.py:660
  93.7 1.8 %shard_map.96 = bf16[4,256,768]{2,1,0:T(8,128)(2,1)} custom-call(s32[3]{0:T(128)S(1)} %pad_add_fusion.place, f32[4,256,768]{2,1,0:T(8,128)S(1)} %shard_map.93.own_ref, bf16[4,256,768]{2,1,0:T(8,128)(2,1)S(1)} %collective-permute-done.18.got_ref), custom_call_target="tpu_custom_call" | custom-call | tf_op jit(solution)/shard_map/pallas_call | solution.py:74
  96.3 1.8 %shard_map.98 = bf16[4,256,768]{2,1,0:T(8,128)(2,1)} custom-call(s32[3]{0:T(128)S(1)} %pad_add_fusion.place, f32[4,256,768]{2,1,0:T(8,128)S(1)} %shard_map.92.own_ref, bf16[4,256,768]{2,1,0:T(8,128)(2,1)S(1)} %collective-permute-done.21.got_ref), custom_call_target="tpu_custom_call" | custom-call | tf_op jit(solution)/shard_map/pallas_call | solution.py:74
  98.1 3.1 %collective-permute-done.24.got_ref = bf16[2,128,256]{2,1,0:T(8,128)(2,1)S(1)} collective-permute-done((bf16[2,128,256]{2,1,0:T(8,128)(2,1)S(1)}, bf16[2,128,256]{2,1,0:T(8,128)(2,1)S(1)}, u32[]{:S(2)}, u32[]{:S(2)}) %collective-permute-start.24) | collective-permute-done | bytes 131104 | tf_op jit(solution)/shard_map/ppermute | solution.py:345
  101.2 1.6 %shard_map.99 = (f32[4,32,1024]{2,1,0:T(8,128)}, f32[4,128,256]{2,1,0:T(8,128)}) custom-call(s32[3]{0:T(128)S(1)} %pad_add_fusion.place, f32[2,128,256]{2,1,0:T(8,128)S(1)} %get-tuple-element.135.mine_ref, bf16[2,128,256]{2,1,0:T(8,128)(2,1)S(1)} %collective-permute-done.24.got_ref, bf16[4,128,256]{2,1,0:T(8,128)(2,1)S(1)} %collective-permute-done.25.down_in), custom_call_target="tpu_custom_call" | custom-call | tf_op jit(solution)/shard_map/pallas_call | solution.py:74
  (61 shorter events, 17.4 us)
Async XLA Ops:
  0.6 4.4 %copy-start.3 = (bf16[1024,768]{1,0:T(8,128)(2,1)S(1)}, bf16[1024,768]{1,0:T(8,128)(2,1)}, u32[]{:S(2)}) copy-start(bf16[1024,768]{1,0:T(8,128)(2,1)} %param.4) | copy-start | bytes 4718596
  1.8 11.5 %collective-permute-start.1 = (bf16[2,4,64,256]{3,2,1,0:T(8,128)(2,1)S(1)}, bf16[2,4,64,256]{3,2,1,0:T(8,128)(2,1)S(1)}, u32[]{:S(2)}, u32[]{:S(2)}) collective-permute-start(bf16[2,4,64,256]{3,2,1,0:T(8,128)(2,1)S(1)} %pad_maximum_fusion.2), channel_id=1, source_target_pairs={{0,1},{1,0},{2,3},{3,2},{4,5},{5,4},{6,7},{7,6},{8,9},{9,8},{10,11... | collective-permute-start | bytes 786440 | tf_op jit(solution)/shard_map/ppermute | solution.py:345
  4.4 1.4 %copy-start.1 = (bf16[1024,768]{1,0:T(8,128)(2,1)S(1)}, bf16[1024,768]{1,0:T(8,128)(2,1)}, u32[]{:S(2)}) copy-start(bf16[1024,768]{1,0:T(8,128)(2,1)} %param.5) | copy-start | bytes 4718596
  4.4 9.3 %collective-permute-start = (bf16[2,4,64,256]{3,2,1,0:T(8,128)(2,1)S(1)}, bf16[2,4,64,256]{3,2,1,0:T(8,128)(2,1)S(1)}, u32[]{:S(2)}, u32[]{:S(2)}) collective-permute-start(bf16[2,4,64,256]{3,2,1,0:T(8,128)(2,1)S(1)} %pad_maximum_fusion.1), channel_id=1, source_target_pairs={{0,2},{1,3},{2,0},{3,1},{4,6},{5,7},{6,4},{7,5},{8,10},{9,11},{10,... | collective-permute-start | bytes 786440 | tf_op jit(solution)/shard_map/ppermute | solution.py:345
  5.8 1.6 %copy-start.2 = (bf16[4,256,1024]{2,1,0:T(8,128)(2,1)S(1)}, bf16[4,256,1024]{2,1,0:T(8,128)(2,1)}, u32[]{:S(2)}) copy-start(bf16[4,256,1024]{2,1,0:T(8,128)(2,1)} %refs_1_.5) | copy-start | bytes 6291460
  5.9 24.6 %collective-permute-start.3 = (bf16[2,256,768]{2,1,0:T(8,128)(2,1)S(1)}, bf16[2,256,768]{2,1,0:T(8,128)(2,1)S(1)}, u32[]{:S(2)}, u32[]{:S(2)}) collective-permute-start(bf16[2,256,768]{2,1,0:T(8,128)(2,1)S(1)} %bitcast.45), channel_id=1, source_target_pairs={{0,2},{1,3},{2,0},{3,1},{4,6},{5,7},{6,4},{7,5},{8,10},{9,11},{10,... | collective-permute-start | bytes 2359304 | tf_op jit(solution)/shard_map/ppermute | solution.py:345
  6.8 23.8 %collective-permute-start.4 = (bf16[2,256,768]{2,1,0:T(8,128)(2,1)S(1)}, bf16[2,256,768]{2,1,0:T(8,128)(2,1)S(1)}, u32[]{:S(2)}, u32[]{:S(2)}) collective-permute-start(bf16[2,256,768]{2,1,0:T(8,128)(2,1)S(1)} %bitcast.44), channel_id=1, source_target_pairs={{0,1},{1,0},{2,3},{3,2},{4,5},{5,4},{6,7},{7,6},{8,9},{9,8},{10,11... | collective-permute-start | bytes 2359304 | tf_op jit(solution)/shard_map/ppermute | solution.py:345
  7.4 9.1 %copy-start = (bf16[4,1024,256]{2,1,0:T(8,128)(2,1)S(1)}, bf16[4,1024,256]{2,1,0:T(8,128)(2,1)}, u32[]{:S(2)}) copy-start(bf16[4,1024,256]{2,1,0:T(8,128)(2,1)} %refs_2_.1) | copy-start | bytes 6291460
  13.8 13.0 %collective-permute-start.2 = (bf16[2,2,4,64,256]{4,3,2,1,0:T(8,128)(2,1)S(1)}, bf16[2,2,4,64,256]{4,3,2,1,0:T(8,128)(2,1)S(1)}, u32[]{:S(2)}, u32[]{:S(2)}) collective-permute-start(bf16[2,2,4,64,256]{4,3,2,1,0:T(8,128)(2,1)S(1)} %pad_maximum_fusion.refs_0_), channel_id=1, source_target_pairs={{0,8},{4,12},{8,0},{12,4},{16,24},{20,28},{24,16},{28,20},{1,9},{5... | collective-permute-start | bytes 1572872 | tf_op jit(solution)/shard_map/ppermute | solution.py:348
  14.3 31.7 %collective-permute-start.6 = (bf16[2,256,768]{2,1,0:T(8,128)(2,1)S(1)}, bf16[2,256,768]{2,1,0:T(8,128)(2,1)S(1)}, u32[]{:S(2)}, u32[]{:S(2)}) collective-permute-start(bf16[2,256,768]{2,1,0:T(8,128)(2,1)S(1)} %bitcast.43), channel_id=1, source_target_pairs={{0,2},{1,3},{2,0},{3,1},{4,6},{5,7},{6,4},{7,5},{8,10},{9,11},{10,... | collective-permute-start | bytes 2359304 | tf_op jit(solution)/shard_map/ppermute | solution.py:345
  15.1 30.9 %collective-permute-start.7 = (bf16[2,256,768]{2,1,0:T(8,128)(2,1)S(1)}, bf16[2,256,768]{2,1,0:T(8,128)(2,1)S(1)}, u32[]{:S(2)}, u32[]{:S(2)}) collective-permute-start(bf16[2,256,768]{2,1,0:T(8,128)(2,1)S(1)} %bitcast.42), channel_id=1, source_target_pairs={{0,1},{1,0},{2,3},{3,2},{4,5},{5,4},{6,7},{7,6},{8,9},{9,8},{10,11... | collective-permute-start | bytes 2359304 | tf_op jit(solution)/shard_map/ppermute | solution.py:345
  30.6 1.9 %collective-permute-start.5 = (bf16[2,4,128,256]{3,2,1,0:T(8,128)(2,1)S(1)}, bf16[2,4,128,256]{3,2,1,0:T(8,128)(2,1)S(1)}, u32[]{:S(2)}, u32[]{:S(2)}) collective-permute-start(bf16[2,4,128,256]{3,2,1,0:T(8,128)(2,1)S(1)} %get-tuple-element.82), channel_id=1, source_target_pairs={{0,4},{4,0},{8,12},{12,8},{16,20},{20,16},{24,28},{28,24},{1,5},{5... | collective-permute-start | bytes 1572872 | tf_op jit(solution)/shard_map/ppermute | solution.py:351
  30.6 3.0 %collective-permute-start.10 = (bf16[2,2,4,64,256]{4,3,2,1,0:T(8,128)(2,1)S(1)}, bf16[2,2,4,64,256]{4,3,2,1,0:T(8,128)(2,1)S(1)}, u32[]{:S(2)}, u32[]{:S(2)}) collective-permute-start(bf16[2,2,4,64,256]{4,3,2,1,0:T(8,128)(2,1)S(1)} %pad_maximum_fusion.refs_0_), channel_id=1, source_target_pairs={{0,4},{4,0},{8,12},{12,8},{16,20},{20,16},{24,28},{28,24},{1,5},{5... | collective-permute-start | bytes 1572872 | tf_op jit(solution)/shard_map/ppermute | solution.py:351
  31.1 4.1 %collective-permute-start.11 = (bf16[2,2,4,64,256]{4,3,2,1,0:T(8,128)(2,1)S(1)}, bf16[2,2,4,64,256]{4,3,2,1,0:T(8,128)(2,1)S(1)}, u32[]{:S(2)}, u32[]{:S(2)}) collective-permute-start(bf16[2,2,4,64,256]{4,3,2,1,0:T(8,128)(2,1)S(1)} %collective-permute-done.2.refs_1_), channel_id=1, source_target_pairs={{0,4},{4,0},{8,12},{12,8},{16,20},{20,16},{24,28},{28,24},{1,5},{5... | collective-permute-start | bytes 1572872 | tf_op jit(solution)/shard_map/ppermute | solution.py:351
  33.1 6.8 %collective-permute-start.9 = (bf16[1,128,256]{2,1,0:T(8,128)(2,1)S(1)}, bf16[1,128,256]{2,1,0:T(8,128)(2,1)S(1)}, u32[]{:S(2)}, u32[]{:S(2)}) collective-permute-start(bf16[1,128,256]{2,1,0:T(8,128)(2,1)S(1)} %get-tuple-element.87), channel_id=1, source_target_pairs={{0,8},{4,12},{8,0},{12,4},{16,24},{20,28},{24,16},{28,20},{1,9},{5... | collective-permute-start | bytes 196616 | tf_op jit(solution)/shard_map/ppermute | solution.py:348
  33.6 6.3 %collective-permute-start.8 = (bf16[1,128,256]{2,1,0:T(8,128)(2,1)S(1)}, bf16[1,128,256]{2,1,0:T(8,128)(2,1)S(1)}, u32[]{:S(2)}, u32[]{:S(2)}) collective-permute-start(bf16[1,128,256]{2,1,0:T(8,128)(2,1)S(1)} %get-tuple-element.86), channel_id=1, source_target_pairs={{0,8},{4,12},{8,0},{12,4},{16,24},{20,28},{24,16},{28,20},{1,9},{5... | collective-permute-start | bytes 196616 | tf_op jit(solution)/shard_map/ppermute | solution.py:348
  40.5 5.5 %collective-permute-start.12 = (bf16[1,128,256]{2,1,0:T(8,128)(2,1)S(1)}, bf16[1,128,256]{2,1,0:T(8,128)(2,1)S(1)}, u32[]{:S(2)}, u32[]{:S(2)}) collective-permute-start(bf16[1,128,256]{2,1,0:T(8,128)(2,1)S(1)} %shard_map.82), channel_id=1, source_target_pairs={{0,16},{4,20},{8,24},{12,28},{16,0},{20,4},{24,8},{28,12},{1,17},{... | collective-permute-start | bytes 196616 | tf_op jit(solution)/shard_map/ppermute | solution.py:348
  51.3 2.7 %collective-permute-start.14 = (bf16[2,4,128,256]{3,2,1,0:T(8,128)(2,1)S(1)}, bf16[2,4,128,256]{3,2,1,0:T(8,128)(2,1)S(1)}, u32[]{:S(2)}, u32[]{:S(2)}) collective-permute-start(bf16[2,4,128,256]{3,2,1,0:T(8,128)(2,1)S(1)} %get-tuple-element.101), channel_id=1, source_target_pairs={{0,4},{4,0},{8,12},{12,8},{16,20},{20,16},{24,28},{28,24},{1,5},{5... | collective-permute-start | bytes 1572872 | tf_op jit(solution)/shard_map/ppermute | solution.py:351
  51.4 2.7 %collective-permute-start.13 = (bf16[4,128,256]{2,1,0:T(8,128)(2,1)S(1)}, bf16[4,128,256]{2,1,0:T(8,128)(2,1)S(1)}, u32[]{:S(2)}, u32[]{:S(2)}) collective-permute-start(bf16[4,128,256]{2,1,0:T(8,128)(2,1)S(1)} %get-tuple-element.100), channel_id=1, source_target_pairs={{0,4},{4,0},{8,12},{12,8},{16,20},{20,16},{24,28},{28,24},{1,5},{5... | collective-permute-start | bytes 786440 | tf_op jit(solution)/shard_map/ppermute | solution.py:351
  53.4 40.3 %collective-permute-start.18 = (bf16[4,256,768]{2,1,0:T(8,128)(2,1)S(1)}, bf16[4,256,768]{2,1,0:T(8,128)(2,1)S(1)}, u32[]{:S(2)}, u32[]{:S(2)}) collective-permute-start(bf16[4,256,768]{2,1,0:T(8,128)(2,1)S(1)} %shard_map.85), channel_id=1, source_target_pairs={{0,1},{1,0},{2,3},{3,2},{4,5},{5,4},{6,7},{7,6},{8,9},{9,8},{10,11... | collective-permute-start | bytes 4718600 | tf_op jit(solution)/shard_map/ppermute | solution.py:345
  55.0 14.9 %collective-permute-start.15 = (bf16[2,4,128,256]{3,2,1,0:T(8,128)(2,1)S(1)}, bf16[2,4,128,256]{3,2,1,0:T(8,128)(2,1)S(1)}, u32[]{:S(2)}, u32[]{:S(2)}) collective-permute-start(bf16[2,4,128,256]{3,2,1,0:T(8,128)(2,1)S(1)} %get-tuple-element.106), channel_id=1, source_target_pairs={{0,8},{4,12},{8,0},{12,4},{16,24},{20,28},{24,16},{28,20},{1,9},{5... | collective-permute-start | bytes 1572872 | tf_op jit(solution)/shard_map/ppermute | solution.py:348
  58.9 37.4 %collective-permute-start.21 = (bf16[4,256,768]{2,1,0:T(8,128)(2,1)S(1)}, bf16[4,256,768]{2,1,0:T(8,128)(2,1)S(1)}, u32[]{:S(2)}, u32[]{:S(2)}) collective-permute-start(bf16[4,256,768]{2,1,0:T(8,128)(2,1)S(1)} %shard_map.88), channel_id=1, source_target_pairs={{0,2},{1,3},{2,0},{3,1},{4,6},{5,7},{6,4},{7,5},{8,10},{9,11},{10,... | collective-permute-start | bytes 4718600 | tf_op jit(solution)/shard_map/ppermute | solution.py:345
  61.6 1.8 %collective-permute-start.16 = (bf16[3,4,64,256]{3,2,1,0:T(8,128)(2,1)S(1)}, bf16[3,4,64,256]{3,2,1,0:T(8,128)(2,1)S(1)}, u32[]{:S(2)}, u32[]{:S(2)}) collective-permute-start(bf16[3,4,64,256]{3,2,1,0:T(8,128)(2,1)S(1)} %get-tuple-element.117), channel_id=1, source_target_pairs={{0,4},{4,0},{8,12},{12,8},{16,20},{20,16},{24,28},{28,24},{1,5},{5... | collective-permute-start | bytes 1179656 | tf_op jit(solution)/shard_map/ppermute | solution.py:351
  61.6 2.3 %collective-permute-start.17 = (bf16[3,4,64,256]{3,2,1,0:T(8,128)(2,1)S(1)}, bf16[3,4,64,256]{3,2,1,0:T(8,128)(2,1)S(1)}, u32[]{:S(2)}, u32[]{:S(2)}) collective-permute-start(bf16[3,4,64,256]{3,2,1,0:T(8,128)(2,1)S(1)} %get-tuple-element.118), channel_id=1, source_target_pairs={{0,4},{4,0},{8,12},{12,8},{16,20},{20,16},{24,28},{28,24},{1,5},{5... | collective-permute-start | bytes 1179656 | tf_op jit(solution)/shard_map/ppermute | solution.py:351
  64.6 12.1 %collective-permute-start.20 = (bf16[3,128,256]{2,1,0:T(8,128)(2,1)S(1)}, bf16[3,128,256]{2,1,0:T(8,128)(2,1)S(1)}, u32[]{:S(2)}, u32[]{:S(2)}) collective-permute-start(bf16[3,128,256]{2,1,0:T(8,128)(2,1)S(1)} %get-tuple-element.126), channel_id=1, source_target_pairs={{0,8},{4,12},{8,0},{12,4},{16,24},{20,28},{24,16},{28,20},{1,9},{5... | collective-permute-start | bytes 589832 | tf_op jit(solution)/shard_map/ppermute | solution.py:348
  70.6 17.0 %collective-permute-start.19 = (bf16[4,128,256]{2,1,0:T(8,128)(2,1)S(1)}, bf16[4,128,256]{2,1,0:T(8,128)(2,1)S(1)}, u32[]{:S(2)}, u32[]{:S(2)}) collective-permute-start(bf16[4,128,256]{2,1,0:T(8,128)(2,1)S(1)} %get-tuple-element.121), channel_id=1, source_target_pairs={{0,16},{4,20},{8,24},{12,28},{16,0},{20,4},{24,8},{28,12},{1,17},{... | collective-permute-start | bytes 786440 | tf_op jit(solution)/shard_map/ppermute | solution.py:348
  73.6 22.0 %collective-permute-start.22 = (bf16[3,128,256]{2,1,0:T(8,128)(2,1)S(1)}, bf16[3,128,256]{2,1,0:T(8,128)(2,1)S(1)}, u32[]{:S(2)}, u32[]{:S(2)}) collective-permute-start(bf16[3,128,256]{2,1,0:T(8,128)(2,1)S(1)} %get-tuple-element.119), channel_id=1, source_target_pairs={{0,8},{4,12},{8,0},{12,4},{16,24},{20,28},{24,16},{28,20},{1,9},{5... | collective-permute-start | bytes 589832 | tf_op jit(solution)/shard_map/ppermute | solution.py:348
  77.3 18.3 %collective-permute-start.23 = (bf16[3,128,256]{2,1,0:T(8,128)(2,1)S(1)}, bf16[3,128,256]{2,1,0:T(8,128)(2,1)S(1)}, u32[]{:S(2)}, u32[]{:S(2)}) collective-permute-start(bf16[3,128,256]{2,1,0:T(8,128)(2,1)S(1)} %shard_map.94), channel_id=1, source_target_pairs={{0,16},{4,20},{8,24},{12,28},{16,0},{20,4},{24,8},{28,12},{1,17},{... | collective-permute-start | bytes 589832 | tf_op jit(solution)/shard_map/ppermute | solution.py:348
  88.2 10.0 %collective-permute-start.25 = (bf16[4,128,256]{2,1,0:T(8,128)(2,1)S(1)}, bf16[4,128,256]{2,1,0:T(8,128)(2,1)S(1)}, u32[]{:S(2)}, u32[]{:S(2)}) collective-permute-start(bf16[4,128,256]{2,1,0:T(8,128)(2,1)S(1)} %shard_map.95), channel_id=1, source_target_pairs={{0,0},{1,8},{2,2},{3,10},{4,4},{5,12},{6,6},{7,14},{8,1},{9,9},{10... | collective-permute-start | bytes 786440 | tf_op jit(solution)/shard_map/ppermute | solution.py:660
  96.2 5.0 %collective-permute-start.24 = (bf16[2,128,256]{2,1,0:T(8,128)(2,1)S(1)}, bf16[2,128,256]{2,1,0:T(8,128)(2,1)S(1)}, u32[]{:S(2)}, u32[]{:S(2)}) collective-permute-start(bf16[2,128,256]{2,1,0:T(8,128)(2,1)S(1)} %get-tuple-element.133), channel_id=1, source_target_pairs={{0,2},{1,3},{2,0},{3,1},{4,6},{5,7},{6,4},{7,5},{8,10},{9,11},{10,... | collective-permute-start | bytes 393224 | tf_op jit(solution)/shard_map/ppermute | solution.py:345

commit v3 on v2

--- a/solution.py
+++ b/solution.py
@@ -70,17 +70,20 @@
     return lax.dot_general(a, b, (((1,), (1,)), ((), ())), preferred_element_type=F32)
 
 
-def call(body, place, grid, ins, outs, mib, scratch=(), span=0.0):
+def call(body, place, grid, ins, outs, mib, scratch=(), span=0.0, alias=None):
     return pl.pallas_call(
         body,
         grid_spec=pltpu.PrefetchScalarGridSpec(
             num_scalar_prefetch=1,
             grid=grid,
-            in_specs=[pl.BlockSpec(b, m) for _, b, m in ins],
+            in_specs=[
+                pl.BlockSpec(b, m) if b else pl.BlockSpec(memory_space=pl.ANY) for _, b, m in ins
+            ],
             out_specs=[pl.BlockSpec(b, m) for _, _, b, m in outs],
             scratch_shapes=list(scratch),
         ),
         out_shape=[jax.ShapeDtypeStruct(s, d) for s, d, _, _ in outs],
+        input_output_aliases=alias or {},
         compiler_params=pltpu.CompilerParams(vmem_limit_bytes=mib * MIB),
         cost_estimate=pl.CostEstimate(
             flops=int(span * 1e9), bytes_accessed=0, transcendentals=0
@@ -309,14 +312,16 @@
     send_ref[...] = total[1:].astype(BF16)
 
 
-def place_body(place, mine_ref, got_ref, down_in, up_ref, down_ref):
+def place_own_body(place, mine_ref, down_in, up_ref, down_ref):
     down_ref[...] = down_in[...].astype(F32)
     width = mine_ref.shape[-1]
-    for ref, side in ((mine_ref, 0), (got_ref, 1)):
-        for at in range(2):
-            where = place[0] ^ (2 * side) ^ at
-            lanes = pl.ds(pl.multiple_of(where * width, width), width)
-            up_ref[:, :, lanes] = ref[at].astype(F32).reshape(*up_ref.shape[:2], width)
+    for at in range(2):
+        lanes = pl.ds(pl.multiple_of((place[0] ^ at) * width, width), width)
+        up_ref[:, :, lanes] = mine_ref[at].reshape(*up_ref.shape[:2], width)
+
+
+def place_near_body(place, got_ref, held_ref, up_ref):
+    up_ref[...] = got_ref[0].astype(F32).reshape(up_ref.shape)
 
 
 def square_device(features, cotangent, up_blocks, down_blocks):
@@ -358,9 +363,10 @@
             for k in (2, 3)
         ]
     )
+    down_b = after((down_blocks,), to_i)[0]
     to_j = jnp.stack(
         [
-            lax.dynamic_slice(down_blocks, (0, (me ^ k) * rows + at, 0), (local, quarter, feat))
+            lax.dynamic_slice(down_b, (0, (me ^ k) * rows + at, 0), (local, quarter, feat))
             for k in (1, 3)
         ]
     )
@@ -501,10 +507,12 @@
     slope_lo_s = own_slope(1, gate_lo)
 
     got_e, far_e = after((got_e, far_e), slope_lo_s)
-    last_e = send_z(up_again(mine_e, far_e), 2)
-
-    x_hi, cot_hi = after((x_hi, cot_hi), last_e)
+    send_e = up_again(mine_e, far_e)
+    last_e = send_z(send_e, 2)
+
+    x_hi = after((x_hi,), send_e)[0]
     hid_hi, gate_hi = near_hidden(x_hi, 1)
+    cot_hi, last_e = after((cot_hi, last_e), hid_hi)
 
     def outputs_of(j, hid, kind):
         return call_once(
@@ -635,6 +643,7 @@
         ],
         [(blocks, F32, one, every)],
         16,
+        span=4.0,
     )[0]
 
     own_out = outputs_of(0, after((hid,), own_grads)[0], F32)
@@ -673,21 +682,41 @@
     )
     got_u = send(send_u, 2)
 
-    got_grads = after((got_grads,), send_u)[0]
-    feature_grads = added(own_grads, got_grads)
-
-    got_u, home_d = after((got_u, home_d), feature_grads)
-    up_grads, down_grads = call(
-        place_body,
+    home_d = after((home_d,), send_u)[0]
+    held, down_grads = call(
+        place_own_body,
         place,
         (1,),
-        [whole(mine_u), whole(got_u), whole(home_d)],
+        [whole(mine_u), whole(home_d)],
         [
             whole_out((local, feat // n_dp, block_hidden), F32),
             whole_out((local, part, feat), F32),
         ],
         8,
     )
+    got_grads = after((got_grads,), held)[0]
+    feature_grads = added(own_grads, got_grads)
+
+    got_u = after((got_u,), feature_grads)[0]
+    up_grads = call(
+        place_near_body,
+        place,
+        (2,),
+        [
+            (got_u, (1,) + shard_u[1:], lambda a, p: (a, 0, 0)),
+            (held, None, None),
+        ],
+        [
+            (
+                (local, feat // n_dp, block_hidden),
+                F32,
+                (local, feat // n_dp, rows),
+                lambda a, p: (0, 0, p[0] ^ 2 ^ a),
+            )
+        ],
+        8,
+        alias={2: 0},
+    )[0]
     wide = (local * feat, tokens)
     return (outputs.reshape(wide), feature_grads.reshape(wide), up_grads, down_grads)
 

time: 103 us -> 102 us (level)
  waiting for transfers between devices: 33.7 us -> 29.8 us
  starting transfers between devices: 25.8 us -> 27.4 us
  Pallas kernels: 39.1 us -> 40.4 us
    ppermute x9, waiting for transfers between devices: 10.1 us -> 4.18 us  [send(): lax.ppermute(value, 'tensor', [(t, t ^ hop) for t in range(n_tensor)])]
    ppermute x1, waiting for transfers between devices: 0.01 us -> 4.57 us  [square_device(): home_d = lax.ppermute(sum_d, ('dp', 'tensor'), swaps)]
    ppermute x1, starting transfers between devices: 5.55 us -> 1.92 us  [square_device(): home_d = lax.ppermute(sum_d, ('dp', 'tensor'), swaps)]
    ppermute x9, starting transfers between devices: 11.5 us -> 14.9 us  [send_z(): return lax.ppermute(value, 'dp', [(d, d ^ 2 * hop) for d in range(n_dp)])]
    ppermute x9, waiting for transfers between devices: 20.4 us -> 17.8 us  [send_z(): return lax.ppermute(value, 'dp', [(d, d ^ 2 * hop) for d in range(n_dp)])]
    ppermute x9, starting transfers between devices: 7.07 us -> 8.89 us  [send(): lax.ppermute(value, 'tensor', [(t, t ^ hop) for t in range(n_tensor)])]
    pallas_call x25 -> x26, Pallas kernels: 39.1 us -> 40.4 us  [call(): pl.pallas_call(body, grid_spec=pltpu.PrefetchScalarGridSpec(num_scalar_pr...]
  transfers between devices with their start and end apart: 26 -> 26, of which waited for: 10 -> 12; matrix products, arithmetic and copies ran while one was open for 1% -> 1% of each run, Pallas kernels for 31% -> 37%
where the time goes in v3:
time: 102 us; the launch traced here: 101 us
  Pallas kernels  40.4 us (40%)
  waiting for transfers between devices  29.8 us (29%)
  starting transfers between devices  27.4 us (27%)
  local copies, waits for them, and re-layouts  2.33 us (2%)
    pallas_call x26, Pallas kernels, call(): pl.pallas_call(body, grid_spec=pltpu.PrefetchScalarGridSpec(num_scalar_pr...  40.4 us
    ppermute x9, waiting for transfers between devices, send_z(): return lax.ppermute(value, 'dp', [(d, d ^ 2 * hop) for d in range(n_dp)])  17.8 us
    ppermute x9, starting transfers between devices, send_z(): return lax.ppermute(value, 'dp', [(d, d ^ 2 * hop) for d in range(n_dp)])  14.9 us
    ppermute x9, starting transfers between devices, send(): lax.ppermute(value, 'tensor', [(t, t ^ hop) for t in range(n_tensor)])  8.89 us
    ppermute x1, waiting for transfers between devices, square_device(): home_d = lax.ppermute(sum_d, ('dp', 'tensor'), swaps)  4.57 us
    ppermute x9, waiting for transfers between devices, send(): lax.ppermute(value, 'tensor', [(t, t ^ hop) for t in range(n_tensor)])  4.18 us
    ppermute x7, waiting for transfers between devices, send_core(): return lax.ppermute(value, 'dp', [(d, d ^ 1) for d in range(n_dp)])  3.24 us
  transfers between devices with their start and end apart: 26, of which 12 were waited for; matrix products, arithmetic and copies ran while one was open for 1% of the time, Pallas kernels for 37%

profile of v3, /device:TPU:12, one launch (start us, length us, event | category | flops | bytes accessed | tf_op | source)
XLA Modules:
  0.0 101.1 jit_solution(3204193102837429409)
XLA Ops:
  3.4 1.6 %collective-permute-start.1 = (bf16[2,4,64,256]{3,2,1,0:T(8,128)(2,1)S(1)}, bf16[2,4,64,256]{3,2,1,0:T(8,128)(2,1)S(1)}, u32[]{:S(2)}, u32[]{:S(2)}) collective-permute-start(bf16[2,4,64,256]{3,2,1,0:T(8,128)(2,1)S(1)} %pad_maximum_fusion.2), channel_id=1, source_target_pairs={{0,1},{1,0},{2,3},{3,2},{4,5},{5,4},{6,7},{7,6},{8,9},{9,8},{10,11... | collective-permute-start | bytes 786440 | tf_op jit(solution)/shard_map/ppermute | solution.py:350
  5.2 1.6 %collective-permute-start.3 = (bf16[2,256,768]{2,1,0:T(8,128)(2,1)S(1)}, bf16[2,256,768]{2,1,0:T(8,128)(2,1)S(1)}, u32[]{:S(2)}, u32[]{:S(2)}) collective-permute-start(bf16[2,256,768]{2,1,0:T(8,128)(2,1)S(1)} %bitcast.45), channel_id=1, source_target_pairs={{0,2},{1,3},{2,0},{3,1},{4,6},{5,7},{6,4},{7,5},{8,10},{9,11},{10,... | collective-permute-start | bytes 2359304 | tf_op jit(solution)/shard_map/ppermute | solution.py:350
  8.1 5.8 %shard_map.75 = (bf16[2,4,4,64,768]{4,3,2,1,0:T(8,128)(2,1)S(1)}, bf16[2,4,4,64,768]{4,3,2,1,0:T(8,128)(2,1)S(1)}) custom-call(s32[3]{0:T(128)S(1)} %pad_add_fusion.place, bf16[4,256,768]{2,1,0:T(8,128)(2,1)S(1)} %bitcast.37, bf16[4,256,1024]{2,1,0:T(8,128)(2,1)S(1)} %copy-done.3), custom_call_target="tpu_custom_call" | custom-call | tf_op jit(solution)/shard_map/pallas_call | solution.py:74
  15.0 1.3 %collective-permute-start.6 = (bf16[2,256,768]{2,1,0:T(8,128)(2,1)S(1)}, bf16[2,256,768]{2,1,0:T(8,128)(2,1)S(1)}, u32[]{:S(2)}, u32[]{:S(2)}) collective-permute-start(bf16[2,256,768]{2,1,0:T(8,128)(2,1)S(1)} %bitcast.42), channel_id=1, source_target_pairs={{0,1},{1,0},{2,3},{3,2},{4,5},{5,4},{6,7},{7,6},{8,9},{9,8},{10,11... | collective-permute-start | bytes 2359304 | tf_op jit(solution)/shard_map/ppermute | solution.py:350
  17.4 1.6 %shard_map.77 = (bf16[2,4,128,256]{3,2,1,0:T(8,128)(2,1)S(1)}, bf16[2,4,128,256]{3,2,1,0:T(8,128)(2,1)S(1)}) custom-call(s32[3]{0:T(128)S(1)} %pad_add_fusion.place, bf16[4,256,768]{2,1,0:T(8,128)(2,1)S(1)} %bitcast.33, bf16[2,4,4,64,768]{4,3,2,1,0:T(8,128)(2,1)S(1)} %get-tuple-element.126.refs_1_.refs_3_, bf16[4,256,768]{2,1,0:T(8,128)(2,1)S(1)} %bitcast.38, ...), custom_call_target="tpu_custom_call" | custom-call | tf_op jit(solution)/shard_map/pallas_call | solution.py:74
  19.0 7.9 %collective-permute-done.2.refs_1_ = bf16[2,2,4,64,256]{4,3,2,1,0:T(8,128)(2,1)S(1)} collective-permute-done((bf16[2,2,4,64,256]{4,3,2,1,0:T(8,128)(2,1)S(1)}, bf16[2,2,4,64,256]{4,3,2,1,0:T(8,128)(2,1)S(1)}, u32[]{:S(2)}, u32[]{:S(2)}) %collective-permute-start.2) | collective-permute-done | bytes 524320 | tf_op jit(solution)/shard_map/ppermute | solution.py:353
  27.9 1.6 %collective-permute-done.4.refs_1_ = bf16[2,256,768]{2,1,0:T(8,128)(2,1)S(1)} collective-permute-done((bf16[2,256,768]{2,1,0:T(8,128)(2,1)S(1)}, bf16[2,256,768]{2,1,0:T(8,128)(2,1)S(1)}, u32[]{:S(2)}, u32[]{:S(2)}) %collective-permute-start.4) | collective-permute-done | bytes 786464 | tf_op jit(solution)/shard_map/ppermute | solution.py:350
  30.1 1.4 %collective-permute-done.5.refs_0_.first_got = bf16[2,4,128,256]{3,2,1,0:T(8,128)(2,1)S(1)} collective-permute-done((bf16[2,4,128,256]{3,2,1,0:T(8,128)(2,1)S(1)}, bf16[2,4,128,256]{3,2,1,0:T(8,128)(2,1)S(1)}, u32[]{:S(2)}, u32[]{:S(2)}) %collective-permute-start.5) | collective-permute-done | bytes 524320 | tf_op jit(solution)/shard_map/ppermute | solution.py:356
  32.2 2.0 %collective-permute-start.7 = (bf16[1,128,256]{2,1,0:T(8,128)(2,1)S(1)}, bf16[1,128,256]{2,1,0:T(8,128)(2,1)S(1)}, u32[]{:S(2)}, u32[]{:S(2)}) collective-permute-start(bf16[1,128,256]{2,1,0:T(8,128)(2,1)S(1)} %get-tuple-element.88), channel_id=1, source_target_pairs={{0,8},{4,12},{8,0},{12,4},{16,24},{20,28},{24,16},{28,20},{1,9},{5... | collective-permute-start | bytes 196616 | tf_op jit(solution)/shard_map/ppermute | solution.py:353
  34.9 3.1 %shard_map.80 = (bf16[2,4,2,64,768]{4,3,2,1,0:T(8,128)(2,1)S(1)}, bf16[2,4,2,64,768]{4,3,2,1,0:T(8,128)(2,1)S(1)}) custom-call(s32[3]{0:T(128)S(1)} %pad_add_fusion.place, bf16[2,256,768]{2,1,0:T(8,128)(2,1)S(1)} %collective-permute-done.3.x_ref.refs_1_, bf16[2,2,4,256,256]{4,3,2,1,0:T(8,128)(2,1)S(1)} %bitcast.22), custom_call_target="tpu_custom_call" | custom-call | tf_op jit(solution)/shard_map/pallas_call | solution.py:74
  39.5 2.7 %collective-permute-start.11 = (bf16[1,128,256]{2,1,0:T(8,128)(2,1)S(1)}, bf16[1,128,256]{2,1,0:T(8,128)(2,1)S(1)}, u32[]{:S(2)}, u32[]{:S(2)}) collective-permute-start(bf16[1,128,256]{2,1,0:T(8,128)(2,1)S(1)} %shard_map.82), channel_id=1, source_target_pairs={{0,16},{4,20},{8,24},{12,28},{16,0},{20,4},{24,8},{28,12},{1,17},{... | collective-permute-start | bytes 196616 | tf_op jit(solution)/shard_map/ppermute | solution.py:353
  42.1 1.5 %collective-permute-done.12.x_ref.refs_2_ = bf16[2,256,768]{2,1,0:T(8,128)(2,1)S(1)} collective-permute-done((bf16[2,256,768]{2,1,0:T(8,128)(2,1)S(1)}, bf16[2,256,768]{2,1,0:T(8,128)(2,1)S(1)}, u32[]{:S(2)}, u32[]{:S(2)}) %collective-permute-start.12) | collective-permute-done | bytes 786464 | tf_op jit(solution)/shard_map/ppermute | solution.py:350
  43.6 3.3 %shard_map.83 = (bf16[2,4,2,64,768]{4,3,2,1,0:T(8,128)(2,1)S(1)}, bf16[2,4,2,64,768]{4,3,2,1,0:T(8,128)(2,1)S(1)}) custom-call(s32[3]{0:T(128)S(1)} %pad_add_fusion.place, bf16[2,256,768]{2,1,0:T(8,128)(2,1)S(1)} %collective-permute-done.12.x_ref.refs_2_, bf16[2,2,4,256,256]{4,3,2,1,0:T(8,128)(2,1)S(1)} %bitcast.23), custom_call_target="tpu_custom_call" | custom-call | tf_op jit(solution)/shard_map/pallas_call | solution.py:74
  46.9 2.0 %shard_map.84 = (bf16[4,128,256]{2,1,0:T(8,128)(2,1)S(1)}, bf16[2,4,128,256]{3,2,1,0:T(8,128)(2,1)S(1)}, bf16[3,4,128,256]{3,2,1,0:T(8,128)(2,1)S(1)}) custom-call(s32[3]{0:T(128)S(1)} %pad_add_fusion.place, bf16[4,256,768]{2,1,0:T(8,128)(2,1)S(1)} %bitcast.35, bf16[2,256,768]{2,1,0:T(8,128)(2,1)S(1)} %collective-permute-done.4.refs_1_, ...), custom_call_target="tpu_custom_call" | custom-call | tf_op jit(solution)/shard_map/pallas_call | solution.py:74
  49.6 1.5 %shard_map.85 = bf16[4,256,768]{2,1,0:T(8,128)(2,1)S(1)} custom-call(s32[3]{0:T(128)S(1)} %pad_add_fusion.place, bf16[2,2,4,256,256]{4,3,2,1,0:T(8,128)(2,1)S(1)} %bitcast.24, bf16[2,2,4,256,256]{4,3,2,1,0:T(8,128)(2,1)S(1)} %bitcast.25, bf16[2,2,4,256,256]{4,3,2,1,0:T(8,128)(2,1)S(1)} %bitcast.26, ...), custom_call_target="tpu_custom_call" | custom-call | tf_op jit(solution)/shard_map/pallas_call | solution.py:74
  51.1 1.6 %collective-permute-start.18 = (bf16[4,256,768]{2,1,0:T(8,128)(2,1)S(1)}, bf16[4,256,768]{2,1,0:T(8,128)(2,1)S(1)}, u32[]{:S(2)}, u32[]{:S(2)}) collective-permute-start(bf16[4,256,768]{2,1,0:T(8,128)(2,1)S(1)} %shard_map.85), channel_id=1, source_target_pairs={{0,1},{1,0},{2,3},{3,2},{4,5},{5,4},{6,7},{7,6},{8,9},{9,8},{10,11... | collective-permute-start | bytes 4718600 | tf_op jit(solution)/shard_map/ppermute | solution.py:350
  54.2 1.7 %shard_map.87 = (bf16[4,4,64,768]{3,2,1,0:T(8,128)(2,1)S(1)}, bf16[4,2,64,768]{3,2,1,0:T(8,128)(2,1)S(1)}, bf16[4,2,64,768]{3,2,1,0:T(8,128)(2,1)S(1)}, bf16[4,2,64,768]{3,2,1,0:T(8,128)(2,1)S(1)}) custom-call(s32[3]{0:T(128)S(1)} %pad_add_fusion.place, bf16[4,256,768]{2,1,0:T(8,128)(2,1)S(1)} %bitcast.36, ...), custom_call_target="tpu_custom_call" | custom-call | tf_op jit(solution)/shard_map/pallas_call | solution.py:74
  55.9 1.5 %shard_map.88 = bf16[4,256,768]{2,1,0:T(8,128)(2,1)S(1)} custom-call(s32[3]{0:T(128)S(1)} %pad_add_fusion.place, bf16[2,2,4,256,256]{4,3,2,1,0:T(8,128)(2,1)S(1)} %bitcast.30, bf16[2,2,4,256,256]{4,3,2,1,0:T(8,128)(2,1)S(1)} %bitcast.31, bf16[4,2,64,768]{3,2,1,0:T(8,128)(2,1)S(1)} %shard_map.81.refs_2_.refs_4_, ...), custom_call_target="tpu_custom_call" | custom-call | tf_op jit(solution)/shard_map/pallas_call | solution.py:74
  58.0 2.1 %shard_map.89 = (bf16[3,4,64,256]{3,2,1,0:T(8,128)(2,1)S(1)}, bf16[3,4,64,256]{3,2,1,0:T(8,128)(2,1)S(1)}, bf16[3,4,128,256]{3,2,1,0:T(8,128)(2,1)S(1)}) custom-call(s32[3]{0:T(128)S(1)} %pad_add_fusion.place, bf16[4,256,768]{2,1,0:T(8,128)(2,1)S(1)} %bitcast.39, bf16[2,256,768]{2,1,0:T(8,128)(2,1)S(1)} %collective-permute-done.3.x_ref.refs_1_, ...), custom_call_target="tpu_custom_call" | custom-call | flops 16000000000 | tf_op jit(solution)/shard_map/pallas_call | solution.py:74
  63.2 1.6 %collective-permute-start.20 = (bf16[3,128,256]{2,1,0:T(8,128)(2,1)S(1)}, bf16[3,128,256]{2,1,0:T(8,128)(2,1)S(1)}, u32[]{:S(2)}, u32[]{:S(2)}) collective-permute-start(bf16[3,128,256]{2,1,0:T(8,128)(2,1)S(1)} %get-tuple-element.129), channel_id=1, source_target_pairs={{0,8},{4,12},{8,0},{12,4},{16,24},{20,28},{24,16},{28,20},{1,9},{5... | collective-permute-start | bytes 589832 | tf_op jit(solution)/shard_map/ppermute | solution.py:353
  65.3 3.3 %collective-permute-done.15.got_ref = bf16[2,4,128,256]{3,2,1,0:T(8,128)(2,1)S(1)} collective-permute-done((bf16[2,4,128,256]{3,2,1,0:T(8,128)(2,1)S(1)}, bf16[2,4,128,256]{3,2,1,0:T(8,128)(2,1)S(1)}, u32[]{:S(2)}, u32[]{:S(2)}) %collective-permute-start.15) | collective-permute-done | bytes 524320 | tf_op jit(solution)/shard_map/ppermute | solution.py:353
  69.2 2.7 %collective-permute-start.19 = (bf16[4,128,256]{2,1,0:T(8,128)(2,1)S(1)}, bf16[4,128,256]{2,1,0:T(8,128)(2,1)S(1)}, u32[]{:S(2)}, u32[]{:S(2)}) collective-permute-start(bf16[4,128,256]{2,1,0:T(8,128)(2,1)S(1)} %get-tuple-element.124), channel_id=1, source_target_pairs={{0,16},{4,20},{8,24},{12,28},{16,0},{20,4},{24,8},{28,12},{1,17},{... | collective-permute-start | bytes 786440 | tf_op jit(solution)/shard_map/ppermute | solution.py:353
  71.9 1.5 %shard_map.92.own_ref = f32[4,256,768]{2,1,0:T(8,128)S(1)} custom-call(s32[3]{0:T(128)S(1)} %pad_add_fusion.place, bf16[4,256,1024]{2,1,0:T(8,128)(2,1)S(1)} %copy-done.3, bf16[4,256,1024]{2,1,0:T(8,128)(2,1)S(1)} %copy-done.3, bf16[4,4,64,768]{3,2,1,0:T(8,128)(2,1)S(1)} %shard_map.76.refs_3_.refs_2_, bf16[4,4,64,768]{3,2,1,0:T(8,128)(2,1)S(1)} %get-tuple-element.118.refs_3_), custom_call_target="tpu_custom_call" | custom-call | flops 4000000000 | tf_op jit(solution)/shard_map/pallas_call | solution.py:74
  73.4 1.5 %shard_map.93.own_ref = f32[4,256,768]{2,1,0:T(8,128)S(1)} custom-call(s32[3]{0:T(128)S(1)} %pad_add_fusion.place, bf16[4,1024,256]{2,1,0:T(8,128)(2,1)S(1)} %copy-done, bf16[4,1024,256]{2,1,0:T(8,128)(2,1)S(1)} %copy-done, bf16[4,1024,256]{2,1,0:T(8,128)(2,1)S(1)} %copy-done, bf16[2,4,4,64,768]{4,3,2,1,0:T(8,128)(2,1)S(1)} %get-tuple-element.126.refs_1_.refs_3_, ...), custom_call_target="tpu_custom_call" | custom-call | tf_op jit(solution)/shard_map/pallas_call | solution.py:74
  76.3 4.5 %collective-permute-start.23 = (bf16[3,128,256]{2,1,0:T(8,128)(2,1)S(1)}, bf16[3,128,256]{2,1,0:T(8,128)(2,1)S(1)}, u32[]{:S(2)}, u32[]{:S(2)}) collective-permute-start(bf16[3,128,256]{2,1,0:T(8,128)(2,1)S(1)} %shard_map.94), channel_id=1, source_target_pairs={{0,16},{4,20},{8,24},{12,28},{16,0},{20,4},{24,8},{28,12},{1,17},{... | collective-permute-start | bytes 589832 | tf_op jit(solution)/shard_map/ppermute | solution.py:353
  80.8 5.9 %collective-permute-done.19.got_ref = bf16[4,128,256]{2,1,0:T(8,128)(2,1)S(1)} collective-permute-done((bf16[4,128,256]{2,1,0:T(8,128)(2,1)S(1)}, bf16[4,128,256]{2,1,0:T(8,128)(2,1)S(1)}, u32[]{:S(2)}, u32[]{:S(2)}) %collective-permute-start.19) | collective-permute-done | bytes 262176 | tf_op jit(solution)/shard_map/ppermute | solution.py:353
  87.3 1.9 %collective-permute-start.24 = (bf16[4,128,256]{2,1,0:T(8,128)(2,1)S(1)}, bf16[4,128,256]{2,1,0:T(8,128)(2,1)S(1)}, u32[]{:S(2)}, u32[]{:S(2)}) collective-permute-start(bf16[4,128,256]{2,1,0:T(8,128)(2,1)S(1)} %shard_map.95), channel_id=1, source_target_pairs={{0,0},{1,8},{2,2},{3,10},{4,4},{5,12},{6,6},{7,14},{8,1},{9,9},{10... | collective-permute-start | bytes 786440 | tf_op jit(solution)/shard_map/ppermute | solution.py:669
  89.2 1.9 %shard_map.96 = bf16[4,256,768]{2,1,0:T(8,128)(2,1)} custom-call(s32[3]{0:T(128)S(1)} %pad_add_fusion.place, f32[4,256,768]{2,1,0:T(8,128)S(1)} %shard_map.93.own_ref, bf16[4,256,768]{2,1,0:T(8,128)(2,1)S(1)} %collective-permute-done.18.got_ref), custom_call_target="tpu_custom_call" | custom-call | tf_op jit(solution)/shard_map/pallas_call | solution.py:74
  91.9 4.6 %collective-permute-done.24.down_in = bf16[4,128,256]{2,1,0:T(8,128)(2,1)S(1)} collective-permute-done((bf16[4,128,256]{2,1,0:T(8,128)(2,1)S(1)}, bf16[4,128,256]{2,1,0:T(8,128)(2,1)S(1)}, u32[]{:S(2)}, u32[]{:S(2)}) %collective-permute-start.24) | collective-permute-done | bytes 262176 | tf_op jit(solution)/shard_map/ppermute | solution.py:669
  96.4 1.6 %shard_map.98 = (f32[4,32,1024]{2,1,0:T(8,128)}, f32[4,128,256]{2,1,0:T(8,128)}) custom-call(s32[3]{0:T(128)S(1)} %pad_add_fusion.place, f32[2,128,256]{2,1,0:T(8,128)S(1)} %get-tuple-element.137.mine_ref, bf16[4,128,256]{2,1,0:T(8,128)(2,1)S(1)} %collective-permute-done.24.down_in), custom_call_target="tpu_custom_call" | custom-call | tf_op jit(solution)/shard_map/pallas_call | solution.py:74
  98.0 1.8 %shard_map.99 = bf16[4,256,768]{2,1,0:T(8,128)(2,1)} custom-call(s32[3]{0:T(128)S(1)} %pad_add_fusion.place, f32[4,256,768]{2,1,0:T(8,128)S(1)} %shard_map.92.own_ref, bf16[4,256,768]{2,1,0:T(8,128)(2,1)S(1)} %collective-permute-done.21.got_ref), custom_call_target="tpu_custom_call" | custom-call | tf_op jit(solution)/shard_map/pallas_call | solution.py:74
  99.8 1.3 %shard_map.100 = f32[4,32,1024]{2,1,0:T(8,128)} custom-call(s32[3]{0:T(128)S(1)} %pad_add_fusion.place, bf16[2,128,256]{2,1,0:T(8,128)(2,1)S(1)} %collective-permute-done.25.got_ref, f32[4,32,1024]{2,1,0:T(8,128)} %get-tuple-element.140.held_ref), custom_call_target="tpu_custom_call", output_to_operand_aliasing={{}: (2, {})} | custom-call | tf_op jit(solution)/shard_map/pallas_call | solution.py:74
  (62 shorter events, 20.4 us)
Async XLA Ops:
  0.6 4.4 %copy-start.2 = (bf16[1024,768]{1,0:T(8,128)(2,1)S(1)}, bf16[1024,768]{1,0:T(8,128)(2,1)}, u32[]{:S(2)}) copy-start(bf16[1024,768]{1,0:T(8,128)(2,1)} %param.4) | copy-start | bytes 4718596
  1.8 12.1 %collective-permute-start = (bf16[2,4,64,256]{3,2,1,0:T(8,128)(2,1)S(1)}, bf16[2,4,64,256]{3,2,1,0:T(8,128)(2,1)S(1)}, u32[]{:S(2)}, u32[]{:S(2)}) collective-permute-start(bf16[2,4,64,256]{3,2,1,0:T(8,128)(2,1)S(1)} %pad_maximum_fusion.1), channel_id=1, source_target_pairs={{0,2},{1,3},{2,0},{3,1},{4,6},{5,7},{6,4},{7,5},{8,10},{9,11},{10,... | collective-permute-start | bytes 786440 | tf_op jit(solution)/shard_map/ppermute | solution.py:350
  3.4 1.7 %copy-start.1 = (bf16[1024,768]{1,0:T(8,128)(2,1)S(1)}, bf16[1024,768]{1,0:T(8,128)(2,1)}, u32[]{:S(2)}) copy-start(bf16[1024,768]{1,0:T(8,128)(2,1)} %param.5) | copy-start | bytes 4718596
  3.4 10.5 %collective-permute-start.1 = (bf16[2,4,64,256]{3,2,1,0:T(8,128)(2,1)S(1)}, bf16[2,4,64,256]{3,2,1,0:T(8,128)(2,1)S(1)}, u32[]{:S(2)}, u32[]{:S(2)}) collective-permute-start(bf16[2,4,64,256]{3,2,1,0:T(8,128)(2,1)S(1)} %pad_maximum_fusion.2), channel_id=1, source_target_pairs={{0,1},{1,0},{2,3},{3,2},{4,5},{5,4},{6,7},{7,6},{8,9},{9,8},{10,11... | collective-permute-start | bytes 786440 | tf_op jit(solution)/shard_map/ppermute | solution.py:350
  5.1 3.0 %copy-start.3 = (bf16[4,256,1024]{2,1,0:T(8,128)(2,1)S(1)}, bf16[4,256,1024]{2,1,0:T(8,128)(2,1)}, u32[]{:S(2)}) copy-start(bf16[4,256,1024]{2,1,0:T(8,128)(2,1)} %refs_1_.5) | copy-start | bytes 6291460
  5.2 22.7 %collective-permute-start.3 = (bf16[2,256,768]{2,1,0:T(8,128)(2,1)S(1)}, bf16[2,256,768]{2,1,0:T(8,128)(2,1)S(1)}, u32[]{:S(2)}, u32[]{:S(2)}) collective-permute-start(bf16[2,256,768]{2,1,0:T(8,128)(2,1)S(1)} %bitcast.45), channel_id=1, source_target_pairs={{0,2},{1,3},{2,0},{3,1},{4,6},{5,7},{6,4},{7,5},{8,10},{9,11},{10,... | collective-permute-start | bytes 2359304 | tf_op jit(solution)/shard_map/ppermute | solution.py:350
  6.8 22.8 %collective-permute-start.4 = (bf16[2,256,768]{2,1,0:T(8,128)(2,1)S(1)}, bf16[2,256,768]{2,1,0:T(8,128)(2,1)S(1)}, u32[]{:S(2)}, u32[]{:S(2)}) collective-permute-start(bf16[2,256,768]{2,1,0:T(8,128)(2,1)S(1)} %bitcast.44), channel_id=1, source_target_pairs={{0,1},{1,0},{2,3},{3,2},{4,5},{5,4},{6,7},{7,6},{8,9},{9,8},{10,11... | collective-permute-start | bytes 2359304 | tf_op jit(solution)/shard_map/ppermute | solution.py:350
  8.1 8.2 %copy-start = (bf16[4,1024,256]{2,1,0:T(8,128)(2,1)S(1)}, bf16[4,1024,256]{2,1,0:T(8,128)(2,1)}, u32[]{:S(2)}) copy-start(bf16[4,1024,256]{2,1,0:T(8,128)(2,1)} %refs_2_.1) | copy-start | bytes 6291460
  14.0 12.9 %collective-permute-start.2 = (bf16[2,2,4,64,256]{4,3,2,1,0:T(8,128)(2,1)S(1)}, bf16[2,2,4,64,256]{4,3,2,1,0:T(8,128)(2,1)S(1)}, u32[]{:S(2)}, u32[]{:S(2)}) collective-permute-start(bf16[2,2,4,64,256]{4,3,2,1,0:T(8,128)(2,1)S(1)} %pad_maximum_fusion.refs_0_), channel_id=1, source_target_pairs={{0,8},{4,12},{8,0},{12,4},{16,24},{20,28},{24,16},{28,20},{1,9},{5... | collective-permute-start | bytes 1572872 | tf_op jit(solution)/shard_map/ppermute | solution.py:353
  14.5 29.1 %collective-permute-start.12 = (bf16[2,256,768]{2,1,0:T(8,128)(2,1)S(1)}, bf16[2,256,768]{2,1,0:T(8,128)(2,1)S(1)}, u32[]{:S(2)}, u32[]{:S(2)}) collective-permute-start(bf16[2,256,768]{2,1,0:T(8,128)(2,1)S(1)} %bitcast.43), channel_id=1, source_target_pairs={{0,2},{1,3},{2,0},{3,1},{4,6},{5,7},{6,4},{7,5},{8,10},{9,11},{10,... | collective-permute-start | bytes 2359304 | tf_op jit(solution)/shard_map/ppermute | solution.py:350
  15.0 31.9 %collective-permute-start.6 = (bf16[2,256,768]{2,1,0:T(8,128)(2,1)S(1)}, bf16[2,256,768]{2,1,0:T(8,128)(2,1)S(1)}, u32[]{:S(2)}, u32[]{:S(2)}) collective-permute-start(bf16[2,256,768]{2,1,0:T(8,128)(2,1)S(1)} %bitcast.42), channel_id=1, source_target_pairs={{0,1},{1,0},{2,3},{3,2},{4,5},{5,4},{6,7},{7,6},{8,9},{9,8},{10,11... | collective-permute-start | bytes 2359304 | tf_op jit(solution)/shard_map/ppermute | solution.py:350
  29.6 1.9 %collective-permute-start.5 = (bf16[2,4,128,256]{3,2,1,0:T(8,128)(2,1)S(1)}, bf16[2,4,128,256]{3,2,1,0:T(8,128)(2,1)S(1)}, u32[]{:S(2)}, u32[]{:S(2)}) collective-permute-start(bf16[2,4,128,256]{3,2,1,0:T(8,128)(2,1)S(1)} %get-tuple-element.85), channel_id=1, source_target_pairs={{0,4},{4,0},{8,12},{12,8},{16,20},{20,16},{24,28},{28,24},{1,5},{5... | collective-permute-start | bytes 1572872 | tf_op jit(solution)/shard_map/ppermute | solution.py:356
  29.6 2.7 %collective-permute-start.9 = (bf16[2,2,4,64,256]{4,3,2,1,0:T(8,128)(2,1)S(1)}, bf16[2,2,4,64,256]{4,3,2,1,0:T(8,128)(2,1)S(1)}, u32[]{:S(2)}, u32[]{:S(2)}) collective-permute-start(bf16[2,2,4,64,256]{4,3,2,1,0:T(8,128)(2,1)S(1)} %pad_maximum_fusion.refs_0_), channel_id=1, source_target_pairs={{0,4},{4,0},{8,12},{12,8},{16,20},{20,16},{24,28},{28,24},{1,5},{5... | collective-permute-start | bytes 1572872 | tf_op jit(solution)/shard_map/ppermute | solution.py:356
  30.1 4.1 %collective-permute-start.10 = (bf16[2,2,4,64,256]{4,3,2,1,0:T(8,128)(2,1)S(1)}, bf16[2,2,4,64,256]{4,3,2,1,0:T(8,128)(2,1)S(1)}, u32[]{:S(2)}, u32[]{:S(2)}) collective-permute-start(bf16[2,2,4,64,256]{4,3,2,1,0:T(8,128)(2,1)S(1)} %collective-permute-done.2.refs_1_), channel_id=1, source_target_pairs={{0,4},{4,0},{8,12},{12,8},{16,20},{20,16},{24,28},{28,24},{1,5},{5... | collective-permute-start | bytes 1572872 | tf_op jit(solution)/shard_map/ppermute | solution.py:356
  32.1 6.8 %collective-permute-start.8 = (bf16[1,128,256]{2,1,0:T(8,128)(2,1)S(1)}, bf16[1,128,256]{2,1,0:T(8,128)(2,1)S(1)}, u32[]{:S(2)}, u32[]{:S(2)}) collective-permute-start(bf16[1,128,256]{2,1,0:T(8,128)(2,1)S(1)} %get-tuple-element.89), channel_id=1, source_target_pairs={{0,8},{4,12},{8,0},{12,4},{16,24},{20,28},{24,16},{28,20},{1,9},{5... | collective-permute-start | bytes 196616 | tf_op jit(solution)/shard_map/ppermute | solution.py:353
  32.2 6.7 %collective-permute-start.7 = (bf16[1,128,256]{2,1,0:T(8,128)(2,1)S(1)}, bf16[1,128,256]{2,1,0:T(8,128)(2,1)S(1)}, u32[]{:S(2)}, u32[]{:S(2)}) collective-permute-start(bf16[1,128,256]{2,1,0:T(8,128)(2,1)S(1)} %get-tuple-element.88), channel_id=1, source_target_pairs={{0,8},{4,12},{8,0},{12,4},{16,24},{20,28},{24,16},{28,20},{1,9},{5... | collective-permute-start | bytes 196616 | tf_op jit(solution)/shard_map/ppermute | solution.py:353
  39.5 7.4 %collective-permute-start.11 = (bf16[1,128,256]{2,1,0:T(8,128)(2,1)S(1)}, bf16[1,128,256]{2,1,0:T(8,128)(2,1)S(1)}, u32[]{:S(2)}, u32[]{:S(2)}) collective-permute-start(bf16[1,128,256]{2,1,0:T(8,128)(2,1)S(1)} %shard_map.82), channel_id=1, source_target_pairs={{0,16},{4,20},{8,24},{12,28},{16,0},{20,4},{24,8},{28,12},{1,17},{... | collective-permute-start | bytes 196616 | tf_op jit(solution)/shard_map/ppermute | solution.py:353
  49.0 3.7 %collective-permute-start.14 = (bf16[2,4,128,256]{3,2,1,0:T(8,128)(2,1)S(1)}, bf16[2,4,128,256]{3,2,1,0:T(8,128)(2,1)S(1)}, u32[]{:S(2)}, u32[]{:S(2)}) collective-permute-start(bf16[2,4,128,256]{3,2,1,0:T(8,128)(2,1)S(1)} %get-tuple-element.104), channel_id=1, source_target_pairs={{0,4},{4,0},{8,12},{12,8},{16,20},{20,16},{24,28},{28,24},{1,5},{5... | collective-permute-start | bytes 1572872 | tf_op jit(solution)/shard_map/ppermute | solution.py:356
  49.1 3.6 %collective-permute-start.13 = (bf16[4,128,256]{2,1,0:T(8,128)(2,1)S(1)}, bf16[4,128,256]{2,1,0:T(8,128)(2,1)S(1)}, u32[]{:S(2)}, u32[]{:S(2)}) collective-permute-start(bf16[4,128,256]{2,1,0:T(8,128)(2,1)S(1)} %get-tuple-element.103), channel_id=1, source_target_pairs={{0,4},{4,0},{8,12},{12,8},{16,20},{20,16},{24,28},{28,24},{1,5},{5... | collective-permute-start | bytes 786440 | tf_op jit(solution)/shard_map/ppermute | solution.py:356
  51.1 38.1 %collective-permute-start.18 = (bf16[4,256,768]{2,1,0:T(8,128)(2,1)S(1)}, bf16[4,256,768]{2,1,0:T(8,128)(2,1)S(1)}, u32[]{:S(2)}, u32[]{:S(2)}) collective-permute-start(bf16[4,256,768]{2,1,0:T(8,128)(2,1)S(1)} %shard_map.85), channel_id=1, source_target_pairs={{0,1},{1,0},{2,3},{3,2},{4,5},{5,4},{6,7},{7,6},{8,9},{9,8},{10,11... | collective-permute-start | bytes 4718600 | tf_op jit(solution)/shard_map/ppermute | solution.py:350
  53.7 14.9 %collective-permute-start.15 = (bf16[2,4,128,256]{3,2,1,0:T(8,128)(2,1)S(1)}, bf16[2,4,128,256]{3,2,1,0:T(8,128)(2,1)S(1)}, u32[]{:S(2)}, u32[]{:S(2)}) collective-permute-start(bf16[2,4,128,256]{3,2,1,0:T(8,128)(2,1)S(1)} %get-tuple-element.109), channel_id=1, source_target_pairs={{0,8},{4,12},{8,0},{12,4},{16,24},{20,28},{24,16},{28,20},{1,9},{5... | collective-permute-start | bytes 1572872 | tf_op jit(solution)/shard_map/ppermute | solution.py:353
  57.5 40.5 %collective-permute-start.21 = (bf16[4,256,768]{2,1,0:T(8,128)(2,1)S(1)}, bf16[4,256,768]{2,1,0:T(8,128)(2,1)S(1)}, u32[]{:S(2)}, u32[]{:S(2)}) collective-permute-start(bf16[4,256,768]{2,1,0:T(8,128)(2,1)S(1)} %shard_map.88), channel_id=1, source_target_pairs={{0,2},{1,3},{2,0},{3,1},{4,6},{5,7},{6,4},{7,5},{8,10},{9,11},{10,... | collective-permute-start | bytes 4718600 | tf_op jit(solution)/shard_map/ppermute | solution.py:350
  60.1 1.8 %collective-permute-start.16 = (bf16[3,4,64,256]{3,2,1,0:T(8,128)(2,1)S(1)}, bf16[3,4,64,256]{3,2,1,0:T(8,128)(2,1)S(1)}, u32[]{:S(2)}, u32[]{:S(2)}) collective-permute-start(bf16[3,4,64,256]{3,2,1,0:T(8,128)(2,1)S(1)} %get-tuple-element.120), channel_id=1, source_target_pairs={{0,4},{4,0},{8,12},{12,8},{16,20},{20,16},{24,28},{28,24},{1,5},{5... | collective-permute-start | bytes 1179656 | tf_op jit(solution)/shard_map/ppermute | solution.py:356
  60.2 2.3 %collective-permute-start.17 = (bf16[3,4,64,256]{3,2,1,0:T(8,128)(2,1)S(1)}, bf16[3,4,64,256]{3,2,1,0:T(8,128)(2,1)S(1)}, u32[]{:S(2)}, u32[]{:S(2)}) collective-permute-start(bf16[3,4,64,256]{3,2,1,0:T(8,128)(2,1)S(1)} %get-tuple-element.121), channel_id=1, source_target_pairs={{0,4},{4,0},{8,12},{12,8},{16,20},{20,16},{24,28},{28,24},{1,5},{5... | collective-permute-start | bytes 1179656 | tf_op jit(solution)/shard_map/ppermute | solution.py:356
  63.2 12.5 %collective-permute-start.20 = (bf16[3,128,256]{2,1,0:T(8,128)(2,1)S(1)}, bf16[3,128,256]{2,1,0:T(8,128)(2,1)S(1)}, u32[]{:S(2)}, u32[]{:S(2)}) collective-permute-start(bf16[3,128,256]{2,1,0:T(8,128)(2,1)S(1)} %get-tuple-element.129), channel_id=1, source_target_pairs={{0,8},{4,12},{8,0},{12,4},{16,24},{20,28},{24,16},{28,20},{1,9},{5... | collective-permute-start | bytes 589832 | tf_op jit(solution)/shard_map/ppermute | solution.py:353
  64.8 26.3 %collective-permute-start.22 = (bf16[3,128,256]{2,1,0:T(8,128)(2,1)S(1)}, bf16[3,128,256]{2,1,0:T(8,128)(2,1)S(1)}, u32[]{:S(2)}, u32[]{:S(2)}) collective-permute-start(bf16[3,128,256]{2,1,0:T(8,128)(2,1)S(1)} %get-tuple-element.122), channel_id=1, source_target_pairs={{0,8},{4,12},{8,0},{12,4},{16,24},{20,28},{24,16},{28,20},{1,9},{5... | collective-permute-start | bytes 589832 | tf_op jit(solution)/shard_map/ppermute | solution.py:353
  69.2 17.5 %collective-permute-start.19 = (bf16[4,128,256]{2,1,0:T(8,128)(2,1)S(1)}, bf16[4,128,256]{2,1,0:T(8,128)(2,1)S(1)}, u32[]{:S(2)}, u32[]{:S(2)}) collective-permute-start(bf16[4,128,256]{2,1,0:T(8,128)(2,1)S(1)} %get-tuple-element.124), channel_id=1, source_target_pairs={{0,16},{4,20},{8,24},{12,28},{16,0},{20,4},{24,8},{28,12},{1,17},{... | collective-permute-start | bytes 786440 | tf_op jit(solution)/shard_map/ppermute | solution.py:353
  76.3 14.8 %collective-permute-start.23 = (bf16[3,128,256]{2,1,0:T(8,128)(2,1)S(1)}, bf16[3,128,256]{2,1,0:T(8,128)(2,1)S(1)}, u32[]{:S(2)}, u32[]{:S(2)}) collective-permute-start(bf16[3,128,256]{2,1,0:T(8,128)(2,1)S(1)} %shard_map.94), channel_id=1, source_target_pairs={{0,16},{4,20},{8,24},{12,28},{16,0},{20,4},{24,8},{28,12},{1,17},{... | collective-permute-start | bytes 589832 | tf_op jit(solution)/shard_map/ppermute | solution.py:353
  87.3 9.2 %collective-permute-start.24 = (bf16[4,128,256]{2,1,0:T(8,128)(2,1)S(1)}, bf16[4,128,256]{2,1,0:T(8,128)(2,1)S(1)}, u32[]{:S(2)}, u32[]{:S(2)}) collective-permute-start(bf16[4,128,256]{2,1,0:T(8,128)(2,1)S(1)} %shard_map.95), channel_id=1, source_target_pairs={{0,0},{1,8},{2,2},{3,10},{4,4},{5,12},{6,6},{7,14},{8,1},{9,9},{10... | collective-permute-start | bytes 786440 | tf_op jit(solution)/shard_map/ppermute | solution.py:669
  91.8 8.1 %collective-permute-start.25 = (bf16[2,128,256]{2,1,0:T(8,128)(2,1)S(1)}, bf16[2,128,256]{2,1,0:T(8,128)(2,1)S(1)}, u32[]{:S(2)}, u32[]{:S(2)}) collective-permute-start(bf16[2,128,256]{2,1,0:T(8,128)(2,1)S(1)} %get-tuple-element.138), channel_id=1, source_target_pairs={{0,2},{1,3},{2,0},{3,1},{4,6},{5,7},{6,4},{7,5},{8,10},{9,11},{10,... | collective-permute-start | bytes 393224 | tf_op jit(solution)/shard_map/ppermute | solution.py:350

commit v4 on v3

--- a/solution.py
+++ b/solution.py
@@ -123,10 +123,6 @@
     )
 
 
-def by_grid(body):
-    return lambda place, *refs: body(pl.program_id(0), pl.num_programs(0), place, *refs)
-
-
 def whole(array):
     rank = array.ndim
     return (array, array.shape, lambda *at: (0,) * rank)
@@ -163,11 +159,7 @@
 
 
 def halves(step, steps, work, lo, hi):
-    if isinstance(step, int):
-        work(*(lo if step < steps // 2 else hi))
-        return
-    pl.when(step < steps // 2)(functools.partial(work, *lo))
-    pl.when(step >= steps // 2)(functools.partial(work, *hi))
+    work(*(lo if step < steps // 2 else hi))
 
 
 def stacked(refs, axis=0):
@@ -188,14 +180,10 @@
     put_slopes(square(cot_ref), [down_ref], [gate_ref], [slope_ref])
 
 
-def late_slopes_body(step, steps, place, own_ref, near_lo, near_hi, *refs):
-    downs, gates, slopes = refs[:4], refs[4:8], refs[8:]
-    put_slopes(square(own_ref), downs[3:], gates[3:], slopes[3:])
-
-    def work(near_ref):
-        put_slopes(square(near_ref), downs[:3], gates[:3], slopes[:3])
-
-    halves(step, steps, work, (near_lo,), (near_hi,))
+def near_slopes_body(step, steps, place, own_ref, near_ref, *refs):
+    downs, gates, slopes = refs[:3], refs[3:6], refs[6:]
+    put_slopes(square(own_ref), downs[:1], gates[:1], slopes[:1])
+    put_slopes(square(near_ref), downs[1:], gates[1:], slopes[1:])
 
 
 def own_terms_body(step, steps, place, cot_ref, hid_ref, x_ref, slope_ref, give_ref, keep_ref, down_s, up_s):
@@ -210,7 +198,7 @@
     keep_ref[1, step] = down_s[core]
 
 
-def down_terms_body(step, steps, place, own_ref, near_lo, near_hi, sn, ns_lo, ns_hi, nn_lo, nn_hi, give_own, give_near, keep_ref, term_s):
+def down_terms_body(step, steps, place, own_ref, near_0, near_1, sn, ns_0, ns_1, nn_0, nn_1, give_own, give_near, keep_ref, term_s):
     core = place[2]
 
     def put(pair, terms, give):
@@ -218,50 +206,49 @@
         give[...] = term_s[pair, 1 - core].reshape(give.shape)
         keep_ref[pair, 0] = term_s[pair, core]
 
+    rows = 2 * term_s.shape[2]
+    hidden = jnp.concatenate([square(sn), stacked((nn_0, nn_1), 1)])
+    mixed = dot_nt(hidden, stacked((near_0, near_1), 1))
+    put(0, mixed[:rows], give_own)
+    put(1, dot_nt(stacked((ns_0, ns_1), 1), square(own_ref)), give_near.at[0])
+    put(2, mixed[rows:], give_near.at[1])
+
+
+def up_terms_body(step, steps, place, x_ref, x_0, x_1, sn_0, sn_1, ns_0, ns_1, nn_0, nn_1, give_lo, give_hi, keep_ref, term_s):
+    core, near = place[2], stacked((x_0, x_1), 1)
+    give_ref = give_lo if step < steps // 2 else give_hi
+    slopes = ((sn_0, sn_1), (ns_0, ns_1), (nn_0, nn_1))
+    for pair, (x, refs) in enumerate(zip((square(x_ref), near, near), slopes)):
+        term_s[...] = dot_nt(x, stacked(refs, 1)).astype(BF16).reshape(term_s.shape)
+        give_ref[pair] = term_s[:, 1 - core]
+        keep_ref[pair] = term_s[:, core]
+
+
+def outputs_body(step, steps, place, d_own, d_near, hid_ref, *refs):
+    *nears, out_ref = refs
+
     def work(near_ref):
-        rows = 2 * term_s.shape[2]
-        mixed = dot_nt(stacked((sn, nn_lo, nn_hi)), square(near_ref))
-        put(0, mixed[:rows], give_own)
-        put(1, dot_nt(stacked((ns_lo, ns_hi)), square(own_ref)), give_near.at[0])
-        put(2, mixed[rows:], give_near.at[1])
-
-    halves(step, steps, work, (near_lo,), (near_hi,))
-
-
-def put_up_term(pair, core, x, slope_ref, give_ref, keep_ref, term_s):
-    term_s[...] = dot_nt(x, square(slope_ref)).astype(BF16).reshape(term_s.shape)
-    give_ref[pair] = term_s[:, 1 - core]
-    keep_ref[pair] = term_s[:, core]
-
-
-def up_terms_body(step, steps, place, x_ref, x_lo, x_hi, sn, lo_s, lo_n, hi_s, hi_n, give_lo, give_hi, keep_ref, term_s):
-    def work(x_near, from_own, from_near, give_ref):
-        near = square(x_near)
-        for pair, (x, ref) in enumerate(((square(x_ref), sn), (near, from_own), (near, from_near))):
-            put_up_term(pair, place[2], x, ref, give_ref, keep_ref, term_s)
-
-    lo, hi = (x_lo, lo_s, lo_n, give_lo), (x_hi, hi_s, hi_n, give_hi)
-    halves(step, steps, work, lo, hi)
-
-
-def outputs_body(step, steps, place, d_own, d_lo, d_hi, hid_ref, lo_ref, hi_ref, out_ref):
-    total = dot_tn(stacked((d_own, d_lo, d_hi)), stacked((hid_ref, lo_ref, hi_ref)))
-    out_ref[0] = total.astype(out_ref.dtype)
-
-
-def near_grads_body(step, steps, place, up_own, up_near, lo_s, lo_n, hi_s, hi_n, out_ref):
-    def work(*slopes):
-        out_ref[0] = dot_nn(stacked((up_own, up_near), 1), stacked(slopes)).astype(BF16)
-
-    halves(step, steps, work, (lo_s, lo_n), (hi_s, hi_n))
-
-
-def grads_body(step, steps, place, up_own, up_near, slope_own, slope_near, out_ref):
-    out_ref[0] = dot_nn(stacked((up_own, up_near), 1), stacked((slope_own, slope_near)))
-
-
-def add_body(place, own_ref, got_ref, out_ref):
-    out_ref[...] = (own_ref[...] + got_ref[...].astype(F32)).astype(BF16)
+        total = dot_tn(stacked((d_own, d_near)), stacked((hid_ref, near_ref)))
+        out_ref[0] = total.astype(out_ref.dtype)
+
+    halves(step, steps, work, nears[:1], nears[-1:])
+
+
+def grads_body(step, steps, place, up_own, up_near, slope_own, *refs):
+    *nears, out_ref = refs
+
+    def work(near_ref):
+        total = dot_nn(stacked((up_own, up_near), 1), stacked((slope_own, near_ref)))
+        out_ref[0] = total.astype(out_ref.dtype)
+
+    halves(step, steps, work, nears[:1], nears[-1:])
+
+
+def add_body(place, own_ref, got_0, got_1, out_ref):
+    width = got_0.shape[-1]
+    for at, ref in enumerate((got_0, got_1)):
+        lanes = slice(at * width, (at + 1) * width)
+        out_ref[:, :, lanes] = (own_ref[:, :, lanes] + ref[...].astype(F32)).astype(BF16)
 
 
 def down_meet_body(place, first, first_got, keep_ref, got_own, got_near, send_ref, mine_ref, total_s):
@@ -330,7 +317,7 @@
     n_dp, n_tensor = lax.axis_size("dp"), lax.axis_size("tensor")
     sub = block_hidden // (local * n_tensor)
     rows = local * sub
-    half, part = local // 2, rows // 2
+    part, span_t = rows // 2, tokens // 2
     factor = 1.0 / math.sqrt(tokens * n_dp)
     me = lax.axis_index("tensor").astype(jnp.int32)
     rank = lax.axis_index("dp").astype(jnp.int32)
@@ -340,11 +327,8 @@
     cot = cotangent.reshape(local, feat, tokens)
     one = (1, feat, tokens)
     blocks = (local, feat, tokens)
+    half_one = (1, feat, span_t)
     every = lambda i, p: (i, 0, 0)
-    least = lambda a, b: min(a, b) if isinstance(a, int) else jnp.minimum(a, b)
-    most = lambda a, b: max(a, b) if isinstance(a, int) else jnp.maximum(a, b)
-    low = lambda i, p: (least(i, half - 1), 0, 0)
-    high = lambda i, p: (most(i - half, 0), 0, 0)
 
     def send(value, hop):
         return lax.ppermute(value, "tensor", [(t, t ^ hop) for t in range(n_tensor)])
@@ -371,79 +355,52 @@
         ]
     )
     from_i, from_j = send(to_i, 2), send(to_j, 1)
-    firsts = after((x[:half], x[half:], cot[:half], cot[half:]), to_i, to_j)
-    x_lo, cot_lo = send(firsts[0], 2), send(firsts[2], 1)
-    x_hi, cot_hi = send(firsts[1], 2), send(firsts[3], 1)
-
-    def hidden_of(source, count, up, span):
-        unit = (2, local, count, sub, tokens)
-        block = (1, local, 1, sub, tokens)
+    firsts = after([v[..., t] for v in (x, cot) for t in (slice(span_t), slice(span_t, tokens))], to_i, to_j)
+    x_0, cot_0 = send(firsts[0], 2), send(firsts[2], 1)
+    x_1, cot_1 = send(firsts[1], 2), send(firsts[3], 1)
+
+    def hidden_of(source, up):
+        width = source.shape[-1]
+        unit = (2, local, local, sub, width)
+        block = (1, local, 1, sub, width)
         where = lambda j, i, p: (j, 0, i, 0, 0)
         return call(
             hidden_body,
             place,
-            (2, count),
-            [(source, one, lambda j, i, p: (i, 0, 0)), up],
+            (2, local),
+            [(source, (1, feat, width), lambda j, i, p: (i, 0, 0)), up],
             [(unit, BF16, block, where), (unit, BF16, block, where)],
             16,
         )
 
-    hid, gate = hidden_of(
-        x, local, (up_blocks, (1, feat, rows), lambda j, i, p: (i, 0, p[0] ^ j)), 0.0
-    )
+    hid, gate = hidden_of(x, (up_blocks, (1, feat, rows), lambda j, i, p: (i, 0, p[0] ^ j)))
     from_i, from_j = after((from_i, from_j), hid)
     share = jnp.stack([from_i, from_j])
     share_z = send_z(share, 1)
 
-    def unit_of(array, j):
-        return (array, (1, 1) + array.shape[2:], lambda i, p: (j, i, 0, 0, 0))
-
-    def down_of(j, which):
+    def unit_of(array, j, t=0):
+        if t is None:
+            return (array, (1, 1) + array.shape[2:], lambda i, p: (j, i, 0, 0, 0))
+        return (array, (1, 1) + array.shape[2:4] + (span_t,), lambda i, p: (j, i, 0, 0, t))
+
+    def down_of(j, near):
         if j == 0:
-            if which == 0:
-                return (down_blocks, (1, rows, feat), lambda i, p: (i, p[0], 0))
-            return (
-                down_blocks,
-                (1, part, feat),
-                lambda i, p: (i, 2 * (p[0] ^ 2) + which - 1, 0),
-            )
-        if which == 0:
-            return (weights, (1, 1, 1, rows, feat), lambda i, p: (1, 0, i, 0, 0))
-        return (weights, (1, 1, 1, part, feat), lambda i, p: (1, 1, i, which - 1, 0))
-
-    def own_slope(which, array):
-        return call_once(
-            slope_body,
-            place,
-            local,
-            [(cot, one, every), down_of(0, which), unit_of(array, 0)],
-            [(array.shape[1:], BF16, (1,) + array.shape[2:], lambda i, p: (i, 0, 0, 0))],
-            20,
-        )[0]
-
-    slope_ss = own_slope(0, gate)
+            return (down_blocks, (1, rows, feat), lambda i, p: (i, p[0] ^ (2 * near), 0))
+        return (weights, (1, 1, 1, rows, feat), lambda i, p: (1, near, i, 0, 0))
+
+    slope_ss = call_once(
+        slope_body,
+        place,
+        local,
+        [(cot, one, every), down_of(0, 0), unit_of(gate, 0, None)],
+        [(gate.shape[1:], BF16, (1,) + gate.shape[2:], lambda i, p: (i, 0, 0, 0))],
+        20,
+    )[0]
+
     at_i = lambda i, p: (0, i, 0, 0)
     strip = (local, 1, sub, tokens)
     shard_u = (n_dp // 2, local * feat // n_dp, rows)
-
-    def up_terms(body, ins, count, gives, span):
-        block = (count, n_dp // 2, feat // n_dp, rows)
-        wide = (count,) + shard_u
-        part_u = (count, n_dp // 2, shard_u[1] // len(gives), rows)
-        return call_once(
-            body,
-            place,
-            local,
-            ins,
-            [
-                (part_u, BF16, block, functools.partial(lambda m, i, p: (0, 0, m(i), 0), m))
-                for m in gives
-            ]
-            + [(wide, BF16, block, lambda i, p: (0, 0, i, 0))],
-            20,
-            scratch=[pltpu.VMEM((n_dp // 2, 2, feat // n_dp, rows), BF16)],
-            span=span,
-        )
+    up_block = (3, n_dp // 2, feat // n_dp, rows)
 
     def up_meet(count, keep, gots):
         piece = (count,) + shard_u[1:]
@@ -468,7 +425,7 @@
         local,
         [
             (cot, one, every),
-            unit_of(hid, 0),
+            unit_of(hid, 0, None),
             (x, one, every),
             (slope_ss, strip, at_i),
         ],
@@ -479,8 +436,8 @@
             pltpu.VMEM((n_dp // 2, 2, feat // n_dp, rows), BF16),
         ],
     )
-    share, share_z, x_lo, cot_lo = after((share, share_z, x_lo, cot_lo), give_e)
-    core_parts = after((share, share_z), x_lo, cot_lo)
+    share, share_z, x_0, cot_0 = after((share, share_z, x_0, cot_0), give_e)
+    core_parts = after((share, share_z), x_0, cot_0)
     weights = call(
         weights_body,
         place,
@@ -490,52 +447,80 @@
         16,
     )[0].reshape(2, 2, local, rows, feat)
 
-    def near_hidden(source, which):
-        up = (
-            weights,
-            (1, 1, 1, feat, rows),
-            lambda j, i, p: (0, j, which * half + i, 0, 0),
-        )
-        return hidden_of(source, half, up, 0.0)
-
-    give_e = after((give_e,), x_lo, cot_lo)[0]
+    give_e = after((give_e,), x_0, cot_0)[0]
     first_got = send_core(give_e)
     send_e, far_e, mine_e = up_meet(1, keep_e, [first_got])
     got_e, far_e = send_z(send_e, 1), send_z(far_e, 1)
-    x_lo = after((x_lo,), weights, send_e)[0]
-    hid_lo, gate_lo = near_hidden(x_lo, 0)
-    slope_lo_s = own_slope(1, gate_lo)
-
-    got_e, far_e = after((got_e, far_e), slope_lo_s)
-    send_e = up_again(mine_e, far_e)
-    last_e = send_z(send_e, 2)
-
-    x_hi = after((x_hi,), send_e)[0]
-    hid_hi, gate_hi = near_hidden(x_hi, 1)
-    cot_hi, last_e = after((cot_hi, last_e), hid_hi)
-
-    def outputs_of(j, hid, kind):
+
+    near_up = lambda j: (weights, (1, 1, 1, feat, rows), lambda i, p: (0, j, i, 0, 0))
+    at_i = lambda i, p: (0, i, 0, 0)
+    strip_t = (local, 1, sub, span_t)
+
+    def near_hidden(source):
+        up = (weights, (1, 1, 1, feat, rows), lambda j, i, p: (0, j, i, 0, 0))
+        return hidden_of(source, up)
+
+    def near_slopes(t, near_cot, near_gate):
+        kind = (local, local, sub, span_t)
+        return call_once(
+            near_slopes_body,
+            place,
+            local,
+            [(cot, half_one, lambda i, p: (i, 0, t)), (near_cot, half_one, every)]
+            + [down_of(0, 1), down_of(1, 0), down_of(1, 1)]
+            + [unit_of(near_gate, 0), unit_of(gate, 1, t), unit_of(near_gate, 1)],
+            [(kind, BF16, (1,) + kind[1:], lambda i, p: (i, 0, 0, 0))] * 3,
+            20,
+        )
+
+    def near_outputs(t, own_hid, near_hid):
         return call_once(
             outputs_body,
             place,
             local,
-            [down_of(j, which) for which in range(3)]
-            + [unit_of(array, j) for array in (hid, hid_lo, hid_hi)],
-            [(blocks, kind, one, every)],
+            [down_of(1, 0), down_of(1, 1), unit_of(own_hid, 1, t), unit_of(near_hid, 1)],
+            [((local, feat, span_t), BF16, half_one, every)],
             16,
         )[0]
 
-    def added(own, got):
+    def near_grads(from_own, from_near):
+        return call_once(
+            grads_body,
+            place,
+            local,
+            [near_up(0), near_up(1), (from_own, strip_t, at_i), (from_near, strip_t, at_i)],
+            [((local, feat, span_t), BF16, half_one, every)],
+            16,
+        )[0]
+
+    def added(own, got_0, got_1):
         pairs_at = lambda i, p: (i, 0, 0)
-        two = (2, feat, tokens)
+        two, two_t = (2, feat, tokens), (2, feat, span_t)
         return call(
             add_body,
             place,
             (local // 2,),
-            [(own, two, pairs_at), (got, two, pairs_at)],
+            [(own, two, pairs_at), (got_0, two_t, pairs_at), (got_1, two_t, pairs_at)],
             [(blocks, BF16, two, pairs_at)],
             20,
         )[0]
+
+    x_0 = after((x_0,), weights, send_e)[0]
+    hid_0, gate_0 = near_hidden(x_0)
+    ns_0, sn_0, nn_0 = near_slopes(0, cot_0, gate_0)
+    out_0 = near_outputs(0, hid, hid_0)
+    got_out_0 = send(out_0, 1)
+    ns_b = after((ns_0,), out_0)[0]
+    dx_0 = near_grads(ns_b, nn_0)
+    got_dx_0 = send(dx_0, 2)
+
+    got_e, far_e = after((got_e, far_e), dx_0)
+    send_e = up_again(mine_e, far_e)
+    last_e = send_z(send_e, 2)
+
+    x_1 = after((x_1,), send_e)[0]
+    hid_1, gate_1 = near_hidden(x_1)
+    cot_1, last_e = after((cot_1, last_e), hid_1)
 
     shard = (2, 2, local, part, feat)
     strip_d = (1, part, feat)
@@ -543,9 +528,9 @@
         down_terms_body,
         place,
         local,
-        [(cot, one, every), (cot_lo, one, low), (cot_hi, one, high)]
-        + [unit_of(hid, 1)]
-        + [unit_of(array, j) for j in (0, 1) for array in (hid_lo, hid_hi)],
+        [(cot, one, every), (cot_0, half_one, every), (cot_1, half_one, every)]
+        + [unit_of(hid, 1, None)]
+        + [unit_of(array, j) for j in (0, 1) for array in (hid_0, hid_1)],
         [
             (shard[2:], BF16, strip_d, every),
             (shard[1:], BF16, (2,) + strip_d, lambda i, p: (0, i, 0, 0)),
@@ -556,9 +541,8 @@
     )
     core_own, core_near = send_core(give_own), send_core(give_near)
     hid_b = after((hid,), give_own)[0]
-    near_out = outputs_of(1, hid_b, BF16)
-    got_out = send(near_out, 1)
-    core_own, core_near = after((core_own, core_near), near_out)
+    out_1 = near_outputs(1, hid_b, hid_1)
+    core_own, core_near = after((core_own, core_near), out_1)
     parts_d = (keep_e, first_got, keep_d, core_own, core_near)
     send_d, mine_d = call(
         down_meet_body,
@@ -570,54 +554,29 @@
         scratch=[pltpu.VMEM(shard, F32)],
     )
     got_d = send_z(send_d, 1)
-    cot_b, *near_b = after((cot, cot_lo, cot_hi), send_d)
-    late = [(1, 0, gate), (1, 1, gate_lo), (1, 2, gate_hi), (0, 2, gate_hi)]
-    slope_sn, slope_lo_n, slope_hi_n, slope_hi_s = call_once(
-        late_slopes_body,
+    cot_1 = after((cot_1,), send_d)[0]
+    ns_1, sn_1, nn_1 = near_slopes(1, cot_1, gate_1)
+    dx_1 = near_grads(ns_1, nn_1)
+
+    x_b = after((x,), dx_1)[0]
+    strips = [(v, strip_t, at_i) for v in (sn_0, sn_1, ns_0, ns_1, nn_0, nn_1)]
+    give_lo, give_hi, keep_u = call_once(
+        up_terms_body,
         place,
         local,
-        [(cot_b, one, every), (near_b[0], one, low), (near_b[1], one, high)]
-        + [down_of(j, which) for j, which, _ in late]
-        + [unit_of(array, j) for j, _, array in late],
-        [
-            (array.shape[1:], BF16, (1,) + array.shape[2:], lambda i, p: (i, 0, 0, 0))
-            for _, _, array in late
+        [(x_b, one, every), (x_0, half_one, every), (x_1, half_one, every)] + strips,
+        [
+            ((3, n_dp // 2, shard_u[1] // 2, rows), BF16, up_block, lambda i, p: (0, 0, min(i, local // 2 - 1), 0)),
+            ((3, n_dp // 2, shard_u[1] // 2, rows), BF16, up_block, lambda i, p: (0, 0, max(i - local // 2, 0), 0)),
+            ((3,) + shard_u, BF16, up_block, lambda i, p: (0, 0, i, 0)),
         ],
         20,
-    )
-
-    at_lo = lambda i, p: (0, least(i, half - 1), 0, 0)
-    at_hi = lambda i, p: (0, most(i - half, 0), 0, 0)
-    near_up = lambda j: (weights, (1, 1, 1, feat, rows), lambda i, p: (0, j, i, 0, 0))
-    near_grads = call_once(
-        near_grads_body,
-        place,
-        local,
-        [
-            near_up(0),
-            near_up(1),
-            (slope_lo_s, strip, at_lo),
-            (slope_lo_n, strip, at_lo),
-            (slope_hi_s, strip, at_hi),
-            (slope_hi_n, strip, at_hi),
-        ],
-        [(blocks, BF16, one, every)],
-        16,
-    )[0]
-    got_grads = send(near_grads, 2)
-
-    x_b = after((x,), near_grads)[0]
-    give_lo, give_hi, keep_u = up_terms(
-        up_terms_body,
-        [(x_b, one, every), (x_lo, one, low), (x_hi, one, high), (slope_sn, strip, at_i)]
-        + [(slope_lo_s, strip, at_lo), (slope_lo_n, strip, at_lo)]
-        + [(slope_hi_s, strip, at_hi), (slope_hi_n, strip, at_hi)],
-        3,
-        [lambda i: least(i, half - 1), lambda i: most(i - half, 0)],
-        16.0,
+        scratch=[pltpu.VMEM((n_dp // 2, 2, feat // n_dp, rows), BF16)],
+        span=16.0,
     )
     send_u, far_u, mine_u = up_meet(3, keep_u, [send_core(give_lo), send_core(give_hi)])
     got_u, far_u = send_z(send_u, 1), send_z(far_u, 1)
+
 
     got_d = after((got_d,), send_u)[0]
     send_d, mine_d = call(
@@ -630,23 +589,44 @@
     )
     got_d = send_z(send_d, 2)
 
+    got_out_0, got_dx_0 = after((got_out_0, got_dx_0), send_d)
+    out_1, dx_1 = after((out_1, dx_1), got_out_0, got_dx_0)
+    got_out_1, got_dx_1 = send(out_1, 1), send(dx_1, 2)
+
     up_b = after((up_blocks,), send_d)[0]
+    at_half = lambda i, p: (0, i % local, 0, 0)
     own_grads = call_once(
         grads_body,
         place,
-        local,
-        [
-            (up_b, (1, feat, rows), lambda i, p: (i, 0, p[0])),
-            (up_b, (1, feat, rows), lambda i, p: (i, 0, p[0] ^ 1)),
-            (slope_ss, strip, at_i),
-            (slope_sn, strip, at_i),
-        ],
-        [(blocks, F32, one, every)],
+        2 * local,
+        [
+            (up_b, (1, feat, rows), lambda i, p: (i % local, 0, p[0])),
+            (up_b, (1, feat, rows), lambda i, p: (i % local, 0, p[0] ^ 1)),
+            (slope_ss, strip_t, lambda i, p: (0, i % local, 0, i // local)),
+            (sn_0, strip_t, at_half),
+            (sn_1, strip_t, at_half),
+        ],
+        [(blocks, F32, half_one, lambda i, p: (i % local, 0, i // local))],
         16,
-        span=4.0,
+        span=8.0,
     )[0]
 
-    own_out = outputs_of(0, after((hid,), own_grads)[0], F32)
+    hid_c = after((hid,), own_grads)[0]
+    in_turn = lambda spec: (spec[0], spec[1], lambda i, p: spec[2](i % local, p))
+    own_out = call_once(
+        outputs_body,
+        place,
+        2 * local,
+        [
+            in_turn(down_of(0, 0)),
+            in_turn(down_of(0, 1)),
+            (hid_c, (1, 1, local, sub, span_t), lambda i, p: (0, i % local, 0, 0, i // local)),
+            in_turn(unit_of(hid_0, 0)),
+            in_turn(unit_of(hid_1, 0)),
+        ],
+        [(blocks, F32, half_one, lambda i, p: (i % local, 0, i // local))],
+        16,
+    )[0]
     far_u = after((far_u,), own_out)[0]
     send_u = up_again(mine_u, far_u)
     last_u = send_z(send_u, 2)
@@ -668,8 +648,8 @@
         swaps.append((device, home))
     home_d = lax.ppermute(sum_d, ("dp", "tensor"), swaps)
 
-    got_out = after((got_out,), sum_d)[0]
-    outputs = added(own_out, got_out)
+    got_out_1 = after((got_out_1,), sum_d)[0]
+    outputs = added(own_out, got_out_0, got_out_1)
 
     got_u, last_u = after((got_u, last_u), outputs)
     send_u, mine_u = call(
@@ -694,8 +674,8 @@
         ],
         8,
     )
-    got_grads = after((got_grads,), held)[0]
-    feature_grads = added(own_grads, got_grads)
+    got_dx_1 = after((got_dx_1,), held)[0]
+    feature_grads = added(own_grads, got_dx_0, got_dx_1)
 
     got_u = after((got_u,), feature_grads)[0]
     up_grads = call(

time: 102 us -> 105 us (1.029)
  Pallas kernels: 40.4 us -> 45.1 us
  waiting for transfers between devices: 29.8 us -> 25.8 us
  local copies, waits for them, and re-layouts: 2.33 us -> 4.03 us
    pallas_call x26 -> x28, Pallas kernels: 40.4 us -> 45.1 us  [call(): pl.pallas_call(body, grid_spec=pltpu.PrefetchScalarGridSpec(num_scalar_pr...]
    ppermute x1, waiting for transfers between devices: 4.57 us -> 1.29 us  [square_device(): home_d = lax.ppermute(sum_d, ('dp', 'tensor'), swaps)]
    ppermute x9 -> x11, starting transfers between devices: 8.89 us -> 10.9 us  [send(): lax.ppermute(value, 'tensor', [(t, t ^ hop) for t in range(n_tensor)])]
    slice x2 -> x1, local copies, waits for them, and re-layouts: 0.21 us -> 1.91 us  [square_device(): v[..., t]]
    ppermute x9, starting transfers between devices: 14.9 us -> 13.5 us  [send_z(): return lax.ppermute(value, 'dp', [(d, d ^ 2 * hop) for d in range(n_dp)])]
    ppermute x9 -> x11, waiting for transfers between devices: 4.18 us -> 4.37 us  [send(): lax.ppermute(value, 'tensor', [(t, t ^ hop) for t in range(n_tensor)])]
  transfers between devices with their start and end apart: 26 -> 28, of which waited for: 12 -> 11; matrix products, arithmetic and copies ran while one was open for 1% -> 3% of each run, Pallas kernels for 37% -> 40%
where the time goes in v4:
time: 105 us; the launch traced here: 104 us
  Pallas kernels  45.1 us (43%)
  starting transfers between devices  28 us (27%)
  waiting for transfers between devices  25.8 us (25%)
  local copies, waits for them, and re-layouts  4.03 us (4%)
    pallas_call x28, Pallas kernels, call(): pl.pallas_call(body, grid_spec=pltpu.PrefetchScalarGridSpec(num_scalar_pr...  45.1 us
    ppermute x9, waiting for transfers between devices, send_z(): return lax.ppermute(value, 'dp', [(d, d ^ 2 * hop) for d in range(n_dp)])  17 us
    ppermute x9, starting transfers between devices, send_z(): return lax.ppermute(value, 'dp', [(d, d ^ 2 * hop) for d in range(n_dp)])  13.5 us
    ppermute x11, starting transfers between devices, send(): lax.ppermute(value, 'tensor', [(t, t ^ hop) for t in range(n_tensor)])  10.9 us
    ppermute x11, waiting for transfers between devices, send(): lax.ppermute(value, 'tensor', [(t, t ^ hop) for t in range(n_tensor)])  4.37 us
    ppermute x7, waiting for transfers between devices, send_core(): return lax.ppermute(value, 'dp', [(d, d ^ 1) for d in range(n_dp)])  3.18 us
  transfers between devices with their start and end apart: 28, of which 11 were waited for; matrix products, arithmetic and copies ran while one was open for 3% of the time, Pallas kernels for 40%

profile of v4, /device:TPU:12, one launch (start us, length us, event | category | flops | bytes accessed | tf_op | source)
XLA Modules:
  0.0 104.2 jit_solution(10737162708579288902)
XLA Ops:
  3.4 1.6 %collective-permute-start.1 = (bf16[2,4,64,256]{3,2,1,0:T(8,128)(2,1)S(1)}, bf16[2,4,64,256]{3,2,1,0:T(8,128)(2,1)S(1)}, u32[]{:S(2)}, u32[]{:S(2)}) collective-permute-start(bf16[2,4,64,256]{3,2,1,0:T(8,128)(2,1)S(1)} %pad_maximum_fusion.2), channel_id=1, source_target_pairs={{0,1},{1,0},{2,3},{3,2},{4,5},{5,4},{6,7},{7,6},{8,9},{9,8},{10,11... | collective-permute-start | bytes 786440 | tf_op jit(solution)/shard_map/ppermute | solution.py:334
  5.0 1.9 %fusion = (bf16[4,256,384]{2,1,0:T(8,128)(2,1)S(1)}, bf16[4,256,384]{2,1,0:T(8,128)(2,1)S(1)}, bf16[4,256,384]{2,1,0:T(8,128)(2,1)S(1)}, bf16[4,256,384]{2,1,0:T(8,128)(2,1)S(1)}) fusion(bf16[4,256,768]{2,1,0:T(8,128)(2,1)S(1)} %bitcast.32, bf16[4,256,768]{2,1,0:T(8,128)(2,1)} %bitcast.38), kind=kLoop, calls=%fused_computation.8 | loop fusion | bytes 6291456 | tf_op jit(solution)/shard_map/slice | solution.py:358
  6.9 1.6 %collective-permute-start.3 = (bf16[4,256,384]{2,1,0:T(8,128)(2,1)S(1)}, bf16[4,256,384]{2,1,0:T(8,128)(2,1)S(1)}, u32[]{:S(2)}, u32[]{:S(2)}) collective-permute-start(bf16[4,256,384]{2,1,0:T(8,128)(2,1)S(1)} %get-tuple-element.86), channel_id=1, source_target_pairs={{0,2},{1,3},{2,0},{3,1},{4,6},{5,7},{6,4},{7,5},{8,10},{9,11},{10,... | collective-permute-start | bytes 2359304 | tf_op jit(solution)/shard_map/ppermute | solution.py:334
  9.1 5.8 %shard_map.75 = (bf16[2,4,4,64,768]{4,3,2,1,0:T(8,128)(2,1)S(1)}, bf16[2,4,4,64,768]{4,3,2,1,0:T(8,128)(2,1)S(1)}) custom-call(s32[3]{0:T(128)S(1)} %pad_add_fusion.place, bf16[4,256,768]{2,1,0:T(8,128)(2,1)S(1)} %bitcast.39, bf16[4,256,1024]{2,1,0:T(8,128)(2,1)S(1)} %copy-done.3), custom_call_target="tpu_custom_call" | custom-call | tf_op jit(solution)/shard_map/pallas_call | solution.py:74
  15.7 1.9 %collective-permute-start.6 = (bf16[4,256,384]{2,1,0:T(8,128)(2,1)S(1)}, bf16[4,256,384]{2,1,0:T(8,128)(2,1)S(1)}, u32[]{:S(2)}, u32[]{:S(2)}) collective-permute-start(bf16[4,256,384]{2,1,0:T(8,128)(2,1)S(1)} %get-tuple-element.91), channel_id=1, source_target_pairs={{0,1},{1,0},{2,3},{3,2},{4,5},{5,4},{6,7},{7,6},{8,9},{9,8},{10,11... | collective-permute-start | bytes 2359304 | tf_op jit(solution)/shard_map/ppermute | solution.py:334
  18.7 1.6 %shard_map.77 = (bf16[2,4,128,256]{3,2,1,0:T(8,128)(2,1)S(1)}, bf16[2,4,128,256]{3,2,1,0:T(8,128)(2,1)S(1)}) custom-call(s32[3]{0:T(128)S(1)} %pad_add_fusion.place, bf16[4,256,768]{2,1,0:T(8,128)(2,1)S(1)} %bitcast.34, bf16[2,4,4,64,768]{4,3,2,1,0:T(8,128)(2,1)S(1)} %get-tuple-element.132.refs_1_.refs_2_.refs_3_, bf16[4,256,768]{2,1,0:T(8,128)(2,1)S(1)} %bitcast.40, ...), custom_call_target="tpu_custom_call" | custom-call | tf_op jit(solution)/shard_map/pallas_call | solution.py:74
  20.3 7.3 %collective-permute-done.2.refs_1_ = bf16[2,2,4,64,256]{4,3,2,1,0:T(8,128)(2,1)S(1)} collective-permute-done((bf16[2,2,4,64,256]{4,3,2,1,0:T(8,128)(2,1)S(1)}, bf16[2,2,4,64,256]{4,3,2,1,0:T(8,128)(2,1)S(1)}, u32[]{:S(2)}, u32[]{:S(2)}) %collective-permute-start.2) | collective-permute-done | bytes 524320 | tf_op jit(solution)/shard_map/ppermute | solution.py:337
  27.8 1.4 %collective-permute-done.4.refs_1_ = bf16[4,256,384]{2,1,0:T(8,128)(2,1)S(1)} collective-permute-done((bf16[4,256,384]{2,1,0:T(8,128)(2,1)S(1)}, bf16[4,256,384]{2,1,0:T(8,128)(2,1)S(1)}, u32[]{:S(2)}, u32[]{:S(2)}) %collective-permute-start.4) | collective-permute-done | bytes 786464 | tf_op jit(solution)/shard_map/ppermute | solution.py:334
  29.7 1.4 %collective-permute-done.5.refs_0_.first_got = bf16[2,4,128,256]{3,2,1,0:T(8,128)(2,1)S(1)} collective-permute-done((bf16[2,4,128,256]{3,2,1,0:T(8,128)(2,1)S(1)}, bf16[2,4,128,256]{3,2,1,0:T(8,128)(2,1)S(1)}, u32[]{:S(2)}, u32[]{:S(2)}) %collective-permute-start.5) | collective-permute-done | bytes 524320 | tf_op jit(solution)/shard_map/ppermute | solution.py:340
  32.0 1.8 %collective-permute-start.7 = (bf16[1,128,256]{2,1,0:T(8,128)(2,1)S(1)}, bf16[1,128,256]{2,1,0:T(8,128)(2,1)S(1)}, u32[]{:S(2)}, u32[]{:S(2)}) collective-permute-start(bf16[1,128,256]{2,1,0:T(8,128)(2,1)S(1)} %get-tuple-element.93), channel_id=1, source_target_pairs={{0,8},{4,12},{8,0},{12,4},{16,24},{20,28},{24,16},{28,20},{1,9},{5... | collective-permute-start | bytes 196616 | tf_op jit(solution)/shard_map/ppermute | solution.py:337
  34.5 4.0 %shard_map.80 = (bf16[2,4,4,64,384]{4,3,2,1,0:T(8,128)(2,1)S(1)}, bf16[2,4,4,64,384]{4,3,2,1,0:T(8,128)(2,1)S(1)}) custom-call(s32[3]{0:T(128)S(1)} %pad_add_fusion.place, bf16[4,256,384]{2,1,0:T(8,128)(2,1)S(1)} %collective-permute-done.3.x_ref.refs_1_, bf16[2,2,4,256,256]{4,3,2,1,0:T(8,128)(2,1)S(1)} %bitcast.18), custom_call_target="tpu_custom_call" | custom-call | tf_op jit(solution)/shard_map/pallas_call | solution.py:74
  39.8 1.5 %shard_map.81 = (bf16[4,4,64,384]{3,2,1,0:T(8,128)(2,1)S(1)}, bf16[4,4,64,384]{3,2,1,0:T(8,128)(2,1)S(1)}, bf16[4,4,64,384]{3,2,1,0:T(8,128)(2,1)S(1)}) custom-call(s32[3]{0:T(128)S(1)} %pad_add_fusion.place, bf16[4,256,768]{2,1,0:T(8,128)(2,1)S(1)} %bitcast.35, bf16[4,256,384]{2,1,0:T(8,128)(2,1)S(1)} %collective-permute-done.4.refs_1_, ...), custom_call_target="tpu_custom_call" | custom-call | tf_op jit(solution)/shard_map/pallas_call | solution.py:74
  43.2 2.7 %collective-permute-start.11 = (bf16[1,128,256]{2,1,0:T(8,128)(2,1)S(1)}, bf16[1,128,256]{2,1,0:T(8,128)(2,1)S(1)}, u32[]{:S(2)}, u32[]{:S(2)}) collective-permute-start(bf16[1,128,256]{2,1,0:T(8,128)(2,1)S(1)} %shard_map.84), channel_id=1, source_target_pairs={{0,16},{4,20},{8,24},{12,28},{16,0},{20,4},{24,8},{28,12},{1,17},{... | collective-permute-start | bytes 196616 | tf_op jit(solution)/shard_map/ppermute | solution.py:337
  45.8 4.2 %shard_map.85 = (bf16[2,4,4,64,384]{4,3,2,1,0:T(8,128)(2,1)S(1)}, bf16[2,4,4,64,384]{4,3,2,1,0:T(8,128)(2,1)S(1)}) custom-call(s32[3]{0:T(128)S(1)} %pad_add_fusion.place, bf16[4,256,384]{2,1,0:T(8,128)(2,1)S(1)} %collective-permute-done.12.x_ref.refs_2_, bf16[2,2,4,256,256]{4,3,2,1,0:T(8,128)(2,1)S(1)} %bitcast.25), custom_call_target="tpu_custom_call" | custom-call | tf_op jit(solution)/shard_map/pallas_call | solution.py:74
  50.1 2.1 %shard_map.86 = (bf16[4,128,256]{2,1,0:T(8,128)(2,1)S(1)}, bf16[2,4,128,256]{3,2,1,0:T(8,128)(2,1)S(1)}, bf16[3,4,128,256]{3,2,1,0:T(8,128)(2,1)S(1)}) custom-call(s32[3]{0:T(128)S(1)} %pad_add_fusion.place, bf16[4,256,768]{2,1,0:T(8,128)(2,1)S(1)} %bitcast.36, bf16[4,256,384]{2,1,0:T(8,128)(2,1)S(1)} %collective-permute-done.4.refs_1_, ...), custom_call_target="tpu_custom_call" | custom-call | tf_op jit(solution)/shard_map/pallas_call | solution.py:74
  52.7 1.9 %collective-permute-start.19 = (bf16[4,256,384]{2,1,0:T(8,128)(2,1)S(1)}, bf16[4,256,384]{2,1,0:T(8,128)(2,1)S(1)}, u32[]{:S(2)}, u32[]{:S(2)}) collective-permute-start(bf16[4,256,384]{2,1,0:T(8,128)(2,1)S(1)} %shard_map.83), channel_id=1, source_target_pairs={{0,2},{1,3},{2,0},{3,1},{4,6},{5,7},{6,4},{7,5},{8,10},{9,11},{10,... | collective-permute-start | bytes 2359304 | tf_op jit(solution)/shard_map/ppermute | solution.py:334
  54.6 1.5 %collective-permute-start.18 = (bf16[4,256,384]{2,1,0:T(8,128)(2,1)S(1)}, bf16[4,256,384]{2,1,0:T(8,128)(2,1)S(1)}, u32[]{:S(2)}, u32[]{:S(2)}) collective-permute-start(bf16[4,256,384]{2,1,0:T(8,128)(2,1)S(1)} %shard_map.82), channel_id=1, source_target_pairs={{0,1},{1,0},{2,3},{3,2},{4,5},{5,4},{6,7},{7,6},{8,9},{9,8},{10,11... | collective-permute-start | bytes 2359304 | tf_op jit(solution)/shard_map/ppermute | solution.py:334
  58.9 1.5 %shard_map.89 = (bf16[4,4,64,384]{3,2,1,0:T(8,128)(2,1)S(1)}, bf16[4,4,64,384]{3,2,1,0:T(8,128)(2,1)S(1)}, bf16[4,4,64,384]{3,2,1,0:T(8,128)(2,1)S(1)}) custom-call(s32[3]{0:T(128)S(1)} %pad_add_fusion.place, bf16[4,256,768]{2,1,0:T(8,128)(2,1)S(1)} %bitcast.37, bf16[4,256,384]{2,1,0:T(8,128)(2,1)S(1)} %collective-permute-done.6.refs_2_.refs_1_, ...), custom_call_target="tpu_custom_call" | custom-call | tf_op jit(solution)/shard_map/pallas_call | solution.py:74
  61.7 2.1 %shard_map.91 = (bf16[3,4,64,256]{3,2,1,0:T(8,128)(2,1)S(1)}, bf16[3,4,64,256]{3,2,1,0:T(8,128)(2,1)S(1)}, bf16[3,4,128,256]{3,2,1,0:T(8,128)(2,1)S(1)}) custom-call(s32[3]{0:T(128)S(1)} %pad_add_fusion.place, bf16[4,256,768]{2,1,0:T(8,128)(2,1)S(1)} %bitcast.41, bf16[4,256,384]{2,1,0:T(8,128)(2,1)S(1)} %collective-permute-done.3.x_ref.refs_1_, ...), custom_call_target="tpu_custom_call" | custom-call | flops 16000000000 | tf_op jit(solution)/shard_map/pallas_call | solution.py:74
  66.8 1.6 %collective-permute-start.22 = (bf16[3,128,256]{2,1,0:T(8,128)(2,1)S(1)}, bf16[3,128,256]{2,1,0:T(8,128)(2,1)S(1)}, u32[]{:S(2)}, u32[]{:S(2)}) collective-permute-start(bf16[3,128,256]{2,1,0:T(8,128)(2,1)S(1)} %get-tuple-element.138), channel_id=1, source_target_pairs={{0,8},{4,12},{8,0},{12,4},{16,24},{20,28},{24,16},{28,20},{1,9},{5... | collective-permute-start | bytes 589832 | tf_op jit(solution)/shard_map/ppermute | solution.py:337
  68.9 4.4 %collective-permute-done.15.got_ref = bf16[2,4,128,256]{3,2,1,0:T(8,128)(2,1)S(1)} collective-permute-done((bf16[2,4,128,256]{3,2,1,0:T(8,128)(2,1)S(1)}, bf16[2,4,128,256]{3,2,1,0:T(8,128)(2,1)S(1)}, u32[]{:S(2)}, u32[]{:S(2)}) %collective-permute-start.15) | collective-permute-done | bytes 524320 | tf_op jit(solution)/shard_map/ppermute | solution.py:337
  74.0 1.6 %collective-permute-start.21 = (bf16[4,128,256]{2,1,0:T(8,128)(2,1)S(1)}, bf16[4,128,256]{2,1,0:T(8,128)(2,1)S(1)}, u32[]{:S(2)}, u32[]{:S(2)}) collective-permute-start(bf16[4,128,256]{2,1,0:T(8,128)(2,1)S(1)} %get-tuple-element.130), channel_id=1, source_target_pairs={{0,16},{4,20},{8,24},{12,28},{16,0},{20,4},{24,8},{28,12},{1,17},{... | collective-permute-start | bytes 786440 | tf_op jit(solution)/shard_map/ppermute | solution.py:337
  76.2 1.8 %shard_map.94.own_ref = f32[4,256,768]{2,1,0:T(8,128)S(1)} custom-call(s32[3]{0:T(128)S(1)} %pad_add_fusion.place, bf16[4,256,1024]{2,1,0:T(8,128)(2,1)S(1)} %copy-done.3, bf16[4,256,1024]{2,1,0:T(8,128)(2,1)S(1)} %copy-done.3, bf16[4,4,64,768]{3,2,1,0:T(8,128)(2,1)S(1)} %shard_map.76.refs_3_.refs_2_, ...), custom_call_target="tpu_custom_call" | custom-call | flops 8000000000 | tf_op jit(solution)/shard_map/pallas_call | solution.py:74
  78.0 1.8 %shard_map.95.own_ref = f32[4,256,768]{2,1,0:T(8,128)S(1)} custom-call(s32[3]{0:T(128)S(1)} %pad_add_fusion.place, bf16[4,1024,256]{2,1,0:T(8,128)(2,1)S(1)} %copy-done.1, bf16[4,1024,256]{2,1,0:T(8,128)(2,1)S(1)} %copy-done.1, bf16[2,4,4,64,768]{4,3,2,1,0:T(8,128)(2,1)S(1)} %get-tuple-element.132.refs_1_.refs_2_.refs_3_, ...), custom_call_target="tpu_custom_call" | custom-call | tf_op jit(solution)/shard_map/pallas_call | solution.py:74
  81.1 4.1 %collective-permute-start.25 = (bf16[3,128,256]{2,1,0:T(8,128)(2,1)S(1)}, bf16[3,128,256]{2,1,0:T(8,128)(2,1)S(1)}, u32[]{:S(2)}, u32[]{:S(2)}) collective-permute-start(bf16[3,128,256]{2,1,0:T(8,128)(2,1)S(1)} %shard_map.96), channel_id=1, source_target_pairs={{0,16},{4,20},{8,24},{12,28},{16,0},{20,4},{24,8},{28,12},{1,17},{... | collective-permute-start | bytes 589832 | tf_op jit(solution)/shard_map/ppermute | solution.py:337
  85.2 4.5 %collective-permute-done.21.got_ref = bf16[4,128,256]{2,1,0:T(8,128)(2,1)S(1)} collective-permute-done((bf16[4,128,256]{2,1,0:T(8,128)(2,1)S(1)}, bf16[4,128,256]{2,1,0:T(8,128)(2,1)S(1)}, u32[]{:S(2)}, u32[]{:S(2)}) %collective-permute-start.21) | collective-permute-done | bytes 262176 | tf_op jit(solution)/shard_map/ppermute | solution.py:337
  90.3 1.9 %collective-permute-start.26 = (bf16[4,128,256]{2,1,0:T(8,128)(2,1)S(1)}, bf16[4,128,256]{2,1,0:T(8,128)(2,1)S(1)}, u32[]{:S(2)}, u32[]{:S(2)}) collective-permute-start(bf16[4,128,256]{2,1,0:T(8,128)(2,1)S(1)} %shard_map.97), channel_id=1, source_target_pairs={{0,0},{1,8},{2,2},{3,10},{4,4},{5,12},{6,6},{7,14},{8,1},{9,9},{10... | collective-permute-start | bytes 786440 | tf_op jit(solution)/shard_map/ppermute | solution.py:649
  92.2 2.8 %collective-permute-done.20.got_1 = bf16[4,256,384]{2,1,0:T(8,128)(2,1)S(1)} collective-permute-done((bf16[4,256,384]{2,1,0:T(8,128)(2,1)S(1)}, bf16[4,256,384]{2,1,0:T(8,128)(2,1)S(1)}, u32[]{:S(2)}, u32[]{:S(2)}) %collective-permute-start.20) | collective-permute-done | bytes 786464 | tf_op jit(solution)/shard_map/ppermute | solution.py:334
  95.0 1.8 %shard_map.98 = bf16[4,256,768]{2,1,0:T(8,128)(2,1)} custom-call(s32[3]{0:T(128)S(1)} %pad_add_fusion.place, f32[4,256,768]{2,1,0:T(8,128)S(1)} %shard_map.95.own_ref, bf16[4,256,384]{2,1,0:T(8,128)(2,1)S(1)} %collective-permute-done.18.got_0, bf16[4,256,384]{2,1,0:T(8,128)(2,1)S(1)} %collective-permute-done.20.got_1), custom_call_target="tpu_custom_call" | custom-call | tf_op jit(solution)/shard_map/pallas_call | solution.py:74
  98.2 1.3 %collective-permute-done.26.down_in = bf16[4,128,256]{2,1,0:T(8,128)(2,1)S(1)} collective-permute-done((bf16[4,128,256]{2,1,0:T(8,128)(2,1)S(1)}, bf16[4,128,256]{2,1,0:T(8,128)(2,1)S(1)}, u32[]{:S(2)}, u32[]{:S(2)}) %collective-permute-start.26) | collective-permute-done | bytes 262176 | tf_op jit(solution)/shard_map/ppermute | solution.py:649
  99.5 1.6 %shard_map.100 = (f32[4,32,1024]{2,1,0:T(8,128)}, f32[4,128,256]{2,1,0:T(8,128)}) custom-call(s32[3]{0:T(128)S(1)} %pad_add_fusion.place, f32[2,128,256]{2,1,0:T(8,128)S(1)} %get-tuple-element.147.mine_ref, bf16[4,128,256]{2,1,0:T(8,128)(2,1)S(1)} %collective-permute-done.26.down_in), custom_call_target="tpu_custom_call" | custom-call | tf_op jit(solution)/shard_map/pallas_call | solution.py:74
  101.0 1.8 %shard_map.101 = bf16[4,256,768]{2,1,0:T(8,128)(2,1)} custom-call(s32[3]{0:T(128)S(1)} %pad_add_fusion.place, f32[4,256,768]{2,1,0:T(8,128)S(1)} %shard_map.94.own_ref, bf16[4,256,384]{2,1,0:T(8,128)(2,1)S(1)} %collective-permute-done.19.got_0, bf16[4,256,384]{2,1,0:T(8,128)(2,1)S(1)} %collective-permute-done.23.got_1), custom_call_target="tpu_custom_call" | custom-call | tf_op jit(solution)/shard_map/pallas_call | solution.py:74
  (67 shorter events, 24.4 us)
Async XLA Ops:
  0.6 4.3 %copy-start = (bf16[1024,768]{1,0:T(8,128)(2,1)S(1)}, bf16[1024,768]{1,0:T(8,128)(2,1)}, u32[]{:S(2)}) copy-start(bf16[1024,768]{1,0:T(8,128)(2,1)} %param.5) | copy-start | bytes 4718596
  1.8 13.1 %collective-permute-start = (bf16[2,4,64,256]{3,2,1,0:T(8,128)(2,1)S(1)}, bf16[2,4,64,256]{3,2,1,0:T(8,128)(2,1)S(1)}, u32[]{:S(2)}, u32[]{:S(2)}) collective-permute-start(bf16[2,4,64,256]{3,2,1,0:T(8,128)(2,1)S(1)} %pad_maximum_fusion.1), channel_id=1, source_target_pairs={{0,2},{1,3},{2,0},{3,1},{4,6},{5,7},{6,4},{7,5},{8,10},{9,11},{10,... | collective-permute-start | bytes 786440 | tf_op jit(solution)/shard_map/ppermute | solution.py:334
  3.4 11.5 %collective-permute-start.1 = (bf16[2,4,64,256]{3,2,1,0:T(8,128)(2,1)S(1)}, bf16[2,4,64,256]{3,2,1,0:T(8,128)(2,1)S(1)}, u32[]{:S(2)}, u32[]{:S(2)}) collective-permute-start(bf16[2,4,64,256]{3,2,1,0:T(8,128)(2,1)S(1)} %pad_maximum_fusion.2), channel_id=1, source_target_pairs={{0,1},{1,0},{2,3},{3,2},{4,5},{5,4},{6,7},{7,6},{8,9},{9,8},{10,11... | collective-permute-start | bytes 786440 | tf_op jit(solution)/shard_map/ppermute | solution.py:334
  5.0 4.1 %copy-start.2 = (bf16[1024,768]{1,0:T(8,128)(2,1)S(1)}, bf16[1024,768]{1,0:T(8,128)(2,1)}, u32[]{:S(2)}) copy-start(bf16[1024,768]{1,0:T(8,128)(2,1)} %param.4) | copy-start | bytes 4718596
  5.0 4.1 %copy-start.3 = (bf16[4,256,1024]{2,1,0:T(8,128)(2,1)S(1)}, bf16[4,256,1024]{2,1,0:T(8,128)(2,1)}, u32[]{:S(2)}) copy-start(bf16[4,256,1024]{2,1,0:T(8,128)(2,1)} %refs_1_.3) | copy-start | bytes 6291460
  6.9 20.9 %collective-permute-start.3 = (bf16[4,256,384]{2,1,0:T(8,128)(2,1)S(1)}, bf16[4,256,384]{2,1,0:T(8,128)(2,1)S(1)}, u32[]{:S(2)}, u32[]{:S(2)}) collective-permute-start(bf16[4,256,384]{2,1,0:T(8,128)(2,1)S(1)} %get-tuple-element.86), channel_id=1, source_target_pairs={{0,2},{1,3},{2,0},{3,1},{4,6},{5,7},{6,4},{7,5},{8,10},{9,11},{10,... | collective-permute-start | bytes 2359304 | tf_op jit(solution)/shard_map/ppermute | solution.py:334
  8.5 20.7 %collective-permute-start.4 = (bf16[4,256,384]{2,1,0:T(8,128)(2,1)S(1)}, bf16[4,256,384]{2,1,0:T(8,128)(2,1)S(1)}, u32[]{:S(2)}, u32[]{:S(2)}) collective-permute-start(bf16[4,256,384]{2,1,0:T(8,128)(2,1)S(1)} %get-tuple-element.87), channel_id=1, source_target_pairs={{0,1},{1,0},{2,3},{3,2},{4,5},{5,4},{6,7},{7,6},{8,9},{9,8},{10,11... | collective-permute-start | bytes 2359304 | tf_op jit(solution)/shard_map/ppermute | solution.py:334
  9.1 8.4 %copy-start.1 = (bf16[4,1024,256]{2,1,0:T(8,128)(2,1)S(1)}, bf16[4,1024,256]{2,1,0:T(8,128)(2,1)}, u32[]{:S(2)}) copy-start(bf16[4,1024,256]{2,1,0:T(8,128)(2,1)} %refs_1_.4) | copy-start | bytes 6291460
  15.0 12.6 %collective-permute-start.2 = (bf16[2,2,4,64,256]{4,3,2,1,0:T(8,128)(2,1)S(1)}, bf16[2,2,4,64,256]{4,3,2,1,0:T(8,128)(2,1)S(1)}, u32[]{:S(2)}, u32[]{:S(2)}) collective-permute-start(bf16[2,2,4,64,256]{4,3,2,1,0:T(8,128)(2,1)S(1)} %pad_maximum_fusion.refs_0_), channel_id=1, source_target_pairs={{0,8},{4,12},{8,0},{12,4},{16,24},{20,28},{24,16},{28,20},{1,9},{5... | collective-permute-start | bytes 1572872 | tf_op jit(solution)/shard_map/ppermute | solution.py:337
  15.5 30.3 %collective-permute-start.12 = (bf16[4,256,384]{2,1,0:T(8,128)(2,1)S(1)}, bf16[4,256,384]{2,1,0:T(8,128)(2,1)S(1)}, u32[]{:S(2)}, u32[]{:S(2)}) collective-permute-start(bf16[4,256,384]{2,1,0:T(8,128)(2,1)S(1)} %get-tuple-element.106), channel_id=1, source_target_pairs={{0,2},{1,3},{2,0},{3,1},{4,6},{5,7},{6,4},{7,5},{8,10},{9,11},{10,... | collective-permute-start | bytes 2359304 | tf_op jit(solution)/shard_map/ppermute | solution.py:334
  15.7 34.4 %collective-permute-start.6 = (bf16[4,256,384]{2,1,0:T(8,128)(2,1)S(1)}, bf16[4,256,384]{2,1,0:T(8,128)(2,1)S(1)}, u32[]{:S(2)}, u32[]{:S(2)}) collective-permute-start(bf16[4,256,384]{2,1,0:T(8,128)(2,1)S(1)} %get-tuple-element.91), channel_id=1, source_target_pairs={{0,1},{1,0},{2,3},{3,2},{4,5},{5,4},{6,7},{7,6},{8,9},{9,8},{10,11... | collective-permute-start | bytes 2359304 | tf_op jit(solution)/shard_map/ppermute | solution.py:334
  29.2 1.9 %collective-permute-start.5 = (bf16[2,4,128,256]{3,2,1,0:T(8,128)(2,1)S(1)}, bf16[2,4,128,256]{3,2,1,0:T(8,128)(2,1)S(1)}, u32[]{:S(2)}, u32[]{:S(2)}) collective-permute-start(bf16[2,4,128,256]{3,2,1,0:T(8,128)(2,1)S(1)} %get-tuple-element.90), channel_id=1, source_target_pairs={{0,4},{4,0},{8,12},{12,8},{16,20},{20,16},{24,28},{28,24},{1,5},{5... | collective-permute-start | bytes 1572872 | tf_op jit(solution)/shard_map/ppermute | solution.py:340
  29.2 2.8 %collective-permute-start.9 = (bf16[2,2,4,64,256]{4,3,2,1,0:T(8,128)(2,1)S(1)}, bf16[2,2,4,64,256]{4,3,2,1,0:T(8,128)(2,1)S(1)}, u32[]{:S(2)}, u32[]{:S(2)}) collective-permute-start(bf16[2,2,4,64,256]{4,3,2,1,0:T(8,128)(2,1)S(1)} %pad_maximum_fusion.refs_0_), channel_id=1, source_target_pairs={{0,4},{4,0},{8,12},{12,8},{16,20},{20,16},{24,28},{28,24},{1,5},{5... | collective-permute-start | bytes 1572872 | tf_op jit(solution)/shard_map/ppermute | solution.py:340
  29.7 4.1 %collective-permute-start.10 = (bf16[2,2,4,64,256]{4,3,2,1,0:T(8,128)(2,1)S(1)}, bf16[2,2,4,64,256]{4,3,2,1,0:T(8,128)(2,1)S(1)}, u32[]{:S(2)}, u32[]{:S(2)}) collective-permute-start(bf16[2,2,4,64,256]{4,3,2,1,0:T(8,128)(2,1)S(1)} %collective-permute-done.2.refs_1_), channel_id=1, source_target_pairs={{0,4},{4,0},{8,12},{12,8},{16,20},{20,16},{24,28},{28,24},{1,5},{5... | collective-permute-start | bytes 1572872 | tf_op jit(solution)/shard_map/ppermute | solution.py:340
  31.7 10.9 %collective-permute-start.8 = (bf16[1,128,256]{2,1,0:T(8,128)(2,1)S(1)}, bf16[1,128,256]{2,1,0:T(8,128)(2,1)S(1)}, u32[]{:S(2)}, u32[]{:S(2)}) collective-permute-start(bf16[1,128,256]{2,1,0:T(8,128)(2,1)S(1)} %get-tuple-element.94), channel_id=1, source_target_pairs={{0,8},{4,12},{8,0},{12,4},{16,24},{20,28},{24,16},{28,20},{1,9},{5... | collective-permute-start | bytes 196616 | tf_op jit(solution)/shard_map/ppermute | solution.py:337
  32.0 10.6 %collective-permute-start.7 = (bf16[1,128,256]{2,1,0:T(8,128)(2,1)S(1)}, bf16[1,128,256]{2,1,0:T(8,128)(2,1)S(1)}, u32[]{:S(2)}, u32[]{:S(2)}) collective-permute-start(bf16[1,128,256]{2,1,0:T(8,128)(2,1)S(1)} %get-tuple-element.93), channel_id=1, source_target_pairs={{0,8},{4,12},{8,0},{12,4},{16,24},{20,28},{24,16},{28,20},{1,9},{5... | collective-permute-start | bytes 196616 | tf_op jit(solution)/shard_map/ppermute | solution.py:337
  43.2 6.9 %collective-permute-start.11 = (bf16[1,128,256]{2,1,0:T(8,128)(2,1)S(1)}, bf16[1,128,256]{2,1,0:T(8,128)(2,1)S(1)}, u32[]{:S(2)}, u32[]{:S(2)}) collective-permute-start(bf16[1,128,256]{2,1,0:T(8,128)(2,1)S(1)} %shard_map.84), channel_id=1, source_target_pairs={{0,16},{4,20},{8,24},{12,28},{16,0},{20,4},{24,8},{28,12},{1,17},{... | collective-permute-start | bytes 196616 | tf_op jit(solution)/shard_map/ppermute | solution.py:337
  52.1 5.3 %collective-permute-start.14 = (bf16[2,4,128,256]{3,2,1,0:T(8,128)(2,1)S(1)}, bf16[2,4,128,256]{3,2,1,0:T(8,128)(2,1)S(1)}, u32[]{:S(2)}, u32[]{:S(2)}) collective-permute-start(bf16[2,4,128,256]{3,2,1,0:T(8,128)(2,1)S(1)} %get-tuple-element.112), channel_id=1, source_target_pairs={{0,4},{4,0},{8,12},{12,8},{16,20},{20,16},{24,28},{28,24},{1,5},{5... | collective-permute-start | bytes 1572872 | tf_op jit(solution)/shard_map/ppermute | solution.py:340
  52.2 5.2 %collective-permute-start.13 = (bf16[4,128,256]{2,1,0:T(8,128)(2,1)S(1)}, bf16[4,128,256]{2,1,0:T(8,128)(2,1)S(1)}, u32[]{:S(2)}, u32[]{:S(2)}) collective-permute-start(bf16[4,128,256]{2,1,0:T(8,128)(2,1)S(1)} %get-tuple-element.111), channel_id=1, source_target_pairs={{0,4},{4,0},{8,12},{12,8},{16,20},{20,16},{24,28},{28,24},{1,5},{5... | collective-permute-start | bytes 786440 | tf_op jit(solution)/shard_map/ppermute | solution.py:340
  52.7 22.9 %collective-permute-start.19 = (bf16[4,256,384]{2,1,0:T(8,128)(2,1)S(1)}, bf16[4,256,384]{2,1,0:T(8,128)(2,1)S(1)}, u32[]{:S(2)}, u32[]{:S(2)}) collective-permute-start(bf16[4,256,384]{2,1,0:T(8,128)(2,1)S(1)} %shard_map.83), channel_id=1, source_target_pairs={{0,2},{1,3},{2,0},{3,1},{4,6},{5,7},{6,4},{7,5},{8,10},{9,11},{10,... | collective-permute-start | bytes 2359304 | tf_op jit(solution)/shard_map/ppermute | solution.py:334
  54.6 21.0 %collective-permute-start.18 = (bf16[4,256,384]{2,1,0:T(8,128)(2,1)S(1)}, bf16[4,256,384]{2,1,0:T(8,128)(2,1)S(1)}, u32[]{:S(2)}, u32[]{:S(2)}) collective-permute-start(bf16[4,256,384]{2,1,0:T(8,128)(2,1)S(1)} %shard_map.82), channel_id=1, source_target_pairs={{0,1},{1,0},{2,3},{3,2},{4,5},{5,4},{6,7},{7,6},{8,9},{9,8},{10,11... | collective-permute-start | bytes 2359304 | tf_op jit(solution)/shard_map/ppermute | solution.py:334
  58.4 14.9 %collective-permute-start.15 = (bf16[2,4,128,256]{3,2,1,0:T(8,128)(2,1)S(1)}, bf16[2,4,128,256]{3,2,1,0:T(8,128)(2,1)S(1)}, u32[]{:S(2)}, u32[]{:S(2)}) collective-permute-start(bf16[2,4,128,256]{3,2,1,0:T(8,128)(2,1)S(1)} %get-tuple-element.117), channel_id=1, source_target_pairs={{0,8},{4,12},{8,0},{12,4},{16,24},{20,28},{24,16},{28,20},{1,9},{5... | collective-permute-start | bytes 1572872 | tf_op jit(solution)/shard_map/ppermute | solution.py:337
  63.8 1.8 %collective-permute-start.16 = (bf16[3,4,64,256]{3,2,1,0:T(8,128)(2,1)S(1)}, bf16[3,4,64,256]{3,2,1,0:T(8,128)(2,1)S(1)}, u32[]{:S(2)}, u32[]{:S(2)}) collective-permute-start(bf16[3,4,64,256]{3,2,1,0:T(8,128)(2,1)S(1)} %get-tuple-element.126), channel_id=1, source_target_pairs={{0,4},{4,0},{8,12},{12,8},{16,20},{20,16},{24,28},{28,24},{1,5},{5... | collective-permute-start | bytes 1179656 | tf_op jit(solution)/shard_map/ppermute | solution.py:340
  63.8 2.3 %collective-permute-start.17 = (bf16[3,4,64,256]{3,2,1,0:T(8,128)(2,1)S(1)}, bf16[3,4,64,256]{3,2,1,0:T(8,128)(2,1)S(1)}, u32[]{:S(2)}, u32[]{:S(2)}) collective-permute-start(bf16[3,4,64,256]{3,2,1,0:T(8,128)(2,1)S(1)} %get-tuple-element.127), channel_id=1, source_target_pairs={{0,4},{4,0},{8,12},{12,8},{16,20},{20,16},{24,28},{28,24},{1,5},{5... | collective-permute-start | bytes 1179656 | tf_op jit(solution)/shard_map/ppermute | solution.py:340
  66.8 13.7 %collective-permute-start.22 = (bf16[3,128,256]{2,1,0:T(8,128)(2,1)S(1)}, bf16[3,128,256]{2,1,0:T(8,128)(2,1)S(1)}, u32[]{:S(2)}, u32[]{:S(2)}) collective-permute-start(bf16[3,128,256]{2,1,0:T(8,128)(2,1)S(1)} %get-tuple-element.138), channel_id=1, source_target_pairs={{0,8},{4,12},{8,0},{12,4},{16,24},{20,28},{24,16},{28,20},{1,9},{5... | collective-permute-start | bytes 589832 | tf_op jit(solution)/shard_map/ppermute | solution.py:337
  68.5 28.4 %collective-permute-start.24 = (bf16[3,128,256]{2,1,0:T(8,128)(2,1)S(1)}, bf16[3,128,256]{2,1,0:T(8,128)(2,1)S(1)}, u32[]{:S(2)}, u32[]{:S(2)}) collective-permute-start(bf16[3,128,256]{2,1,0:T(8,128)(2,1)S(1)} %get-tuple-element.128), channel_id=1, source_target_pairs={{0,8},{4,12},{8,0},{12,4},{16,24},{20,28},{24,16},{28,20},{1,9},{5... | collective-permute-start | bytes 589832 | tf_op jit(solution)/shard_map/ppermute | solution.py:337
  74.0 15.7 %collective-permute-start.21 = (bf16[4,128,256]{2,1,0:T(8,128)(2,1)S(1)}, bf16[4,128,256]{2,1,0:T(8,128)(2,1)S(1)}, u32[]{:S(2)}, u32[]{:S(2)}) collective-permute-start(bf16[4,128,256]{2,1,0:T(8,128)(2,1)S(1)} %get-tuple-element.130), channel_id=1, source_target_pairs={{0,16},{4,20},{8,24},{12,28},{16,0},{20,4},{24,8},{28,12},{1,17},{... | collective-permute-start | bytes 786440 | tf_op jit(solution)/shard_map/ppermute | solution.py:337
  75.6 19.4 %collective-permute-start.20 = (bf16[4,256,384]{2,1,0:T(8,128)(2,1)S(1)}, bf16[4,256,384]{2,1,0:T(8,128)(2,1)S(1)}, u32[]{:S(2)}, u32[]{:S(2)}) collective-permute-start(bf16[4,256,384]{2,1,0:T(8,128)(2,1)S(1)} %shard_map.87), channel_id=1, source_target_pairs={{0,1},{1,0},{2,3},{3,2},{4,5},{5,4},{6,7},{7,6},{8,9},{9,8},{10,11... | collective-permute-start | bytes 2359304 | tf_op jit(solution)/shard_map/ppermute | solution.py:334
  76.1 24.9 %collective-permute-start.23 = (bf16[4,256,384]{2,1,0:T(8,128)(2,1)S(1)}, bf16[4,256,384]{2,1,0:T(8,128)(2,1)S(1)}, u32[]{:S(2)}, u32[]{:S(2)}) collective-permute-start(bf16[4,256,384]{2,1,0:T(8,128)(2,1)S(1)} %shard_map.90), channel_id=1, source_target_pairs={{0,2},{1,3},{2,0},{3,1},{4,6},{5,7},{6,4},{7,5},{8,10},{9,11},{10,... | collective-permute-start | bytes 2359304 | tf_op jit(solution)/shard_map/ppermute | solution.py:334
  81.1 15.8 %collective-permute-start.25 = (bf16[3,128,256]{2,1,0:T(8,128)(2,1)S(1)}, bf16[3,128,256]{2,1,0:T(8,128)(2,1)S(1)}, u32[]{:S(2)}, u32[]{:S(2)}) collective-permute-start(bf16[3,128,256]{2,1,0:T(8,128)(2,1)S(1)} %shard_map.96), channel_id=1, source_target_pairs={{0,16},{4,20},{8,24},{12,28},{16,0},{20,4},{24,8},{28,12},{1,17},{... | collective-permute-start | bytes 589832 | tf_op jit(solution)/shard_map/ppermute | solution.py:337
  90.3 9.2 %collective-permute-start.26 = (bf16[4,128,256]{2,1,0:T(8,128)(2,1)S(1)}, bf16[4,128,256]{2,1,0:T(8,128)(2,1)S(1)}, u32[]{:S(2)}, u32[]{:S(2)}) collective-permute-start(bf16[4,128,256]{2,1,0:T(8,128)(2,1)S(1)} %shard_map.97), channel_id=1, source_target_pairs={{0,0},{1,8},{2,2},{3,10},{4,4},{5,12},{6,6},{7,14},{8,1},{9,9},{10... | collective-permute-start | bytes 786440 | tf_op jit(solution)/shard_map/ppermute | solution.py:649
  97.5 5.4 %collective-permute-start.27 = (bf16[2,128,256]{2,1,0:T(8,128)(2,1)S(1)}, bf16[2,128,256]{2,1,0:T(8,128)(2,1)S(1)}, u32[]{:S(2)}, u32[]{:S(2)}) collective-permute-start(bf16[2,128,256]{2,1,0:T(8,128)(2,1)S(1)} %get-tuple-element.148), channel_id=1, source_target_pairs={{0,2},{1,3},{2,0},{3,1},{4,6},{5,7},{6,4},{7,5},{8,10},{9,11},{10,... | collective-permute-start | bytes 393224 | tf_op jit(solution)/shard_map/ppermute | solution.py:334

commit v5 on v3

--- a/solution.py
+++ b/solution.py
@@ -188,14 +188,25 @@
     put_slopes(square(cot_ref), [down_ref], [gate_ref], [slope_ref])
 
 
-def late_slopes_body(step, steps, place, own_ref, near_lo, near_hi, *refs):
-    downs, gates, slopes = refs[:4], refs[4:8], refs[8:]
-    put_slopes(square(own_ref), downs[3:], gates[3:], slopes[3:])
-
-    def work(near_ref):
-        put_slopes(square(near_ref), downs[:3], gates[:3], slopes[:3])
-
-    halves(step, steps, work, (near_lo,), (near_hi,))
+def late_body(step, steps, place, own_ref, near_lo, near_hi, *refs):
+    downs, gates, (up_own, up_near, lo_s), slopes, out_ref = (
+        refs[:4],
+        refs[4:8],
+        refs[8:11],
+        refs[11:15],
+        refs[15],
+    )
+    count = steps // 2
+    if step < count:
+        here = [ref.at[step] for ref in slopes]
+        put_slopes(square(own_ref), downs[3:], gates[3:], here[3:])
+        near_ref = near_lo if step < count // 2 else near_hi
+        put_slopes(square(near_ref), downs[:3], gates[:3], here[:3])
+        return
+    sn, lo_n, hi_n, hi_s = slopes
+    pair = (lo_s, lo_n) if step - count < count // 2 else (hi_s, hi_n)
+    strips = [ref.at[:, (step - count) % (count // 2)] for ref in pair]
+    out_ref[0] = dot_nn(stacked((up_own, up_near), 1), stacked(strips)).astype(BF16)
 
 
 def own_terms_body(step, steps, place, cot_ref, hid_ref, x_ref, slope_ref, give_ref, keep_ref, down_s, up_s):
@@ -249,13 +260,6 @@
     out_ref[0] = total.astype(out_ref.dtype)
 
 
-def near_grads_body(step, steps, place, up_own, up_near, lo_s, lo_n, hi_s, hi_n, out_ref):
-    def work(*slopes):
-        out_ref[0] = dot_nn(stacked((up_own, up_near), 1), stacked(slopes)).astype(BF16)
-
-    halves(step, steps, work, (lo_s, lo_n), (hi_s, hi_n))
-
-
 def grads_body(step, steps, place, up_own, up_near, slope_own, slope_near, out_ref):
     out_ref[0] = dot_nn(stacked((up_own, up_near), 1), stacked((slope_own, slope_near)))
 
@@ -264,23 +268,26 @@
     out_ref[...] = (own_ref[...] + got_ref[...].astype(F32)).astype(BF16)
 
 
-def down_meet_body(place, first, first_got, keep_ref, got_own, got_near, send_ref, mine_ref, total_s):
-    stay = (place[0] ^ place[1]) & 1
-    total_s[0, 0] = first[1].astype(F32) + first_got[1].astype(F32)
-    total_s[0, 1] = keep_ref[0].astype(F32) + got_own[...].astype(F32)
-    total_s[1] = keep_ref[1:].astype(F32) + got_near[...].astype(F32)
-    mine_ref[...] = total_s[:, stay]
-    send_ref[...] = total_s[:, 1 - stay].astype(BF16)
-
-
-def down_again_body(place, mine_ref, got_ref, send_ref, own_ref):
-    stay = (place[0] // 2) ^ (place[1] // 2)
-    own_ref[...] = mine_ref[stay] + got_ref[stay].astype(F32)
-    send_ref[...] = (mine_ref[1 - stay] + got_ref[1 - stay].astype(F32)).astype(BF16)
-
-
-def down_sum_body(factor, place, own_ref, got_ref, out_ref):
-    out_ref[...] = ((own_ref[...] + got_ref[...].astype(F32)) * factor).astype(BF16)
+def down_meet_body(place, first, first_got, keep_ref, got_own, got_near, far_ref, near_ref, mine_ref):
+    stay_j = (place[0] ^ place[1]) & 1
+    stay_i = (place[0] // 2) ^ (place[1] // 2)
+    kept = ((first.at[1], keep_ref.at[0]), (keep_ref.at[1], keep_ref.at[2]))
+    got = ((first_got.at[1], got_own), (got_near.at[0], got_near.at[1]))
+    for i in range(2):
+        for j in range(2):
+
+            @pl.when(jnp.logical_and(stay_i == i, stay_j == j))
+            def _():
+                total = lambda a, b: kept[a][b][...].astype(F32) + got[a][b][...].astype(F32)
+                far_ref[...] = total(1 - i, 1 - j).astype(BF16)
+                near_ref[...] = total(i, 1 - j).astype(BF16)
+                mine_ref[0] = total(i, j)
+                mine_ref[1] = total(1 - i, j)
+
+
+def down_sum_body(factor, place, mine_ref, near_ref, got_ref, out_ref):
+    total = mine_ref[0] + near_ref[...].astype(F32) + got_ref[...].astype(F32)
+    out_ref[...] = (total * factor).astype(BF16)
 
 
 def up_meet_body(parts, place, keep_ref, *refs):
@@ -560,50 +567,37 @@
     got_out = send(near_out, 1)
     core_own, core_near = after((core_own, core_near), near_out)
     parts_d = (keep_e, first_got, keep_d, core_own, core_near)
-    send_d, mine_d = call(
+    far_d, near_d, mine_d = call(
         down_meet_body,
         place,
         (1,),
         [whole(v) for v in parts_d],
-        [whole_out(shard[1:], BF16), whole_out(shard[1:], F32)],
+        [whole_out(shard[2:], BF16)] * 2 + [whole_out(shard[1:], F32)],
         16,
-        scratch=[pltpu.VMEM(shard, F32)],
-    )
-    got_d = send_z(send_d, 1)
-    cot_b, *near_b = after((cot, cot_lo, cot_hi), send_d)
+    )
+    got_far = send_z(far_d, 1)
+    cot_b, *near_b = after((cot, cot_lo, cot_hi), far_d)
     late = [(1, 0, gate), (1, 1, gate_lo), (1, 2, gate_hi), (0, 2, gate_hi)]
-    slope_sn, slope_lo_n, slope_hi_n, slope_hi_s = call_once(
-        late_slopes_body,
-        place,
-        local,
-        [(cot_b, one, every), (near_b[0], one, low), (near_b[1], one, high)]
-        + [down_of(j, which) for j, which, _ in late]
-        + [unit_of(array, j) for j, _, array in late],
-        [
-            (array.shape[1:], BF16, (1,) + array.shape[2:], lambda i, p: (i, 0, 0, 0))
-            for _, _, array in late
-        ],
-        20,
-    )
-
     at_lo = lambda i, p: (0, least(i, half - 1), 0, 0)
     at_hi = lambda i, p: (0, most(i - half, 0), 0, 0)
+    turn = lambda spec: (spec[0], spec[1], lambda i, p: spec[2](i % local, p))
     near_up = lambda j: (weights, (1, 1, 1, feat, rows), lambda i, p: (0, j, i, 0, 0))
-    near_grads = call_once(
-        near_grads_body,
-        place,
-        local,
-        [
-            near_up(0),
-            near_up(1),
-            (slope_lo_s, strip, at_lo),
-            (slope_lo_n, strip, at_lo),
-            (slope_hi_s, strip, at_hi),
-            (slope_hi_n, strip, at_hi),
-        ],
-        [(blocks, BF16, one, every)],
-        16,
-    )[0]
+    slope_sn, slope_lo_n, slope_hi_n, slope_hi_s, near_grads = call_once(
+        late_body,
+        place,
+        2 * local,
+        [
+            turn(spec)
+            for spec in [(cot_b, one, every), (near_b[0], one, low), (near_b[1], one, high)]
+            + [down_of(j, which) for j, which, _ in late]
+            + [unit_of(array, j) for j, _, array in late]
+            + [near_up(0), near_up(1)]
+        ]
+        + [whole(slope_lo_s)],
+        [whole_out(array.shape[1:], BF16) for _, _, array in late]
+        + [(blocks, BF16, one, lambda i, p: (i % local, 0, 0))],
+        20,
+    )
     got_grads = send(near_grads, 2)
 
     x_b = after((x,), near_grads)[0]
@@ -616,19 +610,15 @@
         [lambda i: least(i, half - 1), lambda i: most(i - half, 0)],
         16.0,
     )
-    send_u, far_u, mine_u = up_meet(3, keep_u, [send_core(give_lo), send_core(give_hi)])
-    got_u, far_u = send_z(send_u, 1), send_z(far_u, 1)
-
-    got_d = after((got_d,), send_u)[0]
-    send_d, mine_d = call(
-        down_again_body,
-        place,
-        (1,),
-        [whole(mine_d), whole(got_d)],
-        [whole_out(shard[2:], BF16), whole_out(shard[2:], F32)],
-        16,
-    )
-    got_d = send_z(send_d, 2)
+    give_lo, give_hi = after((give_lo, give_hi), got_far)
+    gots_u = [send_core(give_lo), send_core(give_hi)]
+    send_u, far_u, mine_u = up_meet(3, keep_u, gots_u)
+    far_u = send_z(far_u, 1)
+
+    got_far = after((got_far,), send_u)[0]
+    send_d = up_again(mine_d, got_far)
+    last_d = send_z(send_d, 2)
+    got_near_d = send_z(after((near_d,), send_d)[0], 1)
 
     up_b = after((up_blocks,), send_d)[0]
     own_grads = call_once(
@@ -648,15 +638,16 @@
 
     own_out = outputs_of(0, after((hid,), own_grads)[0], F32)
     far_u = after((far_u,), own_out)[0]
-    send_u = up_again(mine_u, far_u)
-    last_u = send_z(send_u, 2)
-
-    got_d = after((got_d,), send_u)[0]
+    next_u = up_again(mine_u, far_u)
+    last_u = send_z(next_u, 2)
+    got_u = send_z(after((send_u,), next_u)[0], 1)
+
+    last_d, got_near_d = after((last_d, got_near_d), next_u)
     sum_d = call(
         functools.partial(down_sum_body, factor),
         place,
         (1,),
-        [whole(mine_d), whole(got_d)],
+        [whole(v) for v in (mine_d, got_near_d, last_d)],
         [whole_out(shard[2:], BF16)],
         8,
     )[0]

time: 102 us -> 105 us (1.029)
  waiting for transfers between devices: 29.8 us -> 35 us
  starting transfers between devices: 27.4 us -> 25.2 us
    ppermute x9 -> x10, waiting for transfers between devices: 17.8 us -> 24.3 us  [send_z(): return lax.ppermute(value, 'dp', [(d, d ^ 2 * hop) for d in range(n_dp)])]
    ppermute x9 -> x10, starting transfers between devices: 14.9 us -> 12.3 us  [send_z(): return lax.ppermute(value, 'dp', [(d, d ^ 2 * hop) for d in range(n_dp)])]
    ppermute x1, waiting for transfers between devices: 4.57 us -> 3.27 us  [square_device(): home_d = lax.ppermute(sum_d, ('dp', 'tensor'), swaps)]
    pallas_call x26 -> x25, Pallas kernels: 40.4 us -> 39.6 us  [call(): pl.pallas_call(body, grid_spec=pltpu.PrefetchScalarGridSpec(num_scalar_pr...]
  transfers between devices with their start and end apart: 26 -> 27, of which waited for: 12 -> 13; matrix products, arithmetic and copies ran while one was open for 1% -> 1% of each run, Pallas kernels for 37% -> 35%
where the time goes in v5:
time: 105 us; the launch traced here: 103 us
  Pallas kernels  39.6 us (38%)
  waiting for transfers between devices  35 us (33%)
  starting transfers between devices  25.2 us (24%)
  local copies, waits for them, and re-layouts  2.33 us (2%)
    pallas_call x25, Pallas kernels, call(): pl.pallas_call(body, grid_spec=pltpu.PrefetchScalarGridSpec(num_scalar_pr...  39.6 us
    ppermute x10, waiting for transfers between devices, send_z(): return lax.ppermute(value, 'dp', [(d, d ^ 2 * hop) for d in range(n_dp)])  24.3 us
    ppermute x10, starting transfers between devices, send_z(): return lax.ppermute(value, 'dp', [(d, d ^ 2 * hop) for d in range(n_dp)])  12.3 us
    ppermute x9, starting transfers between devices, send(): lax.ppermute(value, 'tensor', [(t, t ^ hop) for t in range(n_tensor)])  9.4 us
    ppermute x9, waiting for transfers between devices, send(): lax.ppermute(value, 'tensor', [(t, t ^ hop) for t in range(n_tensor)])  4.18 us
    ppermute x1, waiting for transfers between devices, square_device(): home_d = lax.ppermute(sum_d, ('dp', 'tensor'), swaps)  3.27 us
    ppermute x7, waiting for transfers between devices, send_core(): return lax.ppermute(value, 'dp', [(d, d ^ 1) for d in range(n_dp)])  3.24 us
  transfers between devices with their start and end apart: 27, of which 13 were waited for; matrix products, arithmetic and copies ran while one was open for 1% of the time, Pallas kernels for 35%

profile of v5, /device:TPU:12, one launch (start us, length us, event | category | flops | bytes accessed | tf_op | source)
XLA Modules:
  0.0 103.3 jit_solution(4844637694028510347)
XLA Ops:
  3.4 1.6 %collective-permute-start.1 = (bf16[2,4,64,256]{3,2,1,0:T(8,128)(2,1)S(1)}, bf16[2,4,64,256]{3,2,1,0:T(8,128)(2,1)S(1)}, u32[]{:S(2)}, u32[]{:S(2)}) collective-permute-start(bf16[2,4,64,256]{3,2,1,0:T(8,128)(2,1)S(1)} %pad_maximum_fusion.2), channel_id=1, source_target_pairs={{0,1},{1,0},{2,3},{3,2},{4,5},{5,4},{6,7},{7,6},{8,9},{9,8},{10,11... | collective-permute-start | bytes 786440 | tf_op jit(solution)/shard_map/ppermute | solution.py:357
  5.2 1.6 %collective-permute-start.3 = (bf16[2,256,768]{2,1,0:T(8,128)(2,1)S(1)}, bf16[2,256,768]{2,1,0:T(8,128)(2,1)S(1)}, u32[]{:S(2)}, u32[]{:S(2)}) collective-permute-start(bf16[2,256,768]{2,1,0:T(8,128)(2,1)S(1)} %bitcast.45), channel_id=1, source_target_pairs={{0,2},{1,3},{2,0},{3,1},{4,6},{5,7},{6,4},{7,5},{8,10},{9,11},{10,... | collective-permute-start | bytes 2359304 | tf_op jit(solution)/shard_map/ppermute | solution.py:357
  8.1 5.8 %shard_map.75 = (bf16[2,4,4,64,768]{4,3,2,1,0:T(8,128)(2,1)S(1)}, bf16[2,4,4,64,768]{4,3,2,1,0:T(8,128)(2,1)S(1)}) custom-call(s32[3]{0:T(128)S(1)} %pad_add_fusion.place, bf16[4,256,768]{2,1,0:T(8,128)(2,1)S(1)} %bitcast.37, bf16[4,256,1024]{2,1,0:T(8,128)(2,1)S(1)} %copy-done.3), custom_call_target="tpu_custom_call" | custom-call | tf_op jit(solution)/shard_map/pallas_call | solution.py:74
  15.0 1.3 %collective-permute-start.6 = (bf16[2,256,768]{2,1,0:T(8,128)(2,1)S(1)}, bf16[2,256,768]{2,1,0:T(8,128)(2,1)S(1)}, u32[]{:S(2)}, u32[]{:S(2)}) collective-permute-start(bf16[2,256,768]{2,1,0:T(8,128)(2,1)S(1)} %bitcast.42), channel_id=1, source_target_pairs={{0,1},{1,0},{2,3},{3,2},{4,5},{5,4},{6,7},{7,6},{8,9},{9,8},{10,11... | collective-permute-start | bytes 2359304 | tf_op jit(solution)/shard_map/ppermute | solution.py:357
  17.4 1.6 %shard_map.77 = (bf16[2,4,128,256]{3,2,1,0:T(8,128)(2,1)S(1)}, bf16[2,4,128,256]{3,2,1,0:T(8,128)(2,1)S(1)}) custom-call(s32[3]{0:T(128)S(1)} %pad_add_fusion.place, bf16[4,256,768]{2,1,0:T(8,128)(2,1)S(1)} %bitcast.33, bf16[2,4,4,64,768]{4,3,2,1,0:T(8,128)(2,1)S(1)} %get-tuple-element.133.refs_1_.refs_3_, bf16[4,256,768]{2,1,0:T(8,128)(2,1)S(1)} %bitcast.38, ...), custom_call_target="tpu_custom_call" | custom-call | tf_op jit(solution)/shard_map/pallas_call | solution.py:74
  19.0 7.9 %collective-permute-done.2.refs_1_ = bf16[2,2,4,64,256]{4,3,2,1,0:T(8,128)(2,1)S(1)} collective-permute-done((bf16[2,2,4,64,256]{4,3,2,1,0:T(8,128)(2,1)S(1)}, bf16[2,2,4,64,256]{4,3,2,1,0:T(8,128)(2,1)S(1)}, u32[]{:S(2)}, u32[]{:S(2)}) %collective-permute-start.2) | collective-permute-done | bytes 524320 | tf_op jit(solution)/shard_map/ppermute | solution.py:360
  27.9 1.6 %collective-permute-done.4.refs_1_ = bf16[2,256,768]{2,1,0:T(8,128)(2,1)S(1)} collective-permute-done((bf16[2,256,768]{2,1,0:T(8,128)(2,1)S(1)}, bf16[2,256,768]{2,1,0:T(8,128)(2,1)S(1)}, u32[]{:S(2)}, u32[]{:S(2)}) %collective-permute-start.4) | collective-permute-done | bytes 786464 | tf_op jit(solution)/shard_map/ppermute | solution.py:357
  30.1 1.4 %collective-permute-done.5.refs_0_.first_got = bf16[2,4,128,256]{3,2,1,0:T(8,128)(2,1)S(1)} collective-permute-done((bf16[2,4,128,256]{3,2,1,0:T(8,128)(2,1)S(1)}, bf16[2,4,128,256]{3,2,1,0:T(8,128)(2,1)S(1)}, u32[]{:S(2)}, u32[]{:S(2)}) %collective-permute-start.5) | collective-permute-done | bytes 524320 | tf_op jit(solution)/shard_map/ppermute | solution.py:363
  32.2 2.0 %collective-permute-start.7 = (bf16[1,128,256]{2,1,0:T(8,128)(2,1)S(1)}, bf16[1,128,256]{2,1,0:T(8,128)(2,1)S(1)}, u32[]{:S(2)}, u32[]{:S(2)}) collective-permute-start(bf16[1,128,256]{2,1,0:T(8,128)(2,1)S(1)} %get-tuple-element.93), channel_id=1, source_target_pairs={{0,8},{4,12},{8,0},{12,4},{16,24},{20,28},{24,16},{28,20},{1,9},{5... | collective-permute-start | bytes 196616 | tf_op jit(solution)/shard_map/ppermute | solution.py:360
  34.9 3.1 %shard_map.80 = (bf16[2,4,2,64,768]{4,3,2,1,0:T(8,128)(2,1)S(1)}, bf16[2,4,2,64,768]{4,3,2,1,0:T(8,128)(2,1)S(1)}) custom-call(s32[3]{0:T(128)S(1)} %pad_add_fusion.place, bf16[2,256,768]{2,1,0:T(8,128)(2,1)S(1)} %collective-permute-done.3.x_ref.refs_1_, bf16[2,2,4,256,256]{4,3,2,1,0:T(8,128)(2,1)S(1)} %bitcast.22), custom_call_target="tpu_custom_call" | custom-call | tf_op jit(solution)/shard_map/pallas_call | solution.py:74
  39.5 2.7 %collective-permute-start.11 = (bf16[1,128,256]{2,1,0:T(8,128)(2,1)S(1)}, bf16[1,128,256]{2,1,0:T(8,128)(2,1)S(1)}, u32[]{:S(2)}, u32[]{:S(2)}) collective-permute-start(bf16[1,128,256]{2,1,0:T(8,128)(2,1)S(1)} %shard_map.82), channel_id=1, source_target_pairs={{0,16},{4,20},{8,24},{12,28},{16,0},{20,4},{24,8},{28,12},{1,17},{... | collective-permute-start | bytes 196616 | tf_op jit(solution)/shard_map/ppermute | solution.py:360
  42.1 1.5 %collective-permute-done.12.x_ref.refs_2_ = bf16[2,256,768]{2,1,0:T(8,128)(2,1)S(1)} collective-permute-done((bf16[2,256,768]{2,1,0:T(8,128)(2,1)S(1)}, bf16[2,256,768]{2,1,0:T(8,128)(2,1)S(1)}, u32[]{:S(2)}, u32[]{:S(2)}) %collective-permute-start.12) | collective-permute-done | bytes 786464 | tf_op jit(solution)/shard_map/ppermute | solution.py:357
  43.6 3.1 %shard_map.83 = (bf16[2,4,2,64,768]{4,3,2,1,0:T(8,128)(2,1)S(1)}, bf16[2,4,2,64,768]{4,3,2,1,0:T(8,128)(2,1)S(1)}) custom-call(s32[3]{0:T(128)S(1)} %pad_add_fusion.place, bf16[2,256,768]{2,1,0:T(8,128)(2,1)S(1)} %collective-permute-done.12.x_ref.refs_2_, bf16[2,2,4,256,256]{4,3,2,1,0:T(8,128)(2,1)S(1)} %bitcast.23), custom_call_target="tpu_custom_call" | custom-call | tf_op jit(solution)/shard_map/pallas_call | solution.py:74
  46.8 2.0 %shard_map.84 = (bf16[4,128,256]{2,1,0:T(8,128)(2,1)S(1)}, bf16[2,4,128,256]{3,2,1,0:T(8,128)(2,1)S(1)}, bf16[3,4,128,256]{3,2,1,0:T(8,128)(2,1)S(1)}) custom-call(s32[3]{0:T(128)S(1)} %pad_add_fusion.place, bf16[4,256,768]{2,1,0:T(8,128)(2,1)S(1)} %bitcast.35, bf16[2,256,768]{2,1,0:T(8,128)(2,1)S(1)} %collective-permute-done.4.refs_1_, ...), custom_call_target="tpu_custom_call" | custom-call | tf_op jit(solution)/shard_map/pallas_call | solution.py:74
  49.4 1.5 %shard_map.85 = bf16[4,256,768]{2,1,0:T(8,128)(2,1)S(1)} custom-call(s32[3]{0:T(128)S(1)} %pad_add_fusion.place, bf16[2,2,4,256,256]{4,3,2,1,0:T(8,128)(2,1)S(1)} %bitcast.24, bf16[2,2,4,256,256]{4,3,2,1,0:T(8,128)(2,1)S(1)} %bitcast.25, bf16[2,2,4,256,256]{4,3,2,1,0:T(8,128)(2,1)S(1)} %bitcast.26, ...), custom_call_target="tpu_custom_call" | custom-call | tf_op jit(solution)/shard_map/pallas_call | solution.py:74
  50.9 1.6 %collective-permute-start.18 = (bf16[4,256,768]{2,1,0:T(8,128)(2,1)S(1)}, bf16[4,256,768]{2,1,0:T(8,128)(2,1)S(1)}, u32[]{:S(2)}, u32[]{:S(2)}) collective-permute-start(bf16[4,256,768]{2,1,0:T(8,128)(2,1)S(1)} %shard_map.85), channel_id=1, source_target_pairs={{0,1},{1,0},{2,3},{3,2},{4,5},{5,4},{6,7},{7,6},{8,9},{9,8},{10,11... | collective-permute-start | bytes 4718600 | tf_op jit(solution)/shard_map/ppermute | solution.py:357
  54.0 2.5 %shard_map.87 = (bf16[4,4,64,768]{3,2,1,0:T(8,128)(2,1)S(1)}, bf16[4,2,64,768]{3,2,1,0:T(8,128)(2,1)S(1)}, bf16[4,2,64,768]{3,2,1,0:T(8,128)(2,1)S(1)}, bf16[4,2...) custom-call(s32[3]{0:T(128)S(1)} %pad_add_fusion.place, bf16[4,256,768]{2,1,0:T(8,128)(2,1)S(1)} %bitcast.36, ...), custom_call_target="tpu_custom_call" | custom-call | tf_op jit(solution)/shard_map/pallas_call | solution.py:74
  57.1 2.1 %shard_map.88 = (bf16[3,4,64,256]{3,2,1,0:T(8,128)(2,1)S(1)}, bf16[3,4,64,256]{3,2,1,0:T(8,128)(2,1)S(1)}, bf16[3,4,128,256]{3,2,1,0:T(8,128)(2,1)S(1)}) custom-call(s32[3]{0:T(128)S(1)} %pad_add_fusion.place, bf16[4,256,768]{2,1,0:T(8,128)(2,1)S(1)} %bitcast.39, bf16[2,256,768]{2,1,0:T(8,128)(2,1)S(1)} %collective-permute-done.3.x_ref.refs_1_, ...), custom_call_target="tpu_custom_call" | custom-call | flops 16000000000 | tf_op jit(solution)/shard_map/pallas_call | solution.py:74
  59.2 2.3 %collective-permute-done.15.far_ref = bf16[4,128,256]{2,1,0:T(8,128)(2,1)S(1)} collective-permute-done((bf16[4,128,256]{2,1,0:T(8,128)(2,1)S(1)}, bf16[4,128,256]{2,1,0:T(8,128)(2,1)S(1)}, u32[]{:S(2)}, u32[]{:S(2)}) %collective-permute-start.15) | collective-permute-done | bytes 262176 | tf_op jit(solution)/shard_map/ppermute | solution.py:360
  65.2 2.6 %collective-permute-start.19 = (bf16[4,128,256]{2,1,0:T(8,128)(2,1)S(1)}, bf16[4,128,256]{2,1,0:T(8,128)(2,1)S(1)}, u32[]{:S(2)}, u32[]{:S(2)}) collective-permute-start(bf16[4,128,256]{2,1,0:T(8,128)(2,1)S(1)} %shard_map.90), channel_id=1, source_target_pairs={{0,16},{4,20},{8,24},{12,28},{16,0},{20,4},{24,8},{28,12},{1,17},{... | collective-permute-start | bytes 786440 | tf_op jit(solution)/shard_map/ppermute | solution.py:360
  68.3 1.6 %collective-permute-start.20 = (bf16[4,128,256]{2,1,0:T(8,128)(2,1)S(1)}, bf16[4,128,256]{2,1,0:T(8,128)(2,1)S(1)}, u32[]{:S(2)}, u32[]{:S(2)}) collective-permute-start(bf16[4,128,256]{2,1,0:T(8,128)(2,1)S(1)} %get-tuple-element.135), channel_id=1, source_target_pairs={{0,8},{4,12},{8,0},{12,4},{16,24},{20,28},{24,16},{28,20},{1,9},{5... | collective-permute-start | bytes 786440 | tf_op jit(solution)/shard_map/ppermute | solution.py:360
  69.8 1.5 %shard_map.91.own_ref = f32[4,256,768]{2,1,0:T(8,128)S(1)} custom-call(s32[3]{0:T(128)S(1)} %pad_add_fusion.place, bf16[4,256,1024]{2,1,0:T(8,128)(2,1)S(1)} %copy-done.3, bf16[4,256,1024]{2,1,0:T(8,128)(2,1)S(1)} %copy-done.3, bf16[4,4,64,768]{3,2,1,0:T(8,128)(2,1)S(1)} %shard_map.76.refs_3_.refs_2_, bf16[4,4,64,768]{3,2,1,0:T(8,128)(2,1)S(1)} %get-tuple-element.121.refs_3_), custom_call_target="tpu_custom_call" | custom-call | flops 4000000000 | tf_op jit(solution)/shard_map/pallas_call | solution.py:74
  71.4 1.5 %shard_map.92.own_ref = f32[4,256,768]{2,1,0:T(8,128)S(1)} custom-call(s32[3]{0:T(128)S(1)} %pad_add_fusion.place, bf16[4,1024,256]{2,1,0:T(8,128)(2,1)S(1)} %copy-done, bf16[4,1024,256]{2,1,0:T(8,128)(2,1)S(1)} %copy-done, bf16[4,1024,256]{2,1,0:T(8,128)(2,1)S(1)} %copy-done, bf16[2,4,4,64,768]{4,3,2,1,0:T(8,128)(2,1)S(1)} %get-tuple-element.133.refs_1_.refs_3_, ...), custom_call_target="tpu_custom_call" | custom-call | tf_op jit(solution)/shard_map/pallas_call | solution.py:74
  72.9 6.7 %collective-permute-done.21.far_ref = bf16[3,128,256]{2,1,0:T(8,128)(2,1)S(1)} collective-permute-done((bf16[3,128,256]{2,1,0:T(8,128)(2,1)S(1)}, bf16[3,128,256]{2,1,0:T(8,128)(2,1)S(1)}, u32[]{:S(2)}, u32[]{:S(2)}) %collective-permute-start.21) | collective-permute-done | bytes 196640 | tf_op jit(solution)/shard_map/ppermute | solution.py:360
  80.3 4.9 %collective-permute-done.20.near_ref = bf16[4,128,256]{2,1,0:T(8,128)(2,1)S(1)} collective-permute-done((bf16[4,128,256]{2,1,0:T(8,128)(2,1)S(1)}, bf16[4,128,256]{2,1,0:T(8,128)(2,1)S(1)}, u32[]{:S(2)}, u32[]{:S(2)}) %collective-permute-start.20) | collective-permute-done | bytes 262176 | tf_op jit(solution)/shard_map/ppermute | solution.py:360
  85.3 1.9 %collective-permute-start.24 = (bf16[3,128,256]{2,1,0:T(8,128)(2,1)S(1)}, bf16[3,128,256]{2,1,0:T(8,128)(2,1)S(1)}, u32[]{:S(2)}, u32[]{:S(2)}) collective-permute-start(bf16[3,128,256]{2,1,0:T(8,128)(2,1)S(1)} %shard_map.93), channel_id=1, source_target_pairs={{0,16},{4,20},{8,24},{12,28},{16,0},{20,4},{24,8},{28,12},{1,17},{... | collective-permute-start | bytes 589832 | tf_op jit(solution)/shard_map/ppermute | solution.py:360
  87.8 1.9 %collective-permute-start.25 = (bf16[4,128,256]{2,1,0:T(8,128)(2,1)S(1)}, bf16[4,128,256]{2,1,0:T(8,128)(2,1)S(1)}, u32[]{:S(2)}, u32[]{:S(2)}) collective-permute-start(bf16[4,128,256]{2,1,0:T(8,128)(2,1)S(1)} %shard_map.94), channel_id=1, source_target_pairs={{0,0},{1,8},{2,2},{3,10},{4,4},{5,12},{6,6},{7,14},{8,1},{9,9},{10... | collective-permute-start | bytes 786440 | tf_op jit(solution)/shard_map/ppermute | solution.py:660
  89.7 1.9 %shard_map.95 = bf16[4,256,768]{2,1,0:T(8,128)(2,1)} custom-call(s32[3]{0:T(128)S(1)} %pad_add_fusion.place, f32[4,256,768]{2,1,0:T(8,128)S(1)} %shard_map.92.own_ref, bf16[4,256,768]{2,1,0:T(8,128)(2,1)S(1)} %collective-permute-done.18.got_ref), custom_call_target="tpu_custom_call" | custom-call | tf_op jit(solution)/shard_map/pallas_call | solution.py:74
  91.7 2.4 %collective-permute-done.24.refs_5_ = bf16[3,128,256]{2,1,0:T(8,128)(2,1)S(1)} collective-permute-done((bf16[3,128,256]{2,1,0:T(8,128)(2,1)S(1)}, bf16[3,128,256]{2,1,0:T(8,128)(2,1)S(1)}, u32[]{:S(2)}, u32[]{:S(2)}) %collective-permute-start.24) | collective-permute-done | bytes 196640 | tf_op jit(solution)/shard_map/ppermute | solution.py:360
  95.2 3.3 %collective-permute-done.25.down_in = bf16[4,128,256]{2,1,0:T(8,128)(2,1)S(1)} collective-permute-done((bf16[4,128,256]{2,1,0:T(8,128)(2,1)S(1)}, bf16[4,128,256]{2,1,0:T(8,128)(2,1)S(1)}, u32[]{:S(2)}, u32[]{:S(2)}) %collective-permute-start.25) | collective-permute-done | bytes 262176 | tf_op jit(solution)/shard_map/ppermute | solution.py:660
  98.5 1.6 %shard_map.97 = (f32[4,32,1024]{2,1,0:T(8,128)}, f32[4,128,256]{2,1,0:T(8,128)}) custom-call(s32[3]{0:T(128)S(1)} %pad_add_fusion.place, f32[2,128,256]{2,1,0:T(8,128)S(1)} %get-tuple-element.147.mine_ref, bf16[4,128,256]{2,1,0:T(8,128)(2,1)S(1)} %collective-permute-done.25.down_in), custom_call_target="tpu_custom_call" | custom-call | tf_op jit(solution)/shard_map/pallas_call | solution.py:74
  100.1 1.9 %shard_map.98 = bf16[4,256,768]{2,1,0:T(8,128)(2,1)} custom-call(s32[3]{0:T(128)S(1)} %pad_add_fusion.place, f32[4,256,768]{2,1,0:T(8,128)S(1)} %shard_map.91.own_ref, bf16[4,256,768]{2,1,0:T(8,128)(2,1)S(1)} %collective-permute-done.22.got_ref), custom_call_target="tpu_custom_call" | custom-call | tf_op jit(solution)/shard_map/pallas_call | solution.py:74
  (63 shorter events, 21.3 us)
Async XLA Ops:
  0.6 4.4 %copy-start.2 = (bf16[1024,768]{1,0:T(8,128)(2,1)S(1)}, bf16[1024,768]{1,0:T(8,128)(2,1)}, u32[]{:S(2)}) copy-start(bf16[1024,768]{1,0:T(8,128)(2,1)} %param.4) | copy-start | bytes 4718596
  1.8 12.1 %collective-permute-start = (bf16[2,4,64,256]{3,2,1,0:T(8,128)(2,1)S(1)}, bf16[2,4,64,256]{3,2,1,0:T(8,128)(2,1)S(1)}, u32[]{:S(2)}, u32[]{:S(2)}) collective-permute-start(bf16[2,4,64,256]{3,2,1,0:T(8,128)(2,1)S(1)} %pad_maximum_fusion.1), channel_id=1, source_target_pairs={{0,2},{1,3},{2,0},{3,1},{4,6},{5,7},{6,4},{7,5},{8,10},{9,11},{10,... | collective-permute-start | bytes 786440 | tf_op jit(solution)/shard_map/ppermute | solution.py:357
  3.4 1.7 %copy-start.1 = (bf16[1024,768]{1,0:T(8,128)(2,1)S(1)}, bf16[1024,768]{1,0:T(8,128)(2,1)}, u32[]{:S(2)}) copy-start(bf16[1024,768]{1,0:T(8,128)(2,1)} %param.5) | copy-start | bytes 4718596
  3.4 10.5 %collective-permute-start.1 = (bf16[2,4,64,256]{3,2,1,0:T(8,128)(2,1)S(1)}, bf16[2,4,64,256]{3,2,1,0:T(8,128)(2,1)S(1)}, u32[]{:S(2)}, u32[]{:S(2)}) collective-permute-start(bf16[2,4,64,256]{3,2,1,0:T(8,128)(2,1)S(1)} %pad_maximum_fusion.2), channel_id=1, source_target_pairs={{0,1},{1,0},{2,3},{3,2},{4,5},{5,4},{6,7},{7,6},{8,9},{9,8},{10,11... | collective-permute-start | bytes 786440 | tf_op jit(solution)/shard_map/ppermute | solution.py:357
  5.1 3.0 %copy-start.3 = (bf16[4,256,1024]{2,1,0:T(8,128)(2,1)S(1)}, bf16[4,256,1024]{2,1,0:T(8,128)(2,1)}, u32[]{:S(2)}) copy-start(bf16[4,256,1024]{2,1,0:T(8,128)(2,1)} %refs_1_.5) | copy-start | bytes 6291460
  5.2 22.7 %collective-permute-start.3 = (bf16[2,256,768]{2,1,0:T(8,128)(2,1)S(1)}, bf16[2,256,768]{2,1,0:T(8,128)(2,1)S(1)}, u32[]{:S(2)}, u32[]{:S(2)}) collective-permute-start(bf16[2,256,768]{2,1,0:T(8,128)(2,1)S(1)} %bitcast.45), channel_id=1, source_target_pairs={{0,2},{1,3},{2,0},{3,1},{4,6},{5,7},{6,4},{7,5},{8,10},{9,11},{10,... | collective-permute-start | bytes 2359304 | tf_op jit(solution)/shard_map/ppermute | solution.py:357
  6.8 22.8 %collective-permute-start.4 = (bf16[2,256,768]{2,1,0:T(8,128)(2,1)S(1)}, bf16[2,256,768]{2,1,0:T(8,128)(2,1)S(1)}, u32[]{:S(2)}, u32[]{:S(2)}) collective-permute-start(bf16[2,256,768]{2,1,0:T(8,128)(2,1)S(1)} %bitcast.44), channel_id=1, source_target_pairs={{0,1},{1,0},{2,3},{3,2},{4,5},{5,4},{6,7},{7,6},{8,9},{9,8},{10,11... | collective-permute-start | bytes 2359304 | tf_op jit(solution)/shard_map/ppermute | solution.py:357
  8.1 8.2 %copy-start = (bf16[4,1024,256]{2,1,0:T(8,128)(2,1)S(1)}, bf16[4,1024,256]{2,1,0:T(8,128)(2,1)}, u32[]{:S(2)}) copy-start(bf16[4,1024,256]{2,1,0:T(8,128)(2,1)} %refs_2_.1) | copy-start | bytes 6291460
  14.0 12.9 %collective-permute-start.2 = (bf16[2,2,4,64,256]{4,3,2,1,0:T(8,128)(2,1)S(1)}, bf16[2,2,4,64,256]{4,3,2,1,0:T(8,128)(2,1)S(1)}, u32[]{:S(2)}, u32[]{:S(2)}) collective-permute-start(bf16[2,2,4,64,256]{4,3,2,1,0:T(8,128)(2,1)S(1)} %pad_maximum_fusion.refs_0_), channel_id=1, source_target_pairs={{0,8},{4,12},{8,0},{12,4},{16,24},{20,28},{24,16},{28,20},{1,9},{5... | collective-permute-start | bytes 1572872 | tf_op jit(solution)/shard_map/ppermute | solution.py:360
  14.5 29.1 %collective-permute-start.12 = (bf16[2,256,768]{2,1,0:T(8,128)(2,1)S(1)}, bf16[2,256,768]{2,1,0:T(8,128)(2,1)S(1)}, u32[]{:S(2)}, u32[]{:S(2)}) collective-permute-start(bf16[2,256,768]{2,1,0:T(8,128)(2,1)S(1)} %bitcast.43), channel_id=1, source_target_pairs={{0,2},{1,3},{2,0},{3,1},{4,6},{5,7},{6,4},{7,5},{8,10},{9,11},{10,... | collective-permute-start | bytes 2359304 | tf_op jit(solution)/shard_map/ppermute | solution.py:357
  15.0 31.7 %collective-permute-start.6 = (bf16[2,256,768]{2,1,0:T(8,128)(2,1)S(1)}, bf16[2,256,768]{2,1,0:T(8,128)(2,1)S(1)}, u32[]{:S(2)}, u32[]{:S(2)}) collective-permute-start(bf16[2,256,768]{2,1,0:T(8,128)(2,1)S(1)} %bitcast.42), channel_id=1, source_target_pairs={{0,1},{1,0},{2,3},{3,2},{4,5},{5,4},{6,7},{7,6},{8,9},{9,8},{10,11... | collective-permute-start | bytes 2359304 | tf_op jit(solution)/shard_map/ppermute | solution.py:357
  29.6 1.9 %collective-permute-start.5 = (bf16[2,4,128,256]{3,2,1,0:T(8,128)(2,1)S(1)}, bf16[2,4,128,256]{3,2,1,0:T(8,128)(2,1)S(1)}, u32[]{:S(2)}, u32[]{:S(2)}) collective-permute-start(bf16[2,4,128,256]{3,2,1,0:T(8,128)(2,1)S(1)} %get-tuple-element.90), channel_id=1, source_target_pairs={{0,4},{4,0},{8,12},{12,8},{16,20},{20,16},{24,28},{28,24},{1,5},{5... | collective-permute-start | bytes 1572872 | tf_op jit(solution)/shard_map/ppermute | solution.py:363
  29.6 2.7 %collective-permute-start.9 = (bf16[2,2,4,64,256]{4,3,2,1,0:T(8,128)(2,1)S(1)}, bf16[2,2,4,64,256]{4,3,2,1,0:T(8,128)(2,1)S(1)}, u32[]{:S(2)}, u32[]{:S(2)}) collective-permute-start(bf16[2,2,4,64,256]{4,3,2,1,0:T(8,128)(2,1)S(1)} %pad_maximum_fusion.refs_0_), channel_id=1, source_target_pairs={{0,4},{4,0},{8,12},{12,8},{16,20},{20,16},{24,28},{28,24},{1,5},{5... | collective-permute-start | bytes 1572872 | tf_op jit(solution)/shard_map/ppermute | solution.py:363
  30.1 4.1 %collective-permute-start.10 = (bf16[2,2,4,64,256]{4,3,2,1,0:T(8,128)(2,1)S(1)}, bf16[2,2,4,64,256]{4,3,2,1,0:T(8,128)(2,1)S(1)}, u32[]{:S(2)}, u32[]{:S(2)}) collective-permute-start(bf16[2,2,4,64,256]{4,3,2,1,0:T(8,128)(2,1)S(1)} %collective-permute-done.2.refs_1_), channel_id=1, source_target_pairs={{0,4},{4,0},{8,12},{12,8},{16,20},{20,16},{24,28},{28,24},{1,5},{5... | collective-permute-start | bytes 1572872 | tf_op jit(solution)/shard_map/ppermute | solution.py:363
  32.1 6.8 %collective-permute-start.8 = (bf16[1,128,256]{2,1,0:T(8,128)(2,1)S(1)}, bf16[1,128,256]{2,1,0:T(8,128)(2,1)S(1)}, u32[]{:S(2)}, u32[]{:S(2)}) collective-permute-start(bf16[1,128,256]{2,1,0:T(8,128)(2,1)S(1)} %get-tuple-element.94), channel_id=1, source_target_pairs={{0,8},{4,12},{8,0},{12,4},{16,24},{20,28},{24,16},{28,20},{1,9},{5... | collective-permute-start | bytes 196616 | tf_op jit(solution)/shard_map/ppermute | solution.py:360
  32.2 6.7 %collective-permute-start.7 = (bf16[1,128,256]{2,1,0:T(8,128)(2,1)S(1)}, bf16[1,128,256]{2,1,0:T(8,128)(2,1)S(1)}, u32[]{:S(2)}, u32[]{:S(2)}) collective-permute-start(bf16[1,128,256]{2,1,0:T(8,128)(2,1)S(1)} %get-tuple-element.93), channel_id=1, source_target_pairs={{0,8},{4,12},{8,0},{12,4},{16,24},{20,28},{24,16},{28,20},{1,9},{5... | collective-permute-start | bytes 196616 | tf_op jit(solution)/shard_map/ppermute | solution.py:360
  39.5 7.2 %collective-permute-start.11 = (bf16[1,128,256]{2,1,0:T(8,128)(2,1)S(1)}, bf16[1,128,256]{2,1,0:T(8,128)(2,1)S(1)}, u32[]{:S(2)}, u32[]{:S(2)}) collective-permute-start(bf16[1,128,256]{2,1,0:T(8,128)(2,1)S(1)} %shard_map.82), channel_id=1, source_target_pairs={{0,16},{4,20},{8,24},{12,28},{16,0},{20,4},{24,8},{28,12},{1,17},{... | collective-permute-start | bytes 196616 | tf_op jit(solution)/shard_map/ppermute | solution.py:360
  48.8 3.7 %collective-permute-start.14 = (bf16[2,4,128,256]{3,2,1,0:T(8,128)(2,1)S(1)}, bf16[2,4,128,256]{3,2,1,0:T(8,128)(2,1)S(1)}, u32[]{:S(2)}, u32[]{:S(2)}) collective-permute-start(bf16[2,4,128,256]{3,2,1,0:T(8,128)(2,1)S(1)} %get-tuple-element.109), channel_id=1, source_target_pairs={{0,4},{4,0},{8,12},{12,8},{16,20},{20,16},{24,28},{28,24},{1,5},{5... | collective-permute-start | bytes 1572872 | tf_op jit(solution)/shard_map/ppermute | solution.py:363
  48.9 3.6 %collective-permute-start.13 = (bf16[4,128,256]{2,1,0:T(8,128)(2,1)S(1)}, bf16[4,128,256]{2,1,0:T(8,128)(2,1)S(1)}, u32[]{:S(2)}, u32[]{:S(2)}) collective-permute-start(bf16[4,128,256]{2,1,0:T(8,128)(2,1)S(1)} %get-tuple-element.108), channel_id=1, source_target_pairs={{0,4},{4,0},{8,12},{12,8},{16,20},{20,16},{24,28},{28,24},{1,5},{5... | collective-permute-start | bytes 786440 | tf_op jit(solution)/shard_map/ppermute | solution.py:363
  50.9 38.8 %collective-permute-start.18 = (bf16[4,256,768]{2,1,0:T(8,128)(2,1)S(1)}, bf16[4,256,768]{2,1,0:T(8,128)(2,1)S(1)}, u32[]{:S(2)}, u32[]{:S(2)}) collective-permute-start(bf16[4,256,768]{2,1,0:T(8,128)(2,1)S(1)} %shard_map.85), channel_id=1, source_target_pairs={{0,1},{1,0},{2,3},{3,2},{4,5},{5,4},{6,7},{7,6},{8,9},{9,8},{10,11... | collective-permute-start | bytes 4718600 | tf_op jit(solution)/shard_map/ppermute | solution.py:357
  53.5 8.1 %collective-permute-start.15 = (bf16[4,128,256]{2,1,0:T(8,128)(2,1)S(1)}, bf16[4,128,256]{2,1,0:T(8,128)(2,1)S(1)}, u32[]{:S(2)}, u32[]{:S(2)}) collective-permute-start(bf16[4,128,256]{2,1,0:T(8,128)(2,1)S(1)} %get-tuple-element.114), channel_id=1, source_target_pairs={{0,8},{4,12},{8,0},{12,4},{16,24},{20,28},{24,16},{28,20},{1,9},{5... | collective-permute-start | bytes 786440 | tf_op jit(solution)/shard_map/ppermute | solution.py:360
  56.5 43.5 %collective-permute-start.22 = (bf16[4,256,768]{2,1,0:T(8,128)(2,1)S(1)}, bf16[4,256,768]{2,1,0:T(8,128)(2,1)S(1)}, u32[]{:S(2)}, u32[]{:S(2)}) collective-permute-start(bf16[4,256,768]{2,1,0:T(8,128)(2,1)S(1)} %get-tuple-element.119), channel_id=1, source_target_pairs={{0,2},{1,3},{2,0},{3,1},{4,6},{5,7},{6,4},{7,5},{8,10},{9,11},{10,... | collective-permute-start | bytes 4718600 | tf_op jit(solution)/shard_map/ppermute | solution.py:357
  61.5 1.7 %collective-permute-start.16 = (bf16[3,4,64,256]{3,2,1,0:T(8,128)(2,1)S(1)}, bf16[3,4,64,256]{3,2,1,0:T(8,128)(2,1)S(1)}, u32[]{:S(2)}, u32[]{:S(2)}) collective-permute-start(bf16[3,4,64,256]{3,2,1,0:T(8,128)(2,1)S(1)} %get-tuple-element.128), channel_id=1, source_target_pairs={{0,4},{4,0},{8,12},{12,8},{16,20},{20,16},{24,28},{28,24},{1,5},{5... | collective-permute-start | bytes 1179656 | tf_op jit(solution)/shard_map/ppermute | solution.py:363
  61.5 2.3 %collective-permute-start.17 = (bf16[3,4,64,256]{3,2,1,0:T(8,128)(2,1)S(1)}, bf16[3,4,64,256]{3,2,1,0:T(8,128)(2,1)S(1)}, u32[]{:S(2)}, u32[]{:S(2)}) collective-permute-start(bf16[3,4,64,256]{3,2,1,0:T(8,128)(2,1)S(1)} %get-tuple-element.129), channel_id=1, source_target_pairs={{0,4},{4,0},{8,12},{12,8},{16,20},{20,16},{24,28},{28,24},{1,5},{5... | collective-permute-start | bytes 1179656 | tf_op jit(solution)/shard_map/ppermute | solution.py:363
  65.2 22.0 %collective-permute-start.19 = (bf16[4,128,256]{2,1,0:T(8,128)(2,1)S(1)}, bf16[4,128,256]{2,1,0:T(8,128)(2,1)S(1)}, u32[]{:S(2)}, u32[]{:S(2)}) collective-permute-start(bf16[4,128,256]{2,1,0:T(8,128)(2,1)S(1)} %shard_map.90), channel_id=1, source_target_pairs={{0,16},{4,20},{8,24},{12,28},{16,0},{20,4},{24,8},{28,12},{1,17},{... | collective-permute-start | bytes 786440 | tf_op jit(solution)/shard_map/ppermute | solution.py:360
  67.8 11.8 %collective-permute-start.21 = (bf16[3,128,256]{2,1,0:T(8,128)(2,1)S(1)}, bf16[3,128,256]{2,1,0:T(8,128)(2,1)S(1)}, u32[]{:S(2)}, u32[]{:S(2)}) collective-permute-start(bf16[3,128,256]{2,1,0:T(8,128)(2,1)S(1)} %get-tuple-element.137), channel_id=1, source_target_pairs={{0,8},{4,12},{8,0},{12,4},{16,24},{20,28},{24,16},{28,20},{1,9},{5... | collective-permute-start | bytes 589832 | tf_op jit(solution)/shard_map/ppermute | solution.py:360
  68.3 17.0 %collective-permute-start.20 = (bf16[4,128,256]{2,1,0:T(8,128)(2,1)S(1)}, bf16[4,128,256]{2,1,0:T(8,128)(2,1)S(1)}, u32[]{:S(2)}, u32[]{:S(2)}) collective-permute-start(bf16[4,128,256]{2,1,0:T(8,128)(2,1)S(1)} %get-tuple-element.135), channel_id=1, source_target_pairs={{0,8},{4,12},{8,0},{12,4},{16,24},{20,28},{24,16},{28,20},{1,9},{5... | collective-permute-start | bytes 786440 | tf_op jit(solution)/shard_map/ppermute | solution.py:360
  80.2 11.4 %collective-permute-start.23 = (bf16[3,128,256]{2,1,0:T(8,128)(2,1)S(1)}, bf16[3,128,256]{2,1,0:T(8,128)(2,1)S(1)}, u32[]{:S(2)}, u32[]{:S(2)}) collective-permute-start(bf16[3,128,256]{2,1,0:T(8,128)(2,1)S(1)} %get-tuple-element.144), channel_id=1, source_target_pairs={{0,8},{4,12},{8,0},{12,4},{16,24},{20,28},{24,16},{28,20},{1,9},{5... | collective-permute-start | bytes 589832 | tf_op jit(solution)/shard_map/ppermute | solution.py:360
  85.3 8.8 %collective-permute-start.24 = (bf16[3,128,256]{2,1,0:T(8,128)(2,1)S(1)}, bf16[3,128,256]{2,1,0:T(8,128)(2,1)S(1)}, u32[]{:S(2)}, u32[]{:S(2)}) collective-permute-start(bf16[3,128,256]{2,1,0:T(8,128)(2,1)S(1)} %shard_map.93), channel_id=1, source_target_pairs={{0,16},{4,20},{8,24},{12,28},{16,0},{20,4},{24,8},{28,12},{1,17},{... | collective-permute-start | bytes 589832 | tf_op jit(solution)/shard_map/ppermute | solution.py:360
  87.8 10.7 %collective-permute-start.25 = (bf16[4,128,256]{2,1,0:T(8,128)(2,1)S(1)}, bf16[4,128,256]{2,1,0:T(8,128)(2,1)S(1)}, u32[]{:S(2)}, u32[]{:S(2)}) collective-permute-start(bf16[4,128,256]{2,1,0:T(8,128)(2,1)S(1)} %shard_map.94), channel_id=1, source_target_pairs={{0,0},{1,8},{2,2},{3,10},{4,4},{5,12},{6,6},{7,14},{8,1},{9,9},{10... | collective-permute-start | bytes 786440 | tf_op jit(solution)/shard_map/ppermute | solution.py:660
  94.7 7.3 %collective-permute-start.26 = (bf16[2,128,256]{2,1,0:T(8,128)(2,1)S(1)}, bf16[2,128,256]{2,1,0:T(8,128)(2,1)S(1)}, u32[]{:S(2)}, u32[]{:S(2)}) collective-permute-start(bf16[2,128,256]{2,1,0:T(8,128)(2,1)S(1)} %get-tuple-element.148), channel_id=1, source_target_pairs={{0,2},{1,3},{2,0},{3,1},{4,6},{5,7},{6,4},{7,5},{8,10},{9,11},{10,... | collective-permute-start | bytes 393224 | tf_op jit(solution)/shard_map/ppermute | solution.py:357

commit v6 on v5

--- a/solution.py
+++ b/solution.py
@@ -268,26 +268,28 @@
     out_ref[...] = (own_ref[...] + got_ref[...].astype(F32)).astype(BF16)
 
 
-def down_meet_body(place, first, first_got, keep_ref, got_own, got_near, far_ref, near_ref, mine_ref):
-    stay_j = (place[0] ^ place[1]) & 1
-    stay_i = (place[0] // 2) ^ (place[1] // 2)
+def down_meet_body(place, first, first_got, keep_ref, got_own, got_near, send_ref, mine_ref):
+    stay = (place[0] ^ place[1]) & 1
     kept = ((first.at[1], keep_ref.at[0]), (keep_ref.at[1], keep_ref.at[2]))
     got = ((first_got.at[1], got_own), (got_near.at[0], got_near.at[1]))
-    for i in range(2):
-        for j in range(2):
-
-            @pl.when(jnp.logical_and(stay_i == i, stay_j == j))
-            def _():
-                total = lambda a, b: kept[a][b][...].astype(F32) + got[a][b][...].astype(F32)
-                far_ref[...] = total(1 - i, 1 - j).astype(BF16)
-                near_ref[...] = total(i, 1 - j).astype(BF16)
-                mine_ref[0] = total(i, j)
-                mine_ref[1] = total(1 - i, j)
-
-
-def down_sum_body(factor, place, mine_ref, near_ref, got_ref, out_ref):
-    total = mine_ref[0] + near_ref[...].astype(F32) + got_ref[...].astype(F32)
-    out_ref[...] = (total * factor).astype(BF16)
+    for j in range(2):
+
+        @pl.when(stay == j)
+        def _():
+            for i in range(2):
+                total = lambda b: kept[i][b][...].astype(F32) + got[i][b][...].astype(F32)
+                mine_ref[i] = total(j)
+                send_ref[i] = total(1 - j).astype(BF16)
+
+
+def down_again_body(place, mine_ref, got_ref, send_ref, own_ref):
+    stay = (place[0] // 2) ^ (place[1] // 2)
+    own_ref[...] = mine_ref[stay] + got_ref[stay].astype(F32)
+    send_ref[...] = (mine_ref[1 - stay] + got_ref[1 - stay].astype(F32)).astype(BF16)
+
+
+def down_sum_body(factor, place, own_ref, got_ref, out_ref):
+    out_ref[...] = ((own_ref[...] + got_ref[...].astype(F32)) * factor).astype(BF16)
 
 
 def up_meet_body(parts, place, keep_ref, *refs):
@@ -567,16 +569,16 @@
     got_out = send(near_out, 1)
     core_own, core_near = after((core_own, core_near), near_out)
     parts_d = (keep_e, first_got, keep_d, core_own, core_near)
-    far_d, near_d, mine_d = call(
+    send_d, mine_d = call(
         down_meet_body,
         place,
         (1,),
         [whole(v) for v in parts_d],
-        [whole_out(shard[2:], BF16)] * 2 + [whole_out(shard[1:], F32)],
+        [whole_out(shard[1:], BF16), whole_out(shard[1:], F32)],
         16,
     )
-    got_far = send_z(far_d, 1)
-    cot_b, *near_b = after((cot, cot_lo, cot_hi), far_d)
+    got_d = send_z(send_d, 1)
+    cot_b, *near_b = after((cot, cot_lo, cot_hi), send_d)
     late = [(1, 0, gate), (1, 1, gate_lo), (1, 2, gate_hi), (0, 2, gate_hi)]
     at_lo = lambda i, p: (0, least(i, half - 1), 0, 0)
     at_hi = lambda i, p: (0, most(i - half, 0), 0, 0)
@@ -610,15 +612,19 @@
         [lambda i: least(i, half - 1), lambda i: most(i - half, 0)],
         16.0,
     )
-    give_lo, give_hi = after((give_lo, give_hi), got_far)
-    gots_u = [send_core(give_lo), send_core(give_hi)]
-    send_u, far_u, mine_u = up_meet(3, keep_u, gots_u)
-    far_u = send_z(far_u, 1)
-
-    got_far = after((got_far,), send_u)[0]
-    send_d = up_again(mine_d, got_far)
-    last_d = send_z(send_d, 2)
-    got_near_d = send_z(after((near_d,), send_d)[0], 1)
+    send_u, far_u, mine_u = up_meet(3, keep_u, [send_core(give_lo), send_core(give_hi)])
+    got_u, far_u = send_z(send_u, 1), send_z(far_u, 1)
+
+    got_d = after((got_d,), send_u)[0]
+    send_d, mine_d = call(
+        down_again_body,
+        place,
+        (1,),
+        [whole(mine_d), whole(got_d)],
+        [whole_out(shard[2:], BF16), whole_out(shard[2:], F32)],
+        16,
+    )
+    got_d = send_z(send_d, 2)
 
     up_b = after((up_blocks,), send_d)[0]
     own_grads = call_once(
@@ -638,16 +644,15 @@
 
     own_out = outputs_of(0, after((hid,), own_grads)[0], F32)
     far_u = after((far_u,), own_out)[0]
-    next_u = up_again(mine_u, far_u)
-    last_u = send_z(next_u, 2)
-    got_u = send_z(after((send_u,), next_u)[0], 1)
-
-    last_d, got_near_d = after((last_d, got_near_d), next_u)
+    send_u = up_again(mine_u, far_u)
+    last_u = send_z(send_u, 2)
+
+    got_d = after((got_d,), send_u)[0]
     sum_d = call(
         functools.partial(down_sum_body, factor),
         place,
         (1,),
-        [whole(v) for v in (mine_d, got_near_d, last_d)],
+        [whole(mine_d), whole(got_d)],
         [whole_out(shard[2:], BF16)],
         8,
     )[0]

time: 105 us -> 103 us (0.981)
  waiting for transfers between devices: 35 us -> 31.8 us
  starting transfers between devices: 25.2 us -> 27 us
    ppermute x10 -> x9, waiting for transfers between devices: 24.3 us -> 19.8 us  [send_z(): return lax.ppermute(value, 'dp', [(d, d ^ 2 * hop) for d in range(n_dp)])]
    ppermute x10 -> x9, starting transfers between devices: 12.3 us -> 14.6 us  [send_z(): return lax.ppermute(value, 'dp', [(d, d ^ 2 * hop) for d in range(n_dp)])]
    ppermute x1, waiting for transfers between devices: 3.27 us -> 4.57 us  [square_device(): home_d = lax.ppermute(sum_d, ('dp', 'tensor'), swaps)]
  transfers between devices with their start and end apart: 27 -> 26, of which waited for: 13 -> 12; matrix products, arithmetic and copies ran while one was open for 1% -> 1% of each run, Pallas kernels for 35% -> 36%
where the time goes in v6:
time: 103 us; the launch traced here: 102 us
  Pallas kernels  39.6 us (38%)
  waiting for transfers between devices  31.8 us (31%)
  starting transfers between devices  27 us (26%)
  local copies, waits for them, and re-layouts  2.33 us (2%)
    pallas_call x25, Pallas kernels, call(): pl.pallas_call(body, grid_spec=pltpu.PrefetchScalarGridSpec(num_scalar_pr...  39.6 us
    ppermute x9, waiting for transfers between devices, send_z(): return lax.ppermute(value, 'dp', [(d, d ^ 2 * hop) for d in range(n_dp)])  19.8 us
    ppermute x9, starting transfers between devices, send_z(): return lax.ppermute(value, 'dp', [(d, d ^ 2 * hop) for d in range(n_dp)])  14.6 us
    ppermute x9, starting transfers between devices, send(): lax.ppermute(value, 'tensor', [(t, t ^ hop) for t in range(n_tensor)])  8.9 us
    ppermute x1, waiting for transfers between devices, square_device(): home_d = lax.ppermute(sum_d, ('dp', 'tensor'), swaps)  4.57 us
    ppermute x9, waiting for transfers between devices, send(): lax.ppermute(value, 'tensor', [(t, t ^ hop) for t in range(n_tensor)])  4.18 us
    ppermute x7, waiting for transfers between devices, send_core(): return lax.ppermute(value, 'dp', [(d, d ^ 1) for d in range(n_dp)])  3.24 us
  transfers between devices with their start and end apart: 26, of which 12 were waited for; matrix products, arithmetic and copies ran while one was open for 1% of the time, Pallas kernels for 36%

profile of v6, /device:TPU:12, one launch (start us, length us, event | category | flops | bytes accessed | tf_op | source)
XLA Modules:
  0.0 101.9 jit_solution(10836374109516049853)
XLA Ops:
  3.4 1.6 %collective-permute-start.1 = (bf16[2,4,64,256]{3,2,1,0:T(8,128)(2,1)S(1)}, bf16[2,4,64,256]{3,2,1,0:T(8,128)(2,1)S(1)}, u32[]{:S(2)}, u32[]{:S(2)}) collective-permute-start(bf16[2,4,64,256]{3,2,1,0:T(8,128)(2,1)S(1)} %pad_maximum_fusion.2), channel_id=1, source_target_pairs={{0,1},{1,0},{2,3},{3,2},{4,5},{5,4},{6,7},{7,6},{8,9},{9,8},{10,11... | collective-permute-start | bytes 786440 | tf_op jit(solution)/shard_map/ppermute | solution.py:359
  5.2 1.6 %collective-permute-start.3 = (bf16[2,256,768]{2,1,0:T(8,128)(2,1)S(1)}, bf16[2,256,768]{2,1,0:T(8,128)(2,1)S(1)}, u32[]{:S(2)}, u32[]{:S(2)}) collective-permute-start(bf16[2,256,768]{2,1,0:T(8,128)(2,1)S(1)} %bitcast.45), channel_id=1, source_target_pairs={{0,2},{1,3},{2,0},{3,1},{4,6},{5,7},{6,4},{7,5},{8,10},{9,11},{10,... | collective-permute-start | bytes 2359304 | tf_op jit(solution)/shard_map/ppermute | solution.py:359
  8.1 5.8 %shard_map.75 = (bf16[2,4,4,64,768]{4,3,2,1,0:T(8,128)(2,1)S(1)}, bf16[2,4,4,64,768]{4,3,2,1,0:T(8,128)(2,1)S(1)}) custom-call(s32[3]{0:T(128)S(1)} %pad_add_fusion.place, bf16[4,256,768]{2,1,0:T(8,128)(2,1)S(1)} %bitcast.37, bf16[4,256,1024]{2,1,0:T(8,128)(2,1)S(1)} %copy-done.3), custom_call_target="tpu_custom_call" | custom-call | tf_op jit(solution)/shard_map/pallas_call | solution.py:74
  15.0 1.3 %collective-permute-start.6 = (bf16[2,256,768]{2,1,0:T(8,128)(2,1)S(1)}, bf16[2,256,768]{2,1,0:T(8,128)(2,1)S(1)}, u32[]{:S(2)}, u32[]{:S(2)}) collective-permute-start(bf16[2,256,768]{2,1,0:T(8,128)(2,1)S(1)} %bitcast.42), channel_id=1, source_target_pairs={{0,1},{1,0},{2,3},{3,2},{4,5},{5,4},{6,7},{7,6},{8,9},{9,8},{10,11... | collective-permute-start | bytes 2359304 | tf_op jit(solution)/shard_map/ppermute | solution.py:359
  17.4 1.6 %shard_map.77 = (bf16[2,4,128,256]{3,2,1,0:T(8,128)(2,1)S(1)}, bf16[2,4,128,256]{3,2,1,0:T(8,128)(2,1)S(1)}) custom-call(s32[3]{0:T(128)S(1)} %pad_add_fusion.place, bf16[4,256,768]{2,1,0:T(8,128)(2,1)S(1)} %bitcast.33, bf16[2,4,4,64,768]{4,3,2,1,0:T(8,128)(2,1)S(1)} %get-tuple-element.128.refs_1_.refs_3_, bf16[4,256,768]{2,1,0:T(8,128)(2,1)S(1)} %bitcast.38, ...), custom_call_target="tpu_custom_call" | custom-call | tf_op jit(solution)/shard_map/pallas_call | solution.py:74
  19.0 7.9 %collective-permute-done.2.refs_1_ = bf16[2,2,4,64,256]{4,3,2,1,0:T(8,128)(2,1)S(1)} collective-permute-done((bf16[2,2,4,64,256]{4,3,2,1,0:T(8,128)(2,1)S(1)}, bf16[2,2,4,64,256]{4,3,2,1,0:T(8,128)(2,1)S(1)}, u32[]{:S(2)}, u32[]{:S(2)}) %collective-permute-start.2) | collective-permute-done | bytes 524320 | tf_op jit(solution)/shard_map/ppermute | solution.py:362
  27.9 1.6 %collective-permute-done.4.refs_1_ = bf16[2,256,768]{2,1,0:T(8,128)(2,1)S(1)} collective-permute-done((bf16[2,256,768]{2,1,0:T(8,128)(2,1)S(1)}, bf16[2,256,768]{2,1,0:T(8,128)(2,1)S(1)}, u32[]{:S(2)}, u32[]{:S(2)}) %collective-permute-start.4) | collective-permute-done | bytes 786464 | tf_op jit(solution)/shard_map/ppermute | solution.py:359
  30.1 1.4 %collective-permute-done.5.refs_0_.first_got = bf16[2,4,128,256]{3,2,1,0:T(8,128)(2,1)S(1)} collective-permute-done((bf16[2,4,128,256]{3,2,1,0:T(8,128)(2,1)S(1)}, bf16[2,4,128,256]{3,2,1,0:T(8,128)(2,1)S(1)}, u32[]{:S(2)}, u32[]{:S(2)}) %collective-permute-start.5) | collective-permute-done | bytes 524320 | tf_op jit(solution)/shard_map/ppermute | solution.py:365
  32.2 2.0 %collective-permute-start.7 = (bf16[1,128,256]{2,1,0:T(8,128)(2,1)S(1)}, bf16[1,128,256]{2,1,0:T(8,128)(2,1)S(1)}, u32[]{:S(2)}, u32[]{:S(2)}) collective-permute-start(bf16[1,128,256]{2,1,0:T(8,128)(2,1)S(1)} %get-tuple-element.89), channel_id=1, source_target_pairs={{0,8},{4,12},{8,0},{12,4},{16,24},{20,28},{24,16},{28,20},{1,9},{5... | collective-permute-start | bytes 196616 | tf_op jit(solution)/shard_map/ppermute | solution.py:362
  34.9 3.1 %shard_map.80 = (bf16[2,4,2,64,768]{4,3,2,1,0:T(8,128)(2,1)S(1)}, bf16[2,4,2,64,768]{4,3,2,1,0:T(8,128)(2,1)S(1)}) custom-call(s32[3]{0:T(128)S(1)} %pad_add_fusion.place, bf16[2,256,768]{2,1,0:T(8,128)(2,1)S(1)} %collective-permute-done.3.x_ref.refs_1_, bf16[2,2,4,256,256]{4,3,2,1,0:T(8,128)(2,1)S(1)} %bitcast.22), custom_call_target="tpu_custom_call" | custom-call | tf_op jit(solution)/shard_map/pallas_call | solution.py:74
  39.5 2.7 %collective-permute-start.11 = (bf16[1,128,256]{2,1,0:T(8,128)(2,1)S(1)}, bf16[1,128,256]{2,1,0:T(8,128)(2,1)S(1)}, u32[]{:S(2)}, u32[]{:S(2)}) collective-permute-start(bf16[1,128,256]{2,1,0:T(8,128)(2,1)S(1)} %shard_map.82), channel_id=1, source_target_pairs={{0,16},{4,20},{8,24},{12,28},{16,0},{20,4},{24,8},{28,12},{1,17},{... | collective-permute-start | bytes 196616 | tf_op jit(solution)/shard_map/ppermute | solution.py:362
  42.1 1.5 %collective-permute-done.12.x_ref.refs_2_ = bf16[2,256,768]{2,1,0:T(8,128)(2,1)S(1)} collective-permute-done((bf16[2,256,768]{2,1,0:T(8,128)(2,1)S(1)}, bf16[2,256,768]{2,1,0:T(8,128)(2,1)S(1)}, u32[]{:S(2)}, u32[]{:S(2)}) %collective-permute-start.12) | collective-permute-done | bytes 786464 | tf_op jit(solution)/shard_map/ppermute | solution.py:359
  43.6 3.1 %shard_map.83 = (bf16[2,4,2,64,768]{4,3,2,1,0:T(8,128)(2,1)S(1)}, bf16[2,4,2,64,768]{4,3,2,1,0:T(8,128)(2,1)S(1)}) custom-call(s32[3]{0:T(128)S(1)} %pad_add_fusion.place, bf16[2,256,768]{2,1,0:T(8,128)(2,1)S(1)} %collective-permute-done.12.x_ref.refs_2_, bf16[2,2,4,256,256]{4,3,2,1,0:T(8,128)(2,1)S(1)} %bitcast.23), custom_call_target="tpu_custom_call" | custom-call | tf_op jit(solution)/shard_map/pallas_call | solution.py:74
  46.8 2.0 %shard_map.84 = (bf16[4,128,256]{2,1,0:T(8,128)(2,1)S(1)}, bf16[2,4,128,256]{3,2,1,0:T(8,128)(2,1)S(1)}, bf16[3,4,128,256]{3,2,1,0:T(8,128)(2,1)S(1)}) custom-call(s32[3]{0:T(128)S(1)} %pad_add_fusion.place, bf16[4,256,768]{2,1,0:T(8,128)(2,1)S(1)} %bitcast.35, bf16[2,256,768]{2,1,0:T(8,128)(2,1)S(1)} %collective-permute-done.4.refs_1_, ...), custom_call_target="tpu_custom_call" | custom-call | tf_op jit(solution)/shard_map/pallas_call | solution.py:74
  49.4 1.5 %shard_map.85 = bf16[4,256,768]{2,1,0:T(8,128)(2,1)S(1)} custom-call(s32[3]{0:T(128)S(1)} %pad_add_fusion.place, bf16[2,2,4,256,256]{4,3,2,1,0:T(8,128)(2,1)S(1)} %bitcast.24, bf16[2,2,4,256,256]{4,3,2,1,0:T(8,128)(2,1)S(1)} %bitcast.25, bf16[2,2,4,256,256]{4,3,2,1,0:T(8,128)(2,1)S(1)} %bitcast.26, ...), custom_call_target="tpu_custom_call" | custom-call | tf_op jit(solution)/shard_map/pallas_call | solution.py:74
  50.9 1.6 %collective-permute-start.18 = (bf16[4,256,768]{2,1,0:T(8,128)(2,1)S(1)}, bf16[4,256,768]{2,1,0:T(8,128)(2,1)S(1)}, u32[]{:S(2)}, u32[]{:S(2)}) collective-permute-start(bf16[4,256,768]{2,1,0:T(8,128)(2,1)S(1)} %shard_map.85), channel_id=1, source_target_pairs={{0,1},{1,0},{2,3},{3,2},{4,5},{5,4},{6,7},{7,6},{8,9},{9,8},{10,11... | collective-permute-start | bytes 4718600 | tf_op jit(solution)/shard_map/ppermute | solution.py:359
  54.0 2.6 %shard_map.87 = (bf16[4,4,64,768]{3,2,1,0:T(8,128)(2,1)S(1)}, bf16[4,2,64,768]{3,2,1,0:T(8,128)(2,1)S(1)}, bf16[4,2,64,768]{3,2,1,0:T(8,128)(2,1)S(1)}, bf16[4,2...) custom-call(s32[3]{0:T(128)S(1)} %pad_add_fusion.place, bf16[4,256,768]{2,1,0:T(8,128)(2,1)S(1)} %bitcast.36, ...), custom_call_target="tpu_custom_call" | custom-call | tf_op jit(solution)/shard_map/pallas_call | solution.py:74
  57.1 2.1 %shard_map.88 = (bf16[3,4,64,256]{3,2,1,0:T(8,128)(2,1)S(1)}, bf16[3,4,64,256]{3,2,1,0:T(8,128)(2,1)S(1)}, bf16[3,4,128,256]{3,2,1,0:T(8,128)(2,1)S(1)}) custom-call(s32[3]{0:T(128)S(1)} %pad_add_fusion.place, bf16[4,256,768]{2,1,0:T(8,128)(2,1)S(1)} %bitcast.39, bf16[2,256,768]{2,1,0:T(8,128)(2,1)S(1)} %collective-permute-done.3.x_ref.refs_1_, ...), custom_call_target="tpu_custom_call" | custom-call | flops 16000000000 | tf_op jit(solution)/shard_map/pallas_call | solution.py:74
  59.8 1.2 %collective-permute-done.16.refs_0_ = bf16[3,4,64,256]{3,2,1,0:T(8,128)(2,1)S(1)} collective-permute-done((bf16[3,4,64,256]{3,2,1,0:T(8,128)(2,1)S(1)}, bf16[3,4,64,256]{3,2,1,0:T(8,128)(2,1)S(1)}, u32[]{:S(2)}, u32[]{:S(2)}) %collective-permute-start.16) | collective-permute-done | bytes 393248 | tf_op jit(solution)/shard_map/ppermute | solution.py:365
  62.3 1.6 %collective-permute-start.20 = (bf16[3,128,256]{2,1,0:T(8,128)(2,1)S(1)}, bf16[3,128,256]{2,1,0:T(8,128)(2,1)S(1)}, u32[]{:S(2)}, u32[]{:S(2)}) collective-permute-start(bf16[3,128,256]{2,1,0:T(8,128)(2,1)S(1)} %get-tuple-element.131), channel_id=1, source_target_pairs={{0,8},{4,12},{8,0},{12,4},{16,24},{20,28},{24,16},{28,20},{1,9},{5... | collective-permute-start | bytes 589832 | tf_op jit(solution)/shard_map/ppermute | solution.py:362
  64.3 4.0 %collective-permute-done.15.got_ref = bf16[2,4,128,256]{3,2,1,0:T(8,128)(2,1)S(1)} collective-permute-done((bf16[2,4,128,256]{3,2,1,0:T(8,128)(2,1)S(1)}, bf16[2,4,128,256]{3,2,1,0:T(8,128)(2,1)S(1)}, u32[]{:S(2)}, u32[]{:S(2)}) %collective-permute-start.15) | collective-permute-done | bytes 524320 | tf_op jit(solution)/shard_map/ppermute | solution.py:362
  69.0 2.6 %collective-permute-start.19 = (bf16[4,128,256]{2,1,0:T(8,128)(2,1)S(1)}, bf16[4,128,256]{2,1,0:T(8,128)(2,1)S(1)}, u32[]{:S(2)}, u32[]{:S(2)}) collective-permute-start(bf16[4,128,256]{2,1,0:T(8,128)(2,1)S(1)} %get-tuple-element.126), channel_id=1, source_target_pairs={{0,16},{4,20},{8,24},{12,28},{16,0},{20,4},{24,8},{28,12},{1,17},{... | collective-permute-start | bytes 786440 | tf_op jit(solution)/shard_map/ppermute | solution.py:362
  71.6 1.5 %shard_map.91.own_ref = f32[4,256,768]{2,1,0:T(8,128)S(1)} custom-call(s32[3]{0:T(128)S(1)} %pad_add_fusion.place, bf16[4,256,1024]{2,1,0:T(8,128)(2,1)S(1)} %copy-done.3, bf16[4,256,1024]{2,1,0:T(8,128)(2,1)S(1)} %copy-done.3, bf16[4,4,64,768]{3,2,1,0:T(8,128)(2,1)S(1)} %shard_map.76.refs_3_.refs_2_, bf16[4,4,64,768]{3,2,1,0:T(8,128)(2,1)S(1)} %get-tuple-element.117.refs_3_), custom_call_target="tpu_custom_call" | custom-call | flops 4000000000 | tf_op jit(solution)/shard_map/pallas_call | solution.py:74
  73.2 1.5 %shard_map.92.own_ref = f32[4,256,768]{2,1,0:T(8,128)S(1)} custom-call(s32[3]{0:T(128)S(1)} %pad_add_fusion.place, bf16[4,1024,256]{2,1,0:T(8,128)(2,1)S(1)} %copy-done, bf16[4,1024,256]{2,1,0:T(8,128)(2,1)S(1)} %copy-done, bf16[4,1024,256]{2,1,0:T(8,128)(2,1)S(1)} %copy-done, bf16[2,4,4,64,768]{4,3,2,1,0:T(8,128)(2,1)S(1)} %get-tuple-element.128.refs_1_.refs_3_, ...), custom_call_target="tpu_custom_call" | custom-call | tf_op jit(solution)/shard_map/pallas_call | solution.py:74
  76.4 4.1 %collective-permute-start.23 = (bf16[3,128,256]{2,1,0:T(8,128)(2,1)S(1)}, bf16[3,128,256]{2,1,0:T(8,128)(2,1)S(1)}, u32[]{:S(2)}, u32[]{:S(2)}) collective-permute-start(bf16[3,128,256]{2,1,0:T(8,128)(2,1)S(1)} %shard_map.93), channel_id=1, source_target_pairs={{0,16},{4,20},{8,24},{12,28},{16,0},{20,4},{24,8},{28,12},{1,17},{... | collective-permute-start | bytes 589832 | tf_op jit(solution)/shard_map/ppermute | solution.py:362
  80.5 6.8 %collective-permute-done.19.got_ref = bf16[4,128,256]{2,1,0:T(8,128)(2,1)S(1)} collective-permute-done((bf16[4,128,256]{2,1,0:T(8,128)(2,1)S(1)}, bf16[4,128,256]{2,1,0:T(8,128)(2,1)S(1)}, u32[]{:S(2)}, u32[]{:S(2)}) %collective-permute-start.19) | collective-permute-done | bytes 262176 | tf_op jit(solution)/shard_map/ppermute | solution.py:362
  88.0 1.9 %collective-permute-start.24 = (bf16[4,128,256]{2,1,0:T(8,128)(2,1)S(1)}, bf16[4,128,256]{2,1,0:T(8,128)(2,1)S(1)}, u32[]{:S(2)}, u32[]{:S(2)}) collective-permute-start(bf16[4,128,256]{2,1,0:T(8,128)(2,1)S(1)} %shard_map.94), channel_id=1, source_target_pairs={{0,0},{1,8},{2,2},{3,10},{4,4},{5,12},{6,6},{7,14},{8,1},{9,9},{10... | collective-permute-start | bytes 786440 | tf_op jit(solution)/shard_map/ppermute | solution.py:665
  89.9 1.9 %shard_map.95 = bf16[4,256,768]{2,1,0:T(8,128)(2,1)} custom-call(s32[3]{0:T(128)S(1)} %pad_add_fusion.place, f32[4,256,768]{2,1,0:T(8,128)S(1)} %shard_map.92.own_ref, bf16[4,256,768]{2,1,0:T(8,128)(2,1)S(1)} %collective-permute-done.18.got_ref), custom_call_target="tpu_custom_call" | custom-call | tf_op jit(solution)/shard_map/pallas_call | solution.py:74
  92.6 4.6 %collective-permute-done.24.down_in = bf16[4,128,256]{2,1,0:T(8,128)(2,1)S(1)} collective-permute-done((bf16[4,128,256]{2,1,0:T(8,128)(2,1)S(1)}, bf16[4,128,256]{2,1,0:T(8,128)(2,1)S(1)}, u32[]{:S(2)}, u32[]{:S(2)}) %collective-permute-start.24) | collective-permute-done | bytes 262176 | tf_op jit(solution)/shard_map/ppermute | solution.py:665
  97.2 1.6 %shard_map.97 = (f32[4,32,1024]{2,1,0:T(8,128)}, f32[4,128,256]{2,1,0:T(8,128)}) custom-call(s32[3]{0:T(128)S(1)} %pad_add_fusion.place, f32[2,128,256]{2,1,0:T(8,128)S(1)} %get-tuple-element.139.mine_ref, bf16[4,128,256]{2,1,0:T(8,128)(2,1)S(1)} %collective-permute-done.24.down_in), custom_call_target="tpu_custom_call" | custom-call | tf_op jit(solution)/shard_map/pallas_call | solution.py:74
  98.7 1.9 %shard_map.98 = bf16[4,256,768]{2,1,0:T(8,128)(2,1)} custom-call(s32[3]{0:T(128)S(1)} %pad_add_fusion.place, f32[4,256,768]{2,1,0:T(8,128)S(1)} %shard_map.91.own_ref, bf16[4,256,768]{2,1,0:T(8,128)(2,1)S(1)} %collective-permute-done.21.got_ref), custom_call_target="tpu_custom_call" | custom-call | tf_op jit(solution)/shard_map/pallas_call | solution.py:74
  100.7 1.3 %shard_map.99 = f32[4,32,1024]{2,1,0:T(8,128)} custom-call(s32[3]{0:T(128)S(1)} %pad_add_fusion.place, bf16[2,128,256]{2,1,0:T(8,128)(2,1)S(1)} %collective-permute-done.25.got_ref, f32[4,32,1024]{2,1,0:T(8,128)} %get-tuple-element.142.held_ref), custom_call_target="tpu_custom_call", output_to_operand_aliasing={{}: (2, {})} | custom-call | tf_op jit(solution)/shard_map/pallas_call | solution.py:74
  (61 shorter events, 19.4 us)
Async XLA Ops:
  0.6 4.4 %copy-start.2 = (bf16[1024,768]{1,0:T(8,128)(2,1)S(1)}, bf16[1024,768]{1,0:T(8,128)(2,1)}, u32[]{:S(2)}) copy-start(bf16[1024,768]{1,0:T(8,128)(2,1)} %param.4) | copy-start | bytes 4718596
  1.8 12.1 %collective-permute-start = (bf16[2,4,64,256]{3,2,1,0:T(8,128)(2,1)S(1)}, bf16[2,4,64,256]{3,2,1,0:T(8,128)(2,1)S(1)}, u32[]{:S(2)}, u32[]{:S(2)}) collective-permute-start(bf16[2,4,64,256]{3,2,1,0:T(8,128)(2,1)S(1)} %pad_maximum_fusion.1), channel_id=1, source_target_pairs={{0,2},{1,3},{2,0},{3,1},{4,6},{5,7},{6,4},{7,5},{8,10},{9,11},{10,... | collective-permute-start | bytes 786440 | tf_op jit(solution)/shard_map/ppermute | solution.py:359
  3.4 1.7 %copy-start.1 = (bf16[1024,768]{1,0:T(8,128)(2,1)S(1)}, bf16[1024,768]{1,0:T(8,128)(2,1)}, u32[]{:S(2)}) copy-start(bf16[1024,768]{1,0:T(8,128)(2,1)} %param.5) | copy-start | bytes 4718596
  3.4 10.5 %collective-permute-start.1 = (bf16[2,4,64,256]{3,2,1,0:T(8,128)(2,1)S(1)}, bf16[2,4,64,256]{3,2,1,0:T(8,128)(2,1)S(1)}, u32[]{:S(2)}, u32[]{:S(2)}) collective-permute-start(bf16[2,4,64,256]{3,2,1,0:T(8,128)(2,1)S(1)} %pad_maximum_fusion.2), channel_id=1, source_target_pairs={{0,1},{1,0},{2,3},{3,2},{4,5},{5,4},{6,7},{7,6},{8,9},{9,8},{10,11... | collective-permute-start | bytes 786440 | tf_op jit(solution)/shard_map/ppermute | solution.py:359
  5.1 3.0 %copy-start.3 = (bf16[4,256,1024]{2,1,0:T(8,128)(2,1)S(1)}, bf16[4,256,1024]{2,1,0:T(8,128)(2,1)}, u32[]{:S(2)}) copy-start(bf16[4,256,1024]{2,1,0:T(8,128)(2,1)} %refs_1_.5) | copy-start | bytes 6291460
  5.2 22.7 %collective-permute-start.3 = (bf16[2,256,768]{2,1,0:T(8,128)(2,1)S(1)}, bf16[2,256,768]{2,1,0:T(8,128)(2,1)S(1)}, u32[]{:S(2)}, u32[]{:S(2)}) collective-permute-start(bf16[2,256,768]{2,1,0:T(8,128)(2,1)S(1)} %bitcast.45), channel_id=1, source_target_pairs={{0,2},{1,3},{2,0},{3,1},{4,6},{5,7},{6,4},{7,5},{8,10},{9,11},{10,... | collective-permute-start | bytes 2359304 | tf_op jit(solution)/shard_map/ppermute | solution.py:359
  6.8 22.8 %collective-permute-start.4 = (bf16[2,256,768]{2,1,0:T(8,128)(2,1)S(1)}, bf16[2,256,768]{2,1,0:T(8,128)(2,1)S(1)}, u32[]{:S(2)}, u32[]{:S(2)}) collective-permute-start(bf16[2,256,768]{2,1,0:T(8,128)(2,1)S(1)} %bitcast.44), channel_id=1, source_target_pairs={{0,1},{1,0},{2,3},{3,2},{4,5},{5,4},{6,7},{7,6},{8,9},{9,8},{10,11... | collective-permute-start | bytes 2359304 | tf_op jit(solution)/shard_map/ppermute | solution.py:359
  8.1 8.2 %copy-start = (bf16[4,1024,256]{2,1,0:T(8,128)(2,1)S(1)}, bf16[4,1024,256]{2,1,0:T(8,128)(2,1)}, u32[]{:S(2)}) copy-start(bf16[4,1024,256]{2,1,0:T(8,128)(2,1)} %refs_2_.1) | copy-start | bytes 6291460
  14.0 12.9 %collective-permute-start.2 = (bf16[2,2,4,64,256]{4,3,2,1,0:T(8,128)(2,1)S(1)}, bf16[2,2,4,64,256]{4,3,2,1,0:T(8,128)(2,1)S(1)}, u32[]{:S(2)}, u32[]{:S(2)}) collective-permute-start(bf16[2,2,4,64,256]{4,3,2,1,0:T(8,128)(2,1)S(1)} %pad_maximum_fusion.refs_0_), channel_id=1, source_target_pairs={{0,8},{4,12},{8,0},{12,4},{16,24},{20,28},{24,16},{28,20},{1,9},{5... | collective-permute-start | bytes 1572872 | tf_op jit(solution)/shard_map/ppermute | solution.py:362
  14.5 29.1 %collective-permute-start.12 = (bf16[2,256,768]{2,1,0:T(8,128)(2,1)S(1)}, bf16[2,256,768]{2,1,0:T(8,128)(2,1)S(1)}, u32[]{:S(2)}, u32[]{:S(2)}) collective-permute-start(bf16[2,256,768]{2,1,0:T(8,128)(2,1)S(1)} %bitcast.43), channel_id=1, source_target_pairs={{0,2},{1,3},{2,0},{3,1},{4,6},{5,7},{6,4},{7,5},{8,10},{9,11},{10,... | collective-permute-start | bytes 2359304 | tf_op jit(solution)/shard_map/ppermute | solution.py:359
  15.0 31.7 %collective-permute-start.6 = (bf16[2,256,768]{2,1,0:T(8,128)(2,1)S(1)}, bf16[2,256,768]{2,1,0:T(8,128)(2,1)S(1)}, u32[]{:S(2)}, u32[]{:S(2)}) collective-permute-start(bf16[2,256,768]{2,1,0:T(8,128)(2,1)S(1)} %bitcast.42), channel_id=1, source_target_pairs={{0,1},{1,0},{2,3},{3,2},{4,5},{5,4},{6,7},{7,6},{8,9},{9,8},{10,11... | collective-permute-start | bytes 2359304 | tf_op jit(solution)/shard_map/ppermute | solution.py:359
  29.6 1.9 %collective-permute-start.5 = (bf16[2,4,128,256]{3,2,1,0:T(8,128)(2,1)S(1)}, bf16[2,4,128,256]{3,2,1,0:T(8,128)(2,1)S(1)}, u32[]{:S(2)}, u32[]{:S(2)}) collective-permute-start(bf16[2,4,128,256]{3,2,1,0:T(8,128)(2,1)S(1)} %get-tuple-element.86), channel_id=1, source_target_pairs={{0,4},{4,0},{8,12},{12,8},{16,20},{20,16},{24,28},{28,24},{1,5},{5... | collective-permute-start | bytes 1572872 | tf_op jit(solution)/shard_map/ppermute | solution.py:365
  29.6 2.7 %collective-permute-start.9 = (bf16[2,2,4,64,256]{4,3,2,1,0:T(8,128)(2,1)S(1)}, bf16[2,2,4,64,256]{4,3,2,1,0:T(8,128)(2,1)S(1)}, u32[]{:S(2)}, u32[]{:S(2)}) collective-permute-start(bf16[2,2,4,64,256]{4,3,2,1,0:T(8,128)(2,1)S(1)} %pad_maximum_fusion.refs_0_), channel_id=1, source_target_pairs={{0,4},{4,0},{8,12},{12,8},{16,20},{20,16},{24,28},{28,24},{1,5},{5... | collective-permute-start | bytes 1572872 | tf_op jit(solution)/shard_map/ppermute | solution.py:365
  30.1 4.1 %collective-permute-start.10 = (bf16[2,2,4,64,256]{4,3,2,1,0:T(8,128)(2,1)S(1)}, bf16[2,2,4,64,256]{4,3,2,1,0:T(8,128)(2,1)S(1)}, u32[]{:S(2)}, u32[]{:S(2)}) collective-permute-start(bf16[2,2,4,64,256]{4,3,2,1,0:T(8,128)(2,1)S(1)} %collective-permute-done.2.refs_1_), channel_id=1, source_target_pairs={{0,4},{4,0},{8,12},{12,8},{16,20},{20,16},{24,28},{28,24},{1,5},{5... | collective-permute-start | bytes 1572872 | tf_op jit(solution)/shard_map/ppermute | solution.py:365
  32.1 6.8 %collective-permute-start.8 = (bf16[1,128,256]{2,1,0:T(8,128)(2,1)S(1)}, bf16[1,128,256]{2,1,0:T(8,128)(2,1)S(1)}, u32[]{:S(2)}, u32[]{:S(2)}) collective-permute-start(bf16[1,128,256]{2,1,0:T(8,128)(2,1)S(1)} %get-tuple-element.90), channel_id=1, source_target_pairs={{0,8},{4,12},{8,0},{12,4},{16,24},{20,28},{24,16},{28,20},{1,9},{5... | collective-permute-start | bytes 196616 | tf_op jit(solution)/shard_map/ppermute | solution.py:362
  32.2 6.7 %collective-permute-start.7 = (bf16[1,128,256]{2,1,0:T(8,128)(2,1)S(1)}, bf16[1,128,256]{2,1,0:T(8,128)(2,1)S(1)}, u32[]{:S(2)}, u32[]{:S(2)}) collective-permute-start(bf16[1,128,256]{2,1,0:T(8,128)(2,1)S(1)} %get-tuple-element.89), channel_id=1, source_target_pairs={{0,8},{4,12},{8,0},{12,4},{16,24},{20,28},{24,16},{28,20},{1,9},{5... | collective-permute-start | bytes 196616 | tf_op jit(solution)/shard_map/ppermute | solution.py:362
  39.5 7.2 %collective-permute-start.11 = (bf16[1,128,256]{2,1,0:T(8,128)(2,1)S(1)}, bf16[1,128,256]{2,1,0:T(8,128)(2,1)S(1)}, u32[]{:S(2)}, u32[]{:S(2)}) collective-permute-start(bf16[1,128,256]{2,1,0:T(8,128)(2,1)S(1)} %shard_map.82), channel_id=1, source_target_pairs={{0,16},{4,20},{8,24},{12,28},{16,0},{20,4},{24,8},{28,12},{1,17},{... | collective-permute-start | bytes 196616 | tf_op jit(solution)/shard_map/ppermute | solution.py:362
  48.8 3.7 %collective-permute-start.14 = (bf16[2,4,128,256]{3,2,1,0:T(8,128)(2,1)S(1)}, bf16[2,4,128,256]{3,2,1,0:T(8,128)(2,1)S(1)}, u32[]{:S(2)}, u32[]{:S(2)}) collective-permute-start(bf16[2,4,128,256]{3,2,1,0:T(8,128)(2,1)S(1)} %get-tuple-element.105), channel_id=1, source_target_pairs={{0,4},{4,0},{8,12},{12,8},{16,20},{20,16},{24,28},{28,24},{1,5},{5... | collective-permute-start | bytes 1572872 | tf_op jit(solution)/shard_map/ppermute | solution.py:365
  48.9 3.6 %collective-permute-start.13 = (bf16[4,128,256]{2,1,0:T(8,128)(2,1)S(1)}, bf16[4,128,256]{2,1,0:T(8,128)(2,1)S(1)}, u32[]{:S(2)}, u32[]{:S(2)}) collective-permute-start(bf16[4,128,256]{2,1,0:T(8,128)(2,1)S(1)} %get-tuple-element.104), channel_id=1, source_target_pairs={{0,4},{4,0},{8,12},{12,8},{16,20},{20,16},{24,28},{28,24},{1,5},{5... | collective-permute-start | bytes 786440 | tf_op jit(solution)/shard_map/ppermute | solution.py:365
  50.9 39.0 %collective-permute-start.18 = (bf16[4,256,768]{2,1,0:T(8,128)(2,1)S(1)}, bf16[4,256,768]{2,1,0:T(8,128)(2,1)S(1)}, u32[]{:S(2)}, u32[]{:S(2)}) collective-permute-start(bf16[4,256,768]{2,1,0:T(8,128)(2,1)S(1)} %shard_map.85), channel_id=1, source_target_pairs={{0,1},{1,0},{2,3},{3,2},{4,5},{5,4},{6,7},{7,6},{8,9},{9,8},{10,11... | collective-permute-start | bytes 4718600 | tf_op jit(solution)/shard_map/ppermute | solution.py:359
  53.5 14.9 %collective-permute-start.15 = (bf16[2,4,128,256]{3,2,1,0:T(8,128)(2,1)S(1)}, bf16[2,4,128,256]{3,2,1,0:T(8,128)(2,1)S(1)}, u32[]{:S(2)}, u32[]{:S(2)}) collective-permute-start(bf16[2,4,128,256]{3,2,1,0:T(8,128)(2,1)S(1)} %get-tuple-element.110), channel_id=1, source_target_pairs={{0,8},{4,12},{8,0},{12,4},{16,24},{20,28},{24,16},{28,20},{1,9},{5... | collective-permute-start | bytes 1572872 | tf_op jit(solution)/shard_map/ppermute | solution.py:362
  56.5 42.2 %collective-permute-start.21 = (bf16[4,256,768]{2,1,0:T(8,128)(2,1)S(1)}, bf16[4,256,768]{2,1,0:T(8,128)(2,1)S(1)}, u32[]{:S(2)}, u32[]{:S(2)}) collective-permute-start(bf16[4,256,768]{2,1,0:T(8,128)(2,1)S(1)} %get-tuple-element.115), channel_id=1, source_target_pairs={{0,2},{1,3},{2,0},{3,1},{4,6},{5,7},{6,4},{7,5},{8,10},{9,11},{10,... | collective-permute-start | bytes 4718600 | tf_op jit(solution)/shard_map/ppermute | solution.py:359
  59.2 1.8 %collective-permute-start.16 = (bf16[3,4,64,256]{3,2,1,0:T(8,128)(2,1)S(1)}, bf16[3,4,64,256]{3,2,1,0:T(8,128)(2,1)S(1)}, u32[]{:S(2)}, u32[]{:S(2)}) collective-permute-start(bf16[3,4,64,256]{3,2,1,0:T(8,128)(2,1)S(1)} %get-tuple-element.122), channel_id=1, source_target_pairs={{0,4},{4,0},{8,12},{12,8},{16,20},{20,16},{24,28},{28,24},{1,5},{5... | collective-permute-start | bytes 1179656 | tf_op jit(solution)/shard_map/ppermute | solution.py:365
  59.3 2.3 %collective-permute-start.17 = (bf16[3,4,64,256]{3,2,1,0:T(8,128)(2,1)S(1)}, bf16[3,4,64,256]{3,2,1,0:T(8,128)(2,1)S(1)}, u32[]{:S(2)}, u32[]{:S(2)}) collective-permute-start(bf16[3,4,64,256]{3,2,1,0:T(8,128)(2,1)S(1)} %get-tuple-element.123), channel_id=1, source_target_pairs={{0,4},{4,0},{8,12},{12,8},{16,20},{20,16},{24,28},{28,24},{1,5},{5... | collective-permute-start | bytes 1179656 | tf_op jit(solution)/shard_map/ppermute | solution.py:365
  62.3 13.6 %collective-permute-start.20 = (bf16[3,128,256]{2,1,0:T(8,128)(2,1)S(1)}, bf16[3,128,256]{2,1,0:T(8,128)(2,1)S(1)}, u32[]{:S(2)}, u32[]{:S(2)}) collective-permute-start(bf16[3,128,256]{2,1,0:T(8,128)(2,1)S(1)} %get-tuple-element.131), channel_id=1, source_target_pairs={{0,8},{4,12},{8,0},{12,4},{16,24},{20,28},{24,16},{28,20},{1,9},{5... | collective-permute-start | bytes 589832 | tf_op jit(solution)/shard_map/ppermute | solution.py:362
  63.9 28.0 %collective-permute-start.22 = (bf16[3,128,256]{2,1,0:T(8,128)(2,1)S(1)}, bf16[3,128,256]{2,1,0:T(8,128)(2,1)S(1)}, u32[]{:S(2)}, u32[]{:S(2)}) collective-permute-start(bf16[3,128,256]{2,1,0:T(8,128)(2,1)S(1)} %get-tuple-element.124), channel_id=1, source_target_pairs={{0,8},{4,12},{8,0},{12,4},{16,24},{20,28},{24,16},{28,20},{1,9},{5... | collective-permute-start | bytes 589832 | tf_op jit(solution)/shard_map/ppermute | solution.py:362
  69.0 18.4 %collective-permute-start.19 = (bf16[4,128,256]{2,1,0:T(8,128)(2,1)S(1)}, bf16[4,128,256]{2,1,0:T(8,128)(2,1)S(1)}, u32[]{:S(2)}, u32[]{:S(2)}) collective-permute-start(bf16[4,128,256]{2,1,0:T(8,128)(2,1)S(1)} %get-tuple-element.126), channel_id=1, source_target_pairs={{0,16},{4,20},{8,24},{12,28},{16,0},{20,4},{24,8},{28,12},{1,17},{... | collective-permute-start | bytes 786440 | tf_op jit(solution)/shard_map/ppermute | solution.py:362
  76.4 15.5 %collective-permute-start.23 = (bf16[3,128,256]{2,1,0:T(8,128)(2,1)S(1)}, bf16[3,128,256]{2,1,0:T(8,128)(2,1)S(1)}, u32[]{:S(2)}, u32[]{:S(2)}) collective-permute-start(bf16[3,128,256]{2,1,0:T(8,128)(2,1)S(1)} %shard_map.93), channel_id=1, source_target_pairs={{0,16},{4,20},{8,24},{12,28},{16,0},{20,4},{24,8},{28,12},{1,17},{... | collective-permute-start | bytes 589832 | tf_op jit(solution)/shard_map/ppermute | solution.py:362
  88.0 9.2 %collective-permute-start.24 = (bf16[4,128,256]{2,1,0:T(8,128)(2,1)S(1)}, bf16[4,128,256]{2,1,0:T(8,128)(2,1)S(1)}, u32[]{:S(2)}, u32[]{:S(2)}) collective-permute-start(bf16[4,128,256]{2,1,0:T(8,128)(2,1)S(1)} %shard_map.94), channel_id=1, source_target_pairs={{0,0},{1,8},{2,2},{3,10},{4,4},{5,12},{6,6},{7,14},{8,1},{9,9},{10... | collective-permute-start | bytes 786440 | tf_op jit(solution)/shard_map/ppermute | solution.py:665
  92.5 8.1 %collective-permute-start.25 = (bf16[2,128,256]{2,1,0:T(8,128)(2,1)S(1)}, bf16[2,128,256]{2,1,0:T(8,128)(2,1)S(1)}, u32[]{:S(2)}, u32[]{:S(2)}) collective-permute-start(bf16[2,128,256]{2,1,0:T(8,128)(2,1)S(1)} %get-tuple-element.140), channel_id=1, source_target_pairs={{0,2},{1,3},{2,0},{3,1},{4,6},{5,7},{6,4},{7,5},{8,10},{9,11},{10,... | collective-permute-start | bytes 393224 | tf_op jit(solution)/shard_map/ppermute | solution.py:359

commit v7 on v6

--- a/solution.py
+++ b/solution.py
@@ -311,22 +311,16 @@
 
 
 def up_sum_body(factor, place, *refs):
-    ins, (send_ref, mine_ref) = refs[:6], refs[6:]
+    ins, (send_ref, up_ref) = refs[:6], refs[6:]
     first, total = (
         (own[0] + near[...].astype(F32) + far[...].astype(F32)) * factor
         for own, near, far in (ins[:3], ins[3:])
     )
-    mine_ref[0] = first[0]
-    mine_ref[1] = total[0]
     send_ref[...] = total[1:].astype(BF16)
-
-
-def place_own_body(place, mine_ref, down_in, up_ref, down_ref):
-    down_ref[...] = down_in[...].astype(F32)
-    width = mine_ref.shape[-1]
-    for at in range(2):
+    width = send_ref.shape[-1]
+    for at, mine in enumerate((first[0], total[0])):
         lanes = pl.ds(pl.multiple_of((place[0] ^ at) * width, width), width)
-        up_ref[:, :, lanes] = mine_ref[at].reshape(*up_ref.shape[:2], width)
+        up_ref[:, :, lanes] = mine.reshape(*up_ref.shape[:2], width)
 
 
 def place_near_body(place, got_ref, held_ref, up_ref):
@@ -613,7 +607,7 @@
         16.0,
     )
     send_u, far_u, mine_u = up_meet(3, keep_u, [send_core(give_lo), send_core(give_hi)])
-    got_u, far_u = send_z(send_u, 1), send_z(far_u, 1)
+    far_u = send_z(far_u, 1)
 
     got_d = after((got_d,), send_u)[0]
     send_d, mine_d = call(
@@ -625,6 +619,7 @@
         16,
     )
     got_d = send_z(send_d, 2)
+    got_u = send_z(after((send_u,), send_d)[0], 1)
 
     up_b = after((up_blocks,), send_d)[0]
     own_grads = call_once(
@@ -668,32 +663,24 @@
     outputs = added(own_out, got_out)
 
     got_u, last_u = after((got_u, last_u), outputs)
-    send_u, mine_u = call(
+    send_u, held = call(
         functools.partial(up_sum_body, factor),
         place,
         (1,),
         [whole(v) for v in (mine_e, got_e, last_e, mine_u, got_u, last_u)],
-        [whole_out((2,) + shard_u[1:], BF16), whole_out((2,) + shard_u[1:], F32)],
-        8,
-    )
-    got_u = send(send_u, 2)
-
-    home_d = after((home_d,), send_u)[0]
-    held, down_grads = call(
-        place_own_body,
-        place,
-        (1,),
-        [whole(mine_u), whole(home_d)],
-        [
+        [
+            whole_out((2,) + shard_u[1:], BF16),
             whole_out((local, feat // n_dp, block_hidden), F32),
-            whole_out((local, part, feat), F32),
         ],
         8,
     )
+    got_u = send(send_u, 2)
+
     got_grads = after((got_grads,), held)[0]
     feature_grads = added(own_grads, got_grads)
-
-    got_u = after((got_u,), feature_grads)[0]
+    down_grads = after((home_d,), feature_grads)[0].astype(F32)
+
+    got_u = after((got_u,), down_grads)[0]
     up_grads = call(
         place_near_body,
         place,

time: 103 us -> 101 us (0.981)
  starting transfers between devices: 27 us -> 25.9 us
    ppermute x1, waiting for transfers between devices: 4.57 us -> 0.01 us  [square_device(): home_d = lax.ppermute(sum_d, ('dp', 'tensor'), swaps)]
    ppermute x9, starting transfers between devices: 14.6 us -> 10.6 us  [send_z(): return lax.ppermute(value, 'dp', [(d, d ^ 2 * hop) for d in range(n_dp)])]
    ppermute x9, waiting for transfers between devices: 19.8 us -> 22.4 us  [send_z(): return lax.ppermute(value, 'dp', [(d, d ^ 2 * hop) for d in range(n_dp)])]
    ppermute x1, starting transfers between devices: 1.92 us -> 4.3 us  [square_device(): home_d = lax.ppermute(sum_d, ('dp', 'tensor'), swaps)]
    ppermute x9, waiting for transfers between devices: 4.18 us -> 5.82 us  [send(): lax.ppermute(value, 'tensor', [(t, t ^ hop) for t in range(n_tensor)])]
    pallas_call x25 -> x24, Pallas kernels: 39.6 us -> 38.8 us  [call(): pl.pallas_call(body, grid_spec=pltpu.PrefetchScalarGridSpec(num_scalar_pr...]
  transfers between devices with their start and end apart: 26 -> 26, of which waited for: 12 -> 11; matrix products, arithmetic and copies ran while one was open for 1% -> 2% of each run, Pallas kernels for 36% -> 35%
where the time goes in v7:
time: 101 us; the launch traced here: 100 us
  Pallas kernels  38.8 us (38%)
  waiting for transfers between devices  31.4 us (31%)
  starting transfers between devices  25.9 us (26%)
  local copies, waits for them, and re-layouts  2.33 us (2%)
  other arithmetic  1.01 us (1%)
    pallas_call x24, Pallas kernels, call(): pl.pallas_call(body, grid_spec=pltpu.PrefetchScalarGridSpec(num_scalar_pr...  38.8 us
    ppermute x9, waiting for transfers between devices, send_z(): return lax.ppermute(value, 'dp', [(d, d ^ 2 * hop) for d in range(n_dp)])  22.4 us
    ppermute x9, starting transfers between devices, send_z(): return lax.ppermute(value, 'dp', [(d, d ^ 2 * hop) for d in range(n_dp)])  10.6 us
    ppermute x9, starting transfers between devices, send(): lax.ppermute(value, 'tensor', [(t, t ^ hop) for t in range(n_tensor)])  9.39 us
    ppermute x9, waiting for transfers between devices, send(): lax.ppermute(value, 'tensor', [(t, t ^ hop) for t in range(n_tensor)])  5.82 us
    ppermute x1, starting transfers between devices, square_device(): home_d = lax.ppermute(sum_d, ('dp', 'tensor'), swaps)  4.3 us
    ppermute x7, waiting for transfers between devices, send_core(): return lax.ppermute(value, 'dp', [(d, d ^ 1) for d in range(n_dp)])  3.24 us
  transfers between devices with their start and end apart: 26, of which 11 were waited for; matrix products, arithmetic and copies ran while one was open for 2% of the time, Pallas kernels for 35%

profile of v7, /device:TPU:12, one launch (start us, length us, event | category | flops | bytes accessed | tf_op | source)
XLA Modules:
  0.0 100.4 jit_solution(5243350410201047544)
XLA Ops:
  3.4 1.6 %collective-permute-start.1 = (bf16[2,4,64,256]{3,2,1,0:T(8,128)(2,1)S(1)}, bf16[2,4,64,256]{3,2,1,0:T(8,128)(2,1)S(1)}, u32[]{:S(2)}, u32[]{:S(2)}) collective-permute-start(bf16[2,4,64,256]{3,2,1,0:T(8,128)(2,1)S(1)} %pad_maximum_fusion.2), channel_id=1, source_target_pairs={{0,1},{1,0},{2,3},{3,2},{4,5},{5,4},{6,7},{7,6},{8,9},{9,8},{10,11... | collective-permute-start | bytes 786440 | tf_op jit(solution)/shard_map/ppermute | solution.py:353
  5.2 1.6 %collective-permute-start.3 = (bf16[2,256,768]{2,1,0:T(8,128)(2,1)S(1)}, bf16[2,256,768]{2,1,0:T(8,128)(2,1)S(1)}, u32[]{:S(2)}, u32[]{:S(2)}) collective-permute-start(bf16[2,256,768]{2,1,0:T(8,128)(2,1)S(1)} %bitcast.45), channel_id=1, source_target_pairs={{0,2},{1,3},{2,0},{3,1},{4,6},{5,7},{6,4},{7,5},{8,10},{9,11},{10,... | collective-permute-start | bytes 2359304 | tf_op jit(solution)/shard_map/ppermute | solution.py:353
  6.8 1.2 %collective-permute-start.4 = (bf16[2,256,768]{2,1,0:T(8,128)(2,1)S(1)}, bf16[2,256,768]{2,1,0:T(8,128)(2,1)S(1)}, u32[]{:S(2)}, u32[]{:S(2)}) collective-permute-start(bf16[2,256,768]{2,1,0:T(8,128)(2,1)S(1)} %bitcast.44), channel_id=1, source_target_pairs={{0,1},{1,0},{2,3},{3,2},{4,5},{5,4},{6,7},{7,6},{8,9},{9,8},{10,11... | collective-permute-start | bytes 2359304 | tf_op jit(solution)/shard_map/ppermute | solution.py:353
  8.1 5.8 %shard_map.75 = (bf16[2,4,4,64,768]{4,3,2,1,0:T(8,128)(2,1)S(1)}, bf16[2,4,4,64,768]{4,3,2,1,0:T(8,128)(2,1)S(1)}) custom-call(s32[3]{0:T(128)S(1)} %pad_add_fusion.place, bf16[4,256,768]{2,1,0:T(8,128)(2,1)S(1)} %bitcast.37, bf16[4,256,1024]{2,1,0:T(8,128)(2,1)S(1)} %copy-done.3), custom_call_target="tpu_custom_call" | custom-call | tf_op jit(solution)/shard_map/pallas_call | solution.py:74
  15.0 1.3 %collective-permute-start.6 = (bf16[2,256,768]{2,1,0:T(8,128)(2,1)S(1)}, bf16[2,256,768]{2,1,0:T(8,128)(2,1)S(1)}, u32[]{:S(2)}, u32[]{:S(2)}) collective-permute-start(bf16[2,256,768]{2,1,0:T(8,128)(2,1)S(1)} %bitcast.42), channel_id=1, source_target_pairs={{0,1},{1,0},{2,3},{3,2},{4,5},{5,4},{6,7},{7,6},{8,9},{9,8},{10,11... | collective-permute-start | bytes 2359304 | tf_op jit(solution)/shard_map/ppermute | solution.py:353
  17.4 1.6 %shard_map.77 = (bf16[2,4,128,256]{3,2,1,0:T(8,128)(2,1)S(1)}, bf16[2,4,128,256]{3,2,1,0:T(8,128)(2,1)S(1)}) custom-call(s32[3]{0:T(128)S(1)} %pad_add_fusion.place, bf16[4,256,768]{2,1,0:T(8,128)(2,1)S(1)} %bitcast.33, bf16[2,4,4,64,768]{4,3,2,1,0:T(8,128)(2,1)S(1)} %get-tuple-element.127.refs_1_.refs_3_, bf16[4,256,768]{2,1,0:T(8,128)(2,1)S(1)} %bitcast.38, ...), custom_call_target="tpu_custom_call" | custom-call | tf_op jit(solution)/shard_map/pallas_call | solution.py:74
  19.0 7.9 %collective-permute-done.2.refs_1_ = bf16[2,2,4,64,256]{4,3,2,1,0:T(8,128)(2,1)S(1)} collective-permute-done((bf16[2,2,4,64,256]{4,3,2,1,0:T(8,128)(2,1)S(1)}, bf16[2,2,4,64,256]{4,3,2,1,0:T(8,128)(2,1)S(1)}, u32[]{:S(2)}, u32[]{:S(2)}) %collective-permute-start.2) | collective-permute-done | bytes 524320 | tf_op jit(solution)/shard_map/ppermute | solution.py:356
  27.9 1.6 %collective-permute-done.4.refs_1_ = bf16[2,256,768]{2,1,0:T(8,128)(2,1)S(1)} collective-permute-done((bf16[2,256,768]{2,1,0:T(8,128)(2,1)S(1)}, bf16[2,256,768]{2,1,0:T(8,128)(2,1)S(1)}, u32[]{:S(2)}, u32[]{:S(2)}) %collective-permute-start.4) | collective-permute-done | bytes 786464 | tf_op jit(solution)/shard_map/ppermute | solution.py:353
  30.1 1.4 %collective-permute-done.5.refs_0_.first_got = bf16[2,4,128,256]{3,2,1,0:T(8,128)(2,1)S(1)} collective-permute-done((bf16[2,4,128,256]{3,2,1,0:T(8,128)(2,1)S(1)}, bf16[2,4,128,256]{3,2,1,0:T(8,128)(2,1)S(1)}, u32[]{:S(2)}, u32[]{:S(2)}) %collective-permute-start.5) | collective-permute-done | bytes 524320 | tf_op jit(solution)/shard_map/ppermute | solution.py:359
  32.2 2.0 %collective-permute-start.7 = (bf16[1,128,256]{2,1,0:T(8,128)(2,1)S(1)}, bf16[1,128,256]{2,1,0:T(8,128)(2,1)S(1)}, u32[]{:S(2)}, u32[]{:S(2)}) collective-permute-start(bf16[1,128,256]{2,1,0:T(8,128)(2,1)S(1)} %get-tuple-element.88), channel_id=1, source_target_pairs={{0,8},{4,12},{8,0},{12,4},{16,24},{20,28},{24,16},{28,20},{1,9},{5... | collective-permute-start | bytes 196616 | tf_op jit(solution)/shard_map/ppermute | solution.py:356
  34.9 3.1 %shard_map.80 = (bf16[2,4,2,64,768]{4,3,2,1,0:T(8,128)(2,1)S(1)}, bf16[2,4,2,64,768]{4,3,2,1,0:T(8,128)(2,1)S(1)}) custom-call(s32[3]{0:T(128)S(1)} %pad_add_fusion.place, bf16[2,256,768]{2,1,0:T(8,128)(2,1)S(1)} %collective-permute-done.3.x_ref.refs_1_, bf16[2,2,4,256,256]{4,3,2,1,0:T(8,128)(2,1)S(1)} %bitcast.22), custom_call_target="tpu_custom_call" | custom-call | tf_op jit(solution)/shard_map/pallas_call | solution.py:74
  39.5 2.7 %collective-permute-start.11 = (bf16[1,128,256]{2,1,0:T(8,128)(2,1)S(1)}, bf16[1,128,256]{2,1,0:T(8,128)(2,1)S(1)}, u32[]{:S(2)}, u32[]{:S(2)}) collective-permute-start(bf16[1,128,256]{2,1,0:T(8,128)(2,1)S(1)} %shard_map.82), channel_id=1, source_target_pairs={{0,16},{4,20},{8,24},{12,28},{16,0},{20,4},{24,8},{28,12},{1,17},{... | collective-permute-start | bytes 196616 | tf_op jit(solution)/shard_map/ppermute | solution.py:356
  42.1 1.5 %collective-permute-done.12.x_ref.refs_2_ = bf16[2,256,768]{2,1,0:T(8,128)(2,1)S(1)} collective-permute-done((bf16[2,256,768]{2,1,0:T(8,128)(2,1)S(1)}, bf16[2,256,768]{2,1,0:T(8,128)(2,1)S(1)}, u32[]{:S(2)}, u32[]{:S(2)}) %collective-permute-start.12) | collective-permute-done | bytes 786464 | tf_op jit(solution)/shard_map/ppermute | solution.py:353
  43.6 3.1 %shard_map.83 = (bf16[2,4,2,64,768]{4,3,2,1,0:T(8,128)(2,1)S(1)}, bf16[2,4,2,64,768]{4,3,2,1,0:T(8,128)(2,1)S(1)}) custom-call(s32[3]{0:T(128)S(1)} %pad_add_fusion.place, bf16[2,256,768]{2,1,0:T(8,128)(2,1)S(1)} %collective-permute-done.12.x_ref.refs_2_, bf16[2,2,4,256,256]{4,3,2,1,0:T(8,128)(2,1)S(1)} %bitcast.23), custom_call_target="tpu_custom_call" | custom-call | tf_op jit(solution)/shard_map/pallas_call | solution.py:74
  46.8 2.0 %shard_map.84 = (bf16[4,128,256]{2,1,0:T(8,128)(2,1)S(1)}, bf16[2,4,128,256]{3,2,1,0:T(8,128)(2,1)S(1)}, bf16[3,4,128,256]{3,2,1,0:T(8,128)(2,1)S(1)}) custom-call(s32[3]{0:T(128)S(1)} %pad_add_fusion.place, bf16[4,256,768]{2,1,0:T(8,128)(2,1)S(1)} %bitcast.35, bf16[2,256,768]{2,1,0:T(8,128)(2,1)S(1)} %collective-permute-done.4.refs_1_, ...), custom_call_target="tpu_custom_call" | custom-call | tf_op jit(solution)/shard_map/pallas_call | solution.py:74
  49.4 1.5 %shard_map.85 = bf16[4,256,768]{2,1,0:T(8,128)(2,1)S(1)} custom-call(s32[3]{0:T(128)S(1)} %pad_add_fusion.place, bf16[2,2,4,256,256]{4,3,2,1,0:T(8,128)(2,1)S(1)} %bitcast.24, bf16[2,2,4,256,256]{4,3,2,1,0:T(8,128)(2,1)S(1)} %bitcast.25, bf16[2,2,4,256,256]{4,3,2,1,0:T(8,128)(2,1)S(1)} %bitcast.26, ...), custom_call_target="tpu_custom_call" | custom-call | tf_op jit(solution)/shard_map/pallas_call | solution.py:74
  50.9 1.6 %collective-permute-start.18 = (bf16[4,256,768]{2,1,0:T(8,128)(2,1)S(1)}, bf16[4,256,768]{2,1,0:T(8,128)(2,1)S(1)}, u32[]{:S(2)}, u32[]{:S(2)}) collective-permute-start(bf16[4,256,768]{2,1,0:T(8,128)(2,1)S(1)} %shard_map.85), channel_id=1, source_target_pairs={{0,1},{1,0},{2,3},{3,2},{4,5},{5,4},{6,7},{7,6},{8,9},{9,8},{10,11... | collective-permute-start | bytes 4718600 | tf_op jit(solution)/shard_map/ppermute | solution.py:353
  54.0 2.6 %shard_map.87 = (bf16[4,4,64,768]{3,2,1,0:T(8,128)(2,1)S(1)}, bf16[4,2,64,768]{3,2,1,0:T(8,128)(2,1)S(1)}, bf16[4,2,64,768]{3,2,1,0:T(8,128)(2,1)S(1)}, bf16[4,2...) custom-call(s32[3]{0:T(128)S(1)} %pad_add_fusion.place, bf16[4,256,768]{2,1,0:T(8,128)(2,1)S(1)} %bitcast.36, ...), custom_call_target="tpu_custom_call" | custom-call | tf_op jit(solution)/shard_map/pallas_call | solution.py:74
  57.1 2.1 %shard_map.88 = (bf16[3,4,64,256]{3,2,1,0:T(8,128)(2,1)S(1)}, bf16[3,4,64,256]{3,2,1,0:T(8,128)(2,1)S(1)}, bf16[3,4,128,256]{3,2,1,0:T(8,128)(2,1)S(1)}) custom-call(s32[3]{0:T(128)S(1)} %pad_add_fusion.place, bf16[4,256,768]{2,1,0:T(8,128)(2,1)S(1)} %bitcast.39, bf16[2,256,768]{2,1,0:T(8,128)(2,1)S(1)} %collective-permute-done.3.x_ref.refs_1_, ...), custom_call_target="tpu_custom_call" | custom-call | flops 16000000000 | tf_op jit(solution)/shard_map/pallas_call | solution.py:74
  59.8 1.2 %collective-permute-done.16.refs_0_ = bf16[3,4,64,256]{3,2,1,0:T(8,128)(2,1)S(1)} collective-permute-done((bf16[3,4,64,256]{3,2,1,0:T(8,128)(2,1)S(1)}, bf16[3,4,64,256]{3,2,1,0:T(8,128)(2,1)S(1)}, u32[]{:S(2)}, u32[]{:S(2)}) %collective-permute-start.16) | collective-permute-done | bytes 393248 | tf_op jit(solution)/shard_map/ppermute | solution.py:359
  62.3 1.6 %collective-permute-start.20 = (bf16[3,128,256]{2,1,0:T(8,128)(2,1)S(1)}, bf16[3,128,256]{2,1,0:T(8,128)(2,1)S(1)}, u32[]{:S(2)}, u32[]{:S(2)}) collective-permute-start(bf16[3,128,256]{2,1,0:T(8,128)(2,1)S(1)} %get-tuple-element.130), channel_id=1, source_target_pairs={{0,8},{4,12},{8,0},{12,4},{16,24},{20,28},{24,16},{28,20},{1,9},{5... | collective-permute-start | bytes 589832 | tf_op jit(solution)/shard_map/ppermute | solution.py:356
  63.9 4.4 %collective-permute-done.15.got_ref = bf16[2,4,128,256]{3,2,1,0:T(8,128)(2,1)S(1)} collective-permute-done((bf16[2,4,128,256]{3,2,1,0:T(8,128)(2,1)S(1)}, bf16[2,4,128,256]{3,2,1,0:T(8,128)(2,1)S(1)}, u32[]{:S(2)}, u32[]{:S(2)}) %collective-permute-start.15) | collective-permute-done | bytes 524320 | tf_op jit(solution)/shard_map/ppermute | solution.py:356
  69.0 2.6 %collective-permute-start.19 = (bf16[4,128,256]{2,1,0:T(8,128)(2,1)S(1)}, bf16[4,128,256]{2,1,0:T(8,128)(2,1)S(1)}, u32[]{:S(2)}, u32[]{:S(2)}) collective-permute-start(bf16[4,128,256]{2,1,0:T(8,128)(2,1)S(1)} %get-tuple-element.125), channel_id=1, source_target_pairs={{0,16},{4,20},{8,24},{12,28},{16,0},{20,4},{24,8},{28,12},{1,17},{... | collective-permute-start | bytes 786440 | tf_op jit(solution)/shard_map/ppermute | solution.py:356
  71.6 1.5 %shard_map.91.own_ref = f32[4,256,768]{2,1,0:T(8,128)S(1)} custom-call(s32[3]{0:T(128)S(1)} %pad_add_fusion.place, bf16[4,256,1024]{2,1,0:T(8,128)(2,1)S(1)} %copy-done.3, bf16[4,256,1024]{2,1,0:T(8,128)(2,1)S(1)} %copy-done.3, bf16[4,4,64,768]{3,2,1,0:T(8,128)(2,1)S(1)} %shard_map.76.refs_3_.refs_2_, bf16[4,4,64,768]{3,2,1,0:T(8,128)(2,1)S(1)} %get-tuple-element.116.refs_3_), custom_call_target="tpu_custom_call" | custom-call | flops 4000000000 | tf_op jit(solution)/shard_map/pallas_call | solution.py:74
  73.2 1.5 %shard_map.92.own_ref = f32[4,256,768]{2,1,0:T(8,128)S(1)} custom-call(s32[3]{0:T(128)S(1)} %pad_add_fusion.place, bf16[4,1024,256]{2,1,0:T(8,128)(2,1)S(1)} %copy-done, bf16[4,1024,256]{2,1,0:T(8,128)(2,1)S(1)} %copy-done, bf16[4,1024,256]{2,1,0:T(8,128)(2,1)S(1)} %copy-done, bf16[2,4,4,64,768]{4,3,2,1,0:T(8,128)(2,1)S(1)} %get-tuple-element.127.refs_1_.refs_3_, ...), custom_call_target="tpu_custom_call" | custom-call | tf_op jit(solution)/shard_map/pallas_call | solution.py:74
  75.9 10.0 %collective-permute-done.19.got_ref = bf16[4,128,256]{2,1,0:T(8,128)(2,1)S(1)} collective-permute-done((bf16[4,128,256]{2,1,0:T(8,128)(2,1)S(1)}, bf16[4,128,256]{2,1,0:T(8,128)(2,1)S(1)}, u32[]{:S(2)}, u32[]{:S(2)}) %collective-permute-start.19) | collective-permute-done | bytes 262176 | tf_op jit(solution)/shard_map/ppermute | solution.py:356
  86.6 4.3 %collective-permute-start.25 = (bf16[4,128,256]{2,1,0:T(8,128)(2,1)S(1)}, bf16[4,128,256]{2,1,0:T(8,128)(2,1)S(1)}, u32[]{:S(2)}, u32[]{:S(2)}) collective-permute-start(bf16[4,128,256]{2,1,0:T(8,128)(2,1)S(1)} %shard_map.94), channel_id=1, source_target_pairs={{0,0},{1,8},{2,2},{3,10},{4,4},{5,12},{6,6},{7,14},{8,1},{9,9},{10... | collective-permute-start | bytes 786440 | tf_op jit(solution)/shard_map/ppermute | solution.py:660
  90.9 1.9 %shard_map.95 = bf16[4,256,768]{2,1,0:T(8,128)(2,1)} custom-call(s32[3]{0:T(128)S(1)} %pad_add_fusion.place, f32[4,256,768]{2,1,0:T(8,128)S(1)} %shard_map.92.own_ref, bf16[4,256,768]{2,1,0:T(8,128)(2,1)S(1)} %collective-permute-done.18.got_ref), custom_call_target="tpu_custom_call" | custom-call | tf_op jit(solution)/shard_map/pallas_call | solution.py:74
  92.8 1.4 %shard_map.96 = (bf16[2,128,256]{2,1,0:T(8,128)(2,1)S(1)}, f32[4,32,1024]{2,1,0:T(8,128)}) custom-call(s32[3]{0:T(128)S(1)} %pad_add_fusion.place, f32[2,1,128,256]{3,2,1,0:T(8,128)S(1)} %get-tuple-element.87.mine_ref.refs_0_, bf16[1,128,256]{2,1,0:T(8,128)(2,1)S(1)} %collective-permute-done.7.refs_1_, ...), custom_call_target="tpu_custom_call" | custom-call | tf_op jit(solution)/shard_map/pallas_call | solution.py:74
  94.8 1.9 %shard_map.97 = bf16[4,256,768]{2,1,0:T(8,128)(2,1)} custom-call(s32[3]{0:T(128)S(1)} %pad_add_fusion.place, f32[4,256,768]{2,1,0:T(8,128)S(1)} %shard_map.91.own_ref, bf16[4,256,768]{2,1,0:T(8,128)(2,1)S(1)} %collective-permute-done.21.got_ref), custom_call_target="tpu_custom_call" | custom-call | tf_op jit(solution)/shard_map/pallas_call | solution.py:74
  97.5 1.6 %collective-permute-done.24.got_ref = bf16[2,128,256]{2,1,0:T(8,128)(2,1)S(1)} collective-permute-done((bf16[2,128,256]{2,1,0:T(8,128)(2,1)S(1)}, bf16[2,128,256]{2,1,0:T(8,128)(2,1)S(1)}, u32[]{:S(2)}, u32[]{:S(2)}) %collective-permute-start.24) | collective-permute-done | bytes 131104 | tf_op jit(solution)/shard_map/ppermute | solution.py:353
  99.2 1.3 %shard_map.98 = f32[4,32,1024]{2,1,0:T(8,128)} custom-call(s32[3]{0:T(128)S(1)} %pad_add_fusion.place, bf16[2,128,256]{2,1,0:T(8,128)(2,1)S(1)} %collective-permute-done.24.got_ref, f32[4,32,1024]{2,1,0:T(8,128)} %get-tuple-element.139.held_ref), custom_call_target="tpu_custom_call", output_to_operand_aliasing={{}: (2, {})} | custom-call | tf_op jit(solution)/shard_map/pallas_call | solution.py:74
  (61 shorter events, 18.0 us)
Async XLA Ops:
  0.6 4.4 %copy-start.2 = (bf16[1024,768]{1,0:T(8,128)(2,1)S(1)}, bf16[1024,768]{1,0:T(8,128)(2,1)}, u32[]{:S(2)}) copy-start(bf16[1024,768]{1,0:T(8,128)(2,1)} %param.4) | copy-start | bytes 4718596
  1.8 12.1 %collective-permute-start = (bf16[2,4,64,256]{3,2,1,0:T(8,128)(2,1)S(1)}, bf16[2,4,64,256]{3,2,1,0:T(8,128)(2,1)S(1)}, u32[]{:S(2)}, u32[]{:S(2)}) collective-permute-start(bf16[2,4,64,256]{3,2,1,0:T(8,128)(2,1)S(1)} %pad_maximum_fusion.1), channel_id=1, source_target_pairs={{0,2},{1,3},{2,0},{3,1},{4,6},{5,7},{6,4},{7,5},{8,10},{9,11},{10,... | collective-permute-start | bytes 786440 | tf_op jit(solution)/shard_map/ppermute | solution.py:353
  3.4 1.7 %copy-start.1 = (bf16[1024,768]{1,0:T(8,128)(2,1)S(1)}, bf16[1024,768]{1,0:T(8,128)(2,1)}, u32[]{:S(2)}) copy-start(bf16[1024,768]{1,0:T(8,128)(2,1)} %param.5) | copy-start | bytes 4718596
  3.4 10.5 %collective-permute-start.1 = (bf16[2,4,64,256]{3,2,1,0:T(8,128)(2,1)S(1)}, bf16[2,4,64,256]{3,2,1,0:T(8,128)(2,1)S(1)}, u32[]{:S(2)}, u32[]{:S(2)}) collective-permute-start(bf16[2,4,64,256]{3,2,1,0:T(8,128)(2,1)S(1)} %pad_maximum_fusion.2), channel_id=1, source_target_pairs={{0,1},{1,0},{2,3},{3,2},{4,5},{5,4},{6,7},{7,6},{8,9},{9,8},{10,11... | collective-permute-start | bytes 786440 | tf_op jit(solution)/shard_map/ppermute | solution.py:353
  5.1 3.0 %copy-start.3 = (bf16[4,256,1024]{2,1,0:T(8,128)(2,1)S(1)}, bf16[4,256,1024]{2,1,0:T(8,128)(2,1)}, u32[]{:S(2)}) copy-start(bf16[4,256,1024]{2,1,0:T(8,128)(2,1)} %refs_1_.5) | copy-start | bytes 6291460
  5.2 22.7 %collective-permute-start.3 = (bf16[2,256,768]{2,1,0:T(8,128)(2,1)S(1)}, bf16[2,256,768]{2,1,0:T(8,128)(2,1)S(1)}, u32[]{:S(2)}, u32[]{:S(2)}) collective-permute-start(bf16[2,256,768]{2,1,0:T(8,128)(2,1)S(1)} %bitcast.45), channel_id=1, source_target_pairs={{0,2},{1,3},{2,0},{3,1},{4,6},{5,7},{6,4},{7,5},{8,10},{9,11},{10,... | collective-permute-start | bytes 2359304 | tf_op jit(solution)/shard_map/ppermute | solution.py:353
  6.8 22.8 %collective-permute-start.4 = (bf16[2,256,768]{2,1,0:T(8,128)(2,1)S(1)}, bf16[2,256,768]{2,1,0:T(8,128)(2,1)S(1)}, u32[]{:S(2)}, u32[]{:S(2)}) collective-permute-start(bf16[2,256,768]{2,1,0:T(8,128)(2,1)S(1)} %bitcast.44), channel_id=1, source_target_pairs={{0,1},{1,0},{2,3},{3,2},{4,5},{5,4},{6,7},{7,6},{8,9},{9,8},{10,11... | collective-permute-start | bytes 2359304 | tf_op jit(solution)/shard_map/ppermute | solution.py:353
  8.1 8.2 %copy-start = (bf16[4,1024,256]{2,1,0:T(8,128)(2,1)S(1)}, bf16[4,1024,256]{2,1,0:T(8,128)(2,1)}, u32[]{:S(2)}) copy-start(bf16[4,1024,256]{2,1,0:T(8,128)(2,1)} %refs_2_.1) | copy-start | bytes 6291460
  14.0 12.9 %collective-permute-start.2 = (bf16[2,2,4,64,256]{4,3,2,1,0:T(8,128)(2,1)S(1)}, bf16[2,2,4,64,256]{4,3,2,1,0:T(8,128)(2,1)S(1)}, u32[]{:S(2)}, u32[]{:S(2)}) collective-permute-start(bf16[2,2,4,64,256]{4,3,2,1,0:T(8,128)(2,1)S(1)} %pad_maximum_fusion.refs_0_), channel_id=1, source_target_pairs={{0,8},{4,12},{8,0},{12,4},{16,24},{20,28},{24,16},{28,20},{1,9},{5... | collective-permute-start | bytes 1572872 | tf_op jit(solution)/shard_map/ppermute | solution.py:356
  14.5 29.1 %collective-permute-start.12 = (bf16[2,256,768]{2,1,0:T(8,128)(2,1)S(1)}, bf16[2,256,768]{2,1,0:T(8,128)(2,1)S(1)}, u32[]{:S(2)}, u32[]{:S(2)}) collective-permute-start(bf16[2,256,768]{2,1,0:T(8,128)(2,1)S(1)} %bitcast.43), channel_id=1, source_target_pairs={{0,2},{1,3},{2,0},{3,1},{4,6},{5,7},{6,4},{7,5},{8,10},{9,11},{10,... | collective-permute-start | bytes 2359304 | tf_op jit(solution)/shard_map/ppermute | solution.py:353
  15.0 31.7 %collective-permute-start.6 = (bf16[2,256,768]{2,1,0:T(8,128)(2,1)S(1)}, bf16[2,256,768]{2,1,0:T(8,128)(2,1)S(1)}, u32[]{:S(2)}, u32[]{:S(2)}) collective-permute-start(bf16[2,256,768]{2,1,0:T(8,128)(2,1)S(1)} %bitcast.42), channel_id=1, source_target_pairs={{0,1},{1,0},{2,3},{3,2},{4,5},{5,4},{6,7},{7,6},{8,9},{9,8},{10,11... | collective-permute-start | bytes 2359304 | tf_op jit(solution)/shard_map/ppermute | solution.py:353
  29.6 1.9 %collective-permute-start.5 = (bf16[2,4,128,256]{3,2,1,0:T(8,128)(2,1)S(1)}, bf16[2,4,128,256]{3,2,1,0:T(8,128)(2,1)S(1)}, u32[]{:S(2)}, u32[]{:S(2)}) collective-permute-start(bf16[2,4,128,256]{3,2,1,0:T(8,128)(2,1)S(1)} %get-tuple-element.85), channel_id=1, source_target_pairs={{0,4},{4,0},{8,12},{12,8},{16,20},{20,16},{24,28},{28,24},{1,5},{5... | collective-permute-start | bytes 1572872 | tf_op jit(solution)/shard_map/ppermute | solution.py:359
  29.6 2.7 %collective-permute-start.9 = (bf16[2,2,4,64,256]{4,3,2,1,0:T(8,128)(2,1)S(1)}, bf16[2,2,4,64,256]{4,3,2,1,0:T(8,128)(2,1)S(1)}, u32[]{:S(2)}, u32[]{:S(2)}) collective-permute-start(bf16[2,2,4,64,256]{4,3,2,1,0:T(8,128)(2,1)S(1)} %pad_maximum_fusion.refs_0_), channel_id=1, source_target_pairs={{0,4},{4,0},{8,12},{12,8},{16,20},{20,16},{24,28},{28,24},{1,5},{5... | collective-permute-start | bytes 1572872 | tf_op jit(solution)/shard_map/ppermute | solution.py:359
  30.1 4.1 %collective-permute-start.10 = (bf16[2,2,4,64,256]{4,3,2,1,0:T(8,128)(2,1)S(1)}, bf16[2,2,4,64,256]{4,3,2,1,0:T(8,128)(2,1)S(1)}, u32[]{:S(2)}, u32[]{:S(2)}) collective-permute-start(bf16[2,2,4,64,256]{4,3,2,1,0:T(8,128)(2,1)S(1)} %collective-permute-done.2.refs_1_), channel_id=1, source_target_pairs={{0,4},{4,0},{8,12},{12,8},{16,20},{20,16},{24,28},{28,24},{1,5},{5... | collective-permute-start | bytes 1572872 | tf_op jit(solution)/shard_map/ppermute | solution.py:359
  32.1 6.8 %collective-permute-start.8 = (bf16[1,128,256]{2,1,0:T(8,128)(2,1)S(1)}, bf16[1,128,256]{2,1,0:T(8,128)(2,1)S(1)}, u32[]{:S(2)}, u32[]{:S(2)}) collective-permute-start(bf16[1,128,256]{2,1,0:T(8,128)(2,1)S(1)} %get-tuple-element.89), channel_id=1, source_target_pairs={{0,8},{4,12},{8,0},{12,4},{16,24},{20,28},{24,16},{28,20},{1,9},{5... | collective-permute-start | bytes 196616 | tf_op jit(solution)/shard_map/ppermute | solution.py:356
  32.2 6.7 %collective-permute-start.7 = (bf16[1,128,256]{2,1,0:T(8,128)(2,1)S(1)}, bf16[1,128,256]{2,1,0:T(8,128)(2,1)S(1)}, u32[]{:S(2)}, u32[]{:S(2)}) collective-permute-start(bf16[1,128,256]{2,1,0:T(8,128)(2,1)S(1)} %get-tuple-element.88), channel_id=1, source_target_pairs={{0,8},{4,12},{8,0},{12,4},{16,24},{20,28},{24,16},{28,20},{1,9},{5... | collective-permute-start | bytes 196616 | tf_op jit(solution)/shard_map/ppermute | solution.py:356
  39.5 7.2 %collective-permute-start.11 = (bf16[1,128,256]{2,1,0:T(8,128)(2,1)S(1)}, bf16[1,128,256]{2,1,0:T(8,128)(2,1)S(1)}, u32[]{:S(2)}, u32[]{:S(2)}) collective-permute-start(bf16[1,128,256]{2,1,0:T(8,128)(2,1)S(1)} %shard_map.82), channel_id=1, source_target_pairs={{0,16},{4,20},{8,24},{12,28},{16,0},{20,4},{24,8},{28,12},{1,17},{... | collective-permute-start | bytes 196616 | tf_op jit(solution)/shard_map/ppermute | solution.py:356
  48.8 3.7 %collective-permute-start.14 = (bf16[2,4,128,256]{3,2,1,0:T(8,128)(2,1)S(1)}, bf16[2,4,128,256]{3,2,1,0:T(8,128)(2,1)S(1)}, u32[]{:S(2)}, u32[]{:S(2)}) collective-permute-start(bf16[2,4,128,256]{3,2,1,0:T(8,128)(2,1)S(1)} %get-tuple-element.104), channel_id=1, source_target_pairs={{0,4},{4,0},{8,12},{12,8},{16,20},{20,16},{24,28},{28,24},{1,5},{5... | collective-permute-start | bytes 1572872 | tf_op jit(solution)/shard_map/ppermute | solution.py:359
  48.9 3.6 %collective-permute-start.13 = (bf16[4,128,256]{2,1,0:T(8,128)(2,1)S(1)}, bf16[4,128,256]{2,1,0:T(8,128)(2,1)S(1)}, u32[]{:S(2)}, u32[]{:S(2)}) collective-permute-start(bf16[4,128,256]{2,1,0:T(8,128)(2,1)S(1)} %get-tuple-element.103), channel_id=1, source_target_pairs={{0,4},{4,0},{8,12},{12,8},{16,20},{20,16},{24,28},{28,24},{1,5},{5... | collective-permute-start | bytes 786440 | tf_op jit(solution)/shard_map/ppermute | solution.py:359
  50.9 40.0 %collective-permute-start.18 = (bf16[4,256,768]{2,1,0:T(8,128)(2,1)S(1)}, bf16[4,256,768]{2,1,0:T(8,128)(2,1)S(1)}, u32[]{:S(2)}, u32[]{:S(2)}) collective-permute-start(bf16[4,256,768]{2,1,0:T(8,128)(2,1)S(1)} %shard_map.85), channel_id=1, source_target_pairs={{0,1},{1,0},{2,3},{3,2},{4,5},{5,4},{6,7},{7,6},{8,9},{9,8},{10,11... | collective-permute-start | bytes 4718600 | tf_op jit(solution)/shard_map/ppermute | solution.py:353
  53.5 14.9 %collective-permute-start.15 = (bf16[2,4,128,256]{3,2,1,0:T(8,128)(2,1)S(1)}, bf16[2,4,128,256]{3,2,1,0:T(8,128)(2,1)S(1)}, u32[]{:S(2)}, u32[]{:S(2)}) collective-permute-start(bf16[2,4,128,256]{3,2,1,0:T(8,128)(2,1)S(1)} %get-tuple-element.109), channel_id=1, source_target_pairs={{0,8},{4,12},{8,0},{12,4},{16,24},{20,28},{24,16},{28,20},{1,9},{5... | collective-permute-start | bytes 1572872 | tf_op jit(solution)/shard_map/ppermute | solution.py:356
  56.5 38.2 %collective-permute-start.21 = (bf16[4,256,768]{2,1,0:T(8,128)(2,1)S(1)}, bf16[4,256,768]{2,1,0:T(8,128)(2,1)S(1)}, u32[]{:S(2)}, u32[]{:S(2)}) collective-permute-start(bf16[4,256,768]{2,1,0:T(8,128)(2,1)S(1)} %get-tuple-element.114), channel_id=1, source_target_pairs={{0,2},{1,3},{2,0},{3,1},{4,6},{5,7},{6,4},{7,5},{8,10},{9,11},{10,... | collective-permute-start | bytes 4718600 | tf_op jit(solution)/shard_map/ppermute | solution.py:353
  59.2 1.8 %collective-permute-start.16 = (bf16[3,4,64,256]{3,2,1,0:T(8,128)(2,1)S(1)}, bf16[3,4,64,256]{3,2,1,0:T(8,128)(2,1)S(1)}, u32[]{:S(2)}, u32[]{:S(2)}) collective-permute-start(bf16[3,4,64,256]{3,2,1,0:T(8,128)(2,1)S(1)} %get-tuple-element.121), channel_id=1, source_target_pairs={{0,4},{4,0},{8,12},{12,8},{16,20},{20,16},{24,28},{28,24},{1,5},{5... | collective-permute-start | bytes 1179656 | tf_op jit(solution)/shard_map/ppermute | solution.py:359
  59.3 2.3 %collective-permute-start.17 = (bf16[3,4,64,256]{3,2,1,0:T(8,128)(2,1)S(1)}, bf16[3,4,64,256]{3,2,1,0:T(8,128)(2,1)S(1)}, u32[]{:S(2)}, u32[]{:S(2)}) collective-permute-start(bf16[3,4,64,256]{3,2,1,0:T(8,128)(2,1)S(1)} %get-tuple-element.122), channel_id=1, source_target_pairs={{0,4},{4,0},{8,12},{12,8},{16,20},{20,16},{24,28},{28,24},{1,5},{5... | collective-permute-start | bytes 1179656 | tf_op jit(solution)/shard_map/ppermute | solution.py:359
  62.3 12.7 %collective-permute-start.20 = (bf16[3,128,256]{2,1,0:T(8,128)(2,1)S(1)}, bf16[3,128,256]{2,1,0:T(8,128)(2,1)S(1)}, u32[]{:S(2)}, u32[]{:S(2)}) collective-permute-start(bf16[3,128,256]{2,1,0:T(8,128)(2,1)S(1)} %get-tuple-element.130), channel_id=1, source_target_pairs={{0,8},{4,12},{8,0},{12,4},{16,24},{20,28},{24,16},{28,20},{1,9},{5... | collective-permute-start | bytes 589832 | tf_op jit(solution)/shard_map/ppermute | solution.py:356
  69.0 17.0 %collective-permute-start.19 = (bf16[4,128,256]{2,1,0:T(8,128)(2,1)S(1)}, bf16[4,128,256]{2,1,0:T(8,128)(2,1)S(1)}, u32[]{:S(2)}, u32[]{:S(2)}) collective-permute-start(bf16[4,128,256]{2,1,0:T(8,128)(2,1)S(1)} %get-tuple-element.125), channel_id=1, source_target_pairs={{0,16},{4,20},{8,24},{12,28},{16,0},{20,4},{24,8},{28,12},{1,17},{... | collective-permute-start | bytes 786440 | tf_op jit(solution)/shard_map/ppermute | solution.py:356
  74.7 18.1 %collective-permute-start.22 = (bf16[3,128,256]{2,1,0:T(8,128)(2,1)S(1)}, bf16[3,128,256]{2,1,0:T(8,128)(2,1)S(1)}, u32[]{:S(2)}, u32[]{:S(2)}) collective-permute-start(bf16[3,128,256]{2,1,0:T(8,128)(2,1)S(1)} %get-tuple-element.136), channel_id=1, source_target_pairs={{0,8},{4,12},{8,0},{12,4},{16,24},{20,28},{24,16},{28,20},{1,9},{5... | collective-permute-start | bytes 589832 | tf_op jit(solution)/shard_map/ppermute | solution.py:356
  75.5 17.3 %collective-permute-start.23 = (bf16[3,128,256]{2,1,0:T(8,128)(2,1)S(1)}, bf16[3,128,256]{2,1,0:T(8,128)(2,1)S(1)}, u32[]{:S(2)}, u32[]{:S(2)}) collective-permute-start(bf16[3,128,256]{2,1,0:T(8,128)(2,1)S(1)} %shard_map.93), channel_id=1, source_target_pairs={{0,16},{4,20},{8,24},{12,28},{16,0},{20,4},{24,8},{28,12},{1,17},{... | collective-permute-start | bytes 589832 | tf_op jit(solution)/shard_map/ppermute | solution.py:356
  86.6 10.1 %collective-permute-start.25 = (bf16[4,128,256]{2,1,0:T(8,128)(2,1)S(1)}, bf16[4,128,256]{2,1,0:T(8,128)(2,1)S(1)}, u32[]{:S(2)}, u32[]{:S(2)}) collective-permute-start(bf16[4,128,256]{2,1,0:T(8,128)(2,1)S(1)} %shard_map.94), channel_id=1, source_target_pairs={{0,0},{1,8},{2,2},{3,10},{4,4},{5,12},{6,6},{7,14},{8,1},{9,9},{10... | collective-permute-start | bytes 786440 | tf_op jit(solution)/shard_map/ppermute | solution.py:660
  94.2 5.0 %collective-permute-start.24 = (bf16[2,128,256]{2,1,0:T(8,128)(2,1)S(1)}, bf16[2,128,256]{2,1,0:T(8,128)(2,1)S(1)}, u32[]{:S(2)}, u32[]{:S(2)}) collective-permute-start(bf16[2,128,256]{2,1,0:T(8,128)(2,1)S(1)} %get-tuple-element.141), channel_id=1, source_target_pairs={{0,2},{1,3},{2,0},{3,1},{4,6},{5,7},{6,4},{7,5},{8,10},{9,11},{10,... | collective-permute-start | bytes 393224 | tf_op jit(solution)/shard_map/ppermute | solution.py:353

commit v8 on v7

--- a/solution.py
+++ b/solution.py
@@ -323,8 +323,9 @@
         up_ref[:, :, lanes] = mine.reshape(*up_ref.shape[:2], width)
 
 
-def place_near_body(place, got_ref, held_ref, up_ref):
+def place_body(place, got_ref, home_ref, held_ref, up_ref, down_ref):
     up_ref[...] = got_ref[0].astype(F32).reshape(up_ref.shape)
+    down_ref[...] = home_ref[...].astype(F32)
 
 
 def square_device(features, cotangent, up_blocks, down_blocks):
@@ -642,7 +643,10 @@
     send_u = up_again(mine_u, far_u)
     last_u = send_z(send_u, 2)
 
-    got_d = after((got_d,), send_u)[0]
+    got_out = after((got_out,), send_u)[0]
+    outputs = added(own_out, got_out)
+
+    got_d = after((got_d,), outputs)[0]
     sum_d = call(
         functools.partial(down_sum_body, factor),
         place,
@@ -659,10 +663,7 @@
         swaps.append((device, home))
     home_d = lax.ppermute(sum_d, ("dp", "tensor"), swaps)
 
-    got_out = after((got_out,), sum_d)[0]
-    outputs = added(own_out, got_out)
-
-    got_u, last_u = after((got_u, last_u), outputs)
+    got_u, last_u = after((got_u, last_u), sum_d)
     send_u, held = call(
         functools.partial(up_sum_body, factor),
         place,
@@ -678,15 +679,15 @@
 
     got_grads = after((got_grads,), held)[0]
     feature_grads = added(own_grads, got_grads)
-    down_grads = after((home_d,), feature_grads)[0].astype(F32)
-
-    got_u = after((got_u,), down_grads)[0]
-    up_grads = call(
-        place_near_body,
+    got_u, home_d = after((got_u, home_d), feature_grads)
+    pair_d = (local // 2,) + shard[3:]
+    up_grads, down_grads = call(
+        place_body,
         place,
         (2,),
         [
             (got_u, (1,) + shard_u[1:], lambda a, p: (a, 0, 0)),
+            (home_d, pair_d, lambda a, p: (a, 0, 0)),
             (held, None, None),
         ],
         [
@@ -695,11 +696,12 @@
                 F32,
                 (local, feat // n_dp, rows),
                 lambda a, p: (0, 0, p[0] ^ 2 ^ a),
-            )
+            ),
+            ((local,) + shard[3:], F32, pair_d, lambda a, p: (a, 0, 0)),
         ],
         8,
-        alias={2: 0},
-    )[0]
+        alias={3: 0},
+    )
     wide = (local * feat, tokens)
     return (outputs.reshape(wide), feature_grads.reshape(wide), up_grads, down_grads)
 

time: 101 us -> 102 us (level)
  waiting for transfers between devices: 31.4 us -> 34.3 us
    ppermute x9, waiting for transfers between devices: 5.82 us -> 18.1 us  [send(): lax.ppermute(value, 'tensor', [(t, t ^ hop) for t in range(n_tensor)])]
    ppermute x9, waiting for transfers between devices: 22.4 us -> 12.3 us  [send_z(): return lax.ppermute(value, 'dp', [(d, d ^ 2 * hop) for d in range(n_dp)])]
    ppermute x1, starting transfers between devices: 4.3 us -> 3.28 us  [square_device(): home_d = lax.ppermute(sum_d, ('dp', 'tensor'), swaps)]
  transfers between devices with their start and end apart: 26 -> 26, of which waited for: 11 -> 12; matrix products, arithmetic and copies ran while one was open for 2% -> 1% of each run, Pallas kernels for 35% -> 35%
where the time goes in v8:
time: 102 us
  Pallas kernels  39 us (38%)
  waiting for transfers between devices  34.3 us (34%)
  starting transfers between devices  24.9 us (24%)
  local copies, waits for them, and re-layouts  2.33 us (2%)
    pallas_call x24, Pallas kernels, call(): pl.pallas_call(body, grid_spec=pltpu.PrefetchScalarGridSpec(num_scalar_pr...  39 us
    ppermute x9, waiting for transfers between devices, send(): lax.ppermute(value, 'tensor', [(t, t ^ hop) for t in range(n_tensor)])  18.1 us
    ppermute x9, waiting for transfers between devices, send_z(): return lax.ppermute(value, 'dp', [(d, d ^ 2 * hop) for d in range(n_dp)])  12.3 us
    ppermute x9, starting transfers between devices, send_z(): return lax.ppermute(value, 'dp', [(d, d ^ 2 * hop) for d in range(n_dp)])  10.6 us
    ppermute x9, starting transfers between devices, send(): lax.ppermute(value, 'tensor', [(t, t ^ hop) for t in range(n_tensor)])  9.35 us
    ppermute x1, starting transfers between devices, square_device(): home_d = lax.ppermute(sum_d, ('dp', 'tensor'), swaps)  3.28 us
    ppermute x7, waiting for transfers between devices, send_core(): return lax.ppermute(value, 'dp', [(d, d ^ 1) for d in range(n_dp)])  3.24 us
  transfers between devices with their start and end apart: 26, of which 12 were waited for; matrix products, arithmetic and copies ran while one was open for 1% of the time, Pallas kernels for 35%

profile of v8, /device:TPU:12, one launch (start us, length us, event | category | flops | bytes accessed | tf_op | source)
XLA Modules:
  0.0 101.6 jit_solution(7860861418968976301)
XLA Ops:
  3.4 1.6 %collective-permute-start.1 = (bf16[2,4,64,256]{3,2,1,0:T(8,128)(2,1)S(1)}, bf16[2,4,64,256]{3,2,1,0:T(8,128)(2,1)S(1)}, u32[]{:S(2)}, u32[]{:S(2)}) collective-permute-start(bf16[2,4,64,256]{3,2,1,0:T(8,128)(2,1)S(1)} %pad_maximum_fusion.2), channel_id=1, source_target_pairs={{0,1},{1,0},{2,3},{3,2},{4,5},{5,4},{6,7},{7,6},{8,9},{9,8},{10,11... | collective-permute-start | bytes 786440 | tf_op jit(solution)/shard_map/ppermute | solution.py:354
  5.2 1.6 %collective-permute-start.3 = (bf16[2,256,768]{2,1,0:T(8,128)(2,1)S(1)}, bf16[2,256,768]{2,1,0:T(8,128)(2,1)S(1)}, u32[]{:S(2)}, u32[]{:S(2)}) collective-permute-start(bf16[2,256,768]{2,1,0:T(8,128)(2,1)S(1)} %bitcast.45), channel_id=1, source_target_pairs={{0,2},{1,3},{2,0},{3,1},{4,6},{5,7},{6,4},{7,5},{8,10},{9,11},{10,... | collective-permute-start | bytes 2359304 | tf_op jit(solution)/shard_map/ppermute | solution.py:354
  6.8 1.2 %collective-permute-start.4 = (bf16[2,256,768]{2,1,0:T(8,128)(2,1)S(1)}, bf16[2,256,768]{2,1,0:T(8,128)(2,1)S(1)}, u32[]{:S(2)}, u32[]{:S(2)}) collective-permute-start(bf16[2,256,768]{2,1,0:T(8,128)(2,1)S(1)} %bitcast.44), channel_id=1, source_target_pairs={{0,1},{1,0},{2,3},{3,2},{4,5},{5,4},{6,7},{7,6},{8,9},{9,8},{10,11... | collective-permute-start | bytes 2359304 | tf_op jit(solution)/shard_map/ppermute | solution.py:354
  8.1 5.8 %shard_map.75 = (bf16[2,4,4,64,768]{4,3,2,1,0:T(8,128)(2,1)S(1)}, bf16[2,4,4,64,768]{4,3,2,1,0:T(8,128)(2,1)S(1)}) custom-call(s32[3]{0:T(128)S(1)} %pad_add_fusion.place, bf16[4,256,768]{2,1,0:T(8,128)(2,1)S(1)} %bitcast.37, bf16[4,256,1024]{2,1,0:T(8,128)(2,1)S(1)} %copy-done.3), custom_call_target="tpu_custom_call" | custom-call | tf_op jit(solution)/shard_map/pallas_call | solution.py:74
  15.0 1.3 %collective-permute-start.6 = (bf16[2,256,768]{2,1,0:T(8,128)(2,1)S(1)}, bf16[2,256,768]{2,1,0:T(8,128)(2,1)S(1)}, u32[]{:S(2)}, u32[]{:S(2)}) collective-permute-start(bf16[2,256,768]{2,1,0:T(8,128)(2,1)S(1)} %bitcast.42), channel_id=1, source_target_pairs={{0,1},{1,0},{2,3},{3,2},{4,5},{5,4},{6,7},{7,6},{8,9},{9,8},{10,11... | collective-permute-start | bytes 2359304 | tf_op jit(solution)/shard_map/ppermute | solution.py:354
  17.4 1.6 %shard_map.77 = (bf16[2,4,128,256]{3,2,1,0:T(8,128)(2,1)S(1)}, bf16[2,4,128,256]{3,2,1,0:T(8,128)(2,1)S(1)}) custom-call(s32[3]{0:T(128)S(1)} %pad_add_fusion.place, bf16[4,256,768]{2,1,0:T(8,128)(2,1)S(1)} %bitcast.33, bf16[2,4,4,64,768]{4,3,2,1,0:T(8,128)(2,1)S(1)} %get-tuple-element.129.refs_1_.refs_3_, bf16[4,256,768]{2,1,0:T(8,128)(2,1)S(1)} %bitcast.38, ...), custom_call_target="tpu_custom_call" | custom-call | tf_op jit(solution)/shard_map/pallas_call | solution.py:74
  19.0 7.9 %collective-permute-done.2.refs_1_ = bf16[2,2,4,64,256]{4,3,2,1,0:T(8,128)(2,1)S(1)} collective-permute-done((bf16[2,2,4,64,256]{4,3,2,1,0:T(8,128)(2,1)S(1)}, bf16[2,2,4,64,256]{4,3,2,1,0:T(8,128)(2,1)S(1)}, u32[]{:S(2)}, u32[]{:S(2)}) %collective-permute-start.2) | collective-permute-done | bytes 524320 | tf_op jit(solution)/shard_map/ppermute | solution.py:357
  27.9 1.6 %collective-permute-done.4.refs_1_ = bf16[2,256,768]{2,1,0:T(8,128)(2,1)S(1)} collective-permute-done((bf16[2,256,768]{2,1,0:T(8,128)(2,1)S(1)}, bf16[2,256,768]{2,1,0:T(8,128)(2,1)S(1)}, u32[]{:S(2)}, u32[]{:S(2)}) %collective-permute-start.4) | collective-permute-done | bytes 786464 | tf_op jit(solution)/shard_map/ppermute | solution.py:354
  30.1 1.4 %collective-permute-done.5.refs_0_.first_got = bf16[2,4,128,256]{3,2,1,0:T(8,128)(2,1)S(1)} collective-permute-done((bf16[2,4,128,256]{3,2,1,0:T(8,128)(2,1)S(1)}, bf16[2,4,128,256]{3,2,1,0:T(8,128)(2,1)S(1)}, u32[]{:S(2)}, u32[]{:S(2)}) %collective-permute-start.5) | collective-permute-done | bytes 524320 | tf_op jit(solution)/shard_map/ppermute | solution.py:360
  32.2 2.0 %collective-permute-start.7 = (bf16[1,128,256]{2,1,0:T(8,128)(2,1)S(1)}, bf16[1,128,256]{2,1,0:T(8,128)(2,1)S(1)}, u32[]{:S(2)}, u32[]{:S(2)}) collective-permute-start(bf16[1,128,256]{2,1,0:T(8,128)(2,1)S(1)} %get-tuple-element.90), channel_id=1, source_target_pairs={{0,8},{4,12},{8,0},{12,4},{16,24},{20,28},{24,16},{28,20},{1,9},{5... | collective-permute-start | bytes 196616 | tf_op jit(solution)/shard_map/ppermute | solution.py:357
  34.9 3.1 %shard_map.80 = (bf16[2,4,2,64,768]{4,3,2,1,0:T(8,128)(2,1)S(1)}, bf16[2,4,2,64,768]{4,3,2,1,0:T(8,128)(2,1)S(1)}) custom-call(s32[3]{0:T(128)S(1)} %pad_add_fusion.place, bf16[2,256,768]{2,1,0:T(8,128)(2,1)S(1)} %collective-permute-done.3.x_ref.refs_1_, bf16[2,2,4,256,256]{4,3,2,1,0:T(8,128)(2,1)S(1)} %bitcast.22), custom_call_target="tpu_custom_call" | custom-call | tf_op jit(solution)/shard_map/pallas_call | solution.py:74
  39.5 2.7 %collective-permute-start.11 = (bf16[1,128,256]{2,1,0:T(8,128)(2,1)S(1)}, bf16[1,128,256]{2,1,0:T(8,128)(2,1)S(1)}, u32[]{:S(2)}, u32[]{:S(2)}) collective-permute-start(bf16[1,128,256]{2,1,0:T(8,128)(2,1)S(1)} %shard_map.82), channel_id=1, source_target_pairs={{0,16},{4,20},{8,24},{12,28},{16,0},{20,4},{24,8},{28,12},{1,17},{... | collective-permute-start | bytes 196616 | tf_op jit(solution)/shard_map/ppermute | solution.py:357
  42.1 1.5 %collective-permute-done.12.x_ref.refs_2_ = bf16[2,256,768]{2,1,0:T(8,128)(2,1)S(1)} collective-permute-done((bf16[2,256,768]{2,1,0:T(8,128)(2,1)S(1)}, bf16[2,256,768]{2,1,0:T(8,128)(2,1)S(1)}, u32[]{:S(2)}, u32[]{:S(2)}) %collective-permute-start.12) | collective-permute-done | bytes 786464 | tf_op jit(solution)/shard_map/ppermute | solution.py:354
  43.6 3.1 %shard_map.83 = (bf16[2,4,2,64,768]{4,3,2,1,0:T(8,128)(2,1)S(1)}, bf16[2,4,2,64,768]{4,3,2,1,0:T(8,128)(2,1)S(1)}) custom-call(s32[3]{0:T(128)S(1)} %pad_add_fusion.place, bf16[2,256,768]{2,1,0:T(8,128)(2,1)S(1)} %collective-permute-done.12.x_ref.refs_2_, bf16[2,2,4,256,256]{4,3,2,1,0:T(8,128)(2,1)S(1)} %bitcast.23), custom_call_target="tpu_custom_call" | custom-call | tf_op jit(solution)/shard_map/pallas_call | solution.py:74
  46.8 2.0 %shard_map.84 = (bf16[4,128,256]{2,1,0:T(8,128)(2,1)S(1)}, bf16[2,4,128,256]{3,2,1,0:T(8,128)(2,1)S(1)}, bf16[3,4,128,256]{3,2,1,0:T(8,128)(2,1)S(1)}) custom-call(s32[3]{0:T(128)S(1)} %pad_add_fusion.place, bf16[4,256,768]{2,1,0:T(8,128)(2,1)S(1)} %bitcast.35, bf16[2,256,768]{2,1,0:T(8,128)(2,1)S(1)} %collective-permute-done.4.refs_1_, ...), custom_call_target="tpu_custom_call" | custom-call | tf_op jit(solution)/shard_map/pallas_call | solution.py:74
  49.4 1.5 %shard_map.85 = bf16[4,256,768]{2,1,0:T(8,128)(2,1)S(1)} custom-call(s32[3]{0:T(128)S(1)} %pad_add_fusion.place, bf16[2,2,4,256,256]{4,3,2,1,0:T(8,128)(2,1)S(1)} %bitcast.24, bf16[2,2,4,256,256]{4,3,2,1,0:T(8,128)(2,1)S(1)} %bitcast.25, bf16[2,2,4,256,256]{4,3,2,1,0:T(8,128)(2,1)S(1)} %bitcast.26, ...), custom_call_target="tpu_custom_call" | custom-call | tf_op jit(solution)/shard_map/pallas_call | solution.py:74
  50.9 1.6 %collective-permute-start.18 = (bf16[4,256,768]{2,1,0:T(8,128)(2,1)S(1)}, bf16[4,256,768]{2,1,0:T(8,128)(2,1)S(1)}, u32[]{:S(2)}, u32[]{:S(2)}) collective-permute-start(bf16[4,256,768]{2,1,0:T(8,128)(2,1)S(1)} %shard_map.85), channel_id=1, source_target_pairs={{0,1},{1,0},{2,3},{3,2},{4,5},{5,4},{6,7},{7,6},{8,9},{9,8},{10,11... | collective-permute-start | bytes 4718600 | tf_op jit(solution)/shard_map/ppermute | solution.py:354
  54.0 2.6 %shard_map.87 = (bf16[4,4,64,768]{3,2,1,0:T(8,128)(2,1)S(1)}, bf16[4,2,64,768]{3,2,1,0:T(8,128)(2,1)S(1)}, bf16[4,2,64,768]{3,2,1,0:T(8,128)(2,1)S(1)}, bf16[4,2...) custom-call(s32[3]{0:T(128)S(1)} %pad_add_fusion.place, bf16[4,256,768]{2,1,0:T(8,128)(2,1)S(1)} %bitcast.36, ...), custom_call_target="tpu_custom_call" | custom-call | tf_op jit(solution)/shard_map/pallas_call | solution.py:74
  57.1 2.1 %shard_map.88 = (bf16[3,4,64,256]{3,2,1,0:T(8,128)(2,1)S(1)}, bf16[3,4,64,256]{3,2,1,0:T(8,128)(2,1)S(1)}, bf16[3,4,128,256]{3,2,1,0:T(8,128)(2,1)S(1)}) custom-call(s32[3]{0:T(128)S(1)} %pad_add_fusion.place, bf16[4,256,768]{2,1,0:T(8,128)(2,1)S(1)} %bitcast.39, bf16[2,256,768]{2,1,0:T(8,128)(2,1)S(1)} %collective-permute-done.3.x_ref.refs_1_, ...), custom_call_target="tpu_custom_call" | custom-call | flops 16000000000 | tf_op jit(solution)/shard_map/pallas_call | solution.py:74
  59.8 1.2 %collective-permute-done.16.refs_0_ = bf16[3,4,64,256]{3,2,1,0:T(8,128)(2,1)S(1)} collective-permute-done((bf16[3,4,64,256]{3,2,1,0:T(8,128)(2,1)S(1)}, bf16[3,4,64,256]{3,2,1,0:T(8,128)(2,1)S(1)}, u32[]{:S(2)}, u32[]{:S(2)}) %collective-permute-start.16) | collective-permute-done | bytes 393248 | tf_op jit(solution)/shard_map/ppermute | solution.py:360
  62.3 1.6 %collective-permute-start.19 = (bf16[3,128,256]{2,1,0:T(8,128)(2,1)S(1)}, bf16[3,128,256]{2,1,0:T(8,128)(2,1)S(1)}, u32[]{:S(2)}, u32[]{:S(2)}) collective-permute-start(bf16[3,128,256]{2,1,0:T(8,128)(2,1)S(1)} %get-tuple-element.131), channel_id=1, source_target_pairs={{0,8},{4,12},{8,0},{12,4},{16,24},{20,28},{24,16},{28,20},{1,9},{5... | collective-permute-start | bytes 589832 | tf_op jit(solution)/shard_map/ppermute | solution.py:357
  63.9 4.4 %collective-permute-done.15.got_ref = bf16[2,4,128,256]{3,2,1,0:T(8,128)(2,1)S(1)} collective-permute-done((bf16[2,4,128,256]{3,2,1,0:T(8,128)(2,1)S(1)}, bf16[2,4,128,256]{3,2,1,0:T(8,128)(2,1)S(1)}, u32[]{:S(2)}, u32[]{:S(2)}) %collective-permute-start.15) | collective-permute-done | bytes 524320 | tf_op jit(solution)/shard_map/ppermute | solution.py:357
  69.0 2.6 %collective-permute-start.23 = (bf16[4,128,256]{2,1,0:T(8,128)(2,1)S(1)}, bf16[4,128,256]{2,1,0:T(8,128)(2,1)S(1)}, u32[]{:S(2)}, u32[]{:S(2)}) collective-permute-start(bf16[4,128,256]{2,1,0:T(8,128)(2,1)S(1)} %get-tuple-element.127), channel_id=1, source_target_pairs={{0,16},{4,20},{8,24},{12,28},{16,0},{20,4},{24,8},{28,12},{1,17},{... | collective-permute-start | bytes 786440 | tf_op jit(solution)/shard_map/ppermute | solution.py:357
  71.6 1.5 %shard_map.91.own_ref = f32[4,256,768]{2,1,0:T(8,128)S(1)} custom-call(s32[3]{0:T(128)S(1)} %pad_add_fusion.place, bf16[4,256,1024]{2,1,0:T(8,128)(2,1)S(1)} %copy-done.3, bf16[4,256,1024]{2,1,0:T(8,128)(2,1)S(1)} %copy-done.3, bf16[4,4,64,768]{3,2,1,0:T(8,128)(2,1)S(1)} %shard_map.76.refs_3_.refs_2_, bf16[4,4,64,768]{3,2,1,0:T(8,128)(2,1)S(1)} %get-tuple-element.118.refs_3_), custom_call_target="tpu_custom_call" | custom-call | flops 4000000000 | tf_op jit(solution)/shard_map/pallas_call | solution.py:74
  73.2 1.5 %shard_map.92.own_ref = f32[4,256,768]{2,1,0:T(8,128)S(1)} custom-call(s32[3]{0:T(128)S(1)} %pad_add_fusion.place, bf16[4,1024,256]{2,1,0:T(8,128)(2,1)S(1)} %copy-done, bf16[4,1024,256]{2,1,0:T(8,128)(2,1)S(1)} %copy-done, bf16[4,1024,256]{2,1,0:T(8,128)(2,1)S(1)} %copy-done, bf16[2,4,4,64,768]{4,3,2,1,0:T(8,128)(2,1)S(1)} %get-tuple-element.129.refs_1_.refs_3_, ...), custom_call_target="tpu_custom_call" | custom-call | tf_op jit(solution)/shard_map/pallas_call | solution.py:74
  75.9 11.4 %collective-permute-done.18.got_ref = bf16[4,256,768]{2,1,0:T(8,128)(2,1)S(1)} collective-permute-done((bf16[4,256,768]{2,1,0:T(8,128)(2,1)S(1)}, bf16[4,256,768]{2,1,0:T(8,128)(2,1)S(1)}, u32[]{:S(2)}, u32[]{:S(2)}) %collective-permute-start.18) | collective-permute-done | bytes 1572896 | tf_op jit(solution)/shard_map/ppermute | solution.py:354
  87.4 1.9 %shard_map.94 = bf16[4,256,768]{2,1,0:T(8,128)(2,1)} custom-call(s32[3]{0:T(128)S(1)} %pad_add_fusion.place, f32[4,256,768]{2,1,0:T(8,128)S(1)} %shard_map.92.own_ref, bf16[4,256,768]{2,1,0:T(8,128)(2,1)S(1)} %collective-permute-done.18.got_ref), custom_call_target="tpu_custom_call" | custom-call | tf_op jit(solution)/shard_map/pallas_call | solution.py:74
  89.9 3.3 %collective-permute-start.25 = (bf16[4,128,256]{2,1,0:T(8,128)(2,1)S(1)}, bf16[4,128,256]{2,1,0:T(8,128)(2,1)S(1)}, u32[]{:S(2)}, u32[]{:S(2)}) collective-permute-start(bf16[4,128,256]{2,1,0:T(8,128)(2,1)S(1)} %shard_map.95), channel_id=1, source_target_pairs={{0,0},{1,8},{2,2},{3,10},{4,4},{5,12},{6,6},{7,14},{8,1},{9,9},{10... | collective-permute-start | bytes 786440 | tf_op jit(solution)/shard_map/ppermute | solution.py:664
  93.2 1.4 %shard_map.96 = (bf16[2,128,256]{2,1,0:T(8,128)(2,1)S(1)}, f32[4,32,1024]{2,1,0:T(8,128)}) custom-call(s32[3]{0:T(128)S(1)} %pad_add_fusion.place, f32[2,1,128,256]{3,2,1,0:T(8,128)S(1)} %get-tuple-element.89.mine_ref.refs_0_, bf16[1,128,256]{2,1,0:T(8,128)(2,1)S(1)} %collective-permute-done.7.refs_1_, ...), custom_call_target="tpu_custom_call" | custom-call | tf_op jit(solution)/shard_map/pallas_call | solution.py:74
  95.1 1.9 %shard_map.97 = bf16[4,256,768]{2,1,0:T(8,128)(2,1)} custom-call(s32[3]{0:T(128)S(1)} %pad_add_fusion.place, f32[4,256,768]{2,1,0:T(8,128)S(1)} %shard_map.91.own_ref, bf16[4,256,768]{2,1,0:T(8,128)(2,1)S(1)} %collective-permute-done.20.got_ref), custom_call_target="tpu_custom_call" | custom-call | tf_op jit(solution)/shard_map/pallas_call | solution.py:74
  97.0 2.5 %collective-permute-done.24.got_ref = bf16[2,128,256]{2,1,0:T(8,128)(2,1)S(1)} collective-permute-done((bf16[2,128,256]{2,1,0:T(8,128)(2,1)S(1)}, bf16[2,128,256]{2,1,0:T(8,128)(2,1)S(1)}, u32[]{:S(2)}, u32[]{:S(2)}) %collective-permute-start.24) | collective-permute-done | bytes 131104 | tf_op jit(solution)/shard_map/ppermute | solution.py:354
  100.2 1.5 %shard_map.98 = (f32[4,32,1024]{2,1,0:T(8,128)}, f32[4,128,256]{2,1,0:T(8,128)}) custom-call(s32[3]{0:T(128)S(1)} %pad_add_fusion.place, bf16[2,128,256]{2,1,0:T(8,128)(2,1)S(1)} %collective-permute-done.24.got_ref, bf16[4,128,256]{2,1,0:T(8,128)(2,1)S(1)} %collective-permute-done.25.home_ref, ...), custom_call_target="tpu_custom_call", output_to_operand_aliasing={{0}: (3, {})} | custom-call | tf_op jit(solution)/shard_map/pallas_call | solution.py:74
  (60 shorter events, 17.7 us)
Async XLA Ops:
  0.6 4.4 %copy-start.2 = (bf16[1024,768]{1,0:T(8,128)(2,1)S(1)}, bf16[1024,768]{1,0:T(8,128)(2,1)}, u32[]{:S(2)}) copy-start(bf16[1024,768]{1,0:T(8,128)(2,1)} %param.4) | copy-start | bytes 4718596
  1.8 12.1 %collective-permute-start = (bf16[2,4,64,256]{3,2,1,0:T(8,128)(2,1)S(1)}, bf16[2,4,64,256]{3,2,1,0:T(8,128)(2,1)S(1)}, u32[]{:S(2)}, u32[]{:S(2)}) collective-permute-start(bf16[2,4,64,256]{3,2,1,0:T(8,128)(2,1)S(1)} %pad_maximum_fusion.1), channel_id=1, source_target_pairs={{0,2},{1,3},{2,0},{3,1},{4,6},{5,7},{6,4},{7,5},{8,10},{9,11},{10,... | collective-permute-start | bytes 786440 | tf_op jit(solution)/shard_map/ppermute | solution.py:354
  3.4 1.7 %copy-start.1 = (bf16[1024,768]{1,0:T(8,128)(2,1)S(1)}, bf16[1024,768]{1,0:T(8,128)(2,1)}, u32[]{:S(2)}) copy-start(bf16[1024,768]{1,0:T(8,128)(2,1)} %param.5) | copy-start | bytes 4718596
  3.4 10.5 %collective-permute-start.1 = (bf16[2,4,64,256]{3,2,1,0:T(8,128)(2,1)S(1)}, bf16[2,4,64,256]{3,2,1,0:T(8,128)(2,1)S(1)}, u32[]{:S(2)}, u32[]{:S(2)}) collective-permute-start(bf16[2,4,64,256]{3,2,1,0:T(8,128)(2,1)S(1)} %pad_maximum_fusion.2), channel_id=1, source_target_pairs={{0,1},{1,0},{2,3},{3,2},{4,5},{5,4},{6,7},{7,6},{8,9},{9,8},{10,11... | collective-permute-start | bytes 786440 | tf_op jit(solution)/shard_map/ppermute | solution.py:354
  5.1 3.0 %copy-start.3 = (bf16[4,256,1024]{2,1,0:T(8,128)(2,1)S(1)}, bf16[4,256,1024]{2,1,0:T(8,128)(2,1)}, u32[]{:S(2)}) copy-start(bf16[4,256,1024]{2,1,0:T(8,128)(2,1)} %refs_1_.5) | copy-start | bytes 6291460
  5.2 22.7 %collective-permute-start.3 = (bf16[2,256,768]{2,1,0:T(8,128)(2,1)S(1)}, bf16[2,256,768]{2,1,0:T(8,128)(2,1)S(1)}, u32[]{:S(2)}, u32[]{:S(2)}) collective-permute-start(bf16[2,256,768]{2,1,0:T(8,128)(2,1)S(1)} %bitcast.45), channel_id=1, source_target_pairs={{0,2},{1,3},{2,0},{3,1},{4,6},{5,7},{6,4},{7,5},{8,10},{9,11},{10,... | collective-permute-start | bytes 2359304 | tf_op jit(solution)/shard_map/ppermute | solution.py:354
  6.8 22.8 %collective-permute-start.4 = (bf16[2,256,768]{2,1,0:T(8,128)(2,1)S(1)}, bf16[2,256,768]{2,1,0:T(8,128)(2,1)S(1)}, u32[]{:S(2)}, u32[]{:S(2)}) collective-permute-start(bf16[2,256,768]{2,1,0:T(8,128)(2,1)S(1)} %bitcast.44), channel_id=1, source_target_pairs={{0,1},{1,0},{2,3},{3,2},{4,5},{5,4},{6,7},{7,6},{8,9},{9,8},{10,11... | collective-permute-start | bytes 2359304 | tf_op jit(solution)/shard_map/ppermute | solution.py:354
  8.1 8.2 %copy-start = (bf16[4,1024,256]{2,1,0:T(8,128)(2,1)S(1)}, bf16[4,1024,256]{2,1,0:T(8,128)(2,1)}, u32[]{:S(2)}) copy-start(bf16[4,1024,256]{2,1,0:T(8,128)(2,1)} %refs_2_.1) | copy-start | bytes 6291460
  14.0 12.9 %collective-permute-start.2 = (bf16[2,2,4,64,256]{4,3,2,1,0:T(8,128)(2,1)S(1)}, bf16[2,2,4,64,256]{4,3,2,1,0:T(8,128)(2,1)S(1)}, u32[]{:S(2)}, u32[]{:S(2)}) collective-permute-start(bf16[2,2,4,64,256]{4,3,2,1,0:T(8,128)(2,1)S(1)} %pad_maximum_fusion.refs_0_), channel_id=1, source_target_pairs={{0,8},{4,12},{8,0},{12,4},{16,24},{20,28},{24,16},{28,20},{1,9},{5... | collective-permute-start | bytes 1572872 | tf_op jit(solution)/shard_map/ppermute | solution.py:357
  14.5 29.1 %collective-permute-start.12 = (bf16[2,256,768]{2,1,0:T(8,128)(2,1)S(1)}, bf16[2,256,768]{2,1,0:T(8,128)(2,1)S(1)}, u32[]{:S(2)}, u32[]{:S(2)}) collective-permute-start(bf16[2,256,768]{2,1,0:T(8,128)(2,1)S(1)} %bitcast.43), channel_id=1, source_target_pairs={{0,2},{1,3},{2,0},{3,1},{4,6},{5,7},{6,4},{7,5},{8,10},{9,11},{10,... | collective-permute-start | bytes 2359304 | tf_op jit(solution)/shard_map/ppermute | solution.py:354
  15.0 31.7 %collective-permute-start.6 = (bf16[2,256,768]{2,1,0:T(8,128)(2,1)S(1)}, bf16[2,256,768]{2,1,0:T(8,128)(2,1)S(1)}, u32[]{:S(2)}, u32[]{:S(2)}) collective-permute-start(bf16[2,256,768]{2,1,0:T(8,128)(2,1)S(1)} %bitcast.42), channel_id=1, source_target_pairs={{0,1},{1,0},{2,3},{3,2},{4,5},{5,4},{6,7},{7,6},{8,9},{9,8},{10,11... | collective-permute-start | bytes 2359304 | tf_op jit(solution)/shard_map/ppermute | solution.py:354
  29.6 1.9 %collective-permute-start.5 = (bf16[2,4,128,256]{3,2,1,0:T(8,128)(2,1)S(1)}, bf16[2,4,128,256]{3,2,1,0:T(8,128)(2,1)S(1)}, u32[]{:S(2)}, u32[]{:S(2)}) collective-permute-start(bf16[2,4,128,256]{3,2,1,0:T(8,128)(2,1)S(1)} %get-tuple-element.87), channel_id=1, source_target_pairs={{0,4},{4,0},{8,12},{12,8},{16,20},{20,16},{24,28},{28,24},{1,5},{5... | collective-permute-start | bytes 1572872 | tf_op jit(solution)/shard_map/ppermute | solution.py:360
  29.6 2.7 %collective-permute-start.9 = (bf16[2,2,4,64,256]{4,3,2,1,0:T(8,128)(2,1)S(1)}, bf16[2,2,4,64,256]{4,3,2,1,0:T(8,128)(2,1)S(1)}, u32[]{:S(2)}, u32[]{:S(2)}) collective-permute-start(bf16[2,2,4,64,256]{4,3,2,1,0:T(8,128)(2,1)S(1)} %pad_maximum_fusion.refs_0_), channel_id=1, source_target_pairs={{0,4},{4,0},{8,12},{12,8},{16,20},{20,16},{24,28},{28,24},{1,5},{5... | collective-permute-start | bytes 1572872 | tf_op jit(solution)/shard_map/ppermute | solution.py:360
  30.1 4.1 %collective-permute-start.10 = (bf16[2,2,4,64,256]{4,3,2,1,0:T(8,128)(2,1)S(1)}, bf16[2,2,4,64,256]{4,3,2,1,0:T(8,128)(2,1)S(1)}, u32[]{:S(2)}, u32[]{:S(2)}) collective-permute-start(bf16[2,2,4,64,256]{4,3,2,1,0:T(8,128)(2,1)S(1)} %collective-permute-done.2.refs_1_), channel_id=1, source_target_pairs={{0,4},{4,0},{8,12},{12,8},{16,20},{20,16},{24,28},{28,24},{1,5},{5... | collective-permute-start | bytes 1572872 | tf_op jit(solution)/shard_map/ppermute | solution.py:360
  32.1 6.8 %collective-permute-start.8 = (bf16[1,128,256]{2,1,0:T(8,128)(2,1)S(1)}, bf16[1,128,256]{2,1,0:T(8,128)(2,1)S(1)}, u32[]{:S(2)}, u32[]{:S(2)}) collective-permute-start(bf16[1,128,256]{2,1,0:T(8,128)(2,1)S(1)} %get-tuple-element.91), channel_id=1, source_target_pairs={{0,8},{4,12},{8,0},{12,4},{16,24},{20,28},{24,16},{28,20},{1,9},{5... | collective-permute-start | bytes 196616 | tf_op jit(solution)/shard_map/ppermute | solution.py:357
  32.2 6.7 %collective-permute-start.7 = (bf16[1,128,256]{2,1,0:T(8,128)(2,1)S(1)}, bf16[1,128,256]{2,1,0:T(8,128)(2,1)S(1)}, u32[]{:S(2)}, u32[]{:S(2)}) collective-permute-start(bf16[1,128,256]{2,1,0:T(8,128)(2,1)S(1)} %get-tuple-element.90), channel_id=1, source_target_pairs={{0,8},{4,12},{8,0},{12,4},{16,24},{20,28},{24,16},{28,20},{1,9},{5... | collective-permute-start | bytes 196616 | tf_op jit(solution)/shard_map/ppermute | solution.py:357
  39.5 7.2 %collective-permute-start.11 = (bf16[1,128,256]{2,1,0:T(8,128)(2,1)S(1)}, bf16[1,128,256]{2,1,0:T(8,128)(2,1)S(1)}, u32[]{:S(2)}, u32[]{:S(2)}) collective-permute-start(bf16[1,128,256]{2,1,0:T(8,128)(2,1)S(1)} %shard_map.82), channel_id=1, source_target_pairs={{0,16},{4,20},{8,24},{12,28},{16,0},{20,4},{24,8},{28,12},{1,17},{... | collective-permute-start | bytes 196616 | tf_op jit(solution)/shard_map/ppermute | solution.py:357
  48.8 3.7 %collective-permute-start.14 = (bf16[2,4,128,256]{3,2,1,0:T(8,128)(2,1)S(1)}, bf16[2,4,128,256]{3,2,1,0:T(8,128)(2,1)S(1)}, u32[]{:S(2)}, u32[]{:S(2)}) collective-permute-start(bf16[2,4,128,256]{3,2,1,0:T(8,128)(2,1)S(1)} %get-tuple-element.106), channel_id=1, source_target_pairs={{0,4},{4,0},{8,12},{12,8},{16,20},{20,16},{24,28},{28,24},{1,5},{5... | collective-permute-start | bytes 1572872 | tf_op jit(solution)/shard_map/ppermute | solution.py:360
  48.9 3.6 %collective-permute-start.13 = (bf16[4,128,256]{2,1,0:T(8,128)(2,1)S(1)}, bf16[4,128,256]{2,1,0:T(8,128)(2,1)S(1)}, u32[]{:S(2)}, u32[]{:S(2)}) collective-permute-start(bf16[4,128,256]{2,1,0:T(8,128)(2,1)S(1)} %get-tuple-element.105), channel_id=1, source_target_pairs={{0,4},{4,0},{8,12},{12,8},{16,20},{20,16},{24,28},{28,24},{1,5},{5... | collective-permute-start | bytes 786440 | tf_op jit(solution)/shard_map/ppermute | solution.py:360
  50.9 36.5 %collective-permute-start.18 = (bf16[4,256,768]{2,1,0:T(8,128)(2,1)S(1)}, bf16[4,256,768]{2,1,0:T(8,128)(2,1)S(1)}, u32[]{:S(2)}, u32[]{:S(2)}) collective-permute-start(bf16[4,256,768]{2,1,0:T(8,128)(2,1)S(1)} %shard_map.85), channel_id=1, source_target_pairs={{0,1},{1,0},{2,3},{3,2},{4,5},{5,4},{6,7},{7,6},{8,9},{9,8},{10,11... | collective-permute-start | bytes 4718600 | tf_op jit(solution)/shard_map/ppermute | solution.py:354
  53.5 14.9 %collective-permute-start.15 = (bf16[2,4,128,256]{3,2,1,0:T(8,128)(2,1)S(1)}, bf16[2,4,128,256]{3,2,1,0:T(8,128)(2,1)S(1)}, u32[]{:S(2)}, u32[]{:S(2)}) collective-permute-start(bf16[2,4,128,256]{3,2,1,0:T(8,128)(2,1)S(1)} %get-tuple-element.111), channel_id=1, source_target_pairs={{0,8},{4,12},{8,0},{12,4},{16,24},{20,28},{24,16},{28,20},{1,9},{5... | collective-permute-start | bytes 1572872 | tf_op jit(solution)/shard_map/ppermute | solution.py:357
  56.5 38.6 %collective-permute-start.20 = (bf16[4,256,768]{2,1,0:T(8,128)(2,1)S(1)}, bf16[4,256,768]{2,1,0:T(8,128)(2,1)S(1)}, u32[]{:S(2)}, u32[]{:S(2)}) collective-permute-start(bf16[4,256,768]{2,1,0:T(8,128)(2,1)S(1)} %get-tuple-element.116), channel_id=1, source_target_pairs={{0,2},{1,3},{2,0},{3,1},{4,6},{5,7},{6,4},{7,5},{8,10},{9,11},{10,... | collective-permute-start | bytes 4718600 | tf_op jit(solution)/shard_map/ppermute | solution.py:354
  59.2 1.8 %collective-permute-start.16 = (bf16[3,4,64,256]{3,2,1,0:T(8,128)(2,1)S(1)}, bf16[3,4,64,256]{3,2,1,0:T(8,128)(2,1)S(1)}, u32[]{:S(2)}, u32[]{:S(2)}) collective-permute-start(bf16[3,4,64,256]{3,2,1,0:T(8,128)(2,1)S(1)} %get-tuple-element.123), channel_id=1, source_target_pairs={{0,4},{4,0},{8,12},{12,8},{16,20},{20,16},{24,28},{28,24},{1,5},{5... | collective-permute-start | bytes 1179656 | tf_op jit(solution)/shard_map/ppermute | solution.py:360
  59.3 2.3 %collective-permute-start.17 = (bf16[3,4,64,256]{3,2,1,0:T(8,128)(2,1)S(1)}, bf16[3,4,64,256]{3,2,1,0:T(8,128)(2,1)S(1)}, u32[]{:S(2)}, u32[]{:S(2)}) collective-permute-start(bf16[3,4,64,256]{3,2,1,0:T(8,128)(2,1)S(1)} %get-tuple-element.124), channel_id=1, source_target_pairs={{0,4},{4,0},{8,12},{12,8},{16,20},{20,16},{24,28},{28,24},{1,5},{5... | collective-permute-start | bytes 1179656 | tf_op jit(solution)/shard_map/ppermute | solution.py:360
  62.3 12.7 %collective-permute-start.19 = (bf16[3,128,256]{2,1,0:T(8,128)(2,1)S(1)}, bf16[3,128,256]{2,1,0:T(8,128)(2,1)S(1)}, u32[]{:S(2)}, u32[]{:S(2)}) collective-permute-start(bf16[3,128,256]{2,1,0:T(8,128)(2,1)S(1)} %get-tuple-element.131), channel_id=1, source_target_pairs={{0,8},{4,12},{8,0},{12,4},{16,24},{20,28},{24,16},{28,20},{1,9},{5... | collective-permute-start | bytes 589832 | tf_op jit(solution)/shard_map/ppermute | solution.py:357
  69.0 20.3 %collective-permute-start.23 = (bf16[4,128,256]{2,1,0:T(8,128)(2,1)S(1)}, bf16[4,128,256]{2,1,0:T(8,128)(2,1)S(1)}, u32[]{:S(2)}, u32[]{:S(2)}) collective-permute-start(bf16[4,128,256]{2,1,0:T(8,128)(2,1)S(1)} %get-tuple-element.127), channel_id=1, source_target_pairs={{0,16},{4,20},{8,24},{12,28},{16,0},{20,4},{24,8},{28,12},{1,17},{... | collective-permute-start | bytes 786440 | tf_op jit(solution)/shard_map/ppermute | solution.py:357
  74.7 18.5 %collective-permute-start.21 = (bf16[3,128,256]{2,1,0:T(8,128)(2,1)S(1)}, bf16[3,128,256]{2,1,0:T(8,128)(2,1)S(1)}, u32[]{:S(2)}, u32[]{:S(2)}) collective-permute-start(bf16[3,128,256]{2,1,0:T(8,128)(2,1)S(1)} %get-tuple-element.136), channel_id=1, source_target_pairs={{0,8},{4,12},{8,0},{12,4},{16,24},{20,28},{24,16},{28,20},{1,9},{5... | collective-permute-start | bytes 589832 | tf_op jit(solution)/shard_map/ppermute | solution.py:357
  75.5 17.7 %collective-permute-start.22 = (bf16[3,128,256]{2,1,0:T(8,128)(2,1)S(1)}, bf16[3,128,256]{2,1,0:T(8,128)(2,1)S(1)}, u32[]{:S(2)}, u32[]{:S(2)}) collective-permute-start(bf16[3,128,256]{2,1,0:T(8,128)(2,1)S(1)} %shard_map.93), channel_id=1, source_target_pairs={{0,16},{4,20},{8,24},{12,28},{16,0},{20,4},{24,8},{28,12},{1,17},{... | collective-permute-start | bytes 589832 | tf_op jit(solution)/shard_map/ppermute | solution.py:357
  89.9 10.2 %collective-permute-start.25 = (bf16[4,128,256]{2,1,0:T(8,128)(2,1)S(1)}, bf16[4,128,256]{2,1,0:T(8,128)(2,1)S(1)}, u32[]{:S(2)}, u32[]{:S(2)}) collective-permute-start(bf16[4,128,256]{2,1,0:T(8,128)(2,1)S(1)} %shard_map.95), channel_id=1, source_target_pairs={{0,0},{1,8},{2,2},{3,10},{4,4},{5,12},{6,6},{7,14},{8,1},{9,9},{10... | collective-permute-start | bytes 786440 | tf_op jit(solution)/shard_map/ppermute | solution.py:664
  94.6 5.0 %collective-permute-start.24 = (bf16[2,128,256]{2,1,0:T(8,128)(2,1)S(1)}, bf16[2,128,256]{2,1,0:T(8,128)(2,1)S(1)}, u32[]{:S(2)}, u32[]{:S(2)}) collective-permute-start(bf16[2,128,256]{2,1,0:T(8,128)(2,1)S(1)} %get-tuple-element.143), channel_id=1, source_target_pairs={{0,2},{1,3},{2,0},{3,1},{4,6},{5,7},{6,4},{7,5},{8,10},{9,11},{10,... | collective-permute-start | bytes 393224 | tf_op jit(solution)/shard_map/ppermute | solution.py:354

commit v9 on v8

--- a/solution.py
+++ b/solution.py
@@ -643,10 +643,7 @@
     send_u = up_again(mine_u, far_u)
     last_u = send_z(send_u, 2)
 
-    got_out = after((got_out,), send_u)[0]
-    outputs = added(own_out, got_out)
-
-    got_d = after((got_d,), outputs)[0]
+    got_d = after((got_d,), send_u)[0]
     sum_d = call(
         functools.partial(down_sum_body, factor),
         place,
@@ -663,7 +660,10 @@
         swaps.append((device, home))
     home_d = lax.ppermute(sum_d, ("dp", "tensor"), swaps)
 
-    got_u, last_u = after((got_u, last_u), sum_d)
+    got_out = after((got_out,), sum_d)[0]
+    outputs = added(own_out, got_out)
+
+    got_u, last_u = after((got_u, last_u), outputs)
     send_u, held = call(
         functools.partial(up_sum_body, factor),
         place,

time: 102 us -> 101 us (level)
  waiting for transfers between devices: 34.3 us -> 32.2 us
    ppermute x9, waiting for transfers between devices: 18.1 us -> 6.65 us  [send(): lax.ppermute(value, 'tensor', [(t, t ^ hop) for t in range(n_tensor)])]
    ppermute x9, waiting for transfers between devices: 12.3 us -> 22.4 us  [send_z(): return lax.ppermute(value, 'dp', [(d, d ^ 2 * hop) for d in range(n_dp)])]
    ppermute x1, starting transfers between devices: 3.28 us -> 4.3 us  [square_device(): home_d = lax.ppermute(sum_d, ('dp', 'tensor'), swaps)]
  transfers between devices with their start and end apart: 26 -> 26, of which waited for: 12 -> 11; matrix products, arithmetic and copies ran while one was open for 1% -> 1% of each run, Pallas kernels for 35% -> 35%
where the time goes in v9:
time: 101 us
  Pallas kernels  39 us (39%)
  waiting for transfers between devices  32.2 us (32%)
  starting transfers between devices  25.9 us (26%)
  local copies, waits for them, and re-layouts  2.33 us (2%)
    pallas_call x24, Pallas kernels, call(): pl.pallas_call(body, grid_spec=pltpu.PrefetchScalarGridSpec(num_scalar_pr...  39 us
    ppermute x9, waiting for transfers between devices, send_z(): return lax.ppermute(value, 'dp', [(d, d ^ 2 * hop) for d in range(n_dp)])  22.4 us
    ppermute x9, starting transfers between devices, send_z(): return lax.ppermute(value, 'dp', [(d, d ^ 2 * hop) for d in range(n_dp)])  10.6 us
    ppermute x9, starting transfers between devices, send(): lax.ppermute(value, 'tensor', [(t, t ^ hop) for t in range(n_tensor)])  9.39 us
    ppermute x9, waiting for transfers between devices, send(): lax.ppermute(value, 'tensor', [(t, t ^ hop) for t in range(n_tensor)])  6.65 us
    ppermute x1, starting transfers between devices, square_device(): home_d = lax.ppermute(sum_d, ('dp', 'tensor'), swaps)  4.3 us
    ppermute x7, waiting for transfers between devices, send_core(): return lax.ppermute(value, 'dp', [(d, d ^ 1) for d in range(n_dp)])  3.24 us
  transfers between devices with their start and end apart: 26, of which 11 were waited for; matrix products, arithmetic and copies ran while one was open for 1% of the time, Pallas kernels for 35%

profile of v9, /device:TPU:12, one launch (start us, length us, event | category | flops | bytes accessed | tf_op | source)
XLA Modules:
  0.0 100.6 jit_solution(5691202375701774464)
XLA Ops:
  3.4 1.6 %collective-permute-start.1 = (bf16[2,4,64,256]{3,2,1,0:T(8,128)(2,1)S(1)}, bf16[2,4,64,256]{3,2,1,0:T(8,128)(2,1)S(1)}, u32[]{:S(2)}, u32[]{:S(2)}) collective-permute-start(bf16[2,4,64,256]{3,2,1,0:T(8,128)(2,1)S(1)} %pad_maximum_fusion.2), channel_id=1, source_target_pairs={{0,1},{1,0},{2,3},{3,2},{4,5},{5,4},{6,7},{7,6},{8,9},{9,8},{10,11... | collective-permute-start | bytes 786440 | tf_op jit(solution)/shard_map/ppermute | solution.py:354
  5.2 1.6 %collective-permute-start.3 = (bf16[2,256,768]{2,1,0:T(8,128)(2,1)S(1)}, bf16[2,256,768]{2,1,0:T(8,128)(2,1)S(1)}, u32[]{:S(2)}, u32[]{:S(2)}) collective-permute-start(bf16[2,256,768]{2,1,0:T(8,128)(2,1)S(1)} %bitcast.45), channel_id=1, source_target_pairs={{0,2},{1,3},{2,0},{3,1},{4,6},{5,7},{6,4},{7,5},{8,10},{9,11},{10,... | collective-permute-start | bytes 2359304 | tf_op jit(solution)/shard_map/ppermute | solution.py:354
  6.8 1.2 %collective-permute-start.4 = (bf16[2,256,768]{2,1,0:T(8,128)(2,1)S(1)}, bf16[2,256,768]{2,1,0:T(8,128)(2,1)S(1)}, u32[]{:S(2)}, u32[]{:S(2)}) collective-permute-start(bf16[2,256,768]{2,1,0:T(8,128)(2,1)S(1)} %bitcast.44), channel_id=1, source_target_pairs={{0,1},{1,0},{2,3},{3,2},{4,5},{5,4},{6,7},{7,6},{8,9},{9,8},{10,11... | collective-permute-start | bytes 2359304 | tf_op jit(solution)/shard_map/ppermute | solution.py:354
  8.1 5.8 %shard_map.75 = (bf16[2,4,4,64,768]{4,3,2,1,0:T(8,128)(2,1)S(1)}, bf16[2,4,4,64,768]{4,3,2,1,0:T(8,128)(2,1)S(1)}) custom-call(s32[3]{0:T(128)S(1)} %pad_add_fusion.place, bf16[4,256,768]{2,1,0:T(8,128)(2,1)S(1)} %bitcast.37, bf16[4,256,1024]{2,1,0:T(8,128)(2,1)S(1)} %copy-done.3), custom_call_target="tpu_custom_call" | custom-call | tf_op jit(solution)/shard_map/pallas_call | solution.py:74
  15.0 1.3 %collective-permute-start.6 = (bf16[2,256,768]{2,1,0:T(8,128)(2,1)S(1)}, bf16[2,256,768]{2,1,0:T(8,128)(2,1)S(1)}, u32[]{:S(2)}, u32[]{:S(2)}) collective-permute-start(bf16[2,256,768]{2,1,0:T(8,128)(2,1)S(1)} %bitcast.42), channel_id=1, source_target_pairs={{0,1},{1,0},{2,3},{3,2},{4,5},{5,4},{6,7},{7,6},{8,9},{9,8},{10,11... | collective-permute-start | bytes 2359304 | tf_op jit(solution)/shard_map/ppermute | solution.py:354
  17.4 1.6 %shard_map.77 = (bf16[2,4,128,256]{3,2,1,0:T(8,128)(2,1)S(1)}, bf16[2,4,128,256]{3,2,1,0:T(8,128)(2,1)S(1)}) custom-call(s32[3]{0:T(128)S(1)} %pad_add_fusion.place, bf16[4,256,768]{2,1,0:T(8,128)(2,1)S(1)} %bitcast.33, bf16[2,4,4,64,768]{4,3,2,1,0:T(8,128)(2,1)S(1)} %get-tuple-element.129.refs_1_.refs_3_, bf16[4,256,768]{2,1,0:T(8,128)(2,1)S(1)} %bitcast.38, ...), custom_call_target="tpu_custom_call" | custom-call | tf_op jit(solution)/shard_map/pallas_call | solution.py:74
  19.0 7.9 %collective-permute-done.2.refs_1_ = bf16[2,2,4,64,256]{4,3,2,1,0:T(8,128)(2,1)S(1)} collective-permute-done((bf16[2,2,4,64,256]{4,3,2,1,0:T(8,128)(2,1)S(1)}, bf16[2,2,4,64,256]{4,3,2,1,0:T(8,128)(2,1)S(1)}, u32[]{:S(2)}, u32[]{:S(2)}) %collective-permute-start.2) | collective-permute-done | bytes 524320 | tf_op jit(solution)/shard_map/ppermute | solution.py:357
  27.9 1.6 %collective-permute-done.4.refs_1_ = bf16[2,256,768]{2,1,0:T(8,128)(2,1)S(1)} collective-permute-done((bf16[2,256,768]{2,1,0:T(8,128)(2,1)S(1)}, bf16[2,256,768]{2,1,0:T(8,128)(2,1)S(1)}, u32[]{:S(2)}, u32[]{:S(2)}) %collective-permute-start.4) | collective-permute-done | bytes 786464 | tf_op jit(solution)/shard_map/ppermute | solution.py:354
  30.1 1.4 %collective-permute-done.5.refs_0_.first_got = bf16[2,4,128,256]{3,2,1,0:T(8,128)(2,1)S(1)} collective-permute-done((bf16[2,4,128,256]{3,2,1,0:T(8,128)(2,1)S(1)}, bf16[2,4,128,256]{3,2,1,0:T(8,128)(2,1)S(1)}, u32[]{:S(2)}, u32[]{:S(2)}) %collective-permute-start.5) | collective-permute-done | bytes 524320 | tf_op jit(solution)/shard_map/ppermute | solution.py:360
  32.2 2.0 %collective-permute-start.7 = (bf16[1,128,256]{2,1,0:T(8,128)(2,1)S(1)}, bf16[1,128,256]{2,1,0:T(8,128)(2,1)S(1)}, u32[]{:S(2)}, u32[]{:S(2)}) collective-permute-start(bf16[1,128,256]{2,1,0:T(8,128)(2,1)S(1)} %get-tuple-element.90), channel_id=1, source_target_pairs={{0,8},{4,12},{8,0},{12,4},{16,24},{20,28},{24,16},{28,20},{1,9},{5... | collective-permute-start | bytes 196616 | tf_op jit(solution)/shard_map/ppermute | solution.py:357
  34.9 3.1 %shard_map.80 = (bf16[2,4,2,64,768]{4,3,2,1,0:T(8,128)(2,1)S(1)}, bf16[2,4,2,64,768]{4,3,2,1,0:T(8,128)(2,1)S(1)}) custom-call(s32[3]{0:T(128)S(1)} %pad_add_fusion.place, bf16[2,256,768]{2,1,0:T(8,128)(2,1)S(1)} %collective-permute-done.3.x_ref.refs_1_, bf16[2,2,4,256,256]{4,3,2,1,0:T(8,128)(2,1)S(1)} %bitcast.22), custom_call_target="tpu_custom_call" | custom-call | tf_op jit(solution)/shard_map/pallas_call | solution.py:74
  39.5 2.7 %collective-permute-start.11 = (bf16[1,128,256]{2,1,0:T(8,128)(2,1)S(1)}, bf16[1,128,256]{2,1,0:T(8,128)(2,1)S(1)}, u32[]{:S(2)}, u32[]{:S(2)}) collective-permute-start(bf16[1,128,256]{2,1,0:T(8,128)(2,1)S(1)} %shard_map.82), channel_id=1, source_target_pairs={{0,16},{4,20},{8,24},{12,28},{16,0},{20,4},{24,8},{28,12},{1,17},{... | collective-permute-start | bytes 196616 | tf_op jit(solution)/shard_map/ppermute | solution.py:357
  42.1 1.5 %collective-permute-done.12.x_ref.refs_2_ = bf16[2,256,768]{2,1,0:T(8,128)(2,1)S(1)} collective-permute-done((bf16[2,256,768]{2,1,0:T(8,128)(2,1)S(1)}, bf16[2,256,768]{2,1,0:T(8,128)(2,1)S(1)}, u32[]{:S(2)}, u32[]{:S(2)}) %collective-permute-start.12) | collective-permute-done | bytes 786464 | tf_op jit(solution)/shard_map/ppermute | solution.py:354
  43.6 3.1 %shard_map.83 = (bf16[2,4,2,64,768]{4,3,2,1,0:T(8,128)(2,1)S(1)}, bf16[2,4,2,64,768]{4,3,2,1,0:T(8,128)(2,1)S(1)}) custom-call(s32[3]{0:T(128)S(1)} %pad_add_fusion.place, bf16[2,256,768]{2,1,0:T(8,128)(2,1)S(1)} %collective-permute-done.12.x_ref.refs_2_, bf16[2,2,4,256,256]{4,3,2,1,0:T(8,128)(2,1)S(1)} %bitcast.23), custom_call_target="tpu_custom_call" | custom-call | tf_op jit(solution)/shard_map/pallas_call | solution.py:74
  46.8 2.0 %shard_map.84 = (bf16[4,128,256]{2,1,0:T(8,128)(2,1)S(1)}, bf16[2,4,128,256]{3,2,1,0:T(8,128)(2,1)S(1)}, bf16[3,4,128,256]{3,2,1,0:T(8,128)(2,1)S(1)}) custom-call(s32[3]{0:T(128)S(1)} %pad_add_fusion.place, bf16[4,256,768]{2,1,0:T(8,128)(2,1)S(1)} %bitcast.35, bf16[2,256,768]{2,1,0:T(8,128)(2,1)S(1)} %collective-permute-done.4.refs_1_, ...), custom_call_target="tpu_custom_call" | custom-call | tf_op jit(solution)/shard_map/pallas_call | solution.py:74
  49.4 1.5 %shard_map.85 = bf16[4,256,768]{2,1,0:T(8,128)(2,1)S(1)} custom-call(s32[3]{0:T(128)S(1)} %pad_add_fusion.place, bf16[2,2,4,256,256]{4,3,2,1,0:T(8,128)(2,1)S(1)} %bitcast.24, bf16[2,2,4,256,256]{4,3,2,1,0:T(8,128)(2,1)S(1)} %bitcast.25, bf16[2,2,4,256,256]{4,3,2,1,0:T(8,128)(2,1)S(1)} %bitcast.26, ...), custom_call_target="tpu_custom_call" | custom-call | tf_op jit(solution)/shard_map/pallas_call | solution.py:74
  50.9 1.6 %collective-permute-start.18 = (bf16[4,256,768]{2,1,0:T(8,128)(2,1)S(1)}, bf16[4,256,768]{2,1,0:T(8,128)(2,1)S(1)}, u32[]{:S(2)}, u32[]{:S(2)}) collective-permute-start(bf16[4,256,768]{2,1,0:T(8,128)(2,1)S(1)} %shard_map.85), channel_id=1, source_target_pairs={{0,1},{1,0},{2,3},{3,2},{4,5},{5,4},{6,7},{7,6},{8,9},{9,8},{10,11... | collective-permute-start | bytes 4718600 | tf_op jit(solution)/shard_map/ppermute | solution.py:354
  54.0 2.6 %shard_map.87 = (bf16[4,4,64,768]{3,2,1,0:T(8,128)(2,1)S(1)}, bf16[4,2,64,768]{3,2,1,0:T(8,128)(2,1)S(1)}, bf16[4,2,64,768]{3,2,1,0:T(8,128)(2,1)S(1)}, bf16[4,2...) custom-call(s32[3]{0:T(128)S(1)} %pad_add_fusion.place, bf16[4,256,768]{2,1,0:T(8,128)(2,1)S(1)} %bitcast.36, ...), custom_call_target="tpu_custom_call" | custom-call | tf_op jit(solution)/shard_map/pallas_call | solution.py:74
  57.1 2.1 %shard_map.88 = (bf16[3,4,64,256]{3,2,1,0:T(8,128)(2,1)S(1)}, bf16[3,4,64,256]{3,2,1,0:T(8,128)(2,1)S(1)}, bf16[3,4,128,256]{3,2,1,0:T(8,128)(2,1)S(1)}) custom-call(s32[3]{0:T(128)S(1)} %pad_add_fusion.place, bf16[4,256,768]{2,1,0:T(8,128)(2,1)S(1)} %bitcast.39, bf16[2,256,768]{2,1,0:T(8,128)(2,1)S(1)} %collective-permute-done.3.x_ref.refs_1_, ...), custom_call_target="tpu_custom_call" | custom-call | flops 16000000000 | tf_op jit(solution)/shard_map/pallas_call | solution.py:74
  59.8 1.2 %collective-permute-done.16.refs_0_ = bf16[3,4,64,256]{3,2,1,0:T(8,128)(2,1)S(1)} collective-permute-done((bf16[3,4,64,256]{3,2,1,0:T(8,128)(2,1)S(1)}, bf16[3,4,64,256]{3,2,1,0:T(8,128)(2,1)S(1)}, u32[]{:S(2)}, u32[]{:S(2)}) %collective-permute-start.16) | collective-permute-done | bytes 393248 | tf_op jit(solution)/shard_map/ppermute | solution.py:360
  62.3 1.6 %collective-permute-start.20 = (bf16[3,128,256]{2,1,0:T(8,128)(2,1)S(1)}, bf16[3,128,256]{2,1,0:T(8,128)(2,1)S(1)}, u32[]{:S(2)}, u32[]{:S(2)}) collective-permute-start(bf16[3,128,256]{2,1,0:T(8,128)(2,1)S(1)} %get-tuple-element.132), channel_id=1, source_target_pairs={{0,8},{4,12},{8,0},{12,4},{16,24},{20,28},{24,16},{28,20},{1,9},{5... | collective-permute-start | bytes 589832 | tf_op jit(solution)/shard_map/ppermute | solution.py:357
  63.9 4.4 %collective-permute-done.15.got_ref = bf16[2,4,128,256]{3,2,1,0:T(8,128)(2,1)S(1)} collective-permute-done((bf16[2,4,128,256]{3,2,1,0:T(8,128)(2,1)S(1)}, bf16[2,4,128,256]{3,2,1,0:T(8,128)(2,1)S(1)}, u32[]{:S(2)}, u32[]{:S(2)}) %collective-permute-start.15) | collective-permute-done | bytes 524320 | tf_op jit(solution)/shard_map/ppermute | solution.py:357
  69.0 2.6 %collective-permute-start.19 = (bf16[4,128,256]{2,1,0:T(8,128)(2,1)S(1)}, bf16[4,128,256]{2,1,0:T(8,128)(2,1)S(1)}, u32[]{:S(2)}, u32[]{:S(2)}) collective-permute-start(bf16[4,128,256]{2,1,0:T(8,128)(2,1)S(1)} %get-tuple-element.127), channel_id=1, source_target_pairs={{0,16},{4,20},{8,24},{12,28},{16,0},{20,4},{24,8},{28,12},{1,17},{... | collective-permute-start | bytes 786440 | tf_op jit(solution)/shard_map/ppermute | solution.py:357
  71.6 1.5 %shard_map.91.own_ref = f32[4,256,768]{2,1,0:T(8,128)S(1)} custom-call(s32[3]{0:T(128)S(1)} %pad_add_fusion.place, bf16[4,256,1024]{2,1,0:T(8,128)(2,1)S(1)} %copy-done.3, bf16[4,256,1024]{2,1,0:T(8,128)(2,1)S(1)} %copy-done.3, bf16[4,4,64,768]{3,2,1,0:T(8,128)(2,1)S(1)} %shard_map.76.refs_3_.refs_2_, bf16[4,4,64,768]{3,2,1,0:T(8,128)(2,1)S(1)} %get-tuple-element.118.refs_3_), custom_call_target="tpu_custom_call" | custom-call | flops 4000000000 | tf_op jit(solution)/shard_map/pallas_call | solution.py:74
  73.2 1.5 %shard_map.92.own_ref = f32[4,256,768]{2,1,0:T(8,128)S(1)} custom-call(s32[3]{0:T(128)S(1)} %pad_add_fusion.place, bf16[4,1024,256]{2,1,0:T(8,128)(2,1)S(1)} %copy-done, bf16[4,1024,256]{2,1,0:T(8,128)(2,1)S(1)} %copy-done, bf16[4,1024,256]{2,1,0:T(8,128)(2,1)S(1)} %copy-done, bf16[2,4,4,64,768]{4,3,2,1,0:T(8,128)(2,1)S(1)} %get-tuple-element.129.refs_1_.refs_3_, ...), custom_call_target="tpu_custom_call" | custom-call | tf_op jit(solution)/shard_map/pallas_call | solution.py:74
  75.9 10.0 %collective-permute-done.19.got_ref = bf16[4,128,256]{2,1,0:T(8,128)(2,1)S(1)} collective-permute-done((bf16[4,128,256]{2,1,0:T(8,128)(2,1)S(1)}, bf16[4,128,256]{2,1,0:T(8,128)(2,1)S(1)}, u32[]{:S(2)}, u32[]{:S(2)}) %collective-permute-start.19) | collective-permute-done | bytes 262176 | tf_op jit(solution)/shard_map/ppermute | solution.py:357
  86.6 4.3 %collective-permute-start.25 = (bf16[4,128,256]{2,1,0:T(8,128)(2,1)S(1)}, bf16[4,128,256]{2,1,0:T(8,128)(2,1)S(1)}, u32[]{:S(2)}, u32[]{:S(2)}) collective-permute-start(bf16[4,128,256]{2,1,0:T(8,128)(2,1)S(1)} %shard_map.94), channel_id=1, source_target_pairs={{0,0},{1,8},{2,2},{3,10},{4,4},{5,12},{6,6},{7,14},{8,1},{9,9},{10... | collective-permute-start | bytes 786440 | tf_op jit(solution)/shard_map/ppermute | solution.py:661
  90.9 1.9 %shard_map.95 = bf16[4,256,768]{2,1,0:T(8,128)(2,1)} custom-call(s32[3]{0:T(128)S(1)} %pad_add_fusion.place, f32[4,256,768]{2,1,0:T(8,128)S(1)} %shard_map.92.own_ref, bf16[4,256,768]{2,1,0:T(8,128)(2,1)S(1)} %collective-permute-done.18.got_ref), custom_call_target="tpu_custom_call" | custom-call | tf_op jit(solution)/shard_map/pallas_call | solution.py:74
  92.8 1.4 %shard_map.96 = (bf16[2,128,256]{2,1,0:T(8,128)(2,1)S(1)}, f32[4,32,1024]{2,1,0:T(8,128)}) custom-call(s32[3]{0:T(128)S(1)} %pad_add_fusion.place, f32[2,1,128,256]{3,2,1,0:T(8,128)S(1)} %get-tuple-element.89.mine_ref.refs_0_, bf16[1,128,256]{2,1,0:T(8,128)(2,1)S(1)} %collective-permute-done.7.refs_1_, ...), custom_call_target="tpu_custom_call" | custom-call | tf_op jit(solution)/shard_map/pallas_call | solution.py:74
  94.8 1.9 %shard_map.97 = bf16[4,256,768]{2,1,0:T(8,128)(2,1)} custom-call(s32[3]{0:T(128)S(1)} %pad_add_fusion.place, f32[4,256,768]{2,1,0:T(8,128)S(1)} %shard_map.91.own_ref, bf16[4,256,768]{2,1,0:T(8,128)(2,1)S(1)} %collective-permute-done.21.got_ref), custom_call_target="tpu_custom_call" | custom-call | tf_op jit(solution)/shard_map/pallas_call | solution.py:74
  96.7 2.5 %collective-permute-done.24.got_ref = bf16[2,128,256]{2,1,0:T(8,128)(2,1)S(1)} collective-permute-done((bf16[2,128,256]{2,1,0:T(8,128)(2,1)S(1)}, bf16[2,128,256]{2,1,0:T(8,128)(2,1)S(1)}, u32[]{:S(2)}, u32[]{:S(2)}) %collective-permute-start.24) | collective-permute-done | bytes 131104 | tf_op jit(solution)/shard_map/ppermute | solution.py:354
  99.2 1.5 %shard_map.98 = (f32[4,32,1024]{2,1,0:T(8,128)}, f32[4,128,256]{2,1,0:T(8,128)}) custom-call(s32[3]{0:T(128)S(1)} %pad_add_fusion.place, bf16[2,128,256]{2,1,0:T(8,128)(2,1)S(1)} %collective-permute-done.24.got_ref, bf16[4,128,256]{2,1,0:T(8,128)(2,1)S(1)} %collective-permute-done.25.home_ref, ...), custom_call_target="tpu_custom_call", output_to_operand_aliasing={{0}: (3, {})} | custom-call | tf_op jit(solution)/shard_map/pallas_call | solution.py:74
  (60 shorter events, 17.1 us)
Async XLA Ops:
  0.6 4.4 %copy-start.2 = (bf16[1024,768]{1,0:T(8,128)(2,1)S(1)}, bf16[1024,768]{1,0:T(8,128)(2,1)}, u32[]{:S(2)}) copy-start(bf16[1024,768]{1,0:T(8,128)(2,1)} %param.4) | copy-start | bytes 4718596
  1.8 12.1 %collective-permute-start = (bf16[2,4,64,256]{3,2,1,0:T(8,128)(2,1)S(1)}, bf16[2,4,64,256]{3,2,1,0:T(8,128)(2,1)S(1)}, u32[]{:S(2)}, u32[]{:S(2)}) collective-permute-start(bf16[2,4,64,256]{3,2,1,0:T(8,128)(2,1)S(1)} %pad_maximum_fusion.1), channel_id=1, source_target_pairs={{0,2},{1,3},{2,0},{3,1},{4,6},{5,7},{6,4},{7,5},{8,10},{9,11},{10,... | collective-permute-start | bytes 786440 | tf_op jit(solution)/shard_map/ppermute | solution.py:354
  3.4 1.7 %copy-start.1 = (bf16[1024,768]{1,0:T(8,128)(2,1)S(1)}, bf16[1024,768]{1,0:T(8,128)(2,1)}, u32[]{:S(2)}) copy-start(bf16[1024,768]{1,0:T(8,128)(2,1)} %param.5) | copy-start | bytes 4718596
  3.4 10.5 %collective-permute-start.1 = (bf16[2,4,64,256]{3,2,1,0:T(8,128)(2,1)S(1)}, bf16[2,4,64,256]{3,2,1,0:T(8,128)(2,1)S(1)}, u32[]{:S(2)}, u32[]{:S(2)}) collective-permute-start(bf16[2,4,64,256]{3,2,1,0:T(8,128)(2,1)S(1)} %pad_maximum_fusion.2), channel_id=1, source_target_pairs={{0,1},{1,0},{2,3},{3,2},{4,5},{5,4},{6,7},{7,6},{8,9},{9,8},{10,11... | collective-permute-start | bytes 786440 | tf_op jit(solution)/shard_map/ppermute | solution.py:354
  5.1 3.0 %copy-start.3 = (bf16[4,256,1024]{2,1,0:T(8,128)(2,1)S(1)}, bf16[4,256,1024]{2,1,0:T(8,128)(2,1)}, u32[]{:S(2)}) copy-start(bf16[4,256,1024]{2,1,0:T(8,128)(2,1)} %refs_1_.5) | copy-start | bytes 6291460
  5.2 22.7 %collective-permute-start.3 = (bf16[2,256,768]{2,1,0:T(8,128)(2,1)S(1)}, bf16[2,256,768]{2,1,0:T(8,128)(2,1)S(1)}, u32[]{:S(2)}, u32[]{:S(2)}) collective-permute-start(bf16[2,256,768]{2,1,0:T(8,128)(2,1)S(1)} %bitcast.45), channel_id=1, source_target_pairs={{0,2},{1,3},{2,0},{3,1},{4,6},{5,7},{6,4},{7,5},{8,10},{9,11},{10,... | collective-permute-start | bytes 2359304 | tf_op jit(solution)/shard_map/ppermute | solution.py:354
  6.8 22.8 %collective-permute-start.4 = (bf16[2,256,768]{2,1,0:T(8,128)(2,1)S(1)}, bf16[2,256,768]{2,1,0:T(8,128)(2,1)S(1)}, u32[]{:S(2)}, u32[]{:S(2)}) collective-permute-start(bf16[2,256,768]{2,1,0:T(8,128)(2,1)S(1)} %bitcast.44), channel_id=1, source_target_pairs={{0,1},{1,0},{2,3},{3,2},{4,5},{5,4},{6,7},{7,6},{8,9},{9,8},{10,11... | collective-permute-start | bytes 2359304 | tf_op jit(solution)/shard_map/ppermute | solution.py:354
  8.1 8.2 %copy-start = (bf16[4,1024,256]{2,1,0:T(8,128)(2,1)S(1)}, bf16[4,1024,256]{2,1,0:T(8,128)(2,1)}, u32[]{:S(2)}) copy-start(bf16[4,1024,256]{2,1,0:T(8,128)(2,1)} %refs_2_.1) | copy-start | bytes 6291460
  14.0 12.9 %collective-permute-start.2 = (bf16[2,2,4,64,256]{4,3,2,1,0:T(8,128)(2,1)S(1)}, bf16[2,2,4,64,256]{4,3,2,1,0:T(8,128)(2,1)S(1)}, u32[]{:S(2)}, u32[]{:S(2)}) collective-permute-start(bf16[2,2,4,64,256]{4,3,2,1,0:T(8,128)(2,1)S(1)} %pad_maximum_fusion.refs_0_), channel_id=1, source_target_pairs={{0,8},{4,12},{8,0},{12,4},{16,24},{20,28},{24,16},{28,20},{1,9},{5... | collective-permute-start | bytes 1572872 | tf_op jit(solution)/shard_map/ppermute | solution.py:357
  14.5 29.1 %collective-permute-start.12 = (bf16[2,256,768]{2,1,0:T(8,128)(2,1)S(1)}, bf16[2,256,768]{2,1,0:T(8,128)(2,1)S(1)}, u32[]{:S(2)}, u32[]{:S(2)}) collective-permute-start(bf16[2,256,768]{2,1,0:T(8,128)(2,1)S(1)} %bitcast.43), channel_id=1, source_target_pairs={{0,2},{1,3},{2,0},{3,1},{4,6},{5,7},{6,4},{7,5},{8,10},{9,11},{10,... | collective-permute-start | bytes 2359304 | tf_op jit(solution)/shard_map/ppermute | solution.py:354
  15.0 31.7 %collective-permute-start.6 = (bf16[2,256,768]{2,1,0:T(8,128)(2,1)S(1)}, bf16[2,256,768]{2,1,0:T(8,128)(2,1)S(1)}, u32[]{:S(2)}, u32[]{:S(2)}) collective-permute-start(bf16[2,256,768]{2,1,0:T(8,128)(2,1)S(1)} %bitcast.42), channel_id=1, source_target_pairs={{0,1},{1,0},{2,3},{3,2},{4,5},{5,4},{6,7},{7,6},{8,9},{9,8},{10,11... | collective-permute-start | bytes 2359304 | tf_op jit(solution)/shard_map/ppermute | solution.py:354
  29.6 1.9 %collective-permute-start.5 = (bf16[2,4,128,256]{3,2,1,0:T(8,128)(2,1)S(1)}, bf16[2,4,128,256]{3,2,1,0:T(8,128)(2,1)S(1)}, u32[]{:S(2)}, u32[]{:S(2)}) collective-permute-start(bf16[2,4,128,256]{3,2,1,0:T(8,128)(2,1)S(1)} %get-tuple-element.87), channel_id=1, source_target_pairs={{0,4},{4,0},{8,12},{12,8},{16,20},{20,16},{24,28},{28,24},{1,5},{5... | collective-permute-start | bytes 1572872 | tf_op jit(solution)/shard_map/ppermute | solution.py:360
  29.6 2.7 %collective-permute-start.9 = (bf16[2,2,4,64,256]{4,3,2,1,0:T(8,128)(2,1)S(1)}, bf16[2,2,4,64,256]{4,3,2,1,0:T(8,128)(2,1)S(1)}, u32[]{:S(2)}, u32[]{:S(2)}) collective-permute-start(bf16[2,2,4,64,256]{4,3,2,1,0:T(8,128)(2,1)S(1)} %pad_maximum_fusion.refs_0_), channel_id=1, source_target_pairs={{0,4},{4,0},{8,12},{12,8},{16,20},{20,16},{24,28},{28,24},{1,5},{5... | collective-permute-start | bytes 1572872 | tf_op jit(solution)/shard_map/ppermute | solution.py:360
  30.1 4.1 %collective-permute-start.10 = (bf16[2,2,4,64,256]{4,3,2,1,0:T(8,128)(2,1)S(1)}, bf16[2,2,4,64,256]{4,3,2,1,0:T(8,128)(2,1)S(1)}, u32[]{:S(2)}, u32[]{:S(2)}) collective-permute-start(bf16[2,2,4,64,256]{4,3,2,1,0:T(8,128)(2,1)S(1)} %collective-permute-done.2.refs_1_), channel_id=1, source_target_pairs={{0,4},{4,0},{8,12},{12,8},{16,20},{20,16},{24,28},{28,24},{1,5},{5... | collective-permute-start | bytes 1572872 | tf_op jit(solution)/shard_map/ppermute | solution.py:360
  32.1 6.8 %collective-permute-start.8 = (bf16[1,128,256]{2,1,0:T(8,128)(2,1)S(1)}, bf16[1,128,256]{2,1,0:T(8,128)(2,1)S(1)}, u32[]{:S(2)}, u32[]{:S(2)}) collective-permute-start(bf16[1,128,256]{2,1,0:T(8,128)(2,1)S(1)} %get-tuple-element.91), channel_id=1, source_target_pairs={{0,8},{4,12},{8,0},{12,4},{16,24},{20,28},{24,16},{28,20},{1,9},{5... | collective-permute-start | bytes 196616 | tf_op jit(solution)/shard_map/ppermute | solution.py:357
  32.2 6.7 %collective-permute-start.7 = (bf16[1,128,256]{2,1,0:T(8,128)(2,1)S(1)}, bf16[1,128,256]{2,1,0:T(8,128)(2,1)S(1)}, u32[]{:S(2)}, u32[]{:S(2)}) collective-permute-start(bf16[1,128,256]{2,1,0:T(8,128)(2,1)S(1)} %get-tuple-element.90), channel_id=1, source_target_pairs={{0,8},{4,12},{8,0},{12,4},{16,24},{20,28},{24,16},{28,20},{1,9},{5... | collective-permute-start | bytes 196616 | tf_op jit(solution)/shard_map/ppermute | solution.py:357
  39.5 7.2 %collective-permute-start.11 = (bf16[1,128,256]{2,1,0:T(8,128)(2,1)S(1)}, bf16[1,128,256]{2,1,0:T(8,128)(2,1)S(1)}, u32[]{:S(2)}, u32[]{:S(2)}) collective-permute-start(bf16[1,128,256]{2,1,0:T(8,128)(2,1)S(1)} %shard_map.82), channel_id=1, source_target_pairs={{0,16},{4,20},{8,24},{12,28},{16,0},{20,4},{24,8},{28,12},{1,17},{... | collective-permute-start | bytes 196616 | tf_op jit(solution)/shard_map/ppermute | solution.py:357
  48.8 3.7 %collective-permute-start.14 = (bf16[2,4,128,256]{3,2,1,0:T(8,128)(2,1)S(1)}, bf16[2,4,128,256]{3,2,1,0:T(8,128)(2,1)S(1)}, u32[]{:S(2)}, u32[]{:S(2)}) collective-permute-start(bf16[2,4,128,256]{3,2,1,0:T(8,128)(2,1)S(1)} %get-tuple-element.106), channel_id=1, source_target_pairs={{0,4},{4,0},{8,12},{12,8},{16,20},{20,16},{24,28},{28,24},{1,5},{5... | collective-permute-start | bytes 1572872 | tf_op jit(solution)/shard_map/ppermute | solution.py:360
  48.9 3.6 %collective-permute-start.13 = (bf16[4,128,256]{2,1,0:T(8,128)(2,1)S(1)}, bf16[4,128,256]{2,1,0:T(8,128)(2,1)S(1)}, u32[]{:S(2)}, u32[]{:S(2)}) collective-permute-start(bf16[4,128,256]{2,1,0:T(8,128)(2,1)S(1)} %get-tuple-element.105), channel_id=1, source_target_pairs={{0,4},{4,0},{8,12},{12,8},{16,20},{20,16},{24,28},{28,24},{1,5},{5... | collective-permute-start | bytes 786440 | tf_op jit(solution)/shard_map/ppermute | solution.py:360
  50.9 40.0 %collective-permute-start.18 = (bf16[4,256,768]{2,1,0:T(8,128)(2,1)S(1)}, bf16[4,256,768]{2,1,0:T(8,128)(2,1)S(1)}, u32[]{:S(2)}, u32[]{:S(2)}) collective-permute-start(bf16[4,256,768]{2,1,0:T(8,128)(2,1)S(1)} %shard_map.85), channel_id=1, source_target_pairs={{0,1},{1,0},{2,3},{3,2},{4,5},{5,4},{6,7},{7,6},{8,9},{9,8},{10,11... | collective-permute-start | bytes 4718600 | tf_op jit(solution)/shard_map/ppermute | solution.py:354
  53.5 14.9 %collective-permute-start.15 = (bf16[2,4,128,256]{3,2,1,0:T(8,128)(2,1)S(1)}, bf16[2,4,128,256]{3,2,1,0:T(8,128)(2,1)S(1)}, u32[]{:S(2)}, u32[]{:S(2)}) collective-permute-start(bf16[2,4,128,256]{3,2,1,0:T(8,128)(2,1)S(1)} %get-tuple-element.111), channel_id=1, source_target_pairs={{0,8},{4,12},{8,0},{12,4},{16,24},{20,28},{24,16},{28,20},{1,9},{5... | collective-permute-start | bytes 1572872 | tf_op jit(solution)/shard_map/ppermute | solution.py:357
  56.5 38.2 %collective-permute-start.21 = (bf16[4,256,768]{2,1,0:T(8,128)(2,1)S(1)}, bf16[4,256,768]{2,1,0:T(8,128)(2,1)S(1)}, u32[]{:S(2)}, u32[]{:S(2)}) collective-permute-start(bf16[4,256,768]{2,1,0:T(8,128)(2,1)S(1)} %get-tuple-element.116), channel_id=1, source_target_pairs={{0,2},{1,3},{2,0},{3,1},{4,6},{5,7},{6,4},{7,5},{8,10},{9,11},{10,... | collective-permute-start | bytes 4718600 | tf_op jit(solution)/shard_map/ppermute | solution.py:354
  59.2 1.8 %collective-permute-start.16 = (bf16[3,4,64,256]{3,2,1,0:T(8,128)(2,1)S(1)}, bf16[3,4,64,256]{3,2,1,0:T(8,128)(2,1)S(1)}, u32[]{:S(2)}, u32[]{:S(2)}) collective-permute-start(bf16[3,4,64,256]{3,2,1,0:T(8,128)(2,1)S(1)} %get-tuple-element.123), channel_id=1, source_target_pairs={{0,4},{4,0},{8,12},{12,8},{16,20},{20,16},{24,28},{28,24},{1,5},{5... | collective-permute-start | bytes 1179656 | tf_op jit(solution)/shard_map/ppermute | solution.py:360
  59.3 2.3 %collective-permute-start.17 = (bf16[3,4,64,256]{3,2,1,0:T(8,128)(2,1)S(1)}, bf16[3,4,64,256]{3,2,1,0:T(8,128)(2,1)S(1)}, u32[]{:S(2)}, u32[]{:S(2)}) collective-permute-start(bf16[3,4,64,256]{3,2,1,0:T(8,128)(2,1)S(1)} %get-tuple-element.124), channel_id=1, source_target_pairs={{0,4},{4,0},{8,12},{12,8},{16,20},{20,16},{24,28},{28,24},{1,5},{5... | collective-permute-start | bytes 1179656 | tf_op jit(solution)/shard_map/ppermute | solution.py:360
  62.3 12.7 %collective-permute-start.20 = (bf16[3,128,256]{2,1,0:T(8,128)(2,1)S(1)}, bf16[3,128,256]{2,1,0:T(8,128)(2,1)S(1)}, u32[]{:S(2)}, u32[]{:S(2)}) collective-permute-start(bf16[3,128,256]{2,1,0:T(8,128)(2,1)S(1)} %get-tuple-element.132), channel_id=1, source_target_pairs={{0,8},{4,12},{8,0},{12,4},{16,24},{20,28},{24,16},{28,20},{1,9},{5... | collective-permute-start | bytes 589832 | tf_op jit(solution)/shard_map/ppermute | solution.py:357
  69.0 17.0 %collective-permute-start.19 = (bf16[4,128,256]{2,1,0:T(8,128)(2,1)S(1)}, bf16[4,128,256]{2,1,0:T(8,128)(2,1)S(1)}, u32[]{:S(2)}, u32[]{:S(2)}) collective-permute-start(bf16[4,128,256]{2,1,0:T(8,128)(2,1)S(1)} %get-tuple-element.127), channel_id=1, source_target_pairs={{0,16},{4,20},{8,24},{12,28},{16,0},{20,4},{24,8},{28,12},{1,17},{... | collective-permute-start | bytes 786440 | tf_op jit(solution)/shard_map/ppermute | solution.py:357
  74.7 18.1 %collective-permute-start.22 = (bf16[3,128,256]{2,1,0:T(8,128)(2,1)S(1)}, bf16[3,128,256]{2,1,0:T(8,128)(2,1)S(1)}, u32[]{:S(2)}, u32[]{:S(2)}) collective-permute-start(bf16[3,128,256]{2,1,0:T(8,128)(2,1)S(1)} %get-tuple-element.138), channel_id=1, source_target_pairs={{0,8},{4,12},{8,0},{12,4},{16,24},{20,28},{24,16},{28,20},{1,9},{5... | collective-permute-start | bytes 589832 | tf_op jit(solution)/shard_map/ppermute | solution.py:357
  75.5 17.3 %collective-permute-start.23 = (bf16[3,128,256]{2,1,0:T(8,128)(2,1)S(1)}, bf16[3,128,256]{2,1,0:T(8,128)(2,1)S(1)}, u32[]{:S(2)}, u32[]{:S(2)}) collective-permute-start(bf16[3,128,256]{2,1,0:T(8,128)(2,1)S(1)} %shard_map.93), channel_id=1, source_target_pairs={{0,16},{4,20},{8,24},{12,28},{16,0},{20,4},{24,8},{28,12},{1,17},{... | collective-permute-start | bytes 589832 | tf_op jit(solution)/shard_map/ppermute | solution.py:357
  86.6 10.1 %collective-permute-start.25 = (bf16[4,128,256]{2,1,0:T(8,128)(2,1)S(1)}, bf16[4,128,256]{2,1,0:T(8,128)(2,1)S(1)}, u32[]{:S(2)}, u32[]{:S(2)}) collective-permute-start(bf16[4,128,256]{2,1,0:T(8,128)(2,1)S(1)} %shard_map.94), channel_id=1, source_target_pairs={{0,0},{1,8},{2,2},{3,10},{4,4},{5,12},{6,6},{7,14},{8,1},{9,9},{10... | collective-permute-start | bytes 786440 | tf_op jit(solution)/shard_map/ppermute | solution.py:661
  94.2 5.0 %collective-permute-start.24 = (bf16[2,128,256]{2,1,0:T(8,128)(2,1)S(1)}, bf16[2,128,256]{2,1,0:T(8,128)(2,1)S(1)}, u32[]{:S(2)}, u32[]{:S(2)}) collective-permute-start(bf16[2,128,256]{2,1,0:T(8,128)(2,1)S(1)} %get-tuple-element.143), channel_id=1, source_target_pairs={{0,2},{1,3},{2,0},{3,1},{4,6},{5,7},{6,4},{7,5},{8,10},{9,11},{10,... | collective-permute-start | bytes 393224 | tf_op jit(solution)/shard_map/ppermute | solution.py:354

commit v10 on v9

--- a/solution.py
+++ b/solution.py
@@ -530,14 +530,12 @@
         )[0]
 
     def added(own, got):
-        pairs_at = lambda i, p: (i, 0, 0)
-        two = (2, feat, tokens)
         return call(
             add_body,
             place,
-            (local // 2,),
-            [(own, two, pairs_at), (got, two, pairs_at)],
-            [(blocks, BF16, two, pairs_at)],
+            (local,),
+            [(own, one, every), (got, one, every)],
+            [(blocks, BF16, one, every)],
             20,
         )[0]
 
@@ -620,7 +618,6 @@
         16,
     )
     got_d = send_z(send_d, 2)
-    got_u = send_z(after((send_u,), send_d)[0], 1)
 
     up_b = after((up_blocks,), send_d)[0]
     own_grads = call_once(
@@ -640,8 +637,9 @@
 
     own_out = outputs_of(0, after((hid,), own_grads)[0], F32)
     far_u = after((far_u,), own_out)[0]
-    send_u = up_again(mine_u, far_u)
-    last_u = send_z(send_u, 2)
+    next_u = up_again(mine_u, far_u)
+    last_u = send_z(next_u, 2)
+    got_u = send_z(after((send_u,), next_u)[0], 1)
 
     got_d = after((got_d,), send_u)[0]
     sum_d = call(

time: 101 us -> 101 us (level)
  transfers between devices with their start and end apart: 26 -> 26, of which waited for: 11 -> 11; matrix products, arithmetic and copies ran while one was open for 1% -> 1% of each run, Pallas kernels for 35% -> 36%
where the time goes in v10:
time: 101 us
  Pallas kernels  39.9 us (40%)
  waiting for transfers between devices  31.7 us (31%)
  starting transfers between devices  26 us (26%)
  local copies, waits for them, and re-layouts  2.33 us (2%)
    pallas_call x24, Pallas kernels, call(): pl.pallas_call(body, grid_spec=pltpu.PrefetchScalarGridSpec(num_scalar_pr...  39.9 us
    ppermute x9, waiting for transfers between devices, send_z(): return lax.ppermute(value, 'dp', [(d, d ^ 2 * hop) for d in range(n_dp)])  22.3 us
    ppermute x9, starting transfers between devices, send_z(): return lax.ppermute(value, 'dp', [(d, d ^ 2 * hop) for d in range(n_dp)])  10.6 us
    ppermute x9, starting transfers between devices, send(): lax.ppermute(value, 'tensor', [(t, t ^ hop) for t in range(n_tensor)])  9.39 us
    ppermute x9, waiting for transfers between devices, send(): lax.ppermute(value, 'tensor', [(t, t ^ hop) for t in range(n_tensor)])  6.18 us
    ppermute x1, starting transfers between devices, square_device(): home_d = lax.ppermute(sum_d, ('dp', 'tensor'), swaps)  4.3 us
    ppermute x7, waiting for transfers between devices, send_core(): return lax.ppermute(value, 'dp', [(d, d ^ 1) for d in range(n_dp)])  3.24 us
  transfers between devices with their start and end apart: 26, of which 11 were waited for; matrix products, arithmetic and copies ran while one was open for 1% of the time, Pallas kernels for 36%

profile of v10, /device:TPU:12, one launch (start us, length us, event | category | flops | bytes accessed | tf_op | source)
XLA Modules:
  0.0 101.1 jit_solution(1591204846608938863)
XLA Ops:
  3.4 1.6 %collective-permute-start.1 = (bf16[2,4,64,256]{3,2,1,0:T(8,128)(2,1)S(1)}, bf16[2,4,64,256]{3,2,1,0:T(8,128)(2,1)S(1)}, u32[]{:S(2)}, u32[]{:S(2)}) collective-permute-start(bf16[2,4,64,256]{3,2,1,0:T(8,128)(2,1)S(1)} %pad_maximum_fusion.2), channel_id=1, source_target_pairs={{0,1},{1,0},{2,3},{3,2},{4,5},{5,4},{6,7},{7,6},{8,9},{9,8},{10,11... | collective-permute-start | bytes 786440 | tf_op jit(solution)/shard_map/ppermute | solution.py:354
  5.2 1.6 %collective-permute-start.3 = (bf16[2,256,768]{2,1,0:T(8,128)(2,1)S(1)}, bf16[2,256,768]{2,1,0:T(8,128)(2,1)S(1)}, u32[]{:S(2)}, u32[]{:S(2)}) collective-permute-start(bf16[2,256,768]{2,1,0:T(8,128)(2,1)S(1)} %bitcast.45), channel_id=1, source_target_pairs={{0,2},{1,3},{2,0},{3,1},{4,6},{5,7},{6,4},{7,5},{8,10},{9,11},{10,... | collective-permute-start | bytes 2359304 | tf_op jit(solution)/shard_map/ppermute | solution.py:354
  6.8 1.2 %collective-permute-start.4 = (bf16[2,256,768]{2,1,0:T(8,128)(2,1)S(1)}, bf16[2,256,768]{2,1,0:T(8,128)(2,1)S(1)}, u32[]{:S(2)}, u32[]{:S(2)}) collective-permute-start(bf16[2,256,768]{2,1,0:T(8,128)(2,1)S(1)} %bitcast.44), channel_id=1, source_target_pairs={{0,1},{1,0},{2,3},{3,2},{4,5},{5,4},{6,7},{7,6},{8,9},{9,8},{10,11... | collective-permute-start | bytes 2359304 | tf_op jit(solution)/shard_map/ppermute | solution.py:354
  8.1 5.8 %shard_map.75 = (bf16[2,4,4,64,768]{4,3,2,1,0:T(8,128)(2,1)S(1)}, bf16[2,4,4,64,768]{4,3,2,1,0:T(8,128)(2,1)S(1)}) custom-call(s32[3]{0:T(128)S(1)} %pad_add_fusion.place, bf16[4,256,768]{2,1,0:T(8,128)(2,1)S(1)} %bitcast.37, bf16[4,256,1024]{2,1,0:T(8,128)(2,1)S(1)} %copy-done.3), custom_call_target="tpu_custom_call" | custom-call | tf_op jit(solution)/shard_map/pallas_call | solution.py:74
  15.0 1.3 %collective-permute-start.6 = (bf16[2,256,768]{2,1,0:T(8,128)(2,1)S(1)}, bf16[2,256,768]{2,1,0:T(8,128)(2,1)S(1)}, u32[]{:S(2)}, u32[]{:S(2)}) collective-permute-start(bf16[2,256,768]{2,1,0:T(8,128)(2,1)S(1)} %bitcast.42), channel_id=1, source_target_pairs={{0,1},{1,0},{2,3},{3,2},{4,5},{5,4},{6,7},{7,6},{8,9},{9,8},{10,11... | collective-permute-start | bytes 2359304 | tf_op jit(solution)/shard_map/ppermute | solution.py:354
  17.4 1.6 %shard_map.77 = (bf16[2,4,128,256]{3,2,1,0:T(8,128)(2,1)S(1)}, bf16[2,4,128,256]{3,2,1,0:T(8,128)(2,1)S(1)}) custom-call(s32[3]{0:T(128)S(1)} %pad_add_fusion.place, bf16[4,256,768]{2,1,0:T(8,128)(2,1)S(1)} %bitcast.33, bf16[2,4,4,64,768]{4,3,2,1,0:T(8,128)(2,1)S(1)} %get-tuple-element.129.refs_1_.refs_3_, bf16[4,256,768]{2,1,0:T(8,128)(2,1)S(1)} %bitcast.38, ...), custom_call_target="tpu_custom_call" | custom-call | tf_op jit(solution)/shard_map/pallas_call | solution.py:74
  19.0 7.9 %collective-permute-done.2.refs_1_ = bf16[2,2,4,64,256]{4,3,2,1,0:T(8,128)(2,1)S(1)} collective-permute-done((bf16[2,2,4,64,256]{4,3,2,1,0:T(8,128)(2,1)S(1)}, bf16[2,2,4,64,256]{4,3,2,1,0:T(8,128)(2,1)S(1)}, u32[]{:S(2)}, u32[]{:S(2)}) %collective-permute-start.2) | collective-permute-done | bytes 524320 | tf_op jit(solution)/shard_map/ppermute | solution.py:357
  27.9 1.6 %collective-permute-done.4.refs_1_ = bf16[2,256,768]{2,1,0:T(8,128)(2,1)S(1)} collective-permute-done((bf16[2,256,768]{2,1,0:T(8,128)(2,1)S(1)}, bf16[2,256,768]{2,1,0:T(8,128)(2,1)S(1)}, u32[]{:S(2)}, u32[]{:S(2)}) %collective-permute-start.4) | collective-permute-done | bytes 786464 | tf_op jit(solution)/shard_map/ppermute | solution.py:354
  30.1 1.4 %collective-permute-done.5.refs_0_.first_got = bf16[2,4,128,256]{3,2,1,0:T(8,128)(2,1)S(1)} collective-permute-done((bf16[2,4,128,256]{3,2,1,0:T(8,128)(2,1)S(1)}, bf16[2,4,128,256]{3,2,1,0:T(8,128)(2,1)S(1)}, u32[]{:S(2)}, u32[]{:S(2)}) %collective-permute-start.5) | collective-permute-done | bytes 524320 | tf_op jit(solution)/shard_map/ppermute | solution.py:360
  32.2 2.0 %collective-permute-start.7 = (bf16[1,128,256]{2,1,0:T(8,128)(2,1)S(1)}, bf16[1,128,256]{2,1,0:T(8,128)(2,1)S(1)}, u32[]{:S(2)}, u32[]{:S(2)}) collective-permute-start(bf16[1,128,256]{2,1,0:T(8,128)(2,1)S(1)} %get-tuple-element.90), channel_id=1, source_target_pairs={{0,8},{4,12},{8,0},{12,4},{16,24},{20,28},{24,16},{28,20},{1,9},{5... | collective-permute-start | bytes 196616 | tf_op jit(solution)/shard_map/ppermute | solution.py:357
  34.9 3.1 %shard_map.80 = (bf16[2,4,2,64,768]{4,3,2,1,0:T(8,128)(2,1)S(1)}, bf16[2,4,2,64,768]{4,3,2,1,0:T(8,128)(2,1)S(1)}) custom-call(s32[3]{0:T(128)S(1)} %pad_add_fusion.place, bf16[2,256,768]{2,1,0:T(8,128)(2,1)S(1)} %collective-permute-done.3.x_ref.refs_1_, bf16[2,2,4,256,256]{4,3,2,1,0:T(8,128)(2,1)S(1)} %bitcast.22), custom_call_target="tpu_custom_call" | custom-call | tf_op jit(solution)/shard_map/pallas_call | solution.py:74
  39.5 2.7 %collective-permute-start.11 = (bf16[1,128,256]{2,1,0:T(8,128)(2,1)S(1)}, bf16[1,128,256]{2,1,0:T(8,128)(2,1)S(1)}, u32[]{:S(2)}, u32[]{:S(2)}) collective-permute-start(bf16[1,128,256]{2,1,0:T(8,128)(2,1)S(1)} %shard_map.82), channel_id=1, source_target_pairs={{0,16},{4,20},{8,24},{12,28},{16,0},{20,4},{24,8},{28,12},{1,17},{... | collective-permute-start | bytes 196616 | tf_op jit(solution)/shard_map/ppermute | solution.py:357
  42.1 1.5 %collective-permute-done.12.x_ref.refs_2_ = bf16[2,256,768]{2,1,0:T(8,128)(2,1)S(1)} collective-permute-done((bf16[2,256,768]{2,1,0:T(8,128)(2,1)S(1)}, bf16[2,256,768]{2,1,0:T(8,128)(2,1)S(1)}, u32[]{:S(2)}, u32[]{:S(2)}) %collective-permute-start.12) | collective-permute-done | bytes 786464 | tf_op jit(solution)/shard_map/ppermute | solution.py:354
  43.6 3.1 %shard_map.83 = (bf16[2,4,2,64,768]{4,3,2,1,0:T(8,128)(2,1)S(1)}, bf16[2,4,2,64,768]{4,3,2,1,0:T(8,128)(2,1)S(1)}) custom-call(s32[3]{0:T(128)S(1)} %pad_add_fusion.place, bf16[2,256,768]{2,1,0:T(8,128)(2,1)S(1)} %collective-permute-done.12.x_ref.refs_2_, bf16[2,2,4,256,256]{4,3,2,1,0:T(8,128)(2,1)S(1)} %bitcast.23), custom_call_target="tpu_custom_call" | custom-call | tf_op jit(solution)/shard_map/pallas_call | solution.py:74
  46.8 2.0 %shard_map.84 = (bf16[4,128,256]{2,1,0:T(8,128)(2,1)S(1)}, bf16[2,4,128,256]{3,2,1,0:T(8,128)(2,1)S(1)}, bf16[3,4,128,256]{3,2,1,0:T(8,128)(2,1)S(1)}) custom-call(s32[3]{0:T(128)S(1)} %pad_add_fusion.place, bf16[4,256,768]{2,1,0:T(8,128)(2,1)S(1)} %bitcast.35, bf16[2,256,768]{2,1,0:T(8,128)(2,1)S(1)} %collective-permute-done.4.refs_1_, ...), custom_call_target="tpu_custom_call" | custom-call | tf_op jit(solution)/shard_map/pallas_call | solution.py:74
  49.4 1.5 %shard_map.85 = bf16[4,256,768]{2,1,0:T(8,128)(2,1)S(1)} custom-call(s32[3]{0:T(128)S(1)} %pad_add_fusion.place, bf16[2,2,4,256,256]{4,3,2,1,0:T(8,128)(2,1)S(1)} %bitcast.24, bf16[2,2,4,256,256]{4,3,2,1,0:T(8,128)(2,1)S(1)} %bitcast.25, bf16[2,2,4,256,256]{4,3,2,1,0:T(8,128)(2,1)S(1)} %bitcast.26, ...), custom_call_target="tpu_custom_call" | custom-call | tf_op jit(solution)/shard_map/pallas_call | solution.py:74
  50.9 1.6 %collective-permute-start.18 = (bf16[4,256,768]{2,1,0:T(8,128)(2,1)S(1)}, bf16[4,256,768]{2,1,0:T(8,128)(2,1)S(1)}, u32[]{:S(2)}, u32[]{:S(2)}) collective-permute-start(bf16[4,256,768]{2,1,0:T(8,128)(2,1)S(1)} %shard_map.85), channel_id=1, source_target_pairs={{0,1},{1,0},{2,3},{3,2},{4,5},{5,4},{6,7},{7,6},{8,9},{9,8},{10,11... | collective-permute-start | bytes 4718600 | tf_op jit(solution)/shard_map/ppermute | solution.py:354
  54.0 2.6 %shard_map.87 = (bf16[4,4,64,768]{3,2,1,0:T(8,128)(2,1)S(1)}, bf16[4,2,64,768]{3,2,1,0:T(8,128)(2,1)S(1)}, bf16[4,2,64,768]{3,2,1,0:T(8,128)(2,1)S(1)}, bf16[4,2...) custom-call(s32[3]{0:T(128)S(1)} %pad_add_fusion.place, bf16[4,256,768]{2,1,0:T(8,128)(2,1)S(1)} %bitcast.36, ...), custom_call_target="tpu_custom_call" | custom-call | tf_op jit(solution)/shard_map/pallas_call | solution.py:74
  57.1 2.1 %shard_map.88 = (bf16[3,4,64,256]{3,2,1,0:T(8,128)(2,1)S(1)}, bf16[3,4,64,256]{3,2,1,0:T(8,128)(2,1)S(1)}, bf16[3,4,128,256]{3,2,1,0:T(8,128)(2,1)S(1)}) custom-call(s32[3]{0:T(128)S(1)} %pad_add_fusion.place, bf16[4,256,768]{2,1,0:T(8,128)(2,1)S(1)} %bitcast.39, bf16[2,256,768]{2,1,0:T(8,128)(2,1)S(1)} %collective-permute-done.3.x_ref.refs_1_, ...), custom_call_target="tpu_custom_call" | custom-call | flops 16000000000 | tf_op jit(solution)/shard_map/pallas_call | solution.py:74
  59.8 1.2 %collective-permute-done.16.refs_0_ = bf16[3,4,64,256]{3,2,1,0:T(8,128)(2,1)S(1)} collective-permute-done((bf16[3,4,64,256]{3,2,1,0:T(8,128)(2,1)S(1)}, bf16[3,4,64,256]{3,2,1,0:T(8,128)(2,1)S(1)}, u32[]{:S(2)}, u32[]{:S(2)}) %collective-permute-start.16) | collective-permute-done | bytes 393248 | tf_op jit(solution)/shard_map/ppermute | solution.py:360
  62.3 1.6 %collective-permute-start.21 = (bf16[3,128,256]{2,1,0:T(8,128)(2,1)S(1)}, bf16[3,128,256]{2,1,0:T(8,128)(2,1)S(1)}, u32[]{:S(2)}, u32[]{:S(2)}) collective-permute-start(bf16[3,128,256]{2,1,0:T(8,128)(2,1)S(1)} %get-tuple-element.136), channel_id=1, source_target_pairs={{0,8},{4,12},{8,0},{12,4},{16,24},{20,28},{24,16},{28,20},{1,9},{5... | collective-permute-start | bytes 589832 | tf_op jit(solution)/shard_map/ppermute | solution.py:357
  63.9 4.4 %collective-permute-done.15.got_ref = bf16[2,4,128,256]{3,2,1,0:T(8,128)(2,1)S(1)} collective-permute-done((bf16[2,4,128,256]{3,2,1,0:T(8,128)(2,1)S(1)}, bf16[2,4,128,256]{3,2,1,0:T(8,128)(2,1)S(1)}, u32[]{:S(2)}, u32[]{:S(2)}) %collective-permute-start.15) | collective-permute-done | bytes 524320 | tf_op jit(solution)/shard_map/ppermute | solution.py:357
  69.0 2.6 %collective-permute-start.19 = (bf16[4,128,256]{2,1,0:T(8,128)(2,1)S(1)}, bf16[4,128,256]{2,1,0:T(8,128)(2,1)S(1)}, u32[]{:S(2)}, u32[]{:S(2)}) collective-permute-start(bf16[4,128,256]{2,1,0:T(8,128)(2,1)S(1)} %get-tuple-element.127), channel_id=1, source_target_pairs={{0,16},{4,20},{8,24},{12,28},{16,0},{20,4},{24,8},{28,12},{1,17},{... | collective-permute-start | bytes 786440 | tf_op jit(solution)/shard_map/ppermute | solution.py:357
  71.6 1.5 %shard_map.91.own_ref = f32[4,256,768]{2,1,0:T(8,128)S(1)} custom-call(s32[3]{0:T(128)S(1)} %pad_add_fusion.place, bf16[4,256,1024]{2,1,0:T(8,128)(2,1)S(1)} %copy-done.3, bf16[4,256,1024]{2,1,0:T(8,128)(2,1)S(1)} %copy-done.3, bf16[4,4,64,768]{3,2,1,0:T(8,128)(2,1)S(1)} %shard_map.76.refs_3_.refs_2_, bf16[4,4,64,768]{3,2,1,0:T(8,128)(2,1)S(1)} %get-tuple-element.118.refs_3_), custom_call_target="tpu_custom_call" | custom-call | flops 4000000000 | tf_op jit(solution)/shard_map/pallas_call | solution.py:74
  73.2 1.5 %shard_map.92.own_ref = f32[4,256,768]{2,1,0:T(8,128)S(1)} custom-call(s32[3]{0:T(128)S(1)} %pad_add_fusion.place, bf16[4,1024,256]{2,1,0:T(8,128)(2,1)S(1)} %copy-done, bf16[4,1024,256]{2,1,0:T(8,128)(2,1)S(1)} %copy-done, bf16[4,1024,256]{2,1,0:T(8,128)(2,1)S(1)} %copy-done, bf16[2,4,4,64,768]{4,3,2,1,0:T(8,128)(2,1)S(1)} %get-tuple-element.129.refs_1_.refs_3_, ...), custom_call_target="tpu_custom_call" | custom-call | tf_op jit(solution)/shard_map/pallas_call | solution.py:74
  76.0 10.0 %collective-permute-done.19.got_ref = bf16[4,128,256]{2,1,0:T(8,128)(2,1)S(1)} collective-permute-done((bf16[4,128,256]{2,1,0:T(8,128)(2,1)S(1)}, bf16[4,128,256]{2,1,0:T(8,128)(2,1)S(1)}, u32[]{:S(2)}, u32[]{:S(2)}) %collective-permute-start.19) | collective-permute-done | bytes 262176 | tf_op jit(solution)/shard_map/ppermute | solution.py:357
  86.6 4.3 %collective-permute-start.25 = (bf16[4,128,256]{2,1,0:T(8,128)(2,1)S(1)}, bf16[4,128,256]{2,1,0:T(8,128)(2,1)S(1)}, u32[]{:S(2)}, u32[]{:S(2)}) collective-permute-start(bf16[4,128,256]{2,1,0:T(8,128)(2,1)S(1)} %shard_map.93), channel_id=1, source_target_pairs={{0,0},{1,8},{2,2},{3,10},{4,4},{5,12},{6,6},{7,14},{8,1},{9,9},{10... | collective-permute-start | bytes 786440 | tf_op jit(solution)/shard_map/ppermute | solution.py:659
  90.9 2.4 %shard_map.94 = bf16[4,256,768]{2,1,0:T(8,128)(2,1)} custom-call(s32[3]{0:T(128)S(1)} %pad_add_fusion.place, f32[4,256,768]{2,1,0:T(8,128)S(1)} %shard_map.92.own_ref, bf16[4,256,768]{2,1,0:T(8,128)(2,1)S(1)} %collective-permute-done.18.got_ref), custom_call_target="tpu_custom_call" | custom-call | tf_op jit(solution)/shard_map/pallas_call | solution.py:74
  93.3 1.4 %shard_map.96 = (bf16[2,128,256]{2,1,0:T(8,128)(2,1)S(1)}, f32[4,32,1024]{2,1,0:T(8,128)}) custom-call(s32[3]{0:T(128)S(1)} %pad_add_fusion.place, f32[2,1,128,256]{3,2,1,0:T(8,128)S(1)} %get-tuple-element.89.mine_ref.refs_0_, bf16[1,128,256]{2,1,0:T(8,128)(2,1)S(1)} %collective-permute-done.7.refs_1_, ...), custom_call_target="tpu_custom_call" | custom-call | tf_op jit(solution)/shard_map/pallas_call | solution.py:74
  95.2 2.4 %shard_map.97 = bf16[4,256,768]{2,1,0:T(8,128)(2,1)} custom-call(s32[3]{0:T(128)S(1)} %pad_add_fusion.place, f32[4,256,768]{2,1,0:T(8,128)S(1)} %shard_map.91.own_ref, bf16[4,256,768]{2,1,0:T(8,128)(2,1)S(1)} %collective-permute-done.20.got_ref), custom_call_target="tpu_custom_call" | custom-call | tf_op jit(solution)/shard_map/pallas_call | solution.py:74
  97.6 2.0 %collective-permute-done.24.got_ref = bf16[2,128,256]{2,1,0:T(8,128)(2,1)S(1)} collective-permute-done((bf16[2,128,256]{2,1,0:T(8,128)(2,1)S(1)}, bf16[2,128,256]{2,1,0:T(8,128)(2,1)S(1)}, u32[]{:S(2)}, u32[]{:S(2)}) %collective-permute-start.24) | collective-permute-done | bytes 131104 | tf_op jit(solution)/shard_map/ppermute | solution.py:354
  99.6 1.5 %shard_map.98 = (f32[4,32,1024]{2,1,0:T(8,128)}, f32[4,128,256]{2,1,0:T(8,128)}) custom-call(s32[3]{0:T(128)S(1)} %pad_add_fusion.place, bf16[2,128,256]{2,1,0:T(8,128)(2,1)S(1)} %collective-permute-done.24.got_ref, bf16[4,128,256]{2,1,0:T(8,128)(2,1)S(1)} %collective-permute-done.25.home_ref, ...), custom_call_target="tpu_custom_call", output_to_operand_aliasing={{0}: (3, {})} | custom-call | tf_op jit(solution)/shard_map/pallas_call | solution.py:74
  (60 shorter events, 17.2 us)
Async XLA Ops:
  0.6 4.4 %copy-start.2 = (bf16[1024,768]{1,0:T(8,128)(2,1)S(1)}, bf16[1024,768]{1,0:T(8,128)(2,1)}, u32[]{:S(2)}) copy-start(bf16[1024,768]{1,0:T(8,128)(2,1)} %param.4) | copy-start | bytes 4718596
  1.8 12.1 %collective-permute-start = (bf16[2,4,64,256]{3,2,1,0:T(8,128)(2,1)S(1)}, bf16[2,4,64,256]{3,2,1,0:T(8,128)(2,1)S(1)}, u32[]{:S(2)}, u32[]{:S(2)}) collective-permute-start(bf16[2,4,64,256]{3,2,1,0:T(8,128)(2,1)S(1)} %pad_maximum_fusion.1), channel_id=1, source_target_pairs={{0,2},{1,3},{2,0},{3,1},{4,6},{5,7},{6,4},{7,5},{8,10},{9,11},{10,... | collective-permute-start | bytes 786440 | tf_op jit(solution)/shard_map/ppermute | solution.py:354
  3.4 1.7 %copy-start.1 = (bf16[1024,768]{1,0:T(8,128)(2,1)S(1)}, bf16[1024,768]{1,0:T(8,128)(2,1)}, u32[]{:S(2)}) copy-start(bf16[1024,768]{1,0:T(8,128)(2,1)} %param.5) | copy-start | bytes 4718596
  3.4 10.5 %collective-permute-start.1 = (bf16[2,4,64,256]{3,2,1,0:T(8,128)(2,1)S(1)}, bf16[2,4,64,256]{3,2,1,0:T(8,128)(2,1)S(1)}, u32[]{:S(2)}, u32[]{:S(2)}) collective-permute-start(bf16[2,4,64,256]{3,2,1,0:T(8,128)(2,1)S(1)} %pad_maximum_fusion.2), channel_id=1, source_target_pairs={{0,1},{1,0},{2,3},{3,2},{4,5},{5,4},{6,7},{7,6},{8,9},{9,8},{10,11... | collective-permute-start | bytes 786440 | tf_op jit(solution)/shard_map/ppermute | solution.py:354
  5.1 3.0 %copy-start.3 = (bf16[4,256,1024]{2,1,0:T(8,128)(2,1)S(1)}, bf16[4,256,1024]{2,1,0:T(8,128)(2,1)}, u32[]{:S(2)}) copy-start(bf16[4,256,1024]{2,1,0:T(8,128)(2,1)} %refs_1_.5) | copy-start | bytes 6291460
  5.2 22.7 %collective-permute-start.3 = (bf16[2,256,768]{2,1,0:T(8,128)(2,1)S(1)}, bf16[2,256,768]{2,1,0:T(8,128)(2,1)S(1)}, u32[]{:S(2)}, u32[]{:S(2)}) collective-permute-start(bf16[2,256,768]{2,1,0:T(8,128)(2,1)S(1)} %bitcast.45), channel_id=1, source_target_pairs={{0,2},{1,3},{2,0},{3,1},{4,6},{5,7},{6,4},{7,5},{8,10},{9,11},{10,... | collective-permute-start | bytes 2359304 | tf_op jit(solution)/shard_map/ppermute | solution.py:354
  6.8 22.8 %collective-permute-start.4 = (bf16[2,256,768]{2,1,0:T(8,128)(2,1)S(1)}, bf16[2,256,768]{2,1,0:T(8,128)(2,1)S(1)}, u32[]{:S(2)}, u32[]{:S(2)}) collective-permute-start(bf16[2,256,768]{2,1,0:T(8,128)(2,1)S(1)} %bitcast.44), channel_id=1, source_target_pairs={{0,1},{1,0},{2,3},{3,2},{4,5},{5,4},{6,7},{7,6},{8,9},{9,8},{10,11... | collective-permute-start | bytes 2359304 | tf_op jit(solution)/shard_map/ppermute | solution.py:354
  8.1 8.2 %copy-start = (bf16[4,1024,256]{2,1,0:T(8,128)(2,1)S(1)}, bf16[4,1024,256]{2,1,0:T(8,128)(2,1)}, u32[]{:S(2)}) copy-start(bf16[4,1024,256]{2,1,0:T(8,128)(2,1)} %refs_2_.1) | copy-start | bytes 6291460
  14.0 12.9 %collective-permute-start.2 = (bf16[2,2,4,64,256]{4,3,2,1,0:T(8,128)(2,1)S(1)}, bf16[2,2,4,64,256]{4,3,2,1,0:T(8,128)(2,1)S(1)}, u32[]{:S(2)}, u32[]{:S(2)}) collective-permute-start(bf16[2,2,4,64,256]{4,3,2,1,0:T(8,128)(2,1)S(1)} %pad_maximum_fusion.refs_0_), channel_id=1, source_target_pairs={{0,8},{4,12},{8,0},{12,4},{16,24},{20,28},{24,16},{28,20},{1,9},{5... | collective-permute-start | bytes 1572872 | tf_op jit(solution)/shard_map/ppermute | solution.py:357
  14.5 29.1 %collective-permute-start.12 = (bf16[2,256,768]{2,1,0:T(8,128)(2,1)S(1)}, bf16[2,256,768]{2,1,0:T(8,128)(2,1)S(1)}, u32[]{:S(2)}, u32[]{:S(2)}) collective-permute-start(bf16[2,256,768]{2,1,0:T(8,128)(2,1)S(1)} %bitcast.43), channel_id=1, source_target_pairs={{0,2},{1,3},{2,0},{3,1},{4,6},{5,7},{6,4},{7,5},{8,10},{9,11},{10,... | collective-permute-start | bytes 2359304 | tf_op jit(solution)/shard_map/ppermute | solution.py:354
  15.0 31.7 %collective-permute-start.6 = (bf16[2,256,768]{2,1,0:T(8,128)(2,1)S(1)}, bf16[2,256,768]{2,1,0:T(8,128)(2,1)S(1)}, u32[]{:S(2)}, u32[]{:S(2)}) collective-permute-start(bf16[2,256,768]{2,1,0:T(8,128)(2,1)S(1)} %bitcast.42), channel_id=1, source_target_pairs={{0,1},{1,0},{2,3},{3,2},{4,5},{5,4},{6,7},{7,6},{8,9},{9,8},{10,11... | collective-permute-start | bytes 2359304 | tf_op jit(solution)/shard_map/ppermute | solution.py:354
  29.6 1.9 %collective-permute-start.5 = (bf16[2,4,128,256]{3,2,1,0:T(8,128)(2,1)S(1)}, bf16[2,4,128,256]{3,2,1,0:T(8,128)(2,1)S(1)}, u32[]{:S(2)}, u32[]{:S(2)}) collective-permute-start(bf16[2,4,128,256]{3,2,1,0:T(8,128)(2,1)S(1)} %get-tuple-element.87), channel_id=1, source_target_pairs={{0,4},{4,0},{8,12},{12,8},{16,20},{20,16},{24,28},{28,24},{1,5},{5... | collective-permute-start | bytes 1572872 | tf_op jit(solution)/shard_map/ppermute | solution.py:360
  29.6 2.7 %collective-permute-start.9 = (bf16[2,2,4,64,256]{4,3,2,1,0:T(8,128)(2,1)S(1)}, bf16[2,2,4,64,256]{4,3,2,1,0:T(8,128)(2,1)S(1)}, u32[]{:S(2)}, u32[]{:S(2)}) collective-permute-start(bf16[2,2,4,64,256]{4,3,2,1,0:T(8,128)(2,1)S(1)} %pad_maximum_fusion.refs_0_), channel_id=1, source_target_pairs={{0,4},{4,0},{8,12},{12,8},{16,20},{20,16},{24,28},{28,24},{1,5},{5... | collective-permute-start | bytes 1572872 | tf_op jit(solution)/shard_map/ppermute | solution.py:360
  30.1 4.1 %collective-permute-start.10 = (bf16[2,2,4,64,256]{4,3,2,1,0:T(8,128)(2,1)S(1)}, bf16[2,2,4,64,256]{4,3,2,1,0:T(8,128)(2,1)S(1)}, u32[]{:S(2)}, u32[]{:S(2)}) collective-permute-start(bf16[2,2,4,64,256]{4,3,2,1,0:T(8,128)(2,1)S(1)} %collective-permute-done.2.refs_1_), channel_id=1, source_target_pairs={{0,4},{4,0},{8,12},{12,8},{16,20},{20,16},{24,28},{28,24},{1,5},{5... | collective-permute-start | bytes 1572872 | tf_op jit(solution)/shard_map/ppermute | solution.py:360
  32.1 6.8 %collective-permute-start.8 = (bf16[1,128,256]{2,1,0:T(8,128)(2,1)S(1)}, bf16[1,128,256]{2,1,0:T(8,128)(2,1)S(1)}, u32[]{:S(2)}, u32[]{:S(2)}) collective-permute-start(bf16[1,128,256]{2,1,0:T(8,128)(2,1)S(1)} %get-tuple-element.91), channel_id=1, source_target_pairs={{0,8},{4,12},{8,0},{12,4},{16,24},{20,28},{24,16},{28,20},{1,9},{5... | collective-permute-start | bytes 196616 | tf_op jit(solution)/shard_map/ppermute | solution.py:357
  32.2 6.7 %collective-permute-start.7 = (bf16[1,128,256]{2,1,0:T(8,128)(2,1)S(1)}, bf16[1,128,256]{2,1,0:T(8,128)(2,1)S(1)}, u32[]{:S(2)}, u32[]{:S(2)}) collective-permute-start(bf16[1,128,256]{2,1,0:T(8,128)(2,1)S(1)} %get-tuple-element.90), channel_id=1, source_target_pairs={{0,8},{4,12},{8,0},{12,4},{16,24},{20,28},{24,16},{28,20},{1,9},{5... | collective-permute-start | bytes 196616 | tf_op jit(solution)/shard_map/ppermute | solution.py:357
  39.5 7.2 %collective-permute-start.11 = (bf16[1,128,256]{2,1,0:T(8,128)(2,1)S(1)}, bf16[1,128,256]{2,1,0:T(8,128)(2,1)S(1)}, u32[]{:S(2)}, u32[]{:S(2)}) collective-permute-start(bf16[1,128,256]{2,1,0:T(8,128)(2,1)S(1)} %shard_map.82), channel_id=1, source_target_pairs={{0,16},{4,20},{8,24},{12,28},{16,0},{20,4},{24,8},{28,12},{1,17},{... | collective-permute-start | bytes 196616 | tf_op jit(solution)/shard_map/ppermute | solution.py:357
  48.8 3.7 %collective-permute-start.14 = (bf16[2,4,128,256]{3,2,1,0:T(8,128)(2,1)S(1)}, bf16[2,4,128,256]{3,2,1,0:T(8,128)(2,1)S(1)}, u32[]{:S(2)}, u32[]{:S(2)}) collective-permute-start(bf16[2,4,128,256]{3,2,1,0:T(8,128)(2,1)S(1)} %get-tuple-element.106), channel_id=1, source_target_pairs={{0,4},{4,0},{8,12},{12,8},{16,20},{20,16},{24,28},{28,24},{1,5},{5... | collective-permute-start | bytes 1572872 | tf_op jit(solution)/shard_map/ppermute | solution.py:360
  48.9 3.6 %collective-permute-start.13 = (bf16[4,128,256]{2,1,0:T(8,128)(2,1)S(1)}, bf16[4,128,256]{2,1,0:T(8,128)(2,1)S(1)}, u32[]{:S(2)}, u32[]{:S(2)}) collective-permute-start(bf16[4,128,256]{2,1,0:T(8,128)(2,1)S(1)} %get-tuple-element.105), channel_id=1, source_target_pairs={{0,4},{4,0},{8,12},{12,8},{16,20},{20,16},{24,28},{28,24},{1,5},{5... | collective-permute-start | bytes 786440 | tf_op jit(solution)/shard_map/ppermute | solution.py:360
  50.9 40.0 %collective-permute-start.18 = (bf16[4,256,768]{2,1,0:T(8,128)(2,1)S(1)}, bf16[4,256,768]{2,1,0:T(8,128)(2,1)S(1)}, u32[]{:S(2)}, u32[]{:S(2)}) collective-permute-start(bf16[4,256,768]{2,1,0:T(8,128)(2,1)S(1)} %shard_map.85), channel_id=1, source_target_pairs={{0,1},{1,0},{2,3},{3,2},{4,5},{5,4},{6,7},{7,6},{8,9},{9,8},{10,11... | collective-permute-start | bytes 4718600 | tf_op jit(solution)/shard_map/ppermute | solution.py:354
  53.5 14.9 %collective-permute-start.15 = (bf16[2,4,128,256]{3,2,1,0:T(8,128)(2,1)S(1)}, bf16[2,4,128,256]{3,2,1,0:T(8,128)(2,1)S(1)}, u32[]{:S(2)}, u32[]{:S(2)}) collective-permute-start(bf16[2,4,128,256]{3,2,1,0:T(8,128)(2,1)S(1)} %get-tuple-element.111), channel_id=1, source_target_pairs={{0,8},{4,12},{8,0},{12,4},{16,24},{20,28},{24,16},{28,20},{1,9},{5... | collective-permute-start | bytes 1572872 | tf_op jit(solution)/shard_map/ppermute | solution.py:357
  56.5 38.7 %collective-permute-start.20 = (bf16[4,256,768]{2,1,0:T(8,128)(2,1)S(1)}, bf16[4,256,768]{2,1,0:T(8,128)(2,1)S(1)}, u32[]{:S(2)}, u32[]{:S(2)}) collective-permute-start(bf16[4,256,768]{2,1,0:T(8,128)(2,1)S(1)} %get-tuple-element.116), channel_id=1, source_target_pairs={{0,2},{1,3},{2,0},{3,1},{4,6},{5,7},{6,4},{7,5},{8,10},{9,11},{10,... | collective-permute-start | bytes 4718600 | tf_op jit(solution)/shard_map/ppermute | solution.py:354
  59.2 1.8 %collective-permute-start.16 = (bf16[3,4,64,256]{3,2,1,0:T(8,128)(2,1)S(1)}, bf16[3,4,64,256]{3,2,1,0:T(8,128)(2,1)S(1)}, u32[]{:S(2)}, u32[]{:S(2)}) collective-permute-start(bf16[3,4,64,256]{3,2,1,0:T(8,128)(2,1)S(1)} %get-tuple-element.123), channel_id=1, source_target_pairs={{0,4},{4,0},{8,12},{12,8},{16,20},{20,16},{24,28},{28,24},{1,5},{5... | collective-permute-start | bytes 1179656 | tf_op jit(solution)/shard_map/ppermute | solution.py:360
  59.3 2.3 %collective-permute-start.17 = (bf16[3,4,64,256]{3,2,1,0:T(8,128)(2,1)S(1)}, bf16[3,4,64,256]{3,2,1,0:T(8,128)(2,1)S(1)}, u32[]{:S(2)}, u32[]{:S(2)}) collective-permute-start(bf16[3,4,64,256]{3,2,1,0:T(8,128)(2,1)S(1)} %get-tuple-element.124), channel_id=1, source_target_pairs={{0,4},{4,0},{8,12},{12,8},{16,20},{20,16},{24,28},{28,24},{1,5},{5... | collective-permute-start | bytes 1179656 | tf_op jit(solution)/shard_map/ppermute | solution.py:360
  62.3 12.5 %collective-permute-start.21 = (bf16[3,128,256]{2,1,0:T(8,128)(2,1)S(1)}, bf16[3,128,256]{2,1,0:T(8,128)(2,1)S(1)}, u32[]{:S(2)}, u32[]{:S(2)}) collective-permute-start(bf16[3,128,256]{2,1,0:T(8,128)(2,1)S(1)} %get-tuple-element.136), channel_id=1, source_target_pairs={{0,8},{4,12},{8,0},{12,4},{16,24},{20,28},{24,16},{28,20},{1,9},{5... | collective-permute-start | bytes 589832 | tf_op jit(solution)/shard_map/ppermute | solution.py:357
  69.0 17.0 %collective-permute-start.19 = (bf16[4,128,256]{2,1,0:T(8,128)(2,1)S(1)}, bf16[4,128,256]{2,1,0:T(8,128)(2,1)S(1)}, u32[]{:S(2)}, u32[]{:S(2)}) collective-permute-start(bf16[4,128,256]{2,1,0:T(8,128)(2,1)S(1)} %get-tuple-element.127), channel_id=1, source_target_pairs={{0,16},{4,20},{8,24},{12,28},{16,0},{20,4},{24,8},{28,12},{1,17},{... | collective-permute-start | bytes 786440 | tf_op jit(solution)/shard_map/ppermute | solution.py:357
  75.3 18.0 %collective-permute-start.22 = (bf16[3,128,256]{2,1,0:T(8,128)(2,1)S(1)}, bf16[3,128,256]{2,1,0:T(8,128)(2,1)S(1)}, u32[]{:S(2)}, u32[]{:S(2)}) collective-permute-start(bf16[3,128,256]{2,1,0:T(8,128)(2,1)S(1)} %get-tuple-element.138), channel_id=1, source_target_pairs={{0,8},{4,12},{8,0},{12,4},{16,24},{20,28},{24,16},{28,20},{1,9},{5... | collective-permute-start | bytes 589832 | tf_op jit(solution)/shard_map/ppermute | solution.py:357
  75.6 17.7 %collective-permute-start.23 = (bf16[3,128,256]{2,1,0:T(8,128)(2,1)S(1)}, bf16[3,128,256]{2,1,0:T(8,128)(2,1)S(1)}, u32[]{:S(2)}, u32[]{:S(2)}) collective-permute-start(bf16[3,128,256]{2,1,0:T(8,128)(2,1)S(1)} %shard_map.95), channel_id=1, source_target_pairs={{0,16},{4,20},{8,24},{12,28},{16,0},{20,4},{24,8},{28,12},{1,17},{... | collective-permute-start | bytes 589832 | tf_op jit(solution)/shard_map/ppermute | solution.py:357
  86.6 11.1 %collective-permute-start.25 = (bf16[4,128,256]{2,1,0:T(8,128)(2,1)S(1)}, bf16[4,128,256]{2,1,0:T(8,128)(2,1)S(1)}, u32[]{:S(2)}, u32[]{:S(2)}) collective-permute-start(bf16[4,128,256]{2,1,0:T(8,128)(2,1)S(1)} %shard_map.93), channel_id=1, source_target_pairs={{0,0},{1,8},{2,2},{3,10},{4,4},{5,12},{6,6},{7,14},{8,1},{9,9},{10... | collective-permute-start | bytes 786440 | tf_op jit(solution)/shard_map/ppermute | solution.py:659
  94.7 5.0 %collective-permute-start.24 = (bf16[2,128,256]{2,1,0:T(8,128)(2,1)S(1)}, bf16[2,128,256]{2,1,0:T(8,128)(2,1)S(1)}, u32[]{:S(2)}, u32[]{:S(2)}) collective-permute-start(bf16[2,128,256]{2,1,0:T(8,128)(2,1)S(1)} %get-tuple-element.143), channel_id=1, source_target_pairs={{0,2},{1,3},{2,0},{3,1},{4,6},{5,7},{6,4},{7,5},{8,10},{9,11},{10,... | collective-permute-start | bytes 393224 | tf_op jit(solution)/shard_map/ppermute | solution.py:354
